TPU v7x, 32 devices: a whole 2x2x4 slice. The times are simulated.
32 devices in a mesh: docs: 2 (over y), ctx: 8 (over z, x), heads: 2 (over core).
Axes of the slice: x: 2, y: 2, z: 4, core: 2. Of those that a mesh axis runs over, the one named last changes fastest.
Arguments:
- queries_nope: bfloat16 [1536, 512], P(('docs', 'ctx'), 'heads'), parts along dimension 0, may hold values from -6 to 6
- queries_rope: bfloat16 [1536, 256], P(('docs', 'ctx'), 'heads'), parts along dimension 0, may hold values from -13 to 13
- latent: bfloat16 [1536, 512], P(('docs', 'ctx')), parts along dimension 0, may hold values from -6 to 6
- key_rope: bfloat16 [1536, 64], P(('docs', 'ctx')), parts along dimension 0, may hold values from -6 to 6
- key_up: bfloat16 [512, 512], P(None, 'heads'), may hold values from -0.25 to 0.25
- value_up: bfloat16 [512, 512], P(None, 'heads'), may hold values from -0.25 to 0.25
- out_proj: bfloat16 [512, 7168], P('heads'), may hold values from -0.25 to 0.25
- span_order: int32 [32], P('docs'), parts along dimension 0, may hold values from 0 to 15, as said below
Outputs:
- attn_out: bfloat16 [1536, 7168], P(('docs', 'ctx'), 'heads'), parts along dimension 0
There are 2 independent parts, one for each index of `docs`. A program takes and returns all parts, laid end to end along the dimension named above; an argument that names none is the same for every part. Nothing has to cross between parts.
Inputs may be any that keep to these rules, and one draw needn't show every extreme that they name: `span_order`: a permutation of the spans in which entries 2 d and 2 d + 1 sum to 15.
All inputs are finite; a program needn't handle non-finite values.
Results may differ from a plain program's by a relative error of at most 0.01.
Values may be sent and summed in bfloat16 or wider, within the bound.
No kernel may reach another device: no remote copies, remote signals or barrier semaphores. Data moves between devices by JAX's collectives and lax.ppermute only.
A program may use at most 64 MiB of HBM per device.

v0:
```python
import math

import jax
import jax.numpy as jnp
from jax import lax
from jax.sharding import PartitionSpec as P

DC = 512
DH = 128
DR = 64


def block_size(count, limit):
    return max((size for size in range(1, min(count, limit) + 1) if count % size == 0))


def gathered_positions(orders, first_row, count, span_rows):
    row_ids = first_row + jnp.arange(count, dtype=jnp.int32)
    return jnp.take(orders, row_ids // span_rows) * span_rows + row_ids % span_rows


def per_device(
    queries_nope, queries_rope, latent, key_rope, key_up, value_up, out_proj, span_order
):
    tok_rows = latent.shape[0]
    span_rows = tok_rows // 2
    head_count = key_up.shape[1] // DH
    score_scale = 1.0 / math.sqrt(DH + DR)
    own_index = lax.axis_index("ctx")
    own_pair = lax.dynamic_slice_in_dim(span_order, 2 * own_index, 2, 0)
    swapped = own_pair[0] > own_pair[1]

    def earlier_first(array):
        turned = jnp.concatenate([array[span_rows:], array[:span_rows]], axis=0)
        return jnp.where(swapped, turned, array)

    order_low = jnp.minimum(span_order[0::2], span_order[1::2])
    order_high = jnp.maximum(span_order[0::2], span_order[1::2])
    offsets = jnp.arange(span_rows, dtype=jnp.int32)
    low_own = lax.dynamic_slice_in_dim(order_low, own_index, 1, 0)
    high_own = lax.dynamic_slice_in_dim(order_high, own_index, 1, 0)
    query_pos = jnp.concatenate([low_own * span_rows + offsets, high_own * span_rows + offsets])
    nope_query = earlier_first(queries_nope).reshape(tok_rows, head_count, DH)
    rope_query = earlier_first(queries_rope).reshape(tok_rows, head_count, DR)
    key_up_heads = key_up.reshape(DC, head_count, DH)
    query_latent = jnp.einsum(
        "qhd,chd->qhc", nope_query, key_up_heads, preferred_element_type=jnp.float32
    ).astype(jnp.bfloat16)
    latent_sorted = earlier_first(latent)
    rope_sorted = earlier_first(key_rope)

    def update(running, q_latent, q_rope, q_pos, k_latent, k_rope, k_pos):
        run_max, run_total, weighted = running
        scores = jnp.einsum("qhc,kc->hqk", q_latent, k_latent, preferred_element_type=jnp.float32)
        scores = scores + jnp.einsum(
            "qhr,kr->hqk", q_rope, k_rope, preferred_element_type=jnp.float32
        )
        scores = scores * score_scale
        allowed = k_pos[None, None, :] <= q_pos[None, :, None]
        block_max = jnp.max(jnp.where(allowed, scores, jnp.float32(-1e30)), axis=-1)
        new_max = jnp.maximum(run_max, block_max)
        rescale = jnp.exp(run_max - new_max)
        exponent = jnp.where(allowed, jnp.exp(scores - new_max[:, :, None]), jnp.float32(0.0))
        new_total = run_total * rescale + jnp.sum(exponent, axis=-1)
        added = jnp.einsum(
            "hqk,kc->qhc",
            exponent.astype(jnp.bfloat16),
            k_latent,
            preferred_element_type=jnp.float32,
        )
        return (new_max, new_total, weighted * rescale.T[:, :, None] + added)

    initial = (
        jnp.full((head_count, tok_rows), -1e30, jnp.float32),
        jnp.zeros((head_count, tok_rows), jnp.float32),
        jnp.zeros((tok_rows, head_count, DC), jnp.float32),
    )
    low_latent_own = latent_sorted[:span_rows]
    high_latent_own = latent_sorted[span_rows:]
    low_rope_own = rope_sorted[:span_rows]
    high_rope_own = rope_sorted[span_rows:]
    pieces = (
        lax.all_gather(low_latent_own, "ctx", axis=0, tiled=True),
        lax.all_gather(low_rope_own, "ctx", axis=0, tiled=True),
        lax.all_gather(high_latent_own, "ctx", axis=0, tiled=True),
        lax.all_gather(high_rope_own, "ctx", axis=0, tiled=True),
    )
    first_row = jnp.int32(0)
    count = pieces[0].shape[0]
    block_rows = block_size(count, 256)

    def one_block(block_index, state_now):
        offset = block_index * block_rows
        low_latent = lax.dynamic_slice_in_dim(pieces[0], offset, block_rows, 0)
        low_rope = lax.dynamic_slice_in_dim(pieces[1], offset, block_rows, 0)
        high_latent = lax.dynamic_slice_in_dim(pieces[2], offset, block_rows, 0)
        high_rope = lax.dynamic_slice_in_dim(pieces[3], offset, block_rows, 0)
        low_pos = gathered_positions(order_low, first_row + offset, block_rows, span_rows)
        high_pos = gathered_positions(order_high, first_row + offset, block_rows, span_rows)
        both_latent = jnp.concatenate([low_latent, high_latent], axis=0)
        both_rope = jnp.concatenate([low_rope, high_rope], axis=0)
        both_pos = jnp.concatenate([low_pos, high_pos])
        return update(
            state_now, query_latent, rope_query, query_pos, both_latent, both_rope, both_pos
        )

    running = lax.fori_loop(0, count // block_rows, one_block, initial)
    run_total = running[1]
    weighted = running[2]
    context = (weighted / run_total.T[:, :, None]).astype(jnp.bfloat16)
    value_heads = value_up.reshape(DC, head_count, DH)
    per_head = jnp.einsum("qhc,chd->qhd", context, value_heads, preferred_element_type=jnp.float32)
    heads_out = earlier_first(per_head.reshape(tok_rows, head_count * DH).astype(jnp.bfloat16))
    partial_out = jnp.dot(heads_out, out_proj, preferred_element_type=jnp.float32)
    return lax.psum_scatter(
        partial_out.astype(jnp.bfloat16), "heads", scatter_dimension=1, tiled=True
    )


def solution(mesh):
    in_specs = (
        P(("docs", "ctx"), "heads"),
        P(("docs", "ctx"), "heads"),
        P(("docs", "ctx"), None),
        P(("docs", "ctx"), None),
        P(None, "heads"),
        P(None, "heads"),
        P("heads", None),
        P("docs"),
    )
    out_specs = P(("docs", "ctx"), "heads")
    return jax.shard_map(
        per_device, mesh=mesh, in_specs=in_specs, out_specs=out_specs, check_vma=False
    )
```

profile of v0, /device:TPU:0, one launch (start us, length us, event | category | flops | bytes accessed | tf_op | source)
XLA Modules:
  0.0 190.1 jit_solution(6547126733324897240)
XLA Ops:
  6.5 0.8 slice.65
  7.3 0.7 slice.64
  8.1 0.7 dynamic_slice.49
  8.8 0.6 dynamic_slice.50
  9.5 0.6 dynamic_slice.51
  11.3 0.6 fusion.48
  11.9 0.8 copy.22
  14.0 0.7 fusion.44
  14.7 0.7 maximum_select_fusion.3
  15.6 0.8 fusion.43
  16.4 32.3 %all_gather.15 = bf16[384,64]{1,0:T(8,128)(2,1)S(1)} all-gather(bf16[48,64]{1,0:T(8,128)(2,1)S(1)} %get-tuple-element.443), channel_id=1, replica_groups=mesh['docs'=2,'ctx'=8,'heads'=2] {'ctx'}, dimensions={0}, use_global_device_ids=true | all-gather | bytes 55296 | tf_op jit(solution)/shard_map/all_gather | solution.py:86
  48.8 30.6 %all_gather.14 = bf16[384,64]{1,0:T(8,128)(2,1)S(1)} all-gather(bf16[48,64]{1,0:T(8,128)(2,1)S(1)} %get-tuple-element.444), channel_id=1, replica_groups=mesh['docs'=2,'ctx'=8,'heads'=2] {'ctx'}, dimensions={0}, use_global_device_ids=true | all-gather | bytes 55296 | tf_op jit(solution)/shard_map/all_gather | solution.py:84
  79.4 0.8 fusion.42
  80.3 0.9 maximum_select_fusion
  81.2 31.1 %all_gather.13 = bf16[384,512]{1,0:T(8,128)(2,1)S(1)} all-gather(bf16[48,512]{1,0:T(8,128)(2,1)S(1)} %get-tuple-element.433), channel_id=1, replica_groups=mesh['docs'=2,'ctx'=8,'heads'=2] {'ctx'}, dimensions={0}, use_global_device_ids=true | all-gather | bytes 442368 | tf_op jit(solution)/shard_map/all_gather | solution.py:85
  112.3 30.9 %all_gather.12 = bf16[384,512]{1,0:T(8,128)(2,1)S(1)} all-gather(bf16[48,512]{1,0:T(8,128)(2,1)S(1)} %get-tuple-element.434), channel_id=1, replica_groups=mesh['docs'=2,'ctx'=8,'heads'=2] {'ctx'}, dimensions={0}, use_global_device_ids=true | all-gather | bytes 442368 | tf_op jit(solution)/shard_map/all_gather | solution.py:83
  143.4 1.0 fusion.23
  144.4 24.7 %while.20 = (s32[]{:T(128)}, f32[2,96]{1,0:T(2,128)S(1)}, f32[2,96]{1,0:T(2,128)S(1)}, f32[96,2,512]{2,0,1:T(8,128)S(1)}, s32[8]{0:T(128)S(1)}, /*index=5*/s32[8...) while((s32[]{:T(128)}, f32[2,96]{1,0:T(2,128)S(1)}, ...), condition=%wide.region_3.5_spmd.clone, body=%wide.region_0.4_spmd.clone.sunk | while | flops 163187712 | bytes 4369199 | solution.py:107
  144.4 0.7 fusion.71
  145.1 5.0 %fusion.72 = s32[192]{0:T(256)S(1)} fusion(s32[]{:T(128)} %bitcast.112, s32[]{:T(128)} %bitcast.113, s32[]{:T(128)} %bitcast.114, s32[]{:T(128)} %bitcast.115, s32[]{:T(128)} %bitcast.116, s32[]{:T(128)} %bitcast.117, s32[]{:T(128)} %bitcast.118, s32[]{:T(128)} %bitcast.119, s32[]{:T(128)S(6)} %mul.126), kind=kLoop, calls=%fused_computation.25.clone.1 | loop fusion | flops 6912 | bytes 804 | tf_op jit(solution)/shard_map/while/body/eval_jaxpr/add | solution.py:19
  150.2 5.0 %fusion.73 = s32[192]{0:T(256)S(1)} fusion(s32[]{:T(128)} %bitcast.120, s32[]{:T(128)} %bitcast.121, s32[]{:T(128)} %bitcast.122, s32[]{:T(128)} %bitcast.123, s32[]{:T(128)} %bitcast.124, s32[]{:T(128)} %bitcast.125, s32[]{:T(128)} %bitcast.126, s32[]{:T(128)} %bitcast.127, s32[]{:T(128)S(6)} %mul.126), kind=kLoop, calls=%fused_computation.27.clone.1 | loop fusion | flops 6912 | bytes 804 | tf_op jit(solution)/shard_map/while/body/eval_jaxpr/add | solution.py:19
  155.5 0.3 fusion.74
  155.8 0.4 select_reduce_fusion.2
  156.2 0.4 fusion.78
  156.8 0.7 fusion.71
  157.5 5.0 %fusion.72 = s32[192]{0:T(256)S(1)} fusion(s32[]{:T(128)} %bitcast.112, s32[]{:T(128)} %bitcast.113, s32[]{:T(128)} %bitcast.114, s32[]{:T(128)} %bitcast.115, s32[]{:T(128)} %bitcast.116, s32[]{:T(128)} %bitcast.117, s32[]{:T(128)} %bitcast.118, s32[]{:T(128)} %bitcast.119, s32[]{:T(128)S(6)} %mul.126), kind=kLoop, calls=%fused_computation.25.clone.1 | loop fusion | flops 6912 | bytes 804 | tf_op jit(solution)/shard_map/while/body/eval_jaxpr/add | solution.py:19
  162.5 5.0 %fusion.73 = s32[192]{0:T(256)S(1)} fusion(s32[]{:T(128)} %bitcast.120, s32[]{:T(128)} %bitcast.121, s32[]{:T(128)} %bitcast.122, s32[]{:T(128)} %bitcast.123, s32[]{:T(128)} %bitcast.124, s32[]{:T(128)} %bitcast.125, s32[]{:T(128)} %bitcast.126, s32[]{:T(128)} %bitcast.127, s32[]{:T(128)S(6)} %mul.126), kind=kLoop, calls=%fused_computation.27.clone.1 | loop fusion | flops 6912 | bytes 804 | tf_op jit(solution)/shard_map/while/body/eval_jaxpr/add | solution.py:19
  167.8 0.3 fusion.74
  168.1 0.4 select_reduce_fusion.2
  168.5 0.4 fusion.78
  169.4 3.9 %convolution_convert_fusion = bf16[96,7168]{1,0:T(8,128)(2,1)} fusion(bf16[256,7168]{1,0:T(8,128)(2,1)} %param.18, bf16[48,256]{1,0:T(8,128)(2,1)S(1)} %bitcast.131, bf16[48,256]{1,0:T(8,128)(2,1)S(1)} %bitcast.130, pred[]{:T(512)} %bitcast, bf16[2,96,128]{2,1,0:T(8,128)(2,1)S(1)} %convolution_convert_fusion.2), kind=kOutput, calls=%fused_computation.52 | convolution fusion | flops 353132544 | bytes 5144577 | tf_op jit(solution)/shard_map/dot_general | solution.py:114
  173.3 9.9 %reduce-scatter.2.cloned.1.call-done = bf16[96,3584]{1,0:T(8,128)(2,1)} async-done(((bf16[96,7168]{1,0:T(8,128)(2,1)}), bf16[96,3584]{1,0:T(8,128)(2,1)}) %reduce-scatter.2.cloned.1.call-update) | async-done | bytes 688144 | tf_op jit(solution)/shard_map/reduce_scatter | solution.py:115
  (39 shorter events, 1.8 us)
Async XLA Ops:
  6.5 136.8 %copy-start = (bf16[512,256]{1,0:T(8,128)(2,1)S(1)}, bf16[512,256]{1,0:T(8,128)(2,1)}, u32[]{:S(2)}) copy-start(bf16[512,256]{1,0:T(8,128)(2,1)} %param.16) | copy-start | bytes 786436
  6.5 176.7 %reduce-scatter.2.cloned.1.call-start = ((), (), s32[]{:S(2)}) async-start(), calls=%async_computation.1 | async-start | bytes 2064384 | tf_op jit(solution)/shard_map/reduce_scatter | solution.py:115
  144.4 24.7 %copy-start.1 = (bf16[512,256]{1,0:T(8,128)(2,1)S(1)}, bf16[512,256]{1,0:T(8,128)(2,1)}, u32[]{:S(2)}) copy-start(bf16[512,256]{1,0:T(8,128)(2,1)} %param.17) | copy-start | bytes 786436
Sparse Core Ops, SparseCore 0:
  173.5 9.7 reduce-scatter.1
where the time goes:
time: 191 us; the launch traced here: 190 us
  blocking collectives  125 us (65%)
  other arithmetic  22.6 us (12%)
  between operations  16 us (8%)
  waiting for transfers between devices  9.96 us (5%)
  local copies, waits for them, and re-layouts  9.29 us (5%)
  matrix products  7.15 us (4%)
    all_gather x1, blocking collectives, per_device(): lax.all_gather(high_rope_own, 'ctx', axis=0, tiled=True)  32.3 us
    all_gather x1, blocking collectives, per_device(): lax.all_gather(high_latent_own, 'ctx', axis=0, tiled=True)  31.1 us
    all_gather x1, blocking collectives, per_device(): lax.all_gather(low_latent_own, 'ctx', axis=0, tiled=True)  30.9 us
    all_gather x1, blocking collectives, per_device(): lax.all_gather(low_rope_own, 'ctx', axis=0, tiled=True)  30.6 us
    add x4, other arithmetic, gathered_positions(): jnp.take(orders, row_ids // span_rows) * span_rows + row_ids % span_rows  20 us
    reduce_scatter x1, waiting for transfers between devices, per_device(): lax.psum_scatter(partial_out.astype(jnp.bfloat16), 'heads', scatter_dimen...  9.94 us
    dot_general x1, matrix products, per_device(): jnp.dot(heads_out, out_proj, preferred_element_type=jnp.float32)  3.86 us
  transfers between devices with their start and end apart: 1, of which 1 were waited for; matrix products, arithmetic and copies ran while one was open for 0% of the time, Pallas kernels for 0%

commit v1 on v0

v1 whole, which is shorter than its diff:
```python
import functools
import math

import jax
import jax.numpy as jnp
from jax import lax
from jax.experimental import pallas as pl
from jax.experimental.pallas import tpu as pltpu
from jax.sharding import PartitionSpec as P

DC = 512
DH = 128
DR = 64
BF16 = jnp.bfloat16
F32 = jnp.float32
SMALL_VMEM = 20 * 1024 * 1024
LARGE_VMEM = 56 * 1024 * 1024
DIRECT_LIMIT = 8
BLOCK_CHUNKS = 8


def vmem():
    return pl.BlockSpec(memory_space=pltpu.VMEM)


def smem():
    return pl.BlockSpec(memory_space=pltpu.SMEM)


def query_kernel(nope_own, nope_other, rope_own, rope_other, up_own, up_other, out_ref):
    rows = nope_own.shape[0]
    heads = nope_own.shape[1] // DH
    for group, (nope, rope, up) in enumerate(
        ((nope_own, rope_own, up_own), (nope_other, rope_other, up_other))
    ):
        for head in range(heads):
            part = pl.ds((group * heads + head) * rows, rows)
            latent = lax.dot_general(
                nope[:, head * DH : (head + 1) * DH],
                up[:, head * DH : (head + 1) * DH],
                (((1,), (1,)), ((), ())),
                preferred_element_type=F32,
            )
            out_ref[part, :DC] = latent.astype(BF16)
            out_ref[part, DC:] = rope[:, head * DR : (head + 1) * DR]


def attend_kernel(
    chunks, blocks, direct, place, span_order, queries, latent, key_rope, *rest
):
    if direct:
        near = rest[: chunks - 1]
        far = rest[chunks - 1 : 2 * chunks - 2]
        rest = rest[2 * chunks - 2 :]
    else:
        near, far = rest[:2]
        rest = rest[2:]
    (value_own, value_other, proj_own, proj_other, out_ref) = rest[:5]
    keys, running_max, running_sum, context, heads_out = rest[5:]
    rows = latent.shape[0]
    span_rows = rows // 2
    query_rows = queries.shape[0]
    copies = query_rows // rows
    block_rows = keys.shape[0]
    own_index = place[0]
    core = place[1]
    scale = math.log2(math.e) / math.sqrt(DH + DR)

    @pl.when(pl.program_id(0) == 0)
    def attention():
        row = lax.broadcasted_iota(jnp.int32, (rows, 1), 0)
        query_pos = jnp.where(
            row < span_rows,
            span_order[2 * own_index] * span_rows + row,
            span_order[2 * own_index + 1] * span_rows + row - span_rows,
        )
        query_pos = jnp.concatenate([query_pos] * copies, axis=0)
        column = lax.broadcasted_iota(jnp.int32, (1, block_rows), 1)

        def one_block(block, first):
            key_pos = jnp.zeros((1, block_rows), jnp.int32)
            for index in range(block_rows // rows):
                base = index * rows
                if direct:
                    owner = own_index ^ index
                else:
                    owner = block * (block_rows // rows) + index
                for side in range(2):
                    start = base + side * span_rows
                    if direct and index == 0:
                        span = 2 * owner + side
                        keys[pl.ds(start, span_rows), :DC] = latent[pl.ds(side * span_rows, span_rows), :]
                        keys[pl.ds(start, span_rows), DC:] = key_rope[pl.ds(side * span_rows, span_rows), :]
                    else:
                        span = 2 * owner + (core if side == 0 else 1 - core)
                        source = (near, far)[side]
                        if direct:
                            keys[pl.ds(start, span_rows), :] = source[index - 1][...]
                        else:
                            keys[pl.ds(start, span_rows), :] = source[owner]
                    key_pos = jnp.where(
                        column >= start, span_order[span] * span_rows + column - start, key_pos
                    )
            scores = lax.dot_general(
                queries[...], keys[...], (((1,), (1,)), ((), ())), preferred_element_type=F32
            )
            allowed = key_pos <= query_pos
            scores = jnp.where(allowed, scores, F32(-1e30))
            top = jnp.max(scores, axis=-1, keepdims=True)
            if not first:
                old = running_max[...]
                top = jnp.maximum(old, top)
                rescale = jnp.exp2((old - top) * scale)
            expo = jnp.where(allowed, jnp.exp2((scores - top) * scale), F32(0.0))
            total = jnp.sum(expo, axis=-1, keepdims=True)
            added = jnp.dot(expo.astype(BF16), keys[:, :DC], preferred_element_type=F32)
            if not first:
                total = running_sum[...] * rescale + total
                added = context[...] * rescale + added
            return top, total, added

        if blocks == 1:
            top, total, added = one_block(0, True)
        else:
            running_max[...] = jnp.full(running_max.shape, -1e30, F32)
            running_sum[...] = jnp.zeros(running_sum.shape, F32)
            context[...] = jnp.zeros(context.shape, F32)

            def step(block, carry):
                top, total, added = one_block(block, False)
                running_max[...] = top
                running_sum[...] = total
                context[...] = added
                return carry

            lax.fori_loop(0, blocks, step, 0)
            total, added = running_sum[...], context[...]
        mixed = (added / total).astype(BF16)
        heads = value_own.shape[1] // DH
        for group, value in enumerate((value_own, value_other)):
            for head in range(heads):
                place_of = group * heads + head
                per_head = jnp.dot(
                    mixed[place_of * rows : (place_of + 1) * rows],
                    value[:, head * DH : (head + 1) * DH],
                    preferred_element_type=F32,
                )
                heads_out[:, place_of * DH : (place_of + 1) * DH] = per_head.astype(BF16)

    width = heads_out.shape[1] // 2
    out = jnp.dot(heads_out[:, :width], proj_own[...], preferred_element_type=F32)
    out = out + jnp.dot(heads_out[:, width:], proj_other[...], preferred_element_type=F32)
    out_ref[...] = out.astype(BF16)


def per_device(
    chunks, queries_nope, queries_rope, latent, key_rope, key_up, value_up, out_proj, span_order
):
    rows = latent.shape[0]
    span_rows = rows // 2
    width = out_proj.shape[1] // 2
    own_index = lax.axis_index("ctx")
    core = lax.axis_index("heads")
    place = jnp.stack([own_index, core]).astype(jnp.int32)
    direct = chunks <= DIRECT_LIMIT and chunks & (chunks - 1) == 0

    def other_core(array):
        return lax.ppermute(array, "heads", [(0, 1), (1, 0)])

    packed = jnp.concatenate([latent, key_rope], axis=1)
    packed = lax.dynamic_slice_in_dim(packed, core * span_rows, span_rows, 0)
    if direct:
        near = [
            lax.ppermute(packed, "ctx", [(index, index ^ step) for index in range(chunks)])
            for step in range(1, chunks)
        ]
        far = [other_core(chunk) for chunk in near]
        blocks, block_chunks = 1, chunks
    else:
        near = [lax.all_gather(packed, "ctx", axis=0)]
        far = [other_core(near[0])]
        block_chunks = math.gcd(chunks, BLOCK_CHUNKS)
        blocks = chunks // block_chunks
    nope_other = other_core(queries_nope)
    rope_other = other_core(queries_rope)
    up_other = other_core(key_up)
    value_other = other_core(value_up)
    proj_other = other_core(lax.dynamic_slice_in_dim(out_proj, (1 - core) * width, width, 1))

    heads = 2 * (key_up.shape[1] // DH)
    query_rows = heads * rows
    queries = pl.pallas_call(
        query_kernel,
        out_shape=jax.ShapeDtypeStruct((query_rows, DC + DR), BF16),
        in_specs=[vmem()] * 6,
        out_specs=vmem(),
        compiler_params=pltpu.CompilerParams(vmem_limit_bytes=SMALL_VMEM),
        name="queries",
    )(queries_nope, nope_other, queries_rope, rope_other, key_up, up_other)

    tile = width // 4 if width % 512 == 0 else width
    tiles = width // tile
    block_rows = block_chunks * rows
    several = blocks > 1
    grid_spec = pltpu.PrefetchScalarGridSpec(
        num_scalar_prefetch=2,
        grid=(tiles,),
        in_specs=[vmem()] * (3 + len(near) + len(far) + 2)
        + [
            pl.BlockSpec((out_proj.shape[0], tile), lambda t, place, order: (0, place[1] * tiles + t)),
            pl.BlockSpec((out_proj.shape[0], tile), lambda t, place, order: (0, t)),
        ],
        out_specs=pl.BlockSpec((rows, tile), lambda t, place, order: (0, t)),
        scratch_shapes=[
            pltpu.VMEM((block_rows, DC + DR), BF16),
            pltpu.VMEM((query_rows, 1) if several else (8, 128), F32),
            pltpu.VMEM((query_rows, 1) if several else (8, 128), F32),
            pltpu.VMEM((query_rows, DC) if several else (8, 128), F32),
            pltpu.VMEM((rows, heads * DH), BF16),
        ],
    )
    return pl.pallas_call(
        functools.partial(attend_kernel, chunks, blocks, direct),
        out_shape=jax.ShapeDtypeStruct((rows, width), BF16),
        grid_spec=grid_spec,
        compiler_params=pltpu.CompilerParams(vmem_limit_bytes=SMALL_VMEM if direct else LARGE_VMEM),
        name="attend",
    )(
        place,
        span_order,
        queries,
        latent,
        key_rope,
        *near,
        *far,
        value_up,
        value_other,
        out_proj,
        proj_other,
    )


def solution(mesh):
    in_specs = (
        P(("docs", "ctx"), "heads"),
        P(("docs", "ctx"), "heads"),
        P(("docs", "ctx"), None),
        P(("docs", "ctx"), None),
        P(None, "heads"),
        P(None, "heads"),
        P("heads", None),
        P("docs"),
    )
    out_specs = P(("docs", "ctx"), "heads")
    return jax.shard_map(
        functools.partial(per_device, mesh.shape["ctx"]),
        mesh=mesh,
        in_specs=in_specs,
        out_specs=out_specs,
        check_vma=False,
    )
```

time: 191 us -> 42.3 us (0.22)
  the two profiles are of different devices: /device:TPU:0 before, /device:TPU:25 now
where the time goes in v1:
time: 42.3 us; the launch traced here: 41.9 us
  starting transfers between devices  16.6 us (39%)
  local copies, waits for them, and re-layouts  10.1 us (24%)
  waiting for transfers between devices  9.16 us (22%)
  Pallas kernels  5.81 us (14%)
    ppermute x12, starting transfers between devices, other_core(): return lax.ppermute(array, 'heads', [(0, 1), (1, 0)])  9.63 us
    unnamed x31, local copies, waits for them, and re-layouts  7.11 us
    ppermute x7, starting transfers between devices, per_device(): lax.ppermute(packed, 'ctx', [(index, index ^ step) for index in range(chu...  6.95 us
    ppermute x7, waiting for transfers between devices, per_device(): lax.ppermute(packed, 'ctx', [(index, index ^ step) for index in range(chu...  6.35 us
    pallas_call x1, Pallas kernels, per_device(): pl.pallas_call(functools.partial(attend_kernel, chunks, blocks, direct),...  5.51 us
    dynamic_slice x1, local copies, waits for them, and re-layouts, per_device(): lax.dynamic_slice_in_dim(out_proj, (1 - core) * width, width, 1)  2.96 us
    ppermute x12, waiting for transfers between devices, other_core(): return lax.ppermute(array, 'heads', [(0, 1), (1, 0)])  2.81 us
  transfers between devices with their start and end apart: 19, of which 8 were waited for; matrix products, arithmetic and copies ran while one was open for 0% of the time, Pallas kernels for 1%

profile of v1, /device:TPU:25, one launch (start us, length us, event | category | flops | bytes accessed | tf_op | source)
XLA Modules:
  0.0 41.9 jit_solution(12460658322761496908)
XLA Ops:
  0.0 3.0 %constant_dynamic-slice_fusion = bf16[256,3584]{1,0:T(8,128)(2,1)} fusion(bf16[256,7168]{1,0:T(8,128)(2,1)} %rest_16_.1, s32[]{:T(128)S(6)} %select_n.7), kind=kLoop, calls=%fused_computation.3 | loop fusion | bytes 3670020 | tf_op jit(solution)/shard_map/dynamic_slice | solution.py:188
  3.0 0.7 %collective-permute-start.18 = (bf16[256,3584]{1,0:T(8,128)(2,1)}, bf16[256,3584]{1,0:T(8,128)(2,1)S(1)}, u32[]{:S(2)}, u32[]{:S(2)}) collective-permute-start(bf16[256,3584]{1,0:T(8,128)(2,1)} %constant_dynamic-slice_fusion), channel_id=1, source_target_pairs={{0,1},{1,0},{2,3},{3,2},{4,5},{5,4},{6,7},{7,6},{8,9},{9,8},{10,11... | collective-permute-start | bytes 5505032 | tf_op jit(solution)/shard_map/ppermute | solution.py:168
  3.8 1.3 %collective-permute-start.3 = (bf16[48,576]{1,0:T(8,128)(2,1)S(1)}, bf16[48,576]{1,0:T(8,128)(2,1)S(1)}, u32[]{:S(2)}, u32[]{:S(2)}) collective-permute-start(bf16[48,576]{1,0:T(8,128)(2,1)S(1)} %fusion), channel_id=1, source_target_pairs={{0,2},{2,0},{4,6},{6,4},{8,10},{10,8},{12,14},{14,12},{1,3},{3,1},... | collective-permute-start | bytes 165896 | tf_op jit(solution)/shard_map/ppermute | solution.py:174
  5.1 0.8 %collective-permute-start = (bf16[96,256]{1,0:T(8,128)(2,1)S(1)}, bf16[96,256]{1,0:T(8,128)(2,1)S(1)}, u32[]{:S(2)}, u32[]{:S(2)}) collective-permute-start(bf16[96,256]{1,0:T(8,128)(2,1)S(1)} %copy-done.6), channel_id=1, source_target_pairs={{0,1},{1,0},{2,3},{3,2},{4,5},{5,4},{6,7},{7,6},{8,9},{9,8},{10,11... | collective-permute-start | bytes 147464 | tf_op jit(solution)/shard_map/ppermute | solution.py:168
  6.0 1.0 %collective-permute-done.1.rope_other = bf16[96,128]{1,0:T(8,128)(2,1)S(1)} collective-permute-done((bf16[96,128]{1,0:T(8,128)(2,1)S(1)}, bf16[96,128]{1,0:T(8,128)(2,1)S(1)}, u32[]{:S(2)}, u32[]{:S(2)}) %collective-permute-start.1) | collective-permute-done | bytes 24608 | tf_op jit(solution)/shard_map/ppermute | solution.py:168
  7.0 0.6 %copy-done.11 = bf16[96,128]{1,0:T(8,128)(2,1)} copy-done((bf16[96,128]{1,0:T(8,128)(2,1)}, bf16[96,128]{1,0:T(8,128)(2,1)S(1)}, u32[]{:S(2)}) %copy-start.11) | copy-done | bytes 24600
  7.6 0.2 collective-permute-start.4
  7.8 0.6 %copy-done.7 = bf16[96,256]{1,0:T(8,128)(2,1)} copy-done((bf16[96,256]{1,0:T(8,128)(2,1)}, bf16[96,256]{1,0:T(8,128)(2,1)S(1)}, u32[]{:S(2)}) %copy-start.7) | copy-done | bytes 49176
  8.4 2.2 %collective-permute-start.5 = (bf16[48,576]{1,0:T(8,128)(2,1)S(1)}, bf16[48,576]{1,0:T(8,128)(2,1)S(1)}, u32[]{:S(2)}, u32[]{:S(2)}) collective-permute-start(bf16[48,576]{1,0:T(8,128)(2,1)S(1)} %fusion), channel_id=1, source_target_pairs={{0,6},{2,4},{4,2},{6,0},{8,14},{10,12},{12,10},{14,8},{1,7},{3,5},... | collective-permute-start | bytes 165896 | tf_op jit(solution)/shard_map/ppermute | solution.py:174
  10.7 0.4 collective-permute-done.4.rest_1_
  11.1 1.9 %collective-permute-start.7 = (bf16[48,576]{1,0:T(8,128)(2,1)S(1)}, bf16[48,576]{1,0:T(8,128)(2,1)S(1)}, u32[]{:S(2)}, u32[]{:S(2)}) collective-permute-start(bf16[48,576]{1,0:T(8,128)(2,1)S(1)} %fusion), channel_id=1, source_target_pairs={{0,10},{2,8},{4,14},{6,12},{8,2},{10,0},{12,6},{14,4},{1,11},{3,9}... | collective-permute-start | bytes 165896 | tf_op jit(solution)/shard_map/ppermute | solution.py:174
  13.0 0.4 collective-permute-done.5.rest_2_
  13.3 0.9 %collective-permute-start.8 = (bf16[48,576]{1,0:T(8,128)(2,1)S(1)}, bf16[48,576]{1,0:T(8,128)(2,1)S(1)}, u32[]{:S(2)}, u32[]{:S(2)}) collective-permute-start(bf16[48,576]{1,0:T(8,128)(2,1)S(1)} %fusion), channel_id=1, source_target_pairs={{0,12},{2,14},{4,8},{6,10},{8,4},{10,6},{12,0},{14,2},{1,13},{3,15... | collective-permute-start | bytes 165896 | tf_op jit(solution)/shard_map/ppermute | solution.py:174
  14.2 2.5 %collective-permute-done.6.rest_3_ = bf16[48,576]{1,0:T(8,128)(2,1)S(1)} collective-permute-done((bf16[48,576]{1,0:T(8,128)(2,1)S(1)}, bf16[48,576]{1,0:T(8,128)(2,1)S(1)}, u32[]{:S(2)}, u32[]{:S(2)}) %collective-permute-start.6) | collective-permute-done | bytes 55328 | tf_op jit(solution)/shard_map/ppermute | solution.py:174
  16.8 0.4 collective-permute-start.9
  17.2 2.2 %collective-permute-done.7.rest_4_ = bf16[48,576]{1,0:T(8,128)(2,1)S(1)} collective-permute-done((bf16[48,576]{1,0:T(8,128)(2,1)S(1)}, bf16[48,576]{1,0:T(8,128)(2,1)S(1)}, u32[]{:S(2)}, u32[]{:S(2)}) %collective-permute-start.7) | collective-permute-done | bytes 55328 | tf_op jit(solution)/shard_map/ppermute | solution.py:174
  19.4 2.3 %collective-permute-start.17 = (bf16[512,256]{1,0:T(8,128)(2,1)S(1)}, bf16[512,256]{1,0:T(8,128)(2,1)S(1)}, u32[]{:S(2)}, u32[]{:S(2)}) collective-permute-start(bf16[512,256]{1,0:T(8,128)(2,1)S(1)} %copy-done.2), channel_id=1, source_target_pairs={{0,1},{1,0},{2,3},{3,2},{4,5},{5,4},{6,7},{7,6},{8,9},{9,8},{10,11... | collective-permute-start | bytes 786440 | tf_op jit(solution)/shard_map/ppermute | solution.py:168
  21.8 0.9 %collective-permute-done.9.rest_6_ = bf16[48,576]{1,0:T(8,128)(2,1)S(1)} collective-permute-done((bf16[48,576]{1,0:T(8,128)(2,1)S(1)}, bf16[48,576]{1,0:T(8,128)(2,1)S(1)}, u32[]{:S(2)}, u32[]{:S(2)}) %collective-permute-start.9) | collective-permute-done | bytes 55328 | tf_op jit(solution)/shard_map/ppermute | solution.py:174
  22.6 4.7 %collective-permute-start.11 = (bf16[48,576]{1,0:T(8,128)(2,1)S(1)}, bf16[48,576]{1,0:T(8,128)(2,1)S(1)}, u32[]{:S(2)}, u32[]{:S(2)}) collective-permute-start(bf16[48,576]{1,0:T(8,128)(2,1)S(1)} %collective-permute-done.4.rest_1_), channel_id=1, source_target_pairs={{0,1},{1,0},{2,3},{3,2},{4,5},{5,4},{6,7},{7,6},{8,9},{9,8},{10,11... | collective-permute-start | bytes 165896 | tf_op jit(solution)/shard_map/ppermute | solution.py:168
  27.3 0.9 %collective-permute-done.11.rest_8_ = bf16[48,576]{1,0:T(8,128)(2,1)S(1)} collective-permute-done((bf16[48,576]{1,0:T(8,128)(2,1)S(1)}, bf16[48,576]{1,0:T(8,128)(2,1)S(1)}, u32[]{:S(2)}, u32[]{:S(2)}) %collective-permute-start.11) | collective-permute-done | bytes 55328 | tf_op jit(solution)/shard_map/ppermute | solution.py:168
  28.2 0.6 %copy-done.4 = bf16[48,576]{1,0:T(8,128)(2,1)} copy-done((bf16[48,576]{1,0:T(8,128)(2,1)}, bf16[48,576]{1,0:T(8,128)(2,1)S(1)}, u32[]{:S(2)}) %copy-start.4) | copy-done | bytes 55320
  28.9 0.4 collective-permute-start.13
  29.4 0.9 %collective-permute-done.13.rest_10_ = bf16[48,576]{1,0:T(8,128)(2,1)} collective-permute-done((bf16[48,576]{1,0:T(8,128)(2,1)S(1)}, bf16[48,576]{1,0:T(8,128)(2,1)}, u32[]{:S(2)}, u32[]{:S(2)}) %collective-permute-start.13) | collective-permute-done | bytes 55328 | tf_op jit(solution)/shard_map/ppermute | solution.py:168
  30.2 0.4 collective-permute-start.15
  30.6 0.2 collective-permute-start.16
  30.8 0.8 %copy-done.8 = bf16[96,256]{1,0:T(8,128)(2,1)S(1)} copy-done((bf16[96,256]{1,0:T(8,128)(2,1)S(1)}, bf16[96,256]{1,0:T(8,128)(2,1)}, u32[]{:S(2)}) %copy-start.8) | copy-done | bytes 49176
  31.6 0.7 %copy-done.10 = bf16[96,128]{1,0:T(8,128)(2,1)S(1)} copy-done((bf16[96,128]{1,0:T(8,128)(2,1)S(1)}, bf16[96,128]{1,0:T(8,128)(2,1)}, u32[]{:S(2)}) %copy-start.10) | copy-done | bytes 24600
  32.4 0.7 %copy-done.12 = bf16[96,128]{1,0:T(8,128)(2,1)S(1)} copy-done((bf16[96,128]{1,0:T(8,128)(2,1)S(1)}, bf16[96,128]{1,0:T(8,128)(2,1)}, u32[]{:S(2)}) %copy-start.12) | copy-done | bytes 24600
  33.1 0.3 queries.1
  33.5 2.0 %copy-done = bf16[256,7168]{1,0:T(8,128)(2,1)S(1)} copy-done((bf16[256,7168]{1,0:T(8,128)(2,1)S(1)}, bf16[256,7168]{1,0:T(8,128)(2,1)}, u32[]{:S(2)}) %copy-start) | copy-done | bytes 3670040
  35.5 0.8 %copy-done.5 = bf16[48,576]{1,0:T(8,128)(2,1)S(1)} copy-done((bf16[48,576]{1,0:T(8,128)(2,1)S(1)}, bf16[48,576]{1,0:T(8,128)(2,1)}, u32[]{:S(2)}) %copy-start.5) | copy-done | bytes 55320
  36.3 5.5 %attend.1 = bf16[96,3584]{1,0:T(8,128)(2,1)} custom-call(s32[2]{0:T(128)S(1)} %pad_add_fusion.place, s32[16]{0:T(128)S(1)} %copy-done.13, bf16[384,576]{1,0:T(8,128)(2,1)S(1)} %queries.1, bf16[96,512]{1,0:T(8,128)(2,1)S(1)} %copy-done.1, bf16[96,64]{1,0:T(8,128)(2,1)S(1)} %copy.10.key_rope, bf16[48,576]{1,0:T(8,128)(2,1)S(1)} %collective-permute-done.3.rest_0_, ...), custom_call_target="tpu_custom_call" | custom-call | tf_op jit(solution)/shard_map/attend/pallas_call | solution.py:222
  (42 shorter events, 0.6 us)
Async XLA Ops:
  0.0 3.7 %copy-start.9 = (bf16[96,128]{1,0:T(8,128)(2,1)S(1)}, bf16[96,128]{1,0:T(8,128)(2,1)}, u32[]{:S(2)}) copy-start(bf16[96,128]{1,0:T(8,128)(2,1)} %rope_own.1) | copy-start | bytes 73732
  0.0 3.7 %copy-start.14 = (bf16[96,64]{0,1:T(8,128)(2,1)S(1)}, bf16[96,64]{0,1:T(8,128)(2,1)}, u32[]{:S(2)}) copy-start(bf16[96,64]{0,1:T(8,128)(2,1)} %param.11) | copy-start | bytes 36868
  0.0 3.8 %copy-start.1 = (bf16[96,512]{1,0:T(8,128)(2,1)S(1)}, bf16[96,512]{1,0:T(8,128)(2,1)}, u32[]{:S(2)}) copy-start(bf16[96,512]{1,0:T(8,128)(2,1)} %latent.1) | copy-start | bytes 294916
  0.0 5.1 %copy-start.6 = (bf16[96,256]{1,0:T(8,128)(2,1)S(1)}, bf16[96,256]{1,0:T(8,128)(2,1)}, u32[]{:S(2)}) copy-start(bf16[96,256]{1,0:T(8,128)(2,1)} %nope_own.1) | copy-start | bytes 147460
  0.0 5.9 %copy-start.3 = (bf16[512,256]{1,0:T(8,128)(2,1)S(1)}, bf16[512,256]{1,0:T(8,128)(2,1)}, u32[]{:S(2)}) copy-start(bf16[512,256]{1,0:T(8,128)(2,1)} %up_own.1) | copy-start | bytes 786436
  0.0 19.4 %copy-start.2 = (bf16[512,256]{1,0:T(8,128)(2,1)S(1)}, bf16[512,256]{1,0:T(8,128)(2,1)}, u32[]{:S(2)}) copy-start(bf16[512,256]{1,0:T(8,128)(2,1)} %rest_14_.1) | copy-start | bytes 786436
  0.0 33.4 %copy-start.13 = (s32[16]{0:T(128)S(1)}, s32[16]{0:T(128)}, u32[]{:S(2)}) copy-start(s32[16]{0:T(128)} %span_order.1) | copy-start | bytes 196
  3.0 30.4 %collective-permute-start.18 = (bf16[256,3584]{1,0:T(8,128)(2,1)}, bf16[256,3584]{1,0:T(8,128)(2,1)S(1)}, u32[]{:S(2)}, u32[]{:S(2)}) collective-permute-start(bf16[256,3584]{1,0:T(8,128)(2,1)} %constant_dynamic-slice_fusion), channel_id=1, source_target_pairs={{0,1},{1,0},{2,3},{3,2},{4,5},{5,4},{6,7},{7,6},{8,9},{9,8},{10,11... | collective-permute-start | bytes 5505032 | tf_op jit(solution)/shard_map/ppermute | solution.py:168
  3.7 3.3 %collective-permute-start.1 = (bf16[96,128]{1,0:T(8,128)(2,1)S(1)}, bf16[96,128]{1,0:T(8,128)(2,1)S(1)}, u32[]{:S(2)}, u32[]{:S(2)}) collective-permute-start(bf16[96,128]{1,0:T(8,128)(2,1)S(1)} %copy-done.9), channel_id=1, source_target_pairs={{0,1},{1,0},{2,3},{3,2},{4,5},{5,4},{6,7},{7,6},{8,9},{9,8},{10,11... | collective-permute-start | bytes 73736 | tf_op jit(solution)/shard_map/ppermute | solution.py:168
  3.8 6.8 %collective-permute-start.3 = (bf16[48,576]{1,0:T(8,128)(2,1)S(1)}, bf16[48,576]{1,0:T(8,128)(2,1)S(1)}, u32[]{:S(2)}, u32[]{:S(2)}) collective-permute-start(bf16[48,576]{1,0:T(8,128)(2,1)S(1)} %fusion), channel_id=1, source_target_pairs={{0,2},{2,0},{4,6},{6,4},{8,10},{10,8},{12,14},{14,12},{1,3},{3,1},... | collective-permute-start | bytes 165896 | tf_op jit(solution)/shard_map/ppermute | solution.py:174
  5.1 2.7 %collective-permute-start = (bf16[96,256]{1,0:T(8,128)(2,1)S(1)}, bf16[96,256]{1,0:T(8,128)(2,1)S(1)}, u32[]{:S(2)}, u32[]{:S(2)}) collective-permute-start(bf16[96,256]{1,0:T(8,128)(2,1)S(1)} %copy-done.6), channel_id=1, source_target_pairs={{0,1},{1,0},{2,3},{3,2},{4,5},{5,4},{6,7},{7,6},{8,9},{9,8},{10,11... | collective-permute-start | bytes 147464 | tf_op jit(solution)/shard_map/ppermute | solution.py:168
  5.9 24.7 %collective-permute-start.2 = (bf16[512,256]{1,0:T(8,128)(2,1)S(1)}, bf16[512,256]{1,0:T(8,128)(2,1)S(1)}, u32[]{:S(2)}, u32[]{:S(2)}) collective-permute-start(bf16[512,256]{1,0:T(8,128)(2,1)S(1)} %copy-done.3), channel_id=1, source_target_pairs={{0,1},{1,0},{2,3},{3,2},{4,5},{5,4},{6,7},{7,6},{8,9},{9,8},{10,11... | collective-permute-start | bytes 786440 | tf_op jit(solution)/shard_map/ppermute | solution.py:168
  7.6 3.5 %collective-permute-start.4 = (bf16[48,576]{1,0:T(8,128)(2,1)S(1)}, bf16[48,576]{1,0:T(8,128)(2,1)S(1)}, u32[]{:S(2)}, u32[]{:S(2)}) collective-permute-start(bf16[48,576]{1,0:T(8,128)(2,1)S(1)} %fusion), channel_id=1, source_target_pairs={{0,4},{2,6},{4,0},{6,2},{8,12},{10,14},{12,8},{14,10},{1,5},{3,7},... | collective-permute-start | bytes 165896 | tf_op jit(solution)/shard_map/ppermute | solution.py:174
  7.8 0.6 %copy-start.7 = (bf16[96,256]{1,0:T(8,128)(2,1)}, bf16[96,256]{1,0:T(8,128)(2,1)S(1)}, u32[]{:S(2)}) copy-start(bf16[96,256]{1,0:T(8,128)(2,1)S(1)} %collective-permute-done.nope_other) | copy-start | bytes 147460
  8.4 4.9 %collective-permute-start.5 = (bf16[48,576]{1,0:T(8,128)(2,1)S(1)}, bf16[48,576]{1,0:T(8,128)(2,1)S(1)}, u32[]{:S(2)}, u32[]{:S(2)}) collective-permute-start(bf16[48,576]{1,0:T(8,128)(2,1)S(1)} %fusion), channel_id=1, source_target_pairs={{0,6},{2,4},{4,2},{6,0},{8,14},{10,12},{12,10},{14,8},{1,7},{3,5},... | collective-permute-start | bytes 165896 | tf_op jit(solution)/shard_map/ppermute | solution.py:174
  10.6 6.1 %collective-permute-start.6 = (bf16[48,576]{1,0:T(8,128)(2,1)S(1)}, bf16[48,576]{1,0:T(8,128)(2,1)S(1)}, u32[]{:S(2)}, u32[]{:S(2)}) collective-permute-start(bf16[48,576]{1,0:T(8,128)(2,1)S(1)} %fusion), channel_id=1, source_target_pairs={{0,8},{2,10},{4,12},{6,14},{8,0},{10,2},{12,4},{14,6},{1,9},{3,11}... | collective-permute-start | bytes 165896 | tf_op jit(solution)/shard_map/ppermute | solution.py:174
  11.1 8.3 %collective-permute-start.7 = (bf16[48,576]{1,0:T(8,128)(2,1)S(1)}, bf16[48,576]{1,0:T(8,128)(2,1)S(1)}, u32[]{:S(2)}, u32[]{:S(2)}) collective-permute-start(bf16[48,576]{1,0:T(8,128)(2,1)S(1)} %fusion), channel_id=1, source_target_pairs={{0,10},{2,8},{4,14},{6,12},{8,2},{10,0},{12,6},{14,4},{1,11},{3,9}... | collective-permute-start | bytes 165896 | tf_op jit(solution)/shard_map/ppermute | solution.py:174
  13.3 8.4 %collective-permute-start.8 = (bf16[48,576]{1,0:T(8,128)(2,1)S(1)}, bf16[48,576]{1,0:T(8,128)(2,1)S(1)}, u32[]{:S(2)}, u32[]{:S(2)}) collective-permute-start(bf16[48,576]{1,0:T(8,128)(2,1)S(1)} %fusion), channel_id=1, source_target_pairs={{0,12},{2,14},{4,8},{6,10},{8,4},{10,6},{12,0},{14,2},{1,13},{3,15... | collective-permute-start | bytes 165896 | tf_op jit(solution)/shard_map/ppermute | solution.py:174
  16.8 5.9 %collective-permute-start.9 = (bf16[48,576]{1,0:T(8,128)(2,1)S(1)}, bf16[48,576]{1,0:T(8,128)(2,1)S(1)}, u32[]{:S(2)}, u32[]{:S(2)}) collective-permute-start(bf16[48,576]{1,0:T(8,128)(2,1)S(1)} %fusion), channel_id=1, source_target_pairs={{0,14},{2,12},{4,10},{6,8},{8,6},{10,4},{12,2},{14,0},{1,15},{3,13... | collective-permute-start | bytes 165896 | tf_op jit(solution)/shard_map/ppermute | solution.py:174
  19.4 14.1 %collective-permute-start.17 = (bf16[512,256]{1,0:T(8,128)(2,1)S(1)}, bf16[512,256]{1,0:T(8,128)(2,1)S(1)}, u32[]{:S(2)}, u32[]{:S(2)}) collective-permute-start(bf16[512,256]{1,0:T(8,128)(2,1)S(1)} %copy-done.2), channel_id=1, source_target_pairs={{0,1},{1,0},{2,3},{3,2},{4,5},{5,4},{6,7},{7,6},{8,9},{9,8},{10,11... | collective-permute-start | bytes 786440 | tf_op jit(solution)/shard_map/ppermute | solution.py:168
  21.7 5.6 %collective-permute-start.10 = (bf16[48,576]{1,0:T(8,128)(2,1)S(1)}, bf16[48,576]{1,0:T(8,128)(2,1)S(1)}, u32[]{:S(2)}, u32[]{:S(2)}) collective-permute-start(bf16[48,576]{1,0:T(8,128)(2,1)S(1)} %collective-permute-done.3.rest_0_), channel_id=1, source_target_pairs={{0,1},{1,0},{2,3},{3,2},{4,5},{5,4},{6,7},{7,6},{8,9},{9,8},{10,11... | collective-permute-start | bytes 165896 | tf_op jit(solution)/shard_map/ppermute | solution.py:168
  22.6 5.6 %collective-permute-start.11 = (bf16[48,576]{1,0:T(8,128)(2,1)S(1)}, bf16[48,576]{1,0:T(8,128)(2,1)S(1)}, u32[]{:S(2)}, u32[]{:S(2)}) collective-permute-start(bf16[48,576]{1,0:T(8,128)(2,1)S(1)} %collective-permute-done.4.rest_1_), channel_id=1, source_target_pairs={{0,1},{1,0},{2,3},{3,2},{4,5},{5,4},{6,7},{7,6},{8,9},{9,8},{10,11... | collective-permute-start | bytes 165896 | tf_op jit(solution)/shard_map/ppermute | solution.py:168
  27.3 1.9 %collective-permute-start.12 = (bf16[48,576]{1,0:T(8,128)(2,1)S(1)}, bf16[48,576]{1,0:T(8,128)(2,1)}, u32[]{:S(2)}, u32[]{:S(2)}) collective-permute-start(bf16[48,576]{1,0:T(8,128)(2,1)S(1)} %collective-permute-done.5.rest_2_), channel_id=1, source_target_pairs={{0,1},{1,0},{2,3},{3,2},{4,5},{5,4},{6,7},{7,6},{8,9},{9,8},{10,11... | collective-permute-start | bytes 165896 | tf_op jit(solution)/shard_map/ppermute | solution.py:168
  28.9 1.4 %collective-permute-start.13 = (bf16[48,576]{1,0:T(8,128)(2,1)S(1)}, bf16[48,576]{1,0:T(8,128)(2,1)}, u32[]{:S(2)}, u32[]{:S(2)}) collective-permute-start(bf16[48,576]{1,0:T(8,128)(2,1)S(1)} %collective-permute-done.6.rest_3_), channel_id=1, source_target_pairs={{0,1},{1,0},{2,3},{3,2},{4,5},{5,4},{6,7},{7,6},{8,9},{9,8},{10,11... | collective-permute-start | bytes 165896 | tf_op jit(solution)/shard_map/ppermute | solution.py:168
  29.2 4.2 %collective-permute-start.14 = (bf16[48,576]{1,0:T(8,128)(2,1)S(1)}, bf16[48,576]{1,0:T(8,128)(2,1)S(1)}, u32[]{:S(2)}, u32[]{:S(2)}) collective-permute-start(bf16[48,576]{1,0:T(8,128)(2,1)S(1)} %collective-permute-done.7.rest_4_), channel_id=1, source_target_pairs={{0,1},{1,0},{2,3},{3,2},{4,5},{5,4},{6,7},{7,6},{8,9},{9,8},{10,11... | collective-permute-start | bytes 165896 | tf_op jit(solution)/shard_map/ppermute | solution.py:168
  30.2 3.2 %collective-permute-start.15 = (bf16[48,576]{1,0:T(8,128)(2,1)S(1)}, bf16[48,576]{1,0:T(8,128)(2,1)S(1)}, u32[]{:S(2)}, u32[]{:S(2)}) collective-permute-start(bf16[48,576]{1,0:T(8,128)(2,1)S(1)} %collective-permute-done.8.rest_5_), channel_id=1, source_target_pairs={{0,1},{1,0},{2,3},{3,2},{4,5},{5,4},{6,7},{7,6},{8,9},{9,8},{10,11... | collective-permute-start | bytes 165896 | tf_op jit(solution)/shard_map/ppermute | solution.py:168
  30.6 2.8 %collective-permute-start.16 = (bf16[48,576]{1,0:T(8,128)(2,1)S(1)}, bf16[48,576]{1,0:T(8,128)(2,1)S(1)}, u32[]{:S(2)}, u32[]{:S(2)}) collective-permute-start(bf16[48,576]{1,0:T(8,128)(2,1)S(1)} %collective-permute-done.9.rest_6_), channel_id=1, source_target_pairs={{0,1},{1,0},{2,3},{3,2},{4,5},{5,4},{6,7},{7,6},{8,9},{9,8},{10,11... | collective-permute-start | bytes 165896 | tf_op jit(solution)/shard_map/ppermute | solution.py:168
  30.8 0.8 %copy-start.8 = (bf16[96,256]{1,0:T(8,128)(2,1)S(1)}, bf16[96,256]{1,0:T(8,128)(2,1)}, u32[]{:S(2)}) copy-start(bf16[96,256]{1,0:T(8,128)(2,1)} %copy-done.7) | copy-start | bytes 147460
  31.6 0.7 %copy-start.10 = (bf16[96,128]{1,0:T(8,128)(2,1)S(1)}, bf16[96,128]{1,0:T(8,128)(2,1)}, u32[]{:S(2)}) copy-start(bf16[96,128]{1,0:T(8,128)(2,1)} %rope_own.1) | copy-start | bytes 73732
  32.4 0.7 %copy-start.12 = (bf16[96,128]{1,0:T(8,128)(2,1)S(1)}, bf16[96,128]{1,0:T(8,128)(2,1)}, u32[]{:S(2)}) copy-start(bf16[96,128]{1,0:T(8,128)(2,1)} %copy-done.11) | copy-start | bytes 73732
  33.5 2.0 %copy-start = (bf16[256,7168]{1,0:T(8,128)(2,1)S(1)}, bf16[256,7168]{1,0:T(8,128)(2,1)}, u32[]{:S(2)}) copy-start(bf16[256,7168]{1,0:T(8,128)(2,1)} %rest_16_.1) | copy-start | bytes 11010052
  35.5 0.8 %copy-start.5 = (bf16[48,576]{1,0:T(8,128)(2,1)S(1)}, bf16[48,576]{1,0:T(8,128)(2,1)}, u32[]{:S(2)}) copy-start(bf16[48,576]{1,0:T(8,128)(2,1)} %copy-done.4) | copy-start | bytes 165892
  (2 other events, 1.2 us)

commit v2 on v1

--- a/solution.py
+++ b/solution.py
@@ -46,19 +46,12 @@
 
 
 def attend_kernel(
-    chunks, blocks, direct, place, span_order, queries, latent, key_rope, *rest
+    blocks, place, span_order, queries, *rest
 ):
-    if direct:
-        near = rest[: chunks - 1]
-        far = rest[chunks - 1 : 2 * chunks - 2]
-        rest = rest[2 * chunks - 2 :]
-    else:
-        near, far = rest[:2]
-        rest = rest[2:]
-    (value_own, value_other, proj_own, proj_other, out_ref) = rest[:5]
-    keys, running_max, running_sum, context, heads_out = rest[5:]
-    rows = latent.shape[0]
-    span_rows = rows // 2
+    near, far, value_own, value_other, proj, out_ref = rest[:6]
+    keys, running_max, running_sum, context, heads_out = rest[6:]
+    rows = out_ref.shape[0]
+    span_rows = near.shape[1]
     query_rows = queries.shape[0]
     copies = query_rows // rows
     block_rows = keys.shape[0]
@@ -81,23 +74,11 @@
             key_pos = jnp.zeros((1, block_rows), jnp.int32)
             for index in range(block_rows // rows):
                 base = index * rows
-                if direct:
-                    owner = own_index ^ index
-                else:
-                    owner = block * (block_rows // rows) + index
+                owner = block * (block_rows // rows) + index
                 for side in range(2):
                     start = base + side * span_rows
-                    if direct and index == 0:
-                        span = 2 * owner + side
-                        keys[pl.ds(start, span_rows), :DC] = latent[pl.ds(side * span_rows, span_rows), :]
-                        keys[pl.ds(start, span_rows), DC:] = key_rope[pl.ds(side * span_rows, span_rows), :]
-                    else:
-                        span = 2 * owner + (core if side == 0 else 1 - core)
-                        source = (near, far)[side]
-                        if direct:
-                            keys[pl.ds(start, span_rows), :] = source[index - 1][...]
-                        else:
-                            keys[pl.ds(start, span_rows), :] = source[owner]
+                    span = 2 * owner + (core if side == 0 else 1 - core)
+                    keys[pl.ds(start, span_rows), :] = (near, far)[side][owner]
                     key_pos = jnp.where(
                         column >= start, span_order[span] * span_rows + column - start, key_pos
                     )
@@ -145,11 +126,10 @@
                     value[:, head * DH : (head + 1) * DH],
                     preferred_element_type=F32,
                 )
-                heads_out[:, place_of * DH : (place_of + 1) * DH] = per_head.astype(BF16)
-
-    width = heads_out.shape[1] // 2
-    out = jnp.dot(heads_out[:, :width], proj_own[...], preferred_element_type=F32)
-    out = out + jnp.dot(heads_out[:, width:], proj_other[...], preferred_element_type=F32)
+                target = (core ^ group) * heads * DH + head * DH
+                heads_out[:, pl.ds(pl.multiple_of(target, DH), DH)] = per_head.astype(BF16)
+
+    out = jnp.dot(heads_out[...], proj[...], preferred_element_type=F32)
     out_ref[...] = out.astype(BF16)
 
 
@@ -170,22 +150,19 @@
     packed = jnp.concatenate([latent, key_rope], axis=1)
     packed = lax.dynamic_slice_in_dim(packed, core * span_rows, span_rows, 0)
     if direct:
-        near = [
-            lax.ppermute(packed, "ctx", [(index, index ^ step) for index in range(chunks)])
-            for step in range(1, chunks)
-        ]
-        far = [other_core(chunk) for chunk in near]
+        copies = jnp.broadcast_to(packed, (chunks, *packed.shape))
+        near = lax.all_to_all(copies, "ctx", 0, 0)
         blocks, block_chunks = 1, chunks
     else:
-        near = [lax.all_gather(packed, "ctx", axis=0)]
-        far = [other_core(near[0])]
+        near = lax.all_gather(packed, "ctx", axis=0)
         block_chunks = math.gcd(chunks, BLOCK_CHUNKS)
         blocks = chunks // block_chunks
+    far = other_core(near)
     nope_other = other_core(queries_nope)
     rope_other = other_core(queries_rope)
     up_other = other_core(key_up)
     value_other = other_core(value_up)
-    proj_other = other_core(lax.dynamic_slice_in_dim(out_proj, (1 - core) * width, width, 1))
+    proj = lax.all_to_all(out_proj, "heads", 1, 0, tiled=True)
 
     heads = 2 * (key_up.shape[1] // DH)
     query_rows = heads * rows
@@ -205,11 +182,8 @@
     grid_spec = pltpu.PrefetchScalarGridSpec(
         num_scalar_prefetch=2,
         grid=(tiles,),
-        in_specs=[vmem()] * (3 + len(near) + len(far) + 2)
-        + [
-            pl.BlockSpec((out_proj.shape[0], tile), lambda t, place, order: (0, place[1] * tiles + t)),
-            pl.BlockSpec((out_proj.shape[0], tile), lambda t, place, order: (0, t)),
-        ],
+        in_specs=[vmem()] * 5
+        + [pl.BlockSpec((proj.shape[0], tile), lambda t, place, order: (0, t))],
         out_specs=pl.BlockSpec((rows, tile), lambda t, place, order: (0, t)),
         scratch_shapes=[
             pltpu.VMEM((block_rows, DC + DR), BF16),
@@ -220,7 +194,7 @@
         ],
     )
     return pl.pallas_call(
-        functools.partial(attend_kernel, chunks, blocks, direct),
+        functools.partial(attend_kernel, blocks),
         out_shape=jax.ShapeDtypeStruct((rows, width), BF16),
         grid_spec=grid_spec,
         compiler_params=pltpu.CompilerParams(vmem_limit_bytes=SMALL_VMEM if direct else LARGE_VMEM),
@@ -229,14 +203,11 @@
         place,
         span_order,
         queries,
-        latent,
-        key_rope,
-        *near,
-        *far,
+        near,
+        far,
         value_up,
         value_other,
-        out_proj,
-        proj_other,
+        proj,
     )
 
 

time: 42.3 us -> 44 us (1.040)
  the two profiles are of different devices: /device:TPU:25 before, /device:TPU:0 now
where the time goes in v2:
time: 44 us; the launch traced here: 43.5 us
  blocking collectives  20.9 us (48%)
  Pallas kernels  6.83 us (16%)
  starting transfers between devices  6.71 us (15%)
  local copies, waits for them, and re-layouts  5 us (11%)
  waiting for transfers between devices  3.17 us (7%)
  other arithmetic  0.89 us (2%)
    all_to_all x1, blocking collectives, per_device(): near = lax.all_to_all(copies, 'ctx', 0, 0)  20.9 us
    pallas_call x1, Pallas kernels, per_device(): pl.pallas_call(functools.partial(attend_kernel, blocks), out_shape=jax.Sh...  6.52 us
    all_to_all x1, starting transfers between devices, per_device(): proj = lax.all_to_all(out_proj, 'heads', 1, 0, tiled=True)  5.56 us
    all_to_all x1, local copies, waits for them, and re-layouts, per_device(): proj = lax.all_to_all(out_proj, 'heads', 1, 0, tiled=True)  4.13 us
    ppermute x5, waiting for transfers between devices, other_core(): return lax.ppermute(array, 'heads', [(0, 1), (1, 0)])  2.79 us
    ppermute x5, starting transfers between devices, other_core(): return lax.ppermute(array, 'heads', [(0, 1), (1, 0)])  1.15 us
  transfers between devices with their start and end apart: 6, of which 2 were waited for; matrix products, arithmetic and copies ran while one was open for 10% of the time, Pallas kernels for 1%

profile of v2, /device:TPU:0, one launch (start us, length us, event | category | flops | bytes accessed | tf_op | source)
XLA Modules:
  0.0 43.5 jit_solution(1604363085566752234)
XLA Ops:
  0.0 0.8 %copy.9 = bf16[96,64]{1,0:T(8,128)(2,1)S(1)} copy(bf16[96,64]{0,1:T(8,128)(2,1)} %param.11) | data formatting | bytes 24576 | tf_op args[3]
  0.8 0.8 %fusion = bf16[48,576]{1,0:T(8,128)(2,1)S(1)} fusion(s32[]{:T(128)S(6)} %select_n.3, bf16[96,512]{1,0:T(8,128)(2,1)} %param.10, bf16[96,64]{1,0:T(8,128)(2,1)S(1)} %copy.9), kind=kLoop, calls=%fused_computation.3 | loop fusion | flops 110592 | bytes 165892 | tf_op jit(solution)/shard_map/concatenate | solution.py:150
  1.7 20.9 %all_to_all.24.rest_0_ = bf16[8,48,576]{2,1,0:T(8,128)(2,1)S(1)} all-to-all(bf16[8,48,576]{2,1,0:T(8,128)(2,1)S(1)} %broadcast_in_dim.3), channel_id=1, replica_groups=mesh['docs'=2,'ctx'=8,'heads'=2] {'ctx'}, dimensions={0} | all-to-all | bytes 884736 | tf_op jit(solution)/shard_map/all_to_all | solution.py:154
  22.6 0.0 collective-permute-start.3
  22.6 0.5 %collective-permute-start.2 = (bf16[512,256]{1,0:T(8,128)(2,1)}, bf16[512,256]{1,0:T(8,128)(2,1)S(1)}, u32[]{:S(2)}, u32[]{:S(2)}) collective-permute-start(bf16[512,256]{1,0:T(8,128)(2,1)} %up_own.1), channel_id=1, source_target_pairs={{0,1},{1,0},{2,3},{3,2},{4,5},{5,4},{6,7},{7,6},{8,9},{9,8},{10,11... | collective-permute-start | bytes 786440 | tf_op jit(solution)/shard_map/ppermute | solution.py:148
  23.1 0.0 collective-permute-start.4
  23.1 4.1 %copy.13 = bf16[32,2,8,3584]{3,2,0,1:T(8,128)(2,1)} copy(bf16[32,2,8,3584]{3,2,1,0:T(8,128)(2,1)} %bitcast.10) | data formatting | bytes 7340032 | tf_op jit(solution)/shard_map/all_to_all | solution.py:165
  27.2 0.0 copy-start.2
  27.2 0.0 copy-start.3
  27.2 0.0 copy-start
  27.2 0.0 copy-start.1
  27.2 0.0 copy-start.4
  27.2 5.6 %all-to-all-start.1 = ((bf16[256,2,3584]{2,0,1:T(8,128)(2,1)}), bf16[256,2,3584]{2,0,1:T(8,128)(2,1)}, u32[]{:S(2)}, u32[]{:S(2)}) async-start(bf16[256,2,3584]{2,0,1:T(8,128)(2,1)} %bitcast.9), calls=%async_computation.1 | async-start | bytes 7340032 | tf_op jit(solution)/shard_map/all_to_all | solution.py:165
  32.8 0.0 copy-done.2
  32.8 0.6 %collective-permute-start = (bf16[96,256]{1,0:T(8,128)(2,1)S(1)}, bf16[96,256]{1,0:T(8,128)(2,1)S(1)}, u32[]{:S(2)}, u32[]{:S(2)}) collective-permute-start(bf16[96,256]{1,0:T(8,128)(2,1)S(1)} %copy-done.2), channel_id=1, source_target_pairs={{0,1},{1,0},{2,3},{3,2},{4,5},{5,4},{6,7},{7,6},{8,9},{9,8},{10,11... | collective-permute-start | bytes 147464 | tf_op jit(solution)/shard_map/ppermute | solution.py:148
  33.4 0.0 copy-done.3
  33.4 0.1 collective-permute-start.1
  33.4 0.1 pad_add_fusion.place
  33.5 2.8 %collective-permute-done.1.rope_other = bf16[96,128]{1,0:T(8,128)(2,1)S(1)} collective-permute-done((bf16[96,128]{1,0:T(8,128)(2,1)S(1)}, bf16[96,128]{1,0:T(8,128)(2,1)S(1)}, u32[]{:S(2)}, u32[]{:S(2)}) %collective-permute-start.1) | collective-permute-done | bytes 24608 | tf_op jit(solution)/shard_map/ppermute | solution.py:148
  36.3 0.0 collective-permute-done.nope_other
  36.3 0.0 collective-permute-done.2.up_other
  36.3 0.0 copy-done
  36.3 0.3 queries.1
  36.6 0.4 all-to-all-done.1
  37.0 0.0 collective-permute-done.4.rest_3_
  37.0 0.0 collective-permute-done.3.rest_1_
  37.0 0.0 copy-done.1
  37.0 0.0 copy-done.4
  37.0 6.5 %attend.1 = bf16[96,3584]{1,0:T(8,128)(2,1)} custom-call(s32[2]{0:T(128)S(1)} %pad_add_fusion.place, s32[16]{0:T(128)S(1)} %copy-done.4, bf16[384,576]{1,0:T(8,128)(2,1)S(1)} %queries.1, bf16[8,48,576]{2,1,0:T(8,128)(2,1)S(1)} %all_to_all.24.rest_0_, bf16[8,48,576]{2,1,0:T(8,128)(2,1)S(1)} %collective-permute-done.3.rest_1_, bf16[512,256]{1,0:T(8,128)(2,1)S(1)} %copy-done.1, ...), custom_call_target="tpu_custom_call" | custom-call | tf_op jit(solution)/shard_map/attend/pallas_call | solution.py:196
  (1 shorter events, 0.0 us)
Async XLA Ops:
  22.6 14.5 %collective-permute-start.3 = (bf16[8,48,576]{2,1,0:T(8,128)(2,1)S(1)}, bf16[8,48,576]{2,1,0:T(8,128)(2,1)S(1)}, u32[]{:S(2)}, u32[]{:S(2)}) collective-permute-start(bf16[8,48,576]{2,1,0:T(8,128)(2,1)S(1)} %all_to_all.24.rest_0_), channel_id=1, source_target_pairs={{0,1},{1,0},{2,3},{3,2},{4,5},{5,4},{6,7},{7,6},{8,9},{9,8},{10,11... | collective-permute-start | bytes 1327112 | tf_op jit(solution)/shard_map/ppermute | solution.py:148
  22.6 13.7 %collective-permute-start.2 = (bf16[512,256]{1,0:T(8,128)(2,1)}, bf16[512,256]{1,0:T(8,128)(2,1)S(1)}, u32[]{:S(2)}, u32[]{:S(2)}) collective-permute-start(bf16[512,256]{1,0:T(8,128)(2,1)} %up_own.1), channel_id=1, source_target_pairs={{0,1},{1,0},{2,3},{3,2},{4,5},{5,4},{6,7},{7,6},{8,9},{9,8},{10,11... | collective-permute-start | bytes 786440 | tf_op jit(solution)/shard_map/ppermute | solution.py:148
  23.1 13.9 %collective-permute-start.4 = (bf16[512,256]{1,0:T(8,128)(2,1)}, bf16[512,256]{1,0:T(8,128)(2,1)S(1)}, u32[]{:S(2)}, u32[]{:S(2)}) collective-permute-start(bf16[512,256]{1,0:T(8,128)(2,1)} %rest_2_.1), channel_id=1, source_target_pairs={{0,1},{1,0},{2,3},{3,2},{4,5},{5,4},{6,7},{7,6},{8,9},{9,8},{10,11... | collective-permute-start | bytes 786440 | tf_op jit(solution)/shard_map/ppermute | solution.py:148
  27.2 5.6 %copy-start.2 = (bf16[96,256]{1,0:T(8,128)(2,1)S(1)}, bf16[96,256]{1,0:T(8,128)(2,1)}, u32[]{:S(2)}) copy-start(bf16[96,256]{1,0:T(8,128)(2,1)} %nope_own.1) | copy-start | bytes 147460
  27.2 6.2 %copy-start.3 = (bf16[96,128]{1,0:T(8,128)(2,1)S(1)}, bf16[96,128]{1,0:T(8,128)(2,1)}, u32[]{:S(2)}) copy-start(bf16[96,128]{1,0:T(8,128)(2,1)} %rope_own.1) | copy-start | bytes 73732
  27.2 9.1 %copy-start = (bf16[512,256]{1,0:T(8,128)(2,1)S(1)}, bf16[512,256]{1,0:T(8,128)(2,1)}, u32[]{:S(2)}) copy-start(bf16[512,256]{1,0:T(8,128)(2,1)} %up_own.1) | copy-start | bytes 786436
  27.2 9.8 %copy-start.1 = (bf16[512,256]{1,0:T(8,128)(2,1)S(1)}, bf16[512,256]{1,0:T(8,128)(2,1)}, u32[]{:S(2)}) copy-start(bf16[512,256]{1,0:T(8,128)(2,1)} %rest_2_.1) | copy-start | bytes 786436
  27.2 9.8 %copy-start.4 = (s32[16]{0:T(128)S(1)}, s32[16]{0:T(128)}, u32[]{:S(2)}) copy-start(s32[16]{0:T(128)} %span_order.1) | copy-start | bytes 196
  27.2 9.8 %all-to-all-start.1 = ((bf16[256,2,3584]{2,0,1:T(8,128)(2,1)}), bf16[256,2,3584]{2,0,1:T(8,128)(2,1)}, u32[]{:S(2)}, u32[]{:S(2)}) async-start(bf16[256,2,3584]{2,0,1:T(8,128)(2,1)} %bitcast.9), calls=%async_computation.1 | async-start | bytes 7340032 | tf_op jit(solution)/shard_map/all_to_all | solution.py:165
  32.8 3.5 %collective-permute-start = (bf16[96,256]{1,0:T(8,128)(2,1)S(1)}, bf16[96,256]{1,0:T(8,128)(2,1)S(1)}, u32[]{:S(2)}, u32[]{:S(2)}) collective-permute-start(bf16[96,256]{1,0:T(8,128)(2,1)S(1)} %copy-done.2), channel_id=1, source_target_pairs={{0,1},{1,0},{2,3},{3,2},{4,5},{5,4},{6,7},{7,6},{8,9},{9,8},{10,11... | collective-permute-start | bytes 147464 | tf_op jit(solution)/shard_map/ppermute | solution.py:148
  33.4 2.9 %collective-permute-start.1 = (bf16[96,128]{1,0:T(8,128)(2,1)S(1)}, bf16[96,128]{1,0:T(8,128)(2,1)S(1)}, u32[]{:S(2)}, u32[]{:S(2)}) collective-permute-start(bf16[96,128]{1,0:T(8,128)(2,1)S(1)} %copy-done.3), channel_id=1, source_target_pairs={{0,1},{1,0},{2,3},{3,2},{4,5},{5,4},{6,7},{7,6},{8,9},{9,8},{10,11... | collective-permute-start | bytes 73736 | tf_op jit(solution)/shard_map/ppermute | solution.py:148

commit v3 on v0

v3 whole, which is shorter than its diff:
```python
import functools
import math

import jax
import jax.numpy as jnp
from jax import lax
from jax.experimental import pallas as pl
from jax.experimental.pallas import tpu as pltpu
from jax.sharding import PartitionSpec as P

DC = 512
DH = 128
DR = 64
BF16 = jnp.bfloat16
F32 = jnp.float32
MASKED = -1e30
SMALL_VMEM = 20 * 1024 * 1024
LARGE_VMEM = 56 * 1024 * 1024
FAR = (4, 6)
NEAR = (2, 3)
BESIDE = (1, 1)
RELAYED = (5, 7)


def vmem():
    return pl.BlockSpec(memory_space=pltpu.VMEM)


def anywhere():
    return pl.BlockSpec(memory_space=pl.ANY)


def hbm():
    return pl.BlockSpec(memory_space=pltpu.HBM)


def smem():
    return pl.BlockSpec(memory_space=pltpu.SMEM)


def pack_kernel(latent, key_rope, out_ref):
    out_ref[:, :DC] = latent[...]
    out_ref[:, DC:] = key_rope[...].astype(F32).T.astype(BF16)


def bundle_kernel(packed, nope, rope, key_up, value_up, out_proj, small_ref, proj_ref, sems):
    core = lax.axis_index("heads")
    width = proj_ref.shape[1]
    base = pl.multiple_of((1 - core) * width, 128)
    copies = [pltpu.make_async_copy(out_proj.at[:, pl.ds(base, width)], proj_ref, sems.at[0])]
    row = 0
    for index, part in enumerate((key_up, value_up, nope, rope)):
        target = small_ref.at[pl.ds(row, part.shape[0]), pl.ds(0, part.shape[1])]
        copies.append(pltpu.make_async_copy(part, target, sems.at[1 + index]))
        row += part.shape[0]
    for copy in copies:
        copy.start()
    for copy in copies:
        copy.wait()


def query_kernel(order, span_order, nope_own, rope_own, up_own, other, out_ref, bias_ref):
    rows = nope_own.shape[0]
    heads = nope_own.shape[1] // DH
    span_rows = rows // 2
    own_index = lax.axis_index("ctx")
    core = lax.axis_index("heads")
    up_other = other.at[pl.ds(0, DC)]
    nope_other = other.at[pl.ds(2 * DC, rows)]
    rope_other = other.at[pl.ds(2 * DC + rows, rows)]
    for group, (nope, rope, up) in enumerate(
        ((nope_own, rope_own, up_own), (nope_other, rope_other, up_other))
    ):
        for head in range(heads):
            part = pl.ds((group * heads + head) * rows, rows)
            latent = lax.dot_general(
                nope[:, head * DH : (head + 1) * DH],
                up[:, head * DH : (head + 1) * DH],
                (((1,), (1,)), ((), ())),
                preferred_element_type=F32,
            )
            out_ref[part, :DC] = latent.astype(BF16)
            out_ref[part, DC:] = rope[:, head * DR : (head + 1) * DR]
    block_rows = 8 * rows
    row = lax.broadcasted_iota(jnp.int32, (rows, 1), 0)
    query_pos = jnp.where(
        row < span_rows,
        span_order[2 * own_index] * span_rows + row,
        span_order[2 * own_index + 1] * span_rows + row - span_rows,
    )
    column = lax.broadcasted_iota(jnp.int32, (1, block_rows), 1)

    def bias_block(block):
        key_pos = jnp.zeros((1, block_rows), jnp.int32)
        for index in range(8):
            if order is None:
                owner = block * 8 + index
            else:
                owner = own_index ^ jnp.where(core == 0, order[index][0], order[index][1])
            for side in range(2):
                start = index * rows + side * span_rows
                first = span_order[2 * owner + side] * span_rows
                key_pos = jnp.where(column >= start, first + column - start, key_pos)
        return jnp.where(key_pos <= query_pos, F32(0.0), F32(MASKED))

    if order is not None:
        bias_ref[0] = bias_block(0)
    else:

        def step(block, carry):
            bias_ref[block] = bias_block(block)
            return carry

        lax.fori_loop(0, bias_ref.shape[0], step, 0)


def attend_kernel(chunk_count, queries, bias, *rest):
    chunks = rest[:chunk_count]
    value_own, other, proj_own, proj_other, out_ref = rest[chunk_count : chunk_count + 5]
    scratch = rest[chunk_count + 5 :]
    proj, out_tiles, proj_sems, out_sems = scratch[:4]
    blocks, rows, block_rows = bias.shape
    copies = queries.shape[0] // rows
    half = proj_own.shape[0]
    width = out_ref.shape[1]
    core = lax.axis_index("heads")
    scale = math.log2(math.e) / math.sqrt(DH + DR)

    base = pl.multiple_of(core * width, 128)
    fetches = (
        pltpu.make_async_copy(
            proj_own.at[:, pl.ds(base, width)], proj.at[pl.ds(0, half)], proj_sems.at[0]
        ),
        pltpu.make_async_copy(proj_other, proj.at[pl.ds(half, half)], proj_sems.at[1]),
    )
    for fetch in fetches:
        fetch.start()

    def one_block(keys, bias_block, old):
        scores = lax.dot_general(
            queries[...], keys[...], (((1,), (1,)), ((), ())), preferred_element_type=F32
        )
        scores = scores + jnp.concatenate([bias_block] * copies, axis=0)
        top = jnp.max(scores, axis=-1, keepdims=True)
        if old is not None:
            top = jnp.maximum(old[0], top)
            rescale = jnp.exp2((old[0] - top) * scale)
            scores = jnp.where(scores > 0.5 * MASKED, scores, 2.0 * MASKED)
        expo = jnp.exp2((scores - top) * scale)
        total = jnp.sum(expo, axis=-1, keepdims=True)
        added = jnp.dot(expo.astype(BF16), keys[:, :DC], preferred_element_type=F32)
        if old is not None:
            total = old[1] * rescale + total
            added = old[2] * rescale + added
        return top, total, added

    if blocks == 1:
        keys = scratch[4]
        for index, chunk in enumerate(chunks):
            keys[pl.ds(index * rows, rows), :] = chunk[...]
        top, total, added = one_block(keys, bias[0], None)
    else:
        running = scratch[4:7]
        running[0][...] = jnp.full(running[0].shape, MASKED, F32)
        running[1][...] = jnp.zeros(running[1].shape, F32)
        running[2][...] = jnp.zeros(running[2].shape, F32)

        def step(block, carry):
            keys = chunks[0].at[pl.ds(pl.multiple_of(block * block_rows, block_rows), block_rows)]
            new = one_block(keys, bias[block], [state[...] for state in running])
            for state, value in zip(running, new):
                state[...] = value
            return carry

        lax.fori_loop(0, blocks, step, 0)
        total, added = running[1][...], running[2][...]
    mixed = (added / total).astype(BF16)
    heads = value_own.shape[1] // DH
    parts = []
    for group, value in enumerate((value_own, other.at[pl.ds(DC, DC)])):
        for head in range(heads):
            first = (group * heads + head) * rows
            per_head = jnp.dot(
                mixed[first : first + rows],
                value[:, head * DH : (head + 1) * DH],
                preferred_element_type=F32,
            )
            parts.append(per_head.astype(BF16))
    heads_out = jnp.concatenate(parts, axis=1)

    for fetch in fetches:
        fetch.wait()
    tiles = out_sems.shape[0]
    tile = width // tiles
    sends = []
    for index in range(tiles):
        part = pl.ds(index * tile, tile)
        out = jnp.dot(heads_out, proj[:, part], preferred_element_type=F32)
        out_tiles[:, part] = out.astype(BF16)
        sends.append(
            pltpu.make_async_copy(out_tiles.at[:, part], out_ref.at[:, part], out_sems.at[index])
        )
        sends[-1].start()
    for send in sends:
        send.wait()


def per_device(
    count, queries_nope, queries_rope, latent, key_rope, key_up, value_up, out_proj, span_order
):
    rows = latent.shape[0]
    width = out_proj.shape[1] // 2
    heads = 2 * (key_up.shape[1] // DH)
    query_rows = heads * rows
    direct = count == 8
    small = pltpu.CompilerParams(vmem_limit_bytes=SMALL_VMEM)

    def in_hbm(*arrays):
        return [pltpu.with_memory_space_constraint(array, pltpu.HBM) for array in arrays]

    def other_core(array):
        return lax.ppermute(array, "heads", [(0, 1), (1, 0)])

    def partners(array, steps):
        pairs = [
            (2 * index + core, 2 * (index ^ steps[core]) + core)
            for index in range(count)
            for core in range(2)
        ]
        return lax.ppermute(array, ("ctx", "heads"), pairs)

    packed = pl.pallas_call(
        pack_kernel,
        out_shape=jax.ShapeDtypeStruct((rows, DC + DR), BF16),
        in_specs=[vmem()] * 2,
        out_specs=vmem(),
        compiler_params=small,
        name="pack",
    )(*in_hbm(latent, key_rope.T))
    if direct:
        far = partners(packed, FAR)
        near = partners(packed, NEAR)
        beside = partners(packed, BESIDE)
        relayed = partners(far, (1, 1))
        chunks = [packed, beside]
        order = [(0, 0), BESIDE]
        for chunk, steps in ((near, NEAR), (far, FAR), (relayed, RELAYED)):
            chunks += [chunk, other_core(chunk)]
            order += [steps, steps[::-1]]
        blocks = 1
    else:
        chunks = [lax.all_gather(packed, "ctx", axis=0, tiled=True)]
        order = None
        blocks = count // 8

    small_rows = 2 * DC + 2 * rows
    bundle, proj_bundle = pl.pallas_call(
        bundle_kernel,
        out_shape=(
            jax.ShapeDtypeStruct((small_rows, key_up.shape[1]), BF16),
            jax.ShapeDtypeStruct((out_proj.shape[0], width), BF16),
        ),
        in_specs=[anywhere()] + [hbm()] * 5,
        out_specs=(anywhere(), anywhere()),
        scratch_shapes=[pltpu.SemaphoreType.DMA((5,))],
        compiler_params=small,
        name="bundle",
    )(packed, *in_hbm(queries_nope, queries_rope, key_up, value_up, out_proj))
    other = other_core(bundle)
    proj_other = other_core(proj_bundle)

    queries, bias = pl.pallas_call(
        functools.partial(query_kernel, order),
        out_shape=(
            jax.ShapeDtypeStruct((query_rows, DC + DR), BF16),
            jax.ShapeDtypeStruct((blocks, rows, 8 * rows), F32),
        ),
        in_specs=[smem()] + [vmem()] * 4,
        out_specs=(vmem(), vmem()),
        compiler_params=small,
        name="queries",
    )(span_order, queries_nope, queries_rope, key_up, other)

    tiles = 4 if width % 512 == 0 else 1
    scratch = [
        pltpu.VMEM((2 * out_proj.shape[0], width), BF16),
        pltpu.VMEM((rows, width), BF16),
        pltpu.SemaphoreType.DMA((2,)),
        pltpu.SemaphoreType.DMA((tiles,)),
    ]
    if direct:
        scratch.append(pltpu.VMEM((count * rows, DC + DR), BF16))
    else:
        scratch += [pltpu.VMEM((query_rows, size), F32) for size in (1, 1, DC)]
    return pl.pallas_call(
        functools.partial(attend_kernel, len(chunks)),
        out_shape=jax.ShapeDtypeStruct((rows, width), BF16),
        in_specs=[vmem()] * (2 + len(chunks) + 2) + [hbm(), anywhere()],
        out_specs=anywhere(),
        scratch_shapes=scratch,
        compiler_params=pltpu.CompilerParams(
            vmem_limit_bytes=SMALL_VMEM if direct else LARGE_VMEM
        ),
        name="attend",
    )(queries, bias, *chunks, value_up, other, *in_hbm(out_proj), proj_other)


def solution(mesh):
    in_specs = (
        P(("docs", "ctx"), "heads"),
        P(("docs", "ctx"), "heads"),
        P(("docs", "ctx"), None),
        P(("docs", "ctx"), None),
        P(None, "heads"),
        P(None, "heads"),
        P("heads", None),
        P("docs"),
    )
    out_specs = P(("docs", "ctx"), "heads")
    return jax.shard_map(
        functools.partial(per_device, mesh.shape["ctx"]),
        mesh=mesh,
        in_specs=in_specs,
        out_specs=out_specs,
        check_vma=False,
    )
```

time: 191 us -> 23.6 us (0.12)
  blocking collectives: 125 us -> 0 us
  other arithmetic: 22.6 us -> 0 us
  between operations: 16 us -> 0.08 us
  local copies, waits for them, and re-layouts: 9.29 us -> 0.03 us
  starting transfers between devices: 0.01 us -> 8.73 us
  matrix products: 7.15 us -> 0 us
  Pallas kernels: 0 us -> 6.69 us
  waiting for transfers between devices: 9.96 us -> 7.87 us
    all_gather x4 -> x0, blocking collectives: 125 us -> none  [the longest x1 32.3 us: per_device(): lax.all_gather(high_rope_own, 'ctx', axis=0, tiled=True)]
    add x7 -> x0, other arithmetic: 20.1 us -> none  [the longest x4 20 us: gathered_positions(): jnp.take(orders, row_ids // span_rows) * span_rows + row_ids % span_rows]
    reduce_scatter x1 -> x0, waiting for transfers between devices: 9.94 us -> none  [per_device(): lax.psum_scatter(partial_out.astype(jnp.bfloat16), 'heads', scatter_dimen...]
    ppermute x0 -> x9, starting transfers between devices: none -> 8.73 us  [the longest x4 7.62 us: partners(): return lax.ppermute(array, ('ctx', 'heads'), pairs)]
    ppermute x0 -> x9, waiting for transfers between devices: none -> 7.87 us  [the longest x4 7.85 us: partners(): return lax.ppermute(array, ('ctx', 'heads'), pairs)]
    dot_general x9 -> x0, matrix products: 7.15 us -> none  [the longest x1 3.86 us: per_device(): jnp.dot(heads_out, out_proj, preferred_element_type=jnp.float32)]
    pallas_call x0 -> x4, Pallas kernels: none -> 6.69 us  [the longest x1 3.15 us: per_device(): pl.pallas_call(functools.partial(attend_kernel, len(chunks)), out_shape=j...]
    slice x11 -> x0, local copies, waits for them, and re-layouts: 4.48 us -> none  [the longest x6 2.35 us: earlier_first(): turned = jnp.concatenate([array[span_rows:], array[:span_rows]], axis=0)]
  transfers between devices with their start and end apart: 1 -> 9, of which waited for: 1 -> 3; matrix products, arithmetic and copies ran while one was open for 0% -> 0% of each run, Pallas kernels for 0% -> 4%
where the time goes in v3:
time: 23.6 us; the launch traced here: 23.4 us
  starting transfers between devices  8.73 us (37%)
  waiting for transfers between devices  7.87 us (33%)
  Pallas kernels  6.69 us (28%)
    ppermute x4, waiting for transfers between devices, partners(): return lax.ppermute(array, ('ctx', 'heads'), pairs)  7.85 us
    ppermute x4, starting transfers between devices, partners(): return lax.ppermute(array, ('ctx', 'heads'), pairs)  7.62 us
    pallas_call x1, Pallas kernels, per_device(): pl.pallas_call(functools.partial(attend_kernel, len(chunks)), out_shape=j...  3.15 us
    pallas_call x1, Pallas kernels, per_device(): pl.pallas_call(bundle_kernel, out_shape=(jax.ShapeDtypeStruct((small_rows...  1.7 us
    ppermute x5, starting transfers between devices, other_core(): return lax.ppermute(array, 'heads', [(0, 1), (1, 0)])  1.11 us
    pallas_call x1, Pallas kernels, per_device(): pl.pallas_call(pack_kernel, out_shape=jax.ShapeDtypeStruct((rows, DC + DR...  0.99 us
    pallas_call x1, Pallas kernels, per_device(): pl.pallas_call(functools.partial(query_kernel, order), out_shape=(jax.Sha...  0.85 us
  transfers between devices with their start and end apart: 9, of which 3 were waited for; matrix products, arithmetic and copies ran while one was open for 0% of the time, Pallas kernels for 4%

profile of v3, /device:TPU:0, one launch (start us, length us, event | category | flops | bytes accessed | tf_op | source)
XLA Modules:
  0.0 23.4 jit_solution(17288795979096522308)
XLA Ops:
  0.0 1.0 %pack.1.packed.rest_0_ = bf16[96,576]{1,0:T(8,128)(2,1)S(1)} custom-call(bf16[96,512]{1,0:T(8,128)(2,1)} %latent.1, bf16[64,96]{1,0:T(8,128)(2,1)} %bitcast.1), custom_call_target="tpu_custom_call" | custom-call | tf_op jit(solution)/shard_map/pack/pallas_call | solution.py:232
  1.0 0.0 copy-start
  1.0 0.0 copy-start.2
  1.0 0.0 copy-start.3
  1.0 0.0 copy-start.4
  1.0 0.0 copy-start.1
  1.1 1.7 %bundle.1 = (bf16[1216,256]{1,0:T(8,128)(2,1)S(1)}, bf16[256,3584]{1,0:T(8,128)(2,1)S(1)}) custom-call(bf16[96,576]{1,0:T(8,128)(2,1)S(1)} %pack.1.packed.rest_0_, bf16[96,256]{1,0:T(8,128)(2,1)} %nope_own.1, bf16[96,128]{1,0:T(8,128)(2,1)} %rope_own.1, bf16[512,256]{1,0:T(8,128)(2,1)} %up_own.1, bf16[512,256]{1,0:T(8,128)(2,1)} %rest_8_.1, ...), custom_call_target="tpu_custom_call" | custom-call | tf_op jit(solution)/shard_map/bundle/pallas_call | solution.py:257
  2.8 0.5 %collective-permute-start.8 = (bf16[256,3584]{1,0:T(8,128)(2,1)S(1)}, bf16[256,3584]{1,0:T(8,128)(2,1)S(1)}, u32[]{:S(2)}, u32[]{:S(2)}) collective-permute-start(bf16[256,3584]{1,0:T(8,128)(2,1)S(1)} %get-tuple-element.12), channel_id=1, source_target_pairs={{0,1},{1,0},{2,3},{3,2},{4,5},{5,4},{6,7},{7,6},{8,9},{9,8},{10,11... | collective-permute-start | bytes 5505032 | tf_op jit(solution)/shard_map/ppermute | solution.py:222
  3.3 0.1 collective-permute-start
  3.4 4.0 %collective-permute-start.4 = (bf16[96,576]{1,0:T(8,128)(2,1)S(1)}, bf16[96,576]{1,0:T(8,128)(2,1)S(1)}, u32[]{:S(2)}, u32[]{:S(2)}) collective-permute-start(bf16[96,576]{1,0:T(8,128)(2,1)S(1)} %pack.1.packed.rest_0_), channel_id=1, source_target_pairs={{0,8},{1,13},{2,10},{3,15},{4,12},{5,9},{6,14},{7,11},{8,0},{9,5},... | collective-permute-start | bytes 331784 | tf_op jit(solution)/shard_map/ppermute | solution.py:230
  7.4 1.6 %collective-permute-start.2 = (bf16[96,576]{1,0:T(8,128)(2,1)S(1)}, bf16[96,576]{1,0:T(8,128)(2,1)S(1)}, u32[]{:S(2)}, u32[]{:S(2)}) collective-permute-start(bf16[96,576]{1,0:T(8,128)(2,1)S(1)} %pack.1.packed.rest_0_), channel_id=1, source_target_pairs={{0,4},{1,7},{2,6},{3,5},{4,0},{5,3},{6,2},{7,1},{8,12},{9,15},{10,... | collective-permute-start | bytes 331784 | tf_op jit(solution)/shard_map/ppermute | solution.py:230
  9.0 4.9 %collective-permute-done.4.rest_4_ = bf16[96,576]{1,0:T(8,128)(2,1)S(1)} collective-permute-done((bf16[96,576]{1,0:T(8,128)(2,1)S(1)}, bf16[96,576]{1,0:T(8,128)(2,1)S(1)}, u32[]{:S(2)}, u32[]{:S(2)}) %collective-permute-start.4) | collective-permute-done | bytes 110624 | tf_op jit(solution)/shard_map/ppermute | solution.py:230
  13.8 1.5 %collective-permute-start.6 = (bf16[96,576]{1,0:T(8,128)(2,1)S(1)}, bf16[96,576]{1,0:T(8,128)(2,1)S(1)}, u32[]{:S(2)}, u32[]{:S(2)}) collective-permute-start(bf16[96,576]{1,0:T(8,128)(2,1)S(1)} %collective-permute-done.4.rest_4_), channel_id=1, source_target_pairs={{0,2},{1,3},{2,0},{3,1},{4,6},{5,7},{6,4},{7,5},{8,10},{9,11},{10,... | collective-permute-start | bytes 331784 | tf_op jit(solution)/shard_map/ppermute | solution.py:230
  15.3 0.5 %collective-permute-start.1 = (bf16[96,576]{1,0:T(8,128)(2,1)S(1)}, bf16[96,576]{1,0:T(8,128)(2,1)S(1)}, u32[]{:S(2)}, u32[]{:S(2)}) collective-permute-start(bf16[96,576]{1,0:T(8,128)(2,1)S(1)} %pack.1.packed.rest_0_), channel_id=1, source_target_pairs={{0,2},{1,3},{2,0},{3,1},{4,6},{5,7},{6,4},{7,5},{8,10},{9,11},{10,... | collective-permute-start | bytes 331784 | tf_op jit(solution)/shard_map/ppermute | solution.py:230
  15.9 0.0 collective-permute-done.2.rest_2_
  15.9 0.0 collective-permute-start.5
  15.9 2.8 %collective-permute-done.6.rest_6_ = bf16[96,576]{1,0:T(8,128)(2,1)S(1)} collective-permute-done((bf16[96,576]{1,0:T(8,128)(2,1)S(1)}, bf16[96,576]{1,0:T(8,128)(2,1)S(1)}, u32[]{:S(2)}, u32[]{:S(2)}) %collective-permute-start.6) | collective-permute-done | bytes 110624 | tf_op jit(solution)/shard_map/ppermute | solution.py:230
  18.7 0.0 collective-permute-start.3
  18.7 0.0 collective-permute-done.other.rest_9_
  18.7 0.5 %collective-permute-start.7 = (bf16[96,576]{1,0:T(8,128)(2,1)S(1)}, bf16[96,576]{1,0:T(8,128)(2,1)S(1)}, u32[]{:S(2)}, u32[]{:S(2)}) collective-permute-start(bf16[96,576]{1,0:T(8,128)(2,1)S(1)} %collective-permute-done.6.rest_6_), channel_id=1, source_target_pairs={{0,1},{1,0},{2,3},{3,2},{4,5},{5,4},{6,7},{7,6},{8,9},{9,8},{10,11... | collective-permute-start | bytes 331784 | tf_op jit(solution)/shard_map/ppermute | solution.py:222
  19.2 0.0 copy-done
  19.2 0.0 copy-done.2
  19.2 0.0 copy-done.3
  19.2 0.0 copy-done.4
  19.2 0.8 %queries.1 = (bf16[384,576]{1,0:T(8,128)(2,1)S(1)}, f32[1,96,768]{2,1,0:T(8,128)S(1)}) custom-call(s32[16]{0:T(128)S(1)} %copy-done.4, bf16[96,256]{1,0:T(8,128)(2,1)S(1)} %copy-done.2, bf16[96,128]{1,0:T(8,128)(2,1)S(1)} %copy-done.3, bf16[512,256]{1,0:T(8,128)(2,1)S(1)} %copy-done, bf16[1216,256]{1,0:T(8,128)(2,1)S(1)} %collective-permute-done.other.rest_9_), custom_call_target="tpu_custom_call" | custom-call | tf_op jit(solution)/shard_map/queries/pallas_call | solution.py:272
  20.1 0.1 collective-permute-done.1.rest_1_
  20.2 0.0 collective-permute-done.5.rest_5_
  20.2 0.0 collective-permute-done.3.rest_3_
  20.2 0.0 collective-permute-done.7.rest_7_
  20.2 0.0 collective-permute-done.8.rest_11_
  20.2 0.0 copy-done.1
  20.2 3.2 %attend.1 = bf16[96,3584]{1,0:T(8,128)(2,1)} custom-call(bf16[384,576]{1,0:T(8,128)(2,1)S(1)} %get-tuple-element.10.queries, f32[1,96,768]{2,1,0:T(8,128)S(1)} %get-tuple-element.11.bias, bf16[96,576]{1,0:T(8,128)(2,1)S(1)} %pack.1.packed.rest_0_, bf16[96,576]{1,0:T(8,128)(2,1)S(1)} %collective-permute-done.1.rest_1_, ...), custom_call_target="tpu_custom_call" | custom-call | tf_op jit(solution)/shard_map/attend/pallas_call | solution.py:295
Async XLA Ops:
  1.0 18.2 %copy-start = (bf16[512,256]{1,0:T(8,128)(2,1)S(1)}, bf16[512,256]{1,0:T(8,128)(2,1)}, u32[]{:S(2)}) copy-start(bf16[512,256]{1,0:T(8,128)(2,1)} %up_own.1) | copy-start | bytes 786436
  1.0 18.2 %copy-start.2 = (bf16[96,256]{1,0:T(8,128)(2,1)S(1)}, bf16[96,256]{1,0:T(8,128)(2,1)}, u32[]{:S(2)}) copy-start(bf16[96,256]{1,0:T(8,128)(2,1)} %nope_own.1) | copy-start | bytes 147460
  1.0 18.2 %copy-start.3 = (bf16[96,128]{1,0:T(8,128)(2,1)S(1)}, bf16[96,128]{1,0:T(8,128)(2,1)}, u32[]{:S(2)}) copy-start(bf16[96,128]{1,0:T(8,128)(2,1)} %rope_own.1) | copy-start | bytes 73732
  1.0 18.2 %copy-start.4 = (s32[16]{0:T(128)S(1)}, s32[16]{0:T(128)}, u32[]{:S(2)}) copy-start(s32[16]{0:T(128)} %span_order.1) | copy-start | bytes 196
  1.0 19.2 %copy-start.1 = (bf16[512,256]{1,0:T(8,128)(2,1)S(1)}, bf16[512,256]{1,0:T(8,128)(2,1)}, u32[]{:S(2)}) copy-start(bf16[512,256]{1,0:T(8,128)(2,1)} %rest_8_.1) | copy-start | bytes 786436
  2.8 17.5 %collective-permute-start.8 = (bf16[256,3584]{1,0:T(8,128)(2,1)S(1)}, bf16[256,3584]{1,0:T(8,128)(2,1)S(1)}, u32[]{:S(2)}, u32[]{:S(2)}) collective-permute-start(bf16[256,3584]{1,0:T(8,128)(2,1)S(1)} %get-tuple-element.12), channel_id=1, source_target_pairs={{0,1},{1,0},{2,3},{3,2},{4,5},{5,4},{6,7},{7,6},{8,9},{9,8},{10,11... | collective-permute-start | bytes 5505032 | tf_op jit(solution)/shard_map/ppermute | solution.py:222
  3.3 15.4 %collective-permute-start = (bf16[1216,256]{1,0:T(8,128)(2,1)S(1)}, bf16[1216,256]{1,0:T(8,128)(2,1)S(1)}, u32[]{:S(2)}, u32[]{:S(2)}) collective-permute-start(bf16[1216,256]{1,0:T(8,128)(2,1)S(1)} %get-tuple-element.9), channel_id=1, source_target_pairs={{0,1},{1,0},{2,3},{3,2},{4,5},{5,4},{6,7},{7,6},{8,9},{9,8},{10,11... | collective-permute-start | bytes 1867784 | tf_op jit(solution)/shard_map/ppermute | solution.py:222
  3.4 10.5 %collective-permute-start.4 = (bf16[96,576]{1,0:T(8,128)(2,1)S(1)}, bf16[96,576]{1,0:T(8,128)(2,1)S(1)}, u32[]{:S(2)}, u32[]{:S(2)}) collective-permute-start(bf16[96,576]{1,0:T(8,128)(2,1)S(1)} %pack.1.packed.rest_0_), channel_id=1, source_target_pairs={{0,8},{1,13},{2,10},{3,15},{4,12},{5,9},{6,14},{7,11},{8,0},{9,5},... | collective-permute-start | bytes 331784 | tf_op jit(solution)/shard_map/ppermute | solution.py:230
  7.4 8.5 %collective-permute-start.2 = (bf16[96,576]{1,0:T(8,128)(2,1)S(1)}, bf16[96,576]{1,0:T(8,128)(2,1)S(1)}, u32[]{:S(2)}, u32[]{:S(2)}) collective-permute-start(bf16[96,576]{1,0:T(8,128)(2,1)S(1)} %pack.1.packed.rest_0_), channel_id=1, source_target_pairs={{0,4},{1,7},{2,6},{3,5},{4,0},{5,3},{6,2},{7,1},{8,12},{9,15},{10,... | collective-permute-start | bytes 331784 | tf_op jit(solution)/shard_map/ppermute | solution.py:230
  13.8 4.9 %collective-permute-start.6 = (bf16[96,576]{1,0:T(8,128)(2,1)S(1)}, bf16[96,576]{1,0:T(8,128)(2,1)S(1)}, u32[]{:S(2)}, u32[]{:S(2)}) collective-permute-start(bf16[96,576]{1,0:T(8,128)(2,1)S(1)} %collective-permute-done.4.rest_4_), channel_id=1, source_target_pairs={{0,2},{1,3},{2,0},{3,1},{4,6},{5,7},{6,4},{7,5},{8,10},{9,11},{10,... | collective-permute-start | bytes 331784 | tf_op jit(solution)/shard_map/ppermute | solution.py:230
  15.3 4.9 %collective-permute-start.1 = (bf16[96,576]{1,0:T(8,128)(2,1)S(1)}, bf16[96,576]{1,0:T(8,128)(2,1)S(1)}, u32[]{:S(2)}, u32[]{:S(2)}) collective-permute-start(bf16[96,576]{1,0:T(8,128)(2,1)S(1)} %pack.1.packed.rest_0_), channel_id=1, source_target_pairs={{0,2},{1,3},{2,0},{3,1},{4,6},{5,7},{6,4},{7,5},{8,10},{9,11},{10,... | collective-permute-start | bytes 331784 | tf_op jit(solution)/shard_map/ppermute | solution.py:230
  15.9 4.3 %collective-permute-start.5 = (bf16[96,576]{1,0:T(8,128)(2,1)S(1)}, bf16[96,576]{1,0:T(8,128)(2,1)S(1)}, u32[]{:S(2)}, u32[]{:S(2)}) collective-permute-start(bf16[96,576]{1,0:T(8,128)(2,1)S(1)} %collective-permute-done.4.rest_4_), channel_id=1, source_target_pairs={{0,1},{1,0},{2,3},{3,2},{4,5},{5,4},{6,7},{7,6},{8,9},{9,8},{10,11... | collective-permute-start | bytes 331784 | tf_op jit(solution)/shard_map/ppermute | solution.py:222
  18.7 1.5 %collective-permute-start.3 = (bf16[96,576]{1,0:T(8,128)(2,1)S(1)}, bf16[96,576]{1,0:T(8,128)(2,1)S(1)}, u32[]{:S(2)}, u32[]{:S(2)}) collective-permute-start(bf16[96,576]{1,0:T(8,128)(2,1)S(1)} %collective-permute-done.2.rest_2_), channel_id=1, source_target_pairs={{0,1},{1,0},{2,3},{3,2},{4,5},{5,4},{6,7},{7,6},{8,9},{9,8},{10,11... | collective-permute-start | bytes 331784 | tf_op jit(solution)/shard_map/ppermute | solution.py:222
  18.7 1.5 %collective-permute-start.7 = (bf16[96,576]{1,0:T(8,128)(2,1)S(1)}, bf16[96,576]{1,0:T(8,128)(2,1)S(1)}, u32[]{:S(2)}, u32[]{:S(2)}) collective-permute-start(bf16[96,576]{1,0:T(8,128)(2,1)S(1)} %collective-permute-done.6.rest_6_), channel_id=1, source_target_pairs={{0,1},{1,0},{2,3},{3,2},{4,5},{5,4},{6,7},{7,6},{8,9},{9,8},{10,11... | collective-permute-start | bytes 331784 | tf_op jit(solution)/shard_map/ppermute | solution.py:222

commit v4 on v3

v4 whole, which is shorter than its diff:
```python
import functools
import math

import jax
import jax.numpy as jnp
from jax import lax
from jax.experimental import pallas as pl
from jax.experimental.pallas import tpu as pltpu
from jax.sharding import PartitionSpec as P

DC = 512
DH = 128
DR = 64
BF16 = jnp.bfloat16
F32 = jnp.float32
MASKED = -1e30
BLOCK_CHUNKS = 8
CUT_COST, QUERY_COST, EARLY_COST = 0, 0, 30
SMALL_VMEM = 20 * 1024 * 1024
LARGE_VMEM = 56 * 1024 * 1024
FAR = (4, 6)
NEAR = (2, 3)
BESIDE = (1, 1)
RELAYED = (5, 7)


def vmem():
    return pl.BlockSpec(memory_space=pltpu.VMEM)


def anywhere():
    return pl.BlockSpec(memory_space=pl.ANY)


def hbm():
    return pl.BlockSpec(memory_space=pltpu.HBM)


def cost(microseconds):
    return pl.CostEstimate(flops=int(microseconds * 1.1e9), bytes_accessed=0, transcendentals=0)


def smem():
    return pl.BlockSpec(memory_space=pltpu.SMEM)


def pack_kernel(latent, key_rope_turned, out_ref):
    rows = latent.shape[0]
    group = rows // 6
    out_ref[:rows] = latent[...]
    rope = key_rope_turned[...].astype(F32).T.astype(BF16)
    parts = [rope[index * group : (index + 1) * group] for index in range(6)]
    parts.append(jnp.zeros((group, DC - 6 * DR), BF16))
    out_ref[rows:] = jnp.concatenate(parts, axis=1)


def unpack(chunk, keys, base):
    rows = 6 * chunk.shape[0] // 7
    group = rows // 6
    keys[pl.ds(base, rows), :DC] = chunk[:rows]
    for index in range(6):
        part = chunk[rows:, index * DR : (index + 1) * DR]
        keys[pl.ds(base + index * group, group), DC:] = part


def cut_kernel(_, out_proj, out_ref, sem):
    width = out_ref.shape[1]
    base = pl.multiple_of((1 - lax.axis_index("heads")) * width, 128)
    copy = pltpu.make_async_copy(out_proj.at[:, pl.ds(base, width)], out_ref, sem)
    copy.start()
    copy.wait()


def query_kernel(order, span_order, _, nope, rope, up, out_ref, *biases):
    rows = nope.shape[0]
    heads = nope.shape[1] // DH
    span_rows = rows // 2
    own_index = lax.axis_index("ctx")
    core = lax.axis_index("heads")
    for head in range(heads):
        part = pl.ds(head * rows, rows)
        latent = lax.dot_general(
            nope[:, head * DH : (head + 1) * DH],
            up[:, head * DH : (head + 1) * DH],
            (((1,), (1,)), ((), ())),
            preferred_element_type=F32,
        )
        out_ref[part, :DC] = latent.astype(BF16)
        out_ref[part, DC:] = rope[:, head * DR : (head + 1) * DR]
    row = lax.broadcasted_iota(jnp.int32, (rows, 1), 0)
    query_pos = jnp.where(
        row < span_rows,
        span_order[2 * own_index] * span_rows + row,
        span_order[2 * own_index + 1] * span_rows + row - span_rows,
    )

    def bias_of(owners):
        column = lax.broadcasted_iota(jnp.int32, (1, len(owners) * rows), 1)
        key_pos = jnp.zeros(column.shape, jnp.int32)
        for index, owner in enumerate(owners):
            for side in range(2):
                start = index * rows + side * span_rows
                first = span_order[2 * owner + side] * span_rows
                key_pos = jnp.where(column >= start, first + column - start, key_pos)
        return jnp.where(key_pos <= query_pos, F32(0.0), F32(MASKED))

    if order is not None:
        for steps, bias_ref in zip(order, biases):
            bias_ref[0] = bias_of(
                [own_index ^ jnp.where(core == 0, step[0], step[1]) for step in steps]
            )
    else:
        bias_ref = biases[0]

        def step(block, carry):
            bias_ref[block] = bias_of([block * BLOCK_CHUNKS + index for index in range(BLOCK_CHUNKS)])
            return carry

        lax.fori_loop(0, bias_ref.shape[0], step, 0)


def attend_block(queries, keys, bias, old):
    copies = 2 * queries[0].shape[0] // bias.shape[0]
    scale = math.log2(math.e) / math.sqrt(DH + DR)
    both = jnp.concatenate([part[...] for part in queries], axis=0)
    scores = lax.dot_general(
        both, keys[...], (((1,), (1,)), ((), ())), preferred_element_type=F32
    )
    scores = scores + jnp.concatenate([bias] * copies, axis=0)
    top = jnp.max(scores, axis=-1, keepdims=True)
    if old is not None:
        top = jnp.maximum(old[0], top)
        rescale = jnp.exp2((old[0] - top) * scale)
    expo = jnp.exp2((scores - top) * scale)
    total = jnp.sum(expo, axis=-1, keepdims=True)
    added = jnp.dot(expo.astype(BF16), keys[:, :DC], preferred_element_type=F32)
    if old is not None:
        total = old[1] * rescale + total
        added = old[2] * rescale + added
    return top, total, added


def early_kernel(queries_own, queries_other, bias, *rest):
    queries = (queries_own, queries_other)
    chunks, running, keys = rest[:-4], rest[-4:-1], rest[-1]
    blocks, rows, _ = bias.shape
    if blocks == 1:
        for index, chunk in enumerate(chunks):
            unpack(chunk, keys, index * rows)
        values = attend_block(queries, keys, bias[0], None)
        for state, value in zip(running, values):
            state[...] = value
        return
    gathered = chunks[0]

    def fill(block):
        for index in range(BLOCK_CHUNKS):
            unpack(gathered.at[block * BLOCK_CHUNKS + index], keys, index * rows)

    first = lax.axis_index("ctx") // BLOCK_CHUNKS
    fill(first)
    values = attend_block(queries, keys, bias[first], None)
    for state, value in zip(running, values):
        state[...] = value

    def step(index, carry):
        block = index + jnp.where(index >= first, 1, 0)
        fill(block)
        new = attend_block(queries, keys, bias[block], [state[...] for state in running])
        for state, value in zip(running, new):
            state[...] = value
        return carry

    lax.fori_loop(0, blocks - 1, step, 0)


def finish_kernel(late_count, queries_own, queries_other, top, total, context, *rest):
    bias, chunks = rest[:late_count][:1], rest[1 : 1 + late_count]
    rest = rest[len(bias) + len(chunks) :]
    value_own, value_other, proj_own, proj_other, out_ref, proj, out_tiles, keys, proj_sems, out_sems = rest
    rows, width = out_ref.shape
    half = proj_own.shape[0]
    core = lax.axis_index("heads")

    base = pl.multiple_of(core * width, 128)
    fetches = (
        pltpu.make_async_copy(
            proj_own.at[:, pl.ds(base, width)], proj.at[pl.ds(0, half)], proj_sems.at[0]
        ),
        pltpu.make_async_copy(proj_other, proj.at[pl.ds(half, half)], proj_sems.at[1]),
    )
    for fetch in fetches:
        fetch.start()

    running = (top[...], total[...], context[...])
    if late_count:
        for index, chunk in enumerate(chunks):
            unpack(chunk, keys, index * rows)
        running = attend_block((queries_own, queries_other), keys, bias[0][0], running)
    mixed = (running[2] / running[1]).astype(BF16)
    heads = value_own.shape[1] // DH
    parts = []
    for group, value in enumerate((value_own, value_other)):
        for head in range(heads):
            first = (group * heads + head) * rows
            per_head = jnp.dot(
                mixed[first : first + rows],
                value[:, head * DH : (head + 1) * DH],
                preferred_element_type=F32,
            )
            parts.append(per_head.astype(BF16))
    heads_out = jnp.concatenate(parts, axis=1)

    for fetch in fetches:
        fetch.wait()
    tiles = out_sems.shape[0]
    tile = width // tiles
    sends = []
    for index in range(tiles):
        part = pl.ds(index * tile, tile)
        out = jnp.dot(heads_out, proj[:, part], preferred_element_type=F32)
        out_tiles[:, part] = out.astype(BF16)
        sends.append(
            pltpu.make_async_copy(out_tiles.at[:, part], out_ref.at[:, part], out_sems.at[index])
        )
        sends[-1].start()
    for send in sends:
        send.wait()


def per_device(
    count, queries_nope, queries_rope, latent, key_rope, key_up, value_up, out_proj, span_order
):
    rows = latent.shape[0]
    width = out_proj.shape[1] // 2
    heads = 2 * (key_up.shape[1] // DH)
    query_rows = heads * rows
    direct = count == 8
    small = pltpu.CompilerParams(vmem_limit_bytes=SMALL_VMEM)

    def in_hbm(*arrays):
        return [pltpu.with_memory_space_constraint(array, pltpu.HBM) for array in arrays]

    def other_core(array):
        return lax.ppermute(array, "heads", [(0, 1), (1, 0)])

    def partners(array, steps):
        pairs = [
            (2 * index + core, 2 * (index ^ steps[core]) + core)
            for index in range(count)
            for core in range(2)
        ]
        return lax.ppermute(array, ("ctx", "heads"), pairs)

    def cut(after):
        return pl.pallas_call(
            cut_kernel,
            out_shape=jax.ShapeDtypeStruct((out_proj.shape[0], width), BF16),
            in_specs=[anywhere(), hbm()],
            out_specs=anywhere(),
            scratch_shapes=[pltpu.SemaphoreType.DMA],
            compiler_params=small,
            cost_estimate=cost(CUT_COST),
            name="cut",
        )(after, *in_hbm(out_proj))

    packed = pl.pallas_call(
        pack_kernel,
        out_shape=jax.ShapeDtypeStruct((rows + rows // 6, DC), BF16),
        in_specs=[vmem()] * 2,
        out_specs=vmem(),
        compiler_params=small,
        name="pack",
    )(*in_hbm(latent, key_rope.T))
    if direct:
        far = partners(packed, FAR)
        near = partners(packed, NEAR)
        beside = partners(packed, BESIDE)
        proj_cut = cut(near)
        far, _ = lax.optimization_barrier((far, proj_cut))
        relayed = partners(far, (1, 1))
        early = [packed, beside, near, other_core(near), far, other_core(far)]
        late = [relayed, other_core(relayed)]
        order = [
            [(0, 0), BESIDE, NEAR, NEAR[::-1], FAR, FAR[::-1]],
            [RELAYED, RELAYED[::-1]],
        ]
        bias_shapes = [(1, rows, len(steps) * rows) for steps in order]
    else:
        proj_cut = cut(packed)
        early, late, order = [lax.all_gather(packed, "ctx", axis=0)], [], None
        bias_shapes = [(count // BLOCK_CHUNKS, rows, BLOCK_CHUNKS * rows)]

    queries, *biases = pl.pallas_call(
        functools.partial(query_kernel, order),
        out_shape=[jax.ShapeDtypeStruct((query_rows // 2, DC + DR), BF16)]
        + [jax.ShapeDtypeStruct(shape, F32) for shape in bias_shapes],
        in_specs=[smem(), anywhere()] + [vmem()] * 3,
        out_specs=[vmem()] * (1 + len(bias_shapes)),
        compiler_params=small,
        cost_estimate=cost(QUERY_COST),
        name="queries",
    )(span_order, packed, *in_hbm(queries_nope, queries_rope, key_up))
    queries_other = other_core(queries)
    value_other = other_core(value_up)
    proj_other = other_core(proj_cut)
    running = pl.pallas_call(
        early_kernel,
        out_shape=[jax.ShapeDtypeStruct((query_rows, size), F32) for size in (1, 1, DC)],
        in_specs=[vmem()] * (3 + len(early)),
        out_specs=[vmem()] * 3,
        scratch_shapes=[pltpu.VMEM((bias_shapes[0][2], DC + DR), BF16)],
        compiler_params=pltpu.CompilerParams(
            vmem_limit_bytes=SMALL_VMEM if direct else LARGE_VMEM
        ),
        cost_estimate=cost(EARLY_COST),
        name="early",
    )(queries, queries_other, biases[0], *early)

    tiles = 4 if width % 512 == 0 else 1
    return pl.pallas_call(
        functools.partial(finish_kernel, len(late)),
        out_shape=jax.ShapeDtypeStruct((rows, width), BF16),
        in_specs=[vmem()] * (5 + len(biases[1:]) + len(late) + 2) + [hbm(), anywhere()],
        out_specs=anywhere(),
        scratch_shapes=[
            pltpu.VMEM((2 * out_proj.shape[0], width), BF16),
            pltpu.VMEM((rows, width), BF16),
            pltpu.VMEM((max(1, len(late)) * rows, DC + DR), BF16),
            pltpu.SemaphoreType.DMA((2,)),
            pltpu.SemaphoreType.DMA((tiles,)),
        ],
        compiler_params=small,
        name="finish",
    )(
        queries,
        queries_other,
        *running,
        *biases[1:],
        *late,
        value_up,
        value_other,
        *in_hbm(out_proj),
        proj_other,
    )


def solution(mesh):
    in_specs = (
        P(("docs", "ctx"), "heads"),
        P(("docs", "ctx"), "heads"),
        P(("docs", "ctx"), None),
        P(("docs", "ctx"), None),
        P(None, "heads"),
        P(None, "heads"),
        P("heads", None),
        P("docs"),
    )
    out_specs = P(("docs", "ctx"), "heads")
    return jax.shard_map(
        functools.partial(per_device, mesh.shape["ctx"]),
        mesh=mesh,
        in_specs=in_specs,
        out_specs=out_specs,
        check_vma=False,
    )
```

time: 23.6 us -> 22.2 us (0.941)
  waiting for transfers between devices: 7.87 us -> 4.4 us
  Pallas kernels: 6.69 us -> 7.97 us
  local copies, waits for them, and re-layouts: 0.03 us -> 0.66 us
    ppermute x4, waiting for transfers between devices: 7.85 us -> 4.33 us  [partners(): return lax.ppermute(array, ('ctx', 'heads'), pairs)]
    pallas_call x4 -> x5, Pallas kernels: 6.69 us -> 7.97 us  [the longest x1 2.95 us: per_device(): pl.pallas_call(functools.partial(finish_kernel, len(late)), out_shape=jax...]
    unnamed x10 -> x4, local copies, waits for them, and re-layouts: 0.03 us -> 0.66 us
    ppermute x5 -> x6, starting transfers between devices: 1.11 us -> 1.17 us  [other_core(): return lax.ppermute(array, 'heads', [(0, 1), (1, 0)])]
  transfers between devices with their start and end apart: 9 -> 10, of which waited for: 3 -> 4; matrix products, arithmetic and copies ran while one was open for 0% -> 0% of each run, Pallas kernels for 4% -> 18%
where the time goes in v4:
time: 22.2 us; the launch traced here: 22 us
  starting transfers between devices  8.92 us (40%)
  Pallas kernels  7.97 us (36%)
  waiting for transfers between devices  4.4 us (20%)
  local copies, waits for them, and re-layouts  0.66 us (3%)
    ppermute x4, starting transfers between devices, partners(): return lax.ppermute(array, ('ctx', 'heads'), pairs)  7.74 us
    ppermute x4, waiting for transfers between devices, partners(): return lax.ppermute(array, ('ctx', 'heads'), pairs)  4.33 us
    pallas_call x1, Pallas kernels, per_device(): pl.pallas_call(functools.partial(finish_kernel, len(late)), out_shape=jax...  2.95 us
    pallas_call x1, Pallas kernels, cut(): pl.pallas_call(cut_kernel, out_shape=jax.ShapeDtypeStruct((out_proj.shape...  1.51 us
    pallas_call x1, Pallas kernels, per_device(): pl.pallas_call(early_kernel, out_shape=[jax.ShapeDtypeStruct((query_rows,...  1.24 us
    pallas_call x1, Pallas kernels, per_device(): pl.pallas_call(functools.partial(query_kernel, order), out_shape=[jax.Sha...  1.22 us
    ppermute x6, starting transfers between devices, other_core(): return lax.ppermute(array, 'heads', [(0, 1), (1, 0)])  1.17 us
    pallas_call x1, Pallas kernels, per_device(): pl.pallas_call(pack_kernel, out_shape=jax.ShapeDtypeStruct((rows + rows /...  1.05 us
  transfers between devices with their start and end apart: 10, of which 4 were waited for; matrix products, arithmetic and copies ran while one was open for 0% of the time, Pallas kernels for 18%

profile of v4, /device:TPU:0, one launch (start us, length us, event | category | flops | bytes accessed | tf_op | source)
XLA Modules:
  0.0 22.0 jit_solution(6475473255444281914)
XLA Ops:
  0.0 1.0 %pack.1._.rest_0_ = bf16[112,512]{1,0:T(8,128)(2,1)S(1)} custom-call(bf16[96,512]{1,0:T(8,128)(2,1)} %latent.1, bf16[64,96]{1,0:T(8,128)(2,1)} %bitcast.1), custom_call_target="tpu_custom_call" | custom-call | tf_op jit(solution)/shard_map/pack/pallas_call | solution.py:267
  1.0 3.0 %collective-permute-start.2 = (bf16[112,512]{1,0:T(8,128)(2,1)S(1)}, bf16[112,512]{1,0:T(8,128)(2,1)S(1)}, u32[]{:S(2)}, u32[]{:S(2)}) collective-permute-start(bf16[112,512]{1,0:T(8,128)(2,1)S(1)} %pack.1._.rest_0_), channel_id=1, source_target_pairs={{0,4},{1,7},{2,6},{3,5},{4,0},{5,3},{6,2},{7,1},{8,12},{9,15},{10,... | collective-permute-start | bytes 344072 | tf_op jit(solution)/shard_map/ppermute | solution.py:253
  4.1 2.6 %collective-permute-start.4 = (bf16[112,512]{1,0:T(8,128)(2,1)S(1)}, bf16[112,512]{1,0:T(8,128)(2,1)S(1)}, u32[]{:S(2)}, u32[]{:S(2)}) collective-permute-start(bf16[112,512]{1,0:T(8,128)(2,1)S(1)} %pack.1._.rest_0_), channel_id=1, source_target_pairs={{0,8},{1,13},{2,10},{3,15},{4,12},{5,9},{6,14},{7,11},{8,0},{9,5},... | collective-permute-start | bytes 344072 | tf_op jit(solution)/shard_map/ppermute | solution.py:253
  6.7 0.0 copy-start.1
  6.7 0.7 %copy-done.1 = s32[16]{0:T(128)S(1)} copy-done((s32[16]{0:T(128)S(1)}, s32[16]{0:T(128)}, u32[]{:S(2)}) %copy-start.1) | copy-done | bytes 88
  7.3 1.2 %queries.1 = (bf16[192,576]{1,0:T(8,128)(2,1)S(1)}, f32[1,96,576]{2,1,0:T(8,128)S(1)}, f32[1,96,192]{2,1,0:T(8,128)S(1)}) custom-call(s32[16]{0:T(128)S(1)} %copy-done.1, bf16[112,512]{1,0:T(8,128)(2,1)S(1)} %pack.1._.rest_0_, bf16[96,256]{1,0:T(8,128)(2,1)} %nope.1, bf16[96,128]{1,0:T(8,128)(2,1)} %rope.1, bf16[512,256]{1,0:T(8,128)(2,1)} %up.1), custom_call_target="tpu_custom_call" | custom-call | tf_op jit(solution)/shard_map/queries/pallas_call | solution.py:294
  8.6 0.0 copy-start
  8.6 0.2 collective-permute-start
  8.7 1.5 %collective-permute-start.1 = (bf16[112,512]{1,0:T(8,128)(2,1)S(1)}, bf16[112,512]{1,0:T(8,128)(2,1)S(1)}, u32[]{:S(2)}, u32[]{:S(2)}) collective-permute-start(bf16[112,512]{1,0:T(8,128)(2,1)S(1)} %pack.1._.rest_0_), channel_id=1, source_target_pairs={{0,2},{1,3},{2,0},{3,1},{4,6},{5,7},{6,4},{7,5},{8,10},{9,11},{10,... | collective-permute-start | bytes 344072 | tf_op jit(solution)/shard_map/ppermute | solution.py:253
  10.2 0.0 collective-permute-done.2._.rest_2_
  10.2 1.5 %cut.1 = bf16[256,3584]{1,0:T(8,128)(2,1)S(1)} custom-call(bf16[112,512]{1,0:T(8,128)(2,1)S(1)} %collective-permute-done.2._.rest_2_, bf16[256,7168]{1,0:T(8,128)(2,1)} %rest_5_.1), custom_call_target="tpu_custom_call" | custom-call | tf_op jit(solution)/shard_map/cut/pallas_call | solution.py:256
  11.7 1.2 %collective-permute-done.4.rest_4_ = bf16[112,512]{1,0:T(8,128)(2,1)S(1)} collective-permute-done((bf16[112,512]{1,0:T(8,128)(2,1)S(1)}, bf16[112,512]{1,0:T(8,128)(2,1)S(1)}, u32[]{:S(2)}, u32[]{:S(2)}) %collective-permute-start.4) | collective-permute-done | bytes 114720 | tf_op jit(solution)/shard_map/ppermute | solution.py:253
  12.9 0.6 %collective-permute-start.6 = (bf16[112,512]{1,0:T(8,128)(2,1)S(1)}, bf16[112,512]{1,0:T(8,128)(2,1)S(1)}, u32[]{:S(2)}, u32[]{:S(2)}) collective-permute-start(bf16[112,512]{1,0:T(8,128)(2,1)S(1)} %collective-permute-done.4.rest_4_), channel_id=1, source_target_pairs={{0,2},{1,3},{2,0},{3,1},{4,6},{5,7},{6,4},{7,5},{8,10},{9,11},{10,... | collective-permute-start | bytes 344072 | tf_op jit(solution)/shard_map/ppermute | solution.py:253
  13.6 0.0 collective-permute-start.5
  13.6 0.5 %collective-permute-start.3 = (bf16[112,512]{1,0:T(8,128)(2,1)S(1)}, bf16[112,512]{1,0:T(8,128)(2,1)S(1)}, u32[]{:S(2)}, u32[]{:S(2)}) collective-permute-start(bf16[112,512]{1,0:T(8,128)(2,1)S(1)} %collective-permute-done.2._.rest_2_), channel_id=1, source_target_pairs={{0,1},{1,0},{2,3},{3,2},{4,5},{5,4},{6,7},{7,6},{8,9},{9,8},{10,11... | collective-permute-start | bytes 344072 | tf_op jit(solution)/shard_map/ppermute | solution.py:245
  14.1 0.1 collective-permute-done.1.rest_1_
  14.2 0.0 copy-done
  14.2 0.0 collective-permute-start.8
  14.2 0.0 collective-permute-done.queries_other
  14.2 0.5 %collective-permute-start.9 = (bf16[256,3584]{1,0:T(8,128)(2,1)S(1)}, bf16[256,3584]{1,0:T(8,128)(2,1)S(1)}, u32[]{:S(2)}, u32[]{:S(2)}) collective-permute-start(bf16[256,3584]{1,0:T(8,128)(2,1)S(1)} %cut.1), channel_id=1, source_target_pairs={{0,1},{1,0},{2,3},{3,2},{4,5},{5,4},{6,7},{7,6},{8,9},{9,8},{10,11... | collective-permute-start | bytes 5505032 | tf_op jit(solution)/shard_map/ppermute | solution.py:245
  14.7 3.0 %collective-permute-done.6.rest_1_ = bf16[112,512]{1,0:T(8,128)(2,1)S(1)} collective-permute-done((bf16[112,512]{1,0:T(8,128)(2,1)S(1)}, bf16[112,512]{1,0:T(8,128)(2,1)S(1)}, u32[]{:S(2)}, u32[]{:S(2)}) %collective-permute-start.6) | collective-permute-done | bytes 114720 | tf_op jit(solution)/shard_map/ppermute | solution.py:253
  17.7 0.0 collective-permute-start.7
  17.7 0.0 collective-permute-done.5.rest_5_
  17.7 0.0 collective-permute-done.3.rest_3_
  17.7 1.2 %early.1 = (f32[384,1]{1,0:T(8,128)S(1)}, f32[384,1]{1,0:T(8,128)S(1)}, f32[384,512]{1,0:T(8,128)S(1)}) custom-call(bf16[192,576]{1,0:T(8,128)(2,1)S(1)} %get-tuple-element.12.queries_own, bf16[192,576]{1,0:T(8,128)(2,1)S(1)} %collective-permute-done.queries_other, f32[1,96,576]{2,1,0:T(8,128)S(1)} %get-tuple-element.13.bias, ...), custom_call_target="tpu_custom_call" | custom-call | flops 32999999488 | tf_op jit(solution)/shard_map/early/pallas_call | solution.py:307
  19.0 0.0 collective-permute-done.8.rest_4_
  19.0 0.1 collective-permute-done.7.rest_2_
  19.0 0.0 collective-permute-done.9.rest_6_
  19.0 2.9 %finish.1 = bf16[96,3584]{1,0:T(8,128)(2,1)} custom-call(bf16[192,576]{1,0:T(8,128)(2,1)S(1)} %get-tuple-element.12.queries_own, bf16[192,576]{1,0:T(8,128)(2,1)S(1)} %collective-permute-done.queries_other, f32[384,1]{1,0:T(8,128)S(1)} %get-tuple-element.15.top, f32[384,1]{1,0:T(8,128)S(1)} %get-tuple-element.16.total, ...), custom_call_target="tpu_custom_call" | custom-call | tf_op jit(solution)/shard_map/finish/pallas_call | solution.py:321
Async XLA Ops:
  1.0 9.2 %collective-permute-start.2 = (bf16[112,512]{1,0:T(8,128)(2,1)S(1)}, bf16[112,512]{1,0:T(8,128)(2,1)S(1)}, u32[]{:S(2)}, u32[]{:S(2)}) collective-permute-start(bf16[112,512]{1,0:T(8,128)(2,1)S(1)} %pack.1._.rest_0_), channel_id=1, source_target_pairs={{0,4},{1,7},{2,6},{3,5},{4,0},{5,3},{6,2},{7,1},{8,12},{9,15},{10,... | collective-permute-start | bytes 344072 | tf_op jit(solution)/shard_map/ppermute | solution.py:253
  4.1 8.8 %collective-permute-start.4 = (bf16[112,512]{1,0:T(8,128)(2,1)S(1)}, bf16[112,512]{1,0:T(8,128)(2,1)S(1)}, u32[]{:S(2)}, u32[]{:S(2)}) collective-permute-start(bf16[112,512]{1,0:T(8,128)(2,1)S(1)} %pack.1._.rest_0_), channel_id=1, source_target_pairs={{0,8},{1,13},{2,10},{3,15},{4,12},{5,9},{6,14},{7,11},{8,0},{9,5},... | collective-permute-start | bytes 344072 | tf_op jit(solution)/shard_map/ppermute | solution.py:253
  6.7 0.7 %copy-start.1 = (s32[16]{0:T(128)S(1)}, s32[16]{0:T(128)}, u32[]{:S(2)}) copy-start(s32[16]{0:T(128)} %span_order.1) | copy-start | bytes 196
  8.6 5.7 %copy-start = (bf16[512,256]{1,0:T(8,128)(2,1)S(1)}, bf16[512,256]{1,0:T(8,128)(2,1)}, u32[]{:S(2)}) copy-start(bf16[512,256]{1,0:T(8,128)(2,1)} %rest_3_.1) | copy-start | bytes 786436
  8.6 5.7 %collective-permute-start = (bf16[192,576]{1,0:T(8,128)(2,1)S(1)}, bf16[192,576]{1,0:T(8,128)(2,1)S(1)}, u32[]{:S(2)}, u32[]{:S(2)}) collective-permute-start(bf16[192,576]{1,0:T(8,128)(2,1)S(1)} %get-tuple-element.12.queries_own), channel_id=1, source_target_pairs={{0,1},{1,0},{2,3},{3,2},{4,5},{5,4},{6,7},{7,6},{8,9},{9,8},{10,11... | collective-permute-start | bytes 663560 | tf_op jit(solution)/shard_map/ppermute | solution.py:245
  8.7 5.5 %collective-permute-start.1 = (bf16[112,512]{1,0:T(8,128)(2,1)S(1)}, bf16[112,512]{1,0:T(8,128)(2,1)S(1)}, u32[]{:S(2)}, u32[]{:S(2)}) collective-permute-start(bf16[112,512]{1,0:T(8,128)(2,1)S(1)} %pack.1._.rest_0_), channel_id=1, source_target_pairs={{0,2},{1,3},{2,0},{3,1},{4,6},{5,7},{6,4},{7,5},{8,10},{9,11},{10,... | collective-permute-start | bytes 344072 | tf_op jit(solution)/shard_map/ppermute | solution.py:253
  12.9 4.8 %collective-permute-start.6 = (bf16[112,512]{1,0:T(8,128)(2,1)S(1)}, bf16[112,512]{1,0:T(8,128)(2,1)S(1)}, u32[]{:S(2)}, u32[]{:S(2)}) collective-permute-start(bf16[112,512]{1,0:T(8,128)(2,1)S(1)} %collective-permute-done.4.rest_4_), channel_id=1, source_target_pairs={{0,2},{1,3},{2,0},{3,1},{4,6},{5,7},{6,4},{7,5},{8,10},{9,11},{10,... | collective-permute-start | bytes 344072 | tf_op jit(solution)/shard_map/ppermute | solution.py:253
  13.6 4.2 %collective-permute-start.5 = (bf16[112,512]{1,0:T(8,128)(2,1)S(1)}, bf16[112,512]{1,0:T(8,128)(2,1)S(1)}, u32[]{:S(2)}, u32[]{:S(2)}) collective-permute-start(bf16[112,512]{1,0:T(8,128)(2,1)S(1)} %collective-permute-done.4.rest_4_), channel_id=1, source_target_pairs={{0,1},{1,0},{2,3},{3,2},{4,5},{5,4},{6,7},{7,6},{8,9},{9,8},{10,11... | collective-permute-start | bytes 344072 | tf_op jit(solution)/shard_map/ppermute | solution.py:245
  13.6 4.2 %collective-permute-start.3 = (bf16[112,512]{1,0:T(8,128)(2,1)S(1)}, bf16[112,512]{1,0:T(8,128)(2,1)S(1)}, u32[]{:S(2)}, u32[]{:S(2)}) collective-permute-start(bf16[112,512]{1,0:T(8,128)(2,1)S(1)} %collective-permute-done.2._.rest_2_), channel_id=1, source_target_pairs={{0,1},{1,0},{2,3},{3,2},{4,5},{5,4},{6,7},{7,6},{8,9},{9,8},{10,11... | collective-permute-start | bytes 344072 | tf_op jit(solution)/shard_map/ppermute | solution.py:245
  14.2 4.8 %collective-permute-start.8 = (bf16[512,256]{1,0:T(8,128)(2,1)S(1)}, bf16[512,256]{1,0:T(8,128)(2,1)S(1)}, u32[]{:S(2)}, u32[]{:S(2)}) collective-permute-start(bf16[512,256]{1,0:T(8,128)(2,1)S(1)} %copy-done), channel_id=1, source_target_pairs={{0,1},{1,0},{2,3},{3,2},{4,5},{5,4},{6,7},{7,6},{8,9},{9,8},{10,11... | collective-permute-start | bytes 786440 | tf_op jit(solution)/shard_map/ppermute | solution.py:245
  14.2 4.8 %collective-permute-start.9 = (bf16[256,3584]{1,0:T(8,128)(2,1)S(1)}, bf16[256,3584]{1,0:T(8,128)(2,1)S(1)}, u32[]{:S(2)}, u32[]{:S(2)}) collective-permute-start(bf16[256,3584]{1,0:T(8,128)(2,1)S(1)} %cut.1), channel_id=1, source_target_pairs={{0,1},{1,0},{2,3},{3,2},{4,5},{5,4},{6,7},{7,6},{8,9},{9,8},{10,11... | collective-permute-start | bytes 5505032 | tf_op jit(solution)/shard_map/ppermute | solution.py:245
  17.7 1.3 %collective-permute-start.7 = (bf16[112,512]{1,0:T(8,128)(2,1)S(1)}, bf16[112,512]{1,0:T(8,128)(2,1)S(1)}, u32[]{:S(2)}, u32[]{:S(2)}) collective-permute-start(bf16[112,512]{1,0:T(8,128)(2,1)S(1)} %collective-permute-done.6.rest_1_), channel_id=1, source_target_pairs={{0,1},{1,0},{2,3},{3,2},{4,5},{5,4},{6,7},{7,6},{8,9},{9,8},{10,11... | collective-permute-start | bytes 344072 | tf_op jit(solution)/shard_map/ppermute | solution.py:245

commit v5 on v4

v5 whole, which is shorter than its diff:
```python
import functools
import math

import jax
import jax.numpy as jnp
from jax import lax
from jax.experimental import pallas as pl
from jax.experimental.pallas import tpu as pltpu
from jax.sharding import PartitionSpec as P

DC = 512
DH = 128
DR = 64
BF16 = jnp.bfloat16
F32 = jnp.float32
MASKED = -1e30
BLOCK_CHUNKS = 8
CUT_COST, QUERY_COST, FIRST_COST, SECOND_COST = 0, 0, 0, 30
SMALL_VMEM = 20 * 1024 * 1024
LARGE_VMEM = 56 * 1024 * 1024
FAR = (4, 6)
NEAR = (2, 3)
BESIDE = (1, 1)
RELAYED = (5, 7)


def vmem():
    return pl.BlockSpec(memory_space=pltpu.VMEM)


def anywhere():
    return pl.BlockSpec(memory_space=pl.ANY)


def hbm():
    return pl.BlockSpec(memory_space=pltpu.HBM)


def cost(microseconds):
    return pl.CostEstimate(flops=int(microseconds * 1.1e9), bytes_accessed=0, transcendentals=0)


def smem():
    return pl.BlockSpec(memory_space=pltpu.SMEM)


def pack_kernel(latent, key_rope_turned, out_ref):
    rows = latent.shape[0]
    group = rows // 6
    out_ref[:rows] = latent[...]
    rope = key_rope_turned[...].astype(F32).T.astype(BF16)
    parts = [rope[index * group : (index + 1) * group] for index in range(6)]
    parts.append(jnp.zeros((group, DC - 6 * DR), BF16))
    out_ref[rows:] = jnp.concatenate(parts, axis=1)


def unpack(chunk, keys, base):
    rows = 6 * chunk.shape[0] // 7
    group = rows // 6
    keys[pl.ds(base, rows), :DC] = chunk[:rows]
    for index in range(6):
        part = chunk[rows:, index * DR : (index + 1) * DR]
        keys[pl.ds(base + index * group, group), DC:] = part


def cut_kernel(_, out_proj, own_ref, other_ref, sems):
    width = own_ref.shape[1]
    core = lax.axis_index("heads")
    copies = []
    for index, (part, target) in enumerate(((1 - core, other_ref), (core, own_ref))):
        columns = pl.ds(pl.multiple_of(part * width, 128), width)
        copies.append(pltpu.make_async_copy(out_proj.at[:, columns], target, sems.at[index]))
    for copy in copies:
        copy.start()
    for copy in copies:
        copy.wait()


def query_kernel(order, span_order, _, nope, rope, up, *outs):
    rows = nope.shape[0]
    heads = nope.shape[1] // DH
    span_rows = rows // 2
    own_index = lax.axis_index("ctx")
    core = lax.axis_index("heads")
    for head in range(heads):
        latent = lax.dot_general(
            nope[:, head * DH : (head + 1) * DH],
            up[:, head * DH : (head + 1) * DH],
            (((1,), (1,)), ((), ())),
            preferred_element_type=F32,
        )
        outs[head][:, :DC] = latent.astype(BF16)
        outs[head][:, DC:] = rope[:, head * DR : (head + 1) * DR]
    biases = outs[heads:]
    row = lax.broadcasted_iota(jnp.int32, (rows, 1), 0)
    query_pos = jnp.where(
        row < span_rows,
        span_order[2 * own_index] * span_rows + row,
        span_order[2 * own_index + 1] * span_rows + row - span_rows,
    )

    def bias_of(owners):
        column = lax.broadcasted_iota(jnp.int32, (1, len(owners) * rows), 1)
        key_pos = jnp.zeros(column.shape, jnp.int32)
        for index, owner in enumerate(owners):
            for side in range(2):
                start = index * rows + side * span_rows
                first = span_order[2 * owner + side] * span_rows
                key_pos = jnp.where(column >= start, first + column - start, key_pos)
        return jnp.where(key_pos <= query_pos, F32(0.0), F32(MASKED))

    if order is not None:
        for steps, bias_ref in zip(order, biases):
            bias_ref[0] = bias_of(
                [own_index ^ jnp.where(core == 0, step[0], step[1]) for step in steps]
            )
    else:
        bias_ref = biases[0]

        def step(block, carry):
            bias_ref[block] = bias_of([block * BLOCK_CHUNKS + index for index in range(BLOCK_CHUNKS)])
            return carry

        lax.fori_loop(0, bias_ref.shape[0], step, 0)


def attend_block(queries, keys, bias, old):
    copies = len(queries)
    scale = math.log2(math.e) / math.sqrt(DH + DR)
    heads = jnp.concatenate([part[...] for part in queries], axis=0)
    scores = lax.dot_general(
        heads, keys[...], (((1,), (1,)), ((), ())), preferred_element_type=F32
    )
    scores = scores + jnp.concatenate([bias] * copies, axis=0)
    top = jnp.max(scores, axis=-1, keepdims=True)
    if old is not None:
        top = jnp.maximum(old[0], top)
        rescale = jnp.exp2((old[0] - top) * scale)
    expo = jnp.exp2((scores - top) * scale)
    total = jnp.sum(expo, axis=-1, keepdims=True)
    added = jnp.dot(expo.astype(BF16), keys[:, :DC], preferred_element_type=F32)
    if old is not None:
        total = old[1] * rescale + total
        added = old[2] * rescale + added
    return top, total, added


def chunks_kernel(heads, chunk_count, passed, later, *rest):
    queries, bias, rest = rest[:heads], rest[heads], rest[heads + 1 :]
    chunks, rest = rest[:chunk_count], rest[chunk_count + later :]
    if passed:
        rest[-2][...] = rest[0][...]
        rest = rest[1:-2] + rest[-1:]
    old, running, keys = rest[:-4], rest[-4:-1], rest[-1]
    rows = bias.shape[1]
    for index, chunk in enumerate(chunks):
        unpack(chunk, keys, index * rows)
    before = [state[...] for state in old] if old else None
    values = attend_block(queries, keys, bias[0], before)
    for state, value in zip(running, values):
        state[...] = value


def gathered_kernel(heads, *rest):
    queries, (bias, gathered) = rest[:heads], rest[heads : heads + 2]
    running, keys = rest[heads + 2 : heads + 5], rest[heads + 5]
    blocks, rows, _ = bias.shape

    def fill(block):
        for index in range(BLOCK_CHUNKS):
            unpack(gathered.at[block * BLOCK_CHUNKS + index], keys, index * rows)

    first = lax.axis_index("ctx") // BLOCK_CHUNKS
    fill(first)
    values = attend_block(queries, keys, bias[first], None)
    for state, value in zip(running, values):
        state[...] = value

    def step(index, carry):
        block = index + jnp.where(index >= first, 1, 0)
        fill(block)
        new = attend_block(queries, keys, bias[block], [state[...] for state in running])
        for state, value in zip(running, new):
            state[...] = value
        return carry

    lax.fori_loop(0, blocks - 1, step, 0)


def finish_kernel(heads, chunk_count, *rest):
    queries, (top, total, context), rest = rest[:heads], rest[heads : heads + 3], rest[heads + 3 :]
    bias, chunks = rest[:chunk_count][:1], rest[1 : 1 + chunk_count]
    rest = rest[len(bias) + len(chunks) :]
    value_own, value_other, proj_own, proj_other, out_ref, out_tiles, keys, out_sems = rest
    rows, width = out_ref.shape
    running = (top[...], total[...], context[...])
    if chunk_count:
        for index, chunk in enumerate(chunks):
            unpack(chunk, keys, index * rows)
        running = attend_block(queries, keys, bias[0][0], running)
    mixed = (running[2] / running[1]).astype(BF16)
    half = heads // 2
    sides = []
    for group, value in enumerate((value_own, value_other)):
        parts = []
        for head in range(half):
            first = (group * half + head) * rows
            per_head = jnp.dot(
                mixed[first : first + rows],
                value[:, head * DH : (head + 1) * DH],
                preferred_element_type=F32,
            )
            parts.append(per_head.astype(BF16))
        sides.append(jnp.concatenate(parts, axis=1))
    tiles = out_sems.shape[0]
    tile = width // tiles
    sends = []
    for index in range(tiles):
        part = pl.ds(index * tile, tile)
        out = jnp.dot(sides[0], proj_own[:, part], preferred_element_type=F32)
        out = out + jnp.dot(sides[1], proj_other[:, part], preferred_element_type=F32)
        out_tiles[:, part] = out.astype(BF16)
        sends.append(
            pltpu.make_async_copy(out_tiles.at[:, part], out_ref.at[:, part], out_sems.at[index])
        )
        sends[-1].start()
    for send in sends:
        send.wait()


def per_device(
    count, queries_nope, queries_rope, latent, key_rope, key_up, value_up, out_proj, span_order
):
    rows = latent.shape[0]
    width = out_proj.shape[1] // 2
    heads = 2 * (key_up.shape[1] // DH)
    query_rows = heads * rows
    direct = count == 8
    small = pltpu.CompilerParams(vmem_limit_bytes=SMALL_VMEM)

    def in_hbm(*arrays):
        return [pltpu.with_memory_space_constraint(array, pltpu.HBM) for array in arrays]

    def other_core(array):
        return lax.ppermute(array, "heads", [(0, 1), (1, 0)])

    def partners(array, steps):
        pairs = [
            (2 * index + core, 2 * (index ^ steps[core]) + core)
            for index in range(count)
            for core in range(2)
        ]
        return lax.ppermute(array, ("ctx", "heads"), pairs)

    def cut(after):
        return pl.pallas_call(
            cut_kernel,
            out_shape=[jax.ShapeDtypeStruct((out_proj.shape[0], width), BF16)] * 2,
            in_specs=[anywhere(), hbm()],
            out_specs=[anywhere()] * 2,
            scratch_shapes=[pltpu.SemaphoreType.DMA((2,))],
            compiler_params=small,
            cost_estimate=cost(CUT_COST),
            name="cut",
        )(after, *in_hbm(out_proj))

    def attend(name, estimate, queries, bias, chunks, passed, old, *before):
        return pl.pallas_call(
            functools.partial(chunks_kernel, heads, len(chunks), len(passed), len(before)),
            out_shape=[jax.ShapeDtypeStruct((query_rows, size), F32) for size in (1, 1, DC)]
            + [jax.ShapeDtypeStruct(chunk.shape, BF16) for chunk in passed],
            in_specs=[vmem()] * (heads + 1 + len(chunks))
            + [anywhere()] * len(before)
            + [vmem()] * (len(passed) + len(old)),
            out_specs=[vmem()] * (3 + len(passed)),
            scratch_shapes=[pltpu.VMEM((len(chunks) * rows, DC + DR), BF16)],
            compiler_params=small,
            cost_estimate=cost(estimate),
            name=name,
        )(*queries, bias, *chunks, *before, *passed, *old)

    packed = pl.pallas_call(
        pack_kernel,
        out_shape=jax.ShapeDtypeStruct((rows + rows // 6, DC), BF16),
        in_specs=[vmem()] * 2,
        out_specs=vmem(),
        compiler_params=small,
        name="pack",
    )(*in_hbm(latent, key_rope.T))
    if direct:
        order = [
            [(0, 0), BESIDE, NEAR],
            [NEAR[::-1], FAR, FAR[::-1], RELAYED],
            [RELAYED[::-1]],
        ]
        bias_shapes = [(1, rows, len(steps) * rows) for steps in order]
    else:
        order = None
        bias_shapes = [(count // BLOCK_CHUNKS, rows, BLOCK_CHUNKS * rows)]
    outs = pl.pallas_call(
        functools.partial(query_kernel, order),
        out_shape=[jax.ShapeDtypeStruct((rows, DC + DR), BF16)] * (heads // 2)
        + [jax.ShapeDtypeStruct(shape, F32) for shape in bias_shapes],
        in_specs=[smem(), anywhere()] + [vmem()] * 3,
        out_specs=[vmem()] * (heads // 2 + len(bias_shapes)),
        compiler_params=small,
        cost_estimate=cost(QUERY_COST),
        name="queries",
    )(*in_hbm(span_order), packed, *in_hbm(queries_nope, queries_rope, key_up))
    queries, biases = outs[: heads // 2], outs[heads // 2 :]
    both = [*queries, *map(other_core, queries)]
    value_other = other_core(value_up)
    proj_own, proj_cut = cut(queries[0])
    proj_other = other_core(proj_cut)

    if direct:
        far = partners(packed, FAR)
        near = partners(packed, NEAR)
        beside = partners(packed, BESIDE)
        relayed = partners(far, (1, 1))
        *running, far_after = attend(
            "first", FIRST_COST, both, biases[0], [packed, beside, near], [far], [], proj_cut
        )
        last = [other_core(relayed)]
        running = attend(
            "second",
            SECOND_COST,
            both,
            biases[1],
            [other_core(near), far, other_core(far_after), relayed],
            [],
            running,
        )
    else:
        last = []
        running = pl.pallas_call(
            functools.partial(gathered_kernel, heads),
            out_shape=[jax.ShapeDtypeStruct((query_rows, size), F32) for size in (1, 1, DC)],
            in_specs=[vmem()] * (heads + 2),
            out_specs=[vmem()] * 3,
            scratch_shapes=[pltpu.VMEM((BLOCK_CHUNKS * rows, DC + DR), BF16)],
            compiler_params=pltpu.CompilerParams(vmem_limit_bytes=LARGE_VMEM),
            name="gathered",
        )(*both, biases[0], lax.all_gather(packed, "ctx", axis=0))

    tiles = 7 if width % 896 == 0 else 1
    return pl.pallas_call(
        functools.partial(finish_kernel, heads, len(last)),
        out_shape=jax.ShapeDtypeStruct((rows, width), BF16),
        in_specs=[vmem()] * (heads + 3 + len(biases[2:]) + len(last) + 4),
        out_specs=anywhere(),
        scratch_shapes=[
            pltpu.VMEM((rows, width), BF16),
            pltpu.VMEM((rows, DC + DR), BF16),
            pltpu.SemaphoreType.DMA((tiles,)),
        ],
        compiler_params=small,
        name="finish",
    )(*both, *running, *biases[2:], *last, value_up, value_other, proj_own, proj_other)


def solution(mesh):
    in_specs = (
        P(("docs", "ctx"), "heads"),
        P(("docs", "ctx"), "heads"),
        P(("docs", "ctx"), None),
        P(("docs", "ctx"), None),
        P(None, "heads"),
        P(None, "heads"),
        P("heads", None),
        P("docs"),
    )
    out_specs = P(("docs", "ctx"), "heads")
    return jax.shard_map(
        functools.partial(per_device, mesh.shape["ctx"]),
        mesh=mesh,
        in_specs=in_specs,
        out_specs=out_specs,
        check_vma=False,
    )
```

time: 22.2 us -> 21.2 us (0.955)
  waiting for transfers between devices: 4.4 us -> 2.8 us
  Pallas kernels: 7.97 us -> 8.82 us
  local copies, waits for them, and re-layouts: 0.66 us -> 0.01 us
  starting transfers between devices: 8.92 us -> 9.37 us
    ppermute x4, waiting for transfers between devices: 4.33 us -> 2.58 us  [partners(): return lax.ppermute(array, ('ctx', 'heads'), pairs)]
    pallas_call x3 -> x4, Pallas kernels: 5.7 us -> 6.55 us  [the longest x1 2.49 us: per_device(): pl.pallas_call(functools.partial(finish_kernel, heads, len(last)), out_sh...]
    unnamed x4 -> x2, local copies, waits for them, and re-layouts: 0.66 us -> 0.01 us
    ppermute x6 -> x7, starting transfers between devices: 1.17 us -> 1.65 us  [other_core(): return lax.ppermute(array, 'heads', [(0, 1), (1, 0)])]
  transfers between devices with their start and end apart: 10 -> 11, of which waited for: 4 -> 2; matrix products, arithmetic and copies ran while one was open for 0% -> 0% of each run, Pallas kernels for 18% -> 25%
where the time goes in v5:
time: 21.2 us; the launch traced here: 21.1 us
  starting transfers between devices  9.37 us (44%)
  Pallas kernels  8.82 us (42%)
  waiting for transfers between devices  2.8 us (13%)
    ppermute x4, starting transfers between devices, partners(): return lax.ppermute(array, ('ctx', 'heads'), pairs)  7.72 us
    ppermute x4, waiting for transfers between devices, partners(): return lax.ppermute(array, ('ctx', 'heads'), pairs)  2.58 us
    pallas_call x1, Pallas kernels, per_device(): pl.pallas_call(functools.partial(finish_kernel, heads, len(last)), out_sh...  2.49 us
    pallas_call x1, Pallas kernels, cut(): pl.pallas_call(cut_kernel, out_shape=[jax.ShapeDtypeStruct((out_proj.shap...  2.07 us
    pallas_call x2, Pallas kernels, attend(): pl.pallas_call(functools.partial(chunks_kernel, heads, len(chunks), len(p...  2 us
    ppermute x7, starting transfers between devices, other_core(): return lax.ppermute(array, 'heads', [(0, 1), (1, 0)])  1.65 us
    pallas_call x1, Pallas kernels, per_device(): pl.pallas_call(functools.partial(query_kernel, order), out_shape=[jax.Sha...  1.22 us
    pallas_call x1, Pallas kernels, per_device(): pl.pallas_call(pack_kernel, out_shape=jax.ShapeDtypeStruct((rows + rows /...  1.05 us
  transfers between devices with their start and end apart: 11, of which 2 were waited for; matrix products, arithmetic and copies ran while one was open for 0% of the time, Pallas kernels for 25%

profile of v5, /device:TPU:0, one launch (start us, length us, event | category | flops | bytes accessed | tf_op | source)
XLA Modules:
  0.0 21.1 jit_solution(14363796365720237244)
XLA Ops:
  0.0 1.0 %pack.1._.rest_5_ = bf16[112,512]{1,0:T(8,128)(2,1)S(1)} custom-call(bf16[96,512]{1,0:T(8,128)(2,1)} %latent.1, bf16[64,96]{1,0:T(8,128)(2,1)} %bitcast.1), custom_call_target="tpu_custom_call" | custom-call | tf_op jit(solution)/shard_map/pack/pallas_call | solution.py:282
  1.0 4.1 %collective-permute-start.4 = (bf16[112,512]{1,0:T(8,128)(2,1)S(1)}, bf16[112,512]{1,0:T(8,128)(2,1)S(1)}, u32[]{:S(2)}, u32[]{:S(2)}) collective-permute-start(bf16[112,512]{1,0:T(8,128)(2,1)S(1)} %pack.1._.rest_5_), channel_id=1, source_target_pairs={{0,8},{1,13},{2,10},{3,15},{4,12},{5,9},{6,14},{7,11},{8,0},{9,5},... | collective-permute-start | bytes 344072 | tf_op jit(solution)/shard_map/ppermute | solution.py:253
  5.1 1.6 %collective-permute-start.2 = (bf16[112,512]{1,0:T(8,128)(2,1)S(1)}, bf16[112,512]{1,0:T(8,128)(2,1)S(1)}, u32[]{:S(2)}, u32[]{:S(2)}) collective-permute-start(bf16[112,512]{1,0:T(8,128)(2,1)S(1)} %pack.1._.rest_5_), channel_id=1, source_target_pairs={{0,4},{1,7},{2,6},{3,5},{4,0},{5,3},{6,2},{7,1},{8,12},{9,15},{10,... | collective-permute-start | bytes 344072 | tf_op jit(solution)/shard_map/ppermute | solution.py:253
  6.7 1.5 %collective-permute-start.5 = (bf16[112,512]{1,0:T(8,128)(2,1)S(1)}, bf16[112,512]{1,0:T(8,128)(2,1)S(1)}, u32[]{:S(2)}, u32[]{:S(2)}) collective-permute-start(bf16[112,512]{1,0:T(8,128)(2,1)S(1)} %pack.1._.rest_5_), channel_id=1, source_target_pairs={{0,2},{1,3},{2,0},{3,1},{4,6},{5,7},{6,4},{7,5},{8,10},{9,11},{10,... | collective-permute-start | bytes 344072 | tf_op jit(solution)/shard_map/ppermute | solution.py:253
  8.2 1.2 %queries.1 = (bf16[96,576]{1,0:T(8,128)(2,1)S(1)}, bf16[96,576]{1,0:T(8,128)(2,1)S(1)}, f32[1,96,288]{2,1,0:T(8,128)S(1)}, f32[1,96,384]{2,1,0:T(8,128)S(1)}, f32[1,96,96]{2,1,0:T(8,128)S(1)}) custom-call(s32[16]{0:T(128)} %span_order.1, bf16[112,512]{1,0:T(8,128)(2,1)S(1)} %pack.1._.rest_5_, bf16[96,256]{1,0:T(8,128)(2,1)} %nope.1, bf16[96,128]{1,0:T(8,128)(2,1)} %rope.1, ...), custom_call_target="tpu_custom_call" | custom-call | tf_op jit(solution)/shard_map/queries/pallas_call | solution.py:300
  9.4 0.1 collective-permute-start
  9.5 0.5 %collective-permute-start.1 = (bf16[96,576]{1,0:T(8,128)(2,1)S(1)}, bf16[96,576]{1,0:T(8,128)(2,1)S(1)}, u32[]{:S(2)}, u32[]{:S(2)}) collective-permute-start(bf16[96,576]{1,0:T(8,128)(2,1)S(1)} %get-tuple-element.20.rest_1_), channel_id=1, source_target_pairs={{0,1},{1,0},{2,3},{3,2},{4,5},{5,4},{6,7},{7,6},{8,9},{9,8},{10,11... | collective-permute-start | bytes 331784 | tf_op jit(solution)/shard_map/ppermute | solution.py:245
  10.0 2.1 %cut.1 = (bf16[256,3584]{1,0:T(8,128)(2,1)S(1)}, bf16[256,3584]{1,0:T(8,128)(2,1)S(1)}) custom-call(bf16[96,576]{1,0:T(8,128)(2,1)S(1)} %get-tuple-element.19._.rest_0_, bf16[256,7168]{1,0:T(8,128)(2,1)} %out_proj.1), custom_call_target="tpu_custom_call" | custom-call | tf_op jit(solution)/shard_map/cut/pallas_call | solution.py:256
  12.0 0.0 copy-start
  12.1 0.0 collective-permute-done.4.rest_9_.rest_6_
  12.1 0.6 %collective-permute-start.7 = (bf16[112,512]{1,0:T(8,128)(2,1)S(1)}, bf16[112,512]{1,0:T(8,128)(2,1)S(1)}, u32[]{:S(2)}, u32[]{:S(2)}) collective-permute-start(bf16[112,512]{1,0:T(8,128)(2,1)S(1)} %collective-permute-done.4.rest_9_.rest_6_), channel_id=1, source_target_pairs={{0,2},{1,3},{2,0},{3,1},{4,6},{5,7},{6,4},{7,5},{8,10},{9,11},{10,... | collective-permute-start | bytes 344072 | tf_op jit(solution)/shard_map/ppermute | solution.py:253
  12.7 0.0 collective-permute-done.rest_2_
  12.7 0.0 collective-permute-done.1.rest_3_
  12.7 0.0 collective-permute-done.2.rest_7_
  12.7 0.0 collective-permute-done.5.rest_6_
  12.7 0.9 %first.1 = (f32[384,1]{1,0:T(8,128)S(1)}, f32[384,1]{1,0:T(8,128)S(1)}, f32[384,512]{1,0:T(8,128)S(1)}, bf16[112,512]{1,0:T(8,128)(2,1)S(1)}) custom-call(bf16[96,576]{1,0:T(8,128)(2,1)S(1)} %get-tuple-element.19._.rest_0_, bf16[96,576]{1,0:T(8,128)(2,1)S(1)} %get-tuple-element.20.rest_1_, bf16[96,576]{1,0:T(8,128)(2,1)S(1)} %collective-permute-done.rest_2_, ...), custom_call_target="tpu_custom_call" | custom-call | tf_op jit(solution)/shard_map/first/pallas_call | solution.py:268
  13.6 0.1 collective-permute-start.6
  13.7 0.5 %collective-permute-start.3 = (bf16[112,512]{1,0:T(8,128)(2,1)S(1)}, bf16[112,512]{1,0:T(8,128)(2,1)S(1)}, u32[]{:S(2)}, u32[]{:S(2)}) collective-permute-start(bf16[112,512]{1,0:T(8,128)(2,1)S(1)} %collective-permute-done.2.rest_7_), channel_id=1, source_target_pairs={{0,1},{1,0},{2,3},{3,2},{4,5},{5,4},{6,7},{7,6},{8,9},{9,8},{10,11... | collective-permute-start | bytes 344072 | tf_op jit(solution)/shard_map/ppermute | solution.py:245
  14.2 0.1 collective-permute-start.10
  14.3 0.0 copy-done
  14.3 0.4 %collective-permute-start.9 = (bf16[512,256]{1,0:T(8,128)(2,1)S(1)}, bf16[512,256]{1,0:T(8,128)(2,1)S(1)}, u32[]{:S(2)}, u32[]{:S(2)}) collective-permute-start(bf16[512,256]{1,0:T(8,128)(2,1)S(1)} %copy-done), channel_id=1, source_target_pairs={{0,1},{1,0},{2,3},{3,2},{4,5},{5,4},{6,7},{7,6},{8,9},{9,8},{10,11... | collective-permute-start | bytes 786440 | tf_op jit(solution)/shard_map/ppermute | solution.py:245
  14.7 2.6 %collective-permute-done.7.rest_8_ = bf16[112,512]{1,0:T(8,128)(2,1)S(1)} collective-permute-done((bf16[112,512]{1,0:T(8,128)(2,1)S(1)}, bf16[112,512]{1,0:T(8,128)(2,1)S(1)}, u32[]{:S(2)}, u32[]{:S(2)}) %collective-permute-start.7) | collective-permute-done | bytes 114720 | tf_op jit(solution)/shard_map/ppermute | solution.py:253
  17.3 0.0 collective-permute-start.8
  17.3 0.0 collective-permute-done.6.rest_7_
  17.3 0.0 collective-permute-done.3.rest_5_
  17.3 1.1 %second.1 = (f32[384,1]{1,0:T(8,128)S(1)}, f32[384,1]{1,0:T(8,128)S(1)}, f32[384,512]{1,0:T(8,128)S(1)}) custom-call(bf16[96,576]{1,0:T(8,128)(2,1)S(1)} %get-tuple-element.19._.rest_0_, bf16[96,576]{1,0:T(8,128)(2,1)S(1)} %get-tuple-element.20.rest_1_, bf16[96,576]{1,0:T(8,128)(2,1)S(1)} %collective-permute-done.rest_2_, ...), custom_call_target="tpu_custom_call" | custom-call | flops 32999999488 | tf_op jit(solution)/shard_map/second/pallas_call | solution.py:268
  18.4 0.0 collective-permute-done.9.rest_10_
  18.4 0.2 collective-permute-done.8.rest_8_
  18.6 0.0 collective-permute-done.10.rest_12_
  18.6 2.5 %finish.1 = bf16[96,3584]{1,0:T(8,128)(2,1)} custom-call(bf16[96,576]{1,0:T(8,128)(2,1)S(1)} %get-tuple-element.19._.rest_0_, bf16[96,576]{1,0:T(8,128)(2,1)S(1)} %get-tuple-element.20.rest_1_, bf16[96,576]{1,0:T(8,128)(2,1)S(1)} %collective-permute-done.rest_2_, bf16[96,576]{1,0:T(8,128)(2,1)S(1)} %collective-permute-done.1.rest_3_, ...), custom_call_target="tpu_custom_call" | custom-call | tf_op jit(solution)/shard_map/finish/pallas_call | solution.py:347
Async XLA Ops:
  1.0 11.0 %collective-permute-start.4 = (bf16[112,512]{1,0:T(8,128)(2,1)S(1)}, bf16[112,512]{1,0:T(8,128)(2,1)S(1)}, u32[]{:S(2)}, u32[]{:S(2)}) collective-permute-start(bf16[112,512]{1,0:T(8,128)(2,1)S(1)} %pack.1._.rest_5_), channel_id=1, source_target_pairs={{0,8},{1,13},{2,10},{3,15},{4,12},{5,9},{6,14},{7,11},{8,0},{9,5},... | collective-permute-start | bytes 344072 | tf_op jit(solution)/shard_map/ppermute | solution.py:253
  5.1 7.6 %collective-permute-start.2 = (bf16[112,512]{1,0:T(8,128)(2,1)S(1)}, bf16[112,512]{1,0:T(8,128)(2,1)S(1)}, u32[]{:S(2)}, u32[]{:S(2)}) collective-permute-start(bf16[112,512]{1,0:T(8,128)(2,1)S(1)} %pack.1._.rest_5_), channel_id=1, source_target_pairs={{0,4},{1,7},{2,6},{3,5},{4,0},{5,3},{6,2},{7,1},{8,12},{9,15},{10,... | collective-permute-start | bytes 344072 | tf_op jit(solution)/shard_map/ppermute | solution.py:253
  6.7 6.0 %collective-permute-start.5 = (bf16[112,512]{1,0:T(8,128)(2,1)S(1)}, bf16[112,512]{1,0:T(8,128)(2,1)S(1)}, u32[]{:S(2)}, u32[]{:S(2)}) collective-permute-start(bf16[112,512]{1,0:T(8,128)(2,1)S(1)} %pack.1._.rest_5_), channel_id=1, source_target_pairs={{0,2},{1,3},{2,0},{3,1},{4,6},{5,7},{6,4},{7,5},{8,10},{9,11},{10,... | collective-permute-start | bytes 344072 | tf_op jit(solution)/shard_map/ppermute | solution.py:253
  9.4 3.3 %collective-permute-start = (bf16[96,576]{1,0:T(8,128)(2,1)S(1)}, bf16[96,576]{1,0:T(8,128)(2,1)S(1)}, u32[]{:S(2)}, u32[]{:S(2)}) collective-permute-start(bf16[96,576]{1,0:T(8,128)(2,1)S(1)} %get-tuple-element.19._.rest_0_), channel_id=1, source_target_pairs={{0,1},{1,0},{2,3},{3,2},{4,5},{5,4},{6,7},{7,6},{8,9},{9,8},{10,11... | collective-permute-start | bytes 331784 | tf_op jit(solution)/shard_map/ppermute | solution.py:245
  9.5 3.2 %collective-permute-start.1 = (bf16[96,576]{1,0:T(8,128)(2,1)S(1)}, bf16[96,576]{1,0:T(8,128)(2,1)S(1)}, u32[]{:S(2)}, u32[]{:S(2)}) collective-permute-start(bf16[96,576]{1,0:T(8,128)(2,1)S(1)} %get-tuple-element.20.rest_1_), channel_id=1, source_target_pairs={{0,1},{1,0},{2,3},{3,2},{4,5},{5,4},{6,7},{7,6},{8,9},{9,8},{10,11... | collective-permute-start | bytes 331784 | tf_op jit(solution)/shard_map/ppermute | solution.py:245
  12.0 2.2 %copy-start = (bf16[512,256]{1,0:T(8,128)(2,1)S(1)}, bf16[512,256]{1,0:T(8,128)(2,1)}, u32[]{:S(2)}) copy-start(bf16[512,256]{1,0:T(8,128)(2,1)} %rest_9_.1) | copy-start | bytes 786436
  12.1 5.2 %collective-permute-start.7 = (bf16[112,512]{1,0:T(8,128)(2,1)S(1)}, bf16[112,512]{1,0:T(8,128)(2,1)S(1)}, u32[]{:S(2)}, u32[]{:S(2)}) collective-permute-start(bf16[112,512]{1,0:T(8,128)(2,1)S(1)} %collective-permute-done.4.rest_9_.rest_6_), channel_id=1, source_target_pairs={{0,2},{1,3},{2,0},{3,1},{4,6},{5,7},{6,4},{7,5},{8,10},{9,11},{10,... | collective-permute-start | bytes 344072 | tf_op jit(solution)/shard_map/ppermute | solution.py:253
  13.6 3.7 %collective-permute-start.6 = (bf16[112,512]{1,0:T(8,128)(2,1)S(1)}, bf16[112,512]{1,0:T(8,128)(2,1)S(1)}, u32[]{:S(2)}, u32[]{:S(2)}) collective-permute-start(bf16[112,512]{1,0:T(8,128)(2,1)S(1)} %get-tuple-element.24), channel_id=1, source_target_pairs={{0,1},{1,0},{2,3},{3,2},{4,5},{5,4},{6,7},{7,6},{8,9},{9,8},{10,11... | collective-permute-start | bytes 344072 | tf_op jit(solution)/shard_map/ppermute | solution.py:245
  13.7 3.6 %collective-permute-start.3 = (bf16[112,512]{1,0:T(8,128)(2,1)S(1)}, bf16[112,512]{1,0:T(8,128)(2,1)S(1)}, u32[]{:S(2)}, u32[]{:S(2)}) collective-permute-start(bf16[112,512]{1,0:T(8,128)(2,1)S(1)} %collective-permute-done.2.rest_7_), channel_id=1, source_target_pairs={{0,1},{1,0},{2,3},{3,2},{4,5},{5,4},{6,7},{7,6},{8,9},{9,8},{10,11... | collective-permute-start | bytes 344072 | tf_op jit(solution)/shard_map/ppermute | solution.py:245
  14.2 4.4 %collective-permute-start.10 = (bf16[256,3584]{1,0:T(8,128)(2,1)S(1)}, bf16[256,3584]{1,0:T(8,128)(2,1)S(1)}, u32[]{:S(2)}, u32[]{:S(2)}) collective-permute-start(bf16[256,3584]{1,0:T(8,128)(2,1)S(1)} %get-tuple-element.23.rest_8_), channel_id=1, source_target_pairs={{0,1},{1,0},{2,3},{3,2},{4,5},{5,4},{6,7},{7,6},{8,9},{9,8},{10,11... | collective-permute-start | bytes 5505032 | tf_op jit(solution)/shard_map/ppermute | solution.py:245
  14.3 4.1 %collective-permute-start.9 = (bf16[512,256]{1,0:T(8,128)(2,1)S(1)}, bf16[512,256]{1,0:T(8,128)(2,1)S(1)}, u32[]{:S(2)}, u32[]{:S(2)}) collective-permute-start(bf16[512,256]{1,0:T(8,128)(2,1)S(1)} %copy-done), channel_id=1, source_target_pairs={{0,1},{1,0},{2,3},{3,2},{4,5},{5,4},{6,7},{7,6},{8,9},{9,8},{10,11... | collective-permute-start | bytes 786440 | tf_op jit(solution)/shard_map/ppermute | solution.py:245
  17.3 1.3 %collective-permute-start.8 = (bf16[112,512]{1,0:T(8,128)(2,1)S(1)}, bf16[112,512]{1,0:T(8,128)(2,1)S(1)}, u32[]{:S(2)}, u32[]{:S(2)}) collective-permute-start(bf16[112,512]{1,0:T(8,128)(2,1)S(1)} %collective-permute-done.7.rest_8_), channel_id=1, source_target_pairs={{0,1},{1,0},{2,3},{3,2},{4,5},{5,4},{6,7},{7,6},{8,9},{9,8},{10,11... | collective-permute-start | bytes 344072 | tf_op jit(solution)/shard_map/ppermute | solution.py:245

commit v6 on v5

--- a/solution.py
+++ b/solution.py
@@ -15,7 +15,7 @@
 F32 = jnp.float32
 MASKED = -1e30
 BLOCK_CHUNKS = 8
-CUT_COST, QUERY_COST, FIRST_COST, SECOND_COST = 0, 0, 0, 30
+PREPARE_COST, FIRST_COST, SECOND_COST = 0, 0, 30
 SMALL_VMEM = 20 * 1024 * 1024
 LARGE_VMEM = 56 * 1024 * 1024
 FAR = (4, 6)
@@ -63,20 +63,20 @@
         keys[pl.ds(base + index * group, group), DC:] = part
 
 
-def cut_kernel(_, out_proj, own_ref, other_ref, sems):
-    width = own_ref.shape[1]
-    core = lax.axis_index("heads")
-    copies = []
-    for index, (part, target) in enumerate(((1 - core, other_ref), (core, own_ref))):
+def prepare_kernel(order, span_order, _, nope, rope, up, value_up, out_proj, *outs):
+    weights_own, weights_sent, sems = outs[-3:]
+    depth, width = out_proj.shape[0], out_proj.shape[1] // 2
+    fetches = []
+    for index, target in enumerate((weights_sent, weights_own)):
+        part = lax.axis_index("heads") ^ (1 - index)
         columns = pl.ds(pl.multiple_of(part * width, 128), width)
-        copies.append(pltpu.make_async_copy(out_proj.at[:, columns], target, sems.at[index]))
-    for copy in copies:
-        copy.start()
-    for copy in copies:
-        copy.wait()
-
-
-def query_kernel(order, span_order, _, nope, rope, up, *outs):
+        pairs = [(out_proj.at[:, columns], target.at[:, pl.ds(0, width)])]
+        for block in range(DC // depth):
+            place = pl.ds(width + block * value_up.shape[1], value_up.shape[1])
+            pairs.append((value_up.at[pl.ds(block * depth, depth)], target.at[:, place]))
+        for place, pair in enumerate(pairs):
+            fetches.append(pltpu.make_async_copy(*pair, sems.at[index, place]))
+            fetches[-1].start()
     rows = nope.shape[0]
     heads = nope.shape[1] // DH
     span_rows = rows // 2
@@ -91,7 +91,7 @@
         )
         outs[head][:, :DC] = latent.astype(BF16)
         outs[head][:, DC:] = rope[:, head * DR : (head + 1) * DR]
-    biases = outs[heads:]
+    biases = outs[heads:-3]
     row = lax.broadcasted_iota(jnp.int32, (rows, 1), 0)
     query_pos = jnp.where(
         row < span_rows,
@@ -122,6 +122,9 @@
             return carry
 
         lax.fori_loop(0, bias_ref.shape[0], step, 0)
+
+    for fetch in fetches:
+        fetch.wait()
 
 
 def attend_block(queries, keys, bias, old):
@@ -191,7 +194,7 @@
     queries, (top, total, context), rest = rest[:heads], rest[heads : heads + 3], rest[heads + 3 :]
     bias, chunks = rest[:chunk_count][:1], rest[1 : 1 + chunk_count]
     rest = rest[len(bias) + len(chunks) :]
-    value_own, value_other, proj_own, proj_other, out_ref, out_tiles, keys, out_sems = rest
+    weights, (out_ref, out_tiles, keys, out_sems) = rest[:2], rest[2:]
     rows, width = out_ref.shape
     running = (top[...], total[...], context[...])
     if chunk_count:
@@ -200,16 +203,20 @@
         running = attend_block(queries, keys, bias[0][0], running)
     mixed = (running[2] / running[1]).astype(BF16)
     half = heads // 2
+    depth = weights[0].shape[0]
     sides = []
-    for group, value in enumerate((value_own, value_other)):
+    for group, weight in enumerate(weights):
         parts = []
         for head in range(half):
-            first = (group * half + head) * rows
-            per_head = jnp.dot(
-                mixed[first : first + rows],
-                value[:, head * DH : (head + 1) * DH],
-                preferred_element_type=F32,
-            )
+            rows_of = slice((group * half + head) * rows, (group * half + head + 1) * rows)
+            per_head = 0.0
+            for block in range(DC // depth):
+                first = width + block * half * DH + head * DH
+                per_head = per_head + jnp.dot(
+                    mixed[rows_of, block * depth : (block + 1) * depth],
+                    weight[:, first : first + DH],
+                    preferred_element_type=F32,
+                )
             parts.append(per_head.astype(BF16))
         sides.append(jnp.concatenate(parts, axis=1))
     tiles = out_sems.shape[0]
@@ -217,8 +224,8 @@
     sends = []
     for index in range(tiles):
         part = pl.ds(index * tile, tile)
-        out = jnp.dot(sides[0], proj_own[:, part], preferred_element_type=F32)
-        out = out + jnp.dot(sides[1], proj_other[:, part], preferred_element_type=F32)
+        out = jnp.dot(sides[0], weights[0][:, part], preferred_element_type=F32)
+        out = out + jnp.dot(sides[1], weights[1][:, part], preferred_element_type=F32)
         out_tiles[:, part] = out.astype(BF16)
         sends.append(
             pltpu.make_async_copy(out_tiles.at[:, part], out_ref.at[:, part], out_sems.at[index])
@@ -232,7 +239,8 @@
     count, queries_nope, queries_rope, latent, key_rope, key_up, value_up, out_proj, span_order
 ):
     rows = latent.shape[0]
-    width = out_proj.shape[1] // 2
+    depth, width = out_proj.shape[0], out_proj.shape[1] // 2
+    blocks = DC // depth
     heads = 2 * (key_up.shape[1] // DH)
     query_rows = heads * rows
     direct = count == 8
@@ -251,18 +259,6 @@
             for core in range(2)
         ]
         return lax.ppermute(array, ("ctx", "heads"), pairs)
-
-    def cut(after):
-        return pl.pallas_call(
-            cut_kernel,
-            out_shape=[jax.ShapeDtypeStruct((out_proj.shape[0], width), BF16)] * 2,
-            in_specs=[anywhere(), hbm()],
-            out_specs=[anywhere()] * 2,
-            scratch_shapes=[pltpu.SemaphoreType.DMA((2,))],
-            compiler_params=small,
-            cost_estimate=cost(CUT_COST),
-            name="cut",
-        )(after, *in_hbm(out_proj))
 
     def attend(name, estimate, queries, bias, chunks, passed, old, *before):
         return pl.pallas_call(
@@ -298,20 +294,20 @@
         order = None
         bias_shapes = [(count // BLOCK_CHUNKS, rows, BLOCK_CHUNKS * rows)]
     outs = pl.pallas_call(
-        functools.partial(query_kernel, order),
+        functools.partial(prepare_kernel, order),
         out_shape=[jax.ShapeDtypeStruct((rows, DC + DR), BF16)] * (heads // 2)
-        + [jax.ShapeDtypeStruct(shape, F32) for shape in bias_shapes],
-        in_specs=[smem(), anywhere()] + [vmem()] * 3,
-        out_specs=[vmem()] * (heads // 2 + len(bias_shapes)),
+        + [jax.ShapeDtypeStruct(shape, F32) for shape in bias_shapes]
+        + [jax.ShapeDtypeStruct((depth, width + blocks * key_up.shape[1]), BF16)] * 2,
+        in_specs=[smem(), anywhere()] + [vmem()] * 3 + [hbm()] * 2,
+        out_specs=[vmem()] * (heads // 2 + len(bias_shapes)) + [anywhere()] * 2,
+        scratch_shapes=[pltpu.SemaphoreType.DMA((2, 1 + blocks))],
         compiler_params=small,
-        cost_estimate=cost(QUERY_COST),
-        name="queries",
-    )(*in_hbm(span_order), packed, *in_hbm(queries_nope, queries_rope, key_up))
-    queries, biases = outs[: heads // 2], outs[heads // 2 :]
+        cost_estimate=cost(PREPARE_COST),
+        name="prepare",
+    )(*in_hbm(span_order), packed, *in_hbm(queries_nope, queries_rope, key_up, value_up, out_proj))
+    queries, biases = outs[: heads // 2], outs[heads // 2 : -2]
+    weights = [outs[-2], other_core(outs[-1])]
     both = [*queries, *map(other_core, queries)]
-    value_other = other_core(value_up)
-    proj_own, proj_cut = cut(queries[0])
-    proj_other = other_core(proj_cut)
 
     if direct:
         far = partners(packed, FAR)
@@ -319,7 +315,7 @@
         beside = partners(packed, BESIDE)
         relayed = partners(far, (1, 1))
         *running, far_after = attend(
-            "first", FIRST_COST, both, biases[0], [packed, beside, near], [far], [], proj_cut
+            "first", FIRST_COST, both, biases[0], [packed, beside, near], [far], []
         )
         last = [other_core(relayed)]
         running = attend(
@@ -347,7 +343,7 @@
     return pl.pallas_call(
         functools.partial(finish_kernel, heads, len(last)),
         out_shape=jax.ShapeDtypeStruct((rows, width), BF16),
-        in_specs=[vmem()] * (heads + 3 + len(biases[2:]) + len(last) + 4),
+        in_specs=[vmem()] * (heads + 3 + len(biases[2:]) + len(last) + 2),
         out_specs=anywhere(),
         scratch_shapes=[
             pltpu.VMEM((rows, width), BF16),
@@ -356,7 +352,7 @@
         ],
         compiler_params=small,
         name="finish",
-    )(*both, *running, *biases[2:], *last, value_up, value_other, proj_own, proj_other)
+    )(*both, *running, *biases[2:], *last, *weights)
 
 
 def solution(mesh):

time: 21.2 us -> 21.3 us (level)
  waiting for transfers between devices: 2.8 us -> 3.5 us
  starting transfers between devices: 9.37 us -> 8.8 us
    ppermute x7 -> x6, waiting for transfers between devices: 0.21 us -> 0.85 us  [other_core(): return lax.ppermute(array, 'heads', [(0, 1), (1, 0)])]
    ppermute x7 -> x6, starting transfers between devices: 1.65 us -> 1.15 us  [other_core(): return lax.ppermute(array, 'heads', [(0, 1), (1, 0)])]
    pallas_call x2 -> x1, Pallas kernels: 3.29 us -> 3.25 us  [per_device(): pl.pallas_call(functools.partial(prepare_kernel, order), out_shape=[jax.S...]
  transfers between devices with their start and end apart: 11 -> 10, of which waited for: 2 -> 4; matrix products, arithmetic and copies ran while one was open for 0% -> 0% of each run, Pallas kernels for 25% -> 25%
where the time goes in v6:
time: 21.3 us; the launch traced here: 21.1 us
  starting transfers between devices  8.8 us (41%)
  Pallas kernels  8.77 us (41%)
  waiting for transfers between devices  3.5 us (16%)
    ppermute x4, starting transfers between devices, partners(): return lax.ppermute(array, ('ctx', 'heads'), pairs)  7.66 us
    pallas_call x1, Pallas kernels, per_device(): pl.pallas_call(functools.partial(prepare_kernel, order), out_shape=[jax.S...  3.25 us
    ppermute x4, waiting for transfers between devices, partners(): return lax.ppermute(array, ('ctx', 'heads'), pairs)  2.66 us
    pallas_call x1, Pallas kernels, per_device(): pl.pallas_call(functools.partial(finish_kernel, heads, len(last)), out_sh...  2.48 us
    pallas_call x2, Pallas kernels, attend(): pl.pallas_call(functools.partial(chunks_kernel, heads, len(chunks), len(p...  1.99 us
    ppermute x6, starting transfers between devices, other_core(): return lax.ppermute(array, 'heads', [(0, 1), (1, 0)])  1.15 us
    pallas_call x1, Pallas kernels, per_device(): pl.pallas_call(pack_kernel, out_shape=jax.ShapeDtypeStruct((rows + rows /...  1.05 us
    ppermute x6, waiting for transfers between devices, other_core(): return lax.ppermute(array, 'heads', [(0, 1), (1, 0)])  0.85 us
  transfers between devices with their start and end apart: 10, of which 4 were waited for; matrix products, arithmetic and copies ran while one was open for 0% of the time, Pallas kernels for 25%

profile of v6, /device:TPU:0, one launch (start us, length us, event | category | flops | bytes accessed | tf_op | source)
XLA Modules:
  0.0 21.1 jit_solution(2413279902178163984)
XLA Ops:
  0.0 1.0 %pack.1._.rest_5_ = bf16[112,512]{1,0:T(8,128)(2,1)S(1)} custom-call(bf16[96,512]{1,0:T(8,128)(2,1)} %latent.1, bf16[64,96]{1,0:T(8,128)(2,1)} %bitcast.1), custom_call_target="tpu_custom_call" | custom-call | tf_op jit(solution)/shard_map/pack/pallas_call | solution.py:278
  1.0 4.1 %collective-permute-start.4 = (bf16[112,512]{1,0:T(8,128)(2,1)S(1)}, bf16[112,512]{1,0:T(8,128)(2,1)S(1)}, u32[]{:S(2)}, u32[]{:S(2)}) collective-permute-start(bf16[112,512]{1,0:T(8,128)(2,1)S(1)} %pack.1._.rest_5_), channel_id=1, source_target_pairs={{0,8},{1,13},{2,10},{3,15},{4,12},{5,9},{6,14},{7,11},{8,0},{9,5},... | collective-permute-start | bytes 344072 | tf_op jit(solution)/shard_map/ppermute | solution.py:261
  5.1 1.6 %collective-permute-start.2 = (bf16[112,512]{1,0:T(8,128)(2,1)S(1)}, bf16[112,512]{1,0:T(8,128)(2,1)S(1)}, u32[]{:S(2)}, u32[]{:S(2)}) collective-permute-start(bf16[112,512]{1,0:T(8,128)(2,1)S(1)} %pack.1._.rest_5_), channel_id=1, source_target_pairs={{0,4},{1,7},{2,6},{3,5},{4,0},{5,3},{6,2},{7,1},{8,12},{9,15},{10,... | collective-permute-start | bytes 344072 | tf_op jit(solution)/shard_map/ppermute | solution.py:261
  6.7 1.5 %collective-permute-start.5 = (bf16[112,512]{1,0:T(8,128)(2,1)S(1)}, bf16[112,512]{1,0:T(8,128)(2,1)S(1)}, u32[]{:S(2)}, u32[]{:S(2)}) collective-permute-start(bf16[112,512]{1,0:T(8,128)(2,1)S(1)} %pack.1._.rest_5_), channel_id=1, source_target_pairs={{0,2},{1,3},{2,0},{3,1},{4,6},{5,7},{6,4},{7,5},{8,10},{9,11},{10,... | collective-permute-start | bytes 344072 | tf_op jit(solution)/shard_map/ppermute | solution.py:261
  8.2 3.3 %prepare.1 = (bf16[96,576]{1,0:T(8,128)(2,1)S(1)}, bf16[96,576]{1,0:T(8,128)(2,1)S(1)}, f32[1,96,288]{2,1,0:T(8,128)S(1)}, f32[1,96,384]{2,1,0:T(8,128)S(1)}, f3...) custom-call(s32[16]{0:T(128)} %span_order.1, ...), custom_call_target="tpu_custom_call" | custom-call | tf_op jit(solution)/shard_map/prepare/pallas_call | solution.py:296
  11.4 0.1 collective-permute-start
  11.5 0.5 %collective-permute-start.1 = (bf16[96,576]{1,0:T(8,128)(2,1)S(1)}, bf16[96,576]{1,0:T(8,128)(2,1)S(1)}, u32[]{:S(2)}, u32[]{:S(2)}) collective-permute-start(bf16[96,576]{1,0:T(8,128)(2,1)S(1)} %get-tuple-element.20.rest_1_), channel_id=1, source_target_pairs={{0,1},{1,0},{2,3},{3,2},{4,5},{5,4},{6,7},{7,6},{8,9},{9,8},{10,11... | collective-permute-start | bytes 331784 | tf_op jit(solution)/shard_map/ppermute | solution.py:253
  12.0 0.0 collective-permute-done.4.rest_8_.rest_6_
  12.0 0.5 %collective-permute-start.7 = (bf16[112,512]{1,0:T(8,128)(2,1)S(1)}, bf16[112,512]{1,0:T(8,128)(2,1)S(1)}, u32[]{:S(2)}, u32[]{:S(2)}) collective-permute-start(bf16[112,512]{1,0:T(8,128)(2,1)S(1)} %collective-permute-done.4.rest_8_.rest_6_), channel_id=1, source_target_pairs={{0,2},{1,3},{2,0},{3,1},{4,6},{5,7},{6,4},{7,5},{8,10},{9,11},{10,... | collective-permute-start | bytes 344072 | tf_op jit(solution)/shard_map/ppermute | solution.py:261
  12.5 0.0 collective-permute-done.2.rest_7_
  12.5 0.0 collective-permute-start.3
  12.6 0.3 %collective-permute-done.rest_2_ = bf16[96,576]{1,0:T(8,128)(2,1)S(1)} collective-permute-done((bf16[96,576]{1,0:T(8,128)(2,1)S(1)}, bf16[96,576]{1,0:T(8,128)(2,1)S(1)}, u32[]{:S(2)}, u32[]{:S(2)}) %collective-permute-start) | collective-permute-done | bytes 110624 | tf_op jit(solution)/shard_map/ppermute | solution.py:253
  12.8 0.2 collective-permute-done.1.rest_3_
  13.0 0.0 collective-permute-done.5.rest_6_
  13.0 0.9 %first.1 = (f32[384,1]{1,0:T(8,128)S(1)}, f32[384,1]{1,0:T(8,128)S(1)}, f32[384,512]{1,0:T(8,128)S(1)}, bf16[112,512]{1,0:T(8,128)(2,1)S(1)}) custom-call(bf16[96,576]{1,0:T(8,128)(2,1)S(1)} %get-tuple-element.19.rest_0_, bf16[96,576]{1,0:T(8,128)(2,1)S(1)} %get-tuple-element.20.rest_1_, bf16[96,576]{1,0:T(8,128)(2,1)S(1)} %collective-permute-done.rest_2_, ...), custom_call_target="tpu_custom_call" | custom-call | tf_op jit(solution)/shard_map/first/pallas_call | solution.py:264
  13.9 0.4 %collective-permute-start.6 = (bf16[112,512]{1,0:T(8,128)(2,1)S(1)}, bf16[112,512]{1,0:T(8,128)(2,1)S(1)}, u32[]{:S(2)}, u32[]{:S(2)}) collective-permute-start(bf16[112,512]{1,0:T(8,128)(2,1)S(1)} %get-tuple-element.23), channel_id=1, source_target_pairs={{0,1},{1,0},{2,3},{3,2},{4,5},{5,4},{6,7},{7,6},{8,9},{9,8},{10,11... | collective-permute-start | bytes 344072 | tf_op jit(solution)/shard_map/ppermute | solution.py:253
  14.3 0.2 collective-permute-start.9
  14.5 2.6 %collective-permute-done.7.rest_8_ = bf16[112,512]{1,0:T(8,128)(2,1)S(1)} collective-permute-done((bf16[112,512]{1,0:T(8,128)(2,1)S(1)}, bf16[112,512]{1,0:T(8,128)(2,1)S(1)}, u32[]{:S(2)}, u32[]{:S(2)}) %collective-permute-start.7) | collective-permute-done | bytes 114720 | tf_op jit(solution)/shard_map/ppermute | solution.py:261
  17.1 0.0 collective-permute-start.8
  17.1 0.0 collective-permute-done.3.rest_5_
  17.1 0.0 collective-permute-done.6.rest_7_
  17.2 1.1 %second.1 = (f32[384,1]{1,0:T(8,128)S(1)}, f32[384,1]{1,0:T(8,128)S(1)}, f32[384,512]{1,0:T(8,128)S(1)}) custom-call(bf16[96,576]{1,0:T(8,128)(2,1)S(1)} %get-tuple-element.19.rest_0_, bf16[96,576]{1,0:T(8,128)(2,1)S(1)} %get-tuple-element.20.rest_1_, bf16[96,576]{1,0:T(8,128)(2,1)S(1)} %collective-permute-done.rest_2_, ...), custom_call_target="tpu_custom_call" | custom-call | flops 32999999488 | tf_op jit(solution)/shard_map/second/pallas_call | solution.py:264
  18.3 0.4 %collective-permute-done.8.rest_8_ = bf16[112,512]{1,0:T(8,128)(2,1)S(1)} collective-permute-done((bf16[112,512]{1,0:T(8,128)(2,1)S(1)}, bf16[112,512]{1,0:T(8,128)(2,1)S(1)}, u32[]{:S(2)}, u32[]{:S(2)}) %collective-permute-start.8) | collective-permute-done | bytes 114720 | tf_op jit(solution)/shard_map/ppermute | solution.py:253
  18.6 0.0 collective-permute-done.9.rest_10_
  18.6 2.5 %finish.1 = bf16[96,3584]{1,0:T(8,128)(2,1)} custom-call(bf16[96,576]{1,0:T(8,128)(2,1)S(1)} %get-tuple-element.19.rest_0_, bf16[96,576]{1,0:T(8,128)(2,1)S(1)} %get-tuple-element.20.rest_1_, bf16[96,576]{1,0:T(8,128)(2,1)S(1)} %collective-permute-done.rest_2_, bf16[96,576]{1,0:T(8,128)(2,1)S(1)} %collective-permute-done.1.rest_3_, ...), custom_call_target="tpu_custom_call" | custom-call | tf_op jit(solution)/shard_map/finish/pallas_call | solution.py:343
Async XLA Ops:
  1.0 11.0 %collective-permute-start.4 = (bf16[112,512]{1,0:T(8,128)(2,1)S(1)}, bf16[112,512]{1,0:T(8,128)(2,1)S(1)}, u32[]{:S(2)}, u32[]{:S(2)}) collective-permute-start(bf16[112,512]{1,0:T(8,128)(2,1)S(1)} %pack.1._.rest_5_), channel_id=1, source_target_pairs={{0,8},{1,13},{2,10},{3,15},{4,12},{5,9},{6,14},{7,11},{8,0},{9,5},... | collective-permute-start | bytes 344072 | tf_op jit(solution)/shard_map/ppermute | solution.py:261
  5.1 7.4 %collective-permute-start.2 = (bf16[112,512]{1,0:T(8,128)(2,1)S(1)}, bf16[112,512]{1,0:T(8,128)(2,1)S(1)}, u32[]{:S(2)}, u32[]{:S(2)}) collective-permute-start(bf16[112,512]{1,0:T(8,128)(2,1)S(1)} %pack.1._.rest_5_), channel_id=1, source_target_pairs={{0,4},{1,7},{2,6},{3,5},{4,0},{5,3},{6,2},{7,1},{8,12},{9,15},{10,... | collective-permute-start | bytes 344072 | tf_op jit(solution)/shard_map/ppermute | solution.py:261
  6.7 6.3 %collective-permute-start.5 = (bf16[112,512]{1,0:T(8,128)(2,1)S(1)}, bf16[112,512]{1,0:T(8,128)(2,1)S(1)}, u32[]{:S(2)}, u32[]{:S(2)}) collective-permute-start(bf16[112,512]{1,0:T(8,128)(2,1)S(1)} %pack.1._.rest_5_), channel_id=1, source_target_pairs={{0,2},{1,3},{2,0},{3,1},{4,6},{5,7},{6,4},{7,5},{8,10},{9,11},{10,... | collective-permute-start | bytes 344072 | tf_op jit(solution)/shard_map/ppermute | solution.py:261
  11.4 1.4 %collective-permute-start = (bf16[96,576]{1,0:T(8,128)(2,1)S(1)}, bf16[96,576]{1,0:T(8,128)(2,1)S(1)}, u32[]{:S(2)}, u32[]{:S(2)}) collective-permute-start(bf16[96,576]{1,0:T(8,128)(2,1)S(1)} %get-tuple-element.19.rest_0_), channel_id=1, source_target_pairs={{0,1},{1,0},{2,3},{3,2},{4,5},{5,4},{6,7},{7,6},{8,9},{9,8},{10,11... | collective-permute-start | bytes 331784 | tf_op jit(solution)/shard_map/ppermute | solution.py:253
  11.5 1.5 %collective-permute-start.1 = (bf16[96,576]{1,0:T(8,128)(2,1)S(1)}, bf16[96,576]{1,0:T(8,128)(2,1)S(1)}, u32[]{:S(2)}, u32[]{:S(2)}) collective-permute-start(bf16[96,576]{1,0:T(8,128)(2,1)S(1)} %get-tuple-element.20.rest_1_), channel_id=1, source_target_pairs={{0,1},{1,0},{2,3},{3,2},{4,5},{5,4},{6,7},{7,6},{8,9},{9,8},{10,11... | collective-permute-start | bytes 331784 | tf_op jit(solution)/shard_map/ppermute | solution.py:253
  12.0 5.1 %collective-permute-start.7 = (bf16[112,512]{1,0:T(8,128)(2,1)S(1)}, bf16[112,512]{1,0:T(8,128)(2,1)S(1)}, u32[]{:S(2)}, u32[]{:S(2)}) collective-permute-start(bf16[112,512]{1,0:T(8,128)(2,1)S(1)} %collective-permute-done.4.rest_8_.rest_6_), channel_id=1, source_target_pairs={{0,2},{1,3},{2,0},{3,1},{4,6},{5,7},{6,4},{7,5},{8,10},{9,11},{10,... | collective-permute-start | bytes 344072 | tf_op jit(solution)/shard_map/ppermute | solution.py:261
  12.5 4.6 %collective-permute-start.3 = (bf16[112,512]{1,0:T(8,128)(2,1)S(1)}, bf16[112,512]{1,0:T(8,128)(2,1)S(1)}, u32[]{:S(2)}, u32[]{:S(2)}) collective-permute-start(bf16[112,512]{1,0:T(8,128)(2,1)S(1)} %collective-permute-done.2.rest_7_), channel_id=1, source_target_pairs={{0,1},{1,0},{2,3},{3,2},{4,5},{5,4},{6,7},{7,6},{8,9},{9,8},{10,11... | collective-permute-start | bytes 344072 | tf_op jit(solution)/shard_map/ppermute | solution.py:253
  13.9 3.2 %collective-permute-start.6 = (bf16[112,512]{1,0:T(8,128)(2,1)S(1)}, bf16[112,512]{1,0:T(8,128)(2,1)S(1)}, u32[]{:S(2)}, u32[]{:S(2)}) collective-permute-start(bf16[112,512]{1,0:T(8,128)(2,1)S(1)} %get-tuple-element.23), channel_id=1, source_target_pairs={{0,1},{1,0},{2,3},{3,2},{4,5},{5,4},{6,7},{7,6},{8,9},{9,8},{10,11... | collective-permute-start | bytes 344072 | tf_op jit(solution)/shard_map/ppermute | solution.py:253
  14.3 4.3 %collective-permute-start.9 = (bf16[256,4096]{1,0:T(8,128)(2,1)S(1)}, bf16[256,4096]{1,0:T(8,128)(2,1)S(1)}, u32[]{:S(2)}, u32[]{:S(2)}) collective-permute-start(bf16[256,4096]{1,0:T(8,128)(2,1)S(1)} %get-tuple-element.32), channel_id=1, source_target_pairs={{0,1},{1,0},{2,3},{3,2},{4,5},{5,4},{6,7},{7,6},{8,9},{9,8},{10,11... | collective-permute-start | bytes 6291464 | tf_op jit(solution)/shard_map/ppermute | solution.py:253
  17.1 1.5 %collective-permute-start.8 = (bf16[112,512]{1,0:T(8,128)(2,1)S(1)}, bf16[112,512]{1,0:T(8,128)(2,1)S(1)}, u32[]{:S(2)}, u32[]{:S(2)}) collective-permute-start(bf16[112,512]{1,0:T(8,128)(2,1)S(1)} %collective-permute-done.7.rest_8_), channel_id=1, source_target_pairs={{0,1},{1,0},{2,3},{3,2},{4,5},{5,4},{6,7},{7,6},{8,9},{9,8},{10,11... | collective-permute-start | bytes 344072 | tf_op jit(solution)/shard_map/ppermute | solution.py:253

commit v7 on v6

--- a/solution.py
+++ b/solution.py
@@ -63,20 +63,31 @@
         keys[pl.ds(base + index * group, group), DC:] = part
 
 
-def prepare_kernel(order, span_order, _, nope, rope, up, value_up, out_proj, *outs):
-    weights_own, weights_sent, sems = outs[-3:]
+def fetch_weights(value_up, out_proj, target, other, sems):
     depth, width = out_proj.shape[0], out_proj.shape[1] // 2
-    fetches = []
-    for index, target in enumerate((weights_sent, weights_own)):
-        part = lax.axis_index("heads") ^ (1 - index)
-        columns = pl.ds(pl.multiple_of(part * width, 128), width)
-        pairs = [(out_proj.at[:, columns], target.at[:, pl.ds(0, width)])]
-        for block in range(DC // depth):
-            place = pl.ds(width + block * value_up.shape[1], value_up.shape[1])
-            pairs.append((value_up.at[pl.ds(block * depth, depth)], target.at[:, place]))
-        for place, pair in enumerate(pairs):
-            fetches.append(pltpu.make_async_copy(*pair, sems.at[index, place]))
-            fetches[-1].start()
+    part = lax.axis_index("heads") ^ other
+    columns = pl.ds(pl.multiple_of(part * width, 128), width)
+    pairs = [(out_proj.at[:, columns], target.at[:, pl.ds(0, width)])]
+    for block in range(DC // depth):
+        place = pl.ds(width + block * value_up.shape[1], value_up.shape[1])
+        pairs.append((value_up.at[pl.ds(block * depth, depth)], target.at[:, place]))
+    fetches = [pltpu.make_async_copy(*pair, sems.at[i]) for i, pair in enumerate(pairs)]
+    for fetch in fetches:
+        fetch.start()
+    return fetches
+
+
+def prepare_kernel(order, span_order, _, nope_in, rope_in, up_in, value_up, out_proj, *outs):
+    weights_sent, nope, rope, up, input_sems, sems = outs[-6:]
+    inputs = [
+        pltpu.make_async_copy(source, target, input_sems.at[index])
+        for index, (source, target) in enumerate(((nope_in, nope), (rope_in, rope), (up_in, up)))
+    ]
+    for fetch in inputs:
+        fetch.start()
+    fetches = fetch_weights(value_up, out_proj, weights_sent, 1, sems)
+    for fetch in inputs:
+        fetch.wait()
     rows = nope.shape[0]
     heads = nope.shape[1] // DH
     span_rows = rows // 2
@@ -91,7 +102,7 @@
         )
         outs[head][:, :DC] = latent.astype(BF16)
         outs[head][:, DC:] = rope[:, head * DR : (head + 1) * DR]
-    biases = outs[heads:-3]
+    biases = outs[heads:-6]
     row = lax.broadcasted_iota(jnp.int32, (rows, 1), 0)
     query_pos = jnp.where(
         row < span_rows,
@@ -148,13 +159,17 @@
     return top, total, added
 
 
-def chunks_kernel(heads, chunk_count, passed, later, *rest):
+def chunks_kernel(heads, chunk_count, old_count, extras, *rest):
     queries, bias, rest = rest[:heads], rest[heads], rest[heads + 1 :]
-    chunks, rest = rest[:chunk_count], rest[chunk_count + later :]
-    if passed:
-        rest[-2][...] = rest[0][...]
-        rest = rest[1:-2] + rest[-1:]
-    old, running, keys = rest[:-4], rest[-4:-1], rest[-1]
+    chunks, rest = rest[:chunk_count], rest[chunk_count:]
+    old, rest = rest[:old_count], rest[old_count:]
+    if extras:
+        (value_up, out_proj, passed), rest = rest[:3], rest[3:]
+        running, (weights, handed), (keys, sems) = rest[:3], rest[3:5], rest[5:]
+        fetches = fetch_weights(value_up, out_proj, weights, 0, sems)
+        handed[...] = passed[...]
+    else:
+        running, (keys,) = rest[:3], rest[3:]
     rows = bias.shape[1]
     for index, chunk in enumerate(chunks):
         unpack(chunk, keys, index * rows)
@@ -162,11 +177,15 @@
     values = attend_block(queries, keys, bias[0], before)
     for state, value in zip(running, values):
         state[...] = value
+    if extras:
+        for fetch in fetches:
+            fetch.wait()
 
 
 def gathered_kernel(heads, *rest):
-    queries, (bias, gathered) = rest[:heads], rest[heads : heads + 2]
-    running, keys = rest[heads + 2 : heads + 5], rest[heads + 5]
+    queries, (bias, gathered, value_up, out_proj) = rest[:heads], rest[heads : heads + 4]
+    running, (weights, keys, sems) = rest[heads + 4 : heads + 7], rest[heads + 7 :]
+    fetches = fetch_weights(value_up, out_proj, weights, 0, sems)
     blocks, rows, _ = bias.shape
 
     def fill(block):
@@ -188,6 +207,8 @@
         return carry
 
     lax.fori_loop(0, blocks - 1, step, 0)
+    for fetch in fetches:
+        fetch.wait()
 
 
 def finish_kernel(heads, chunk_count, *rest):
@@ -260,20 +281,22 @@
         ]
         return lax.ppermute(array, ("ctx", "heads"), pairs)
 
-    def attend(name, estimate, queries, bias, chunks, passed, old, *before):
+    weights_shape = jax.ShapeDtypeStruct((depth, width + blocks * key_up.shape[1]), BF16)
+
+    def attend(name, estimate, queries, bias, chunks, old=(), extras=()):
+        more = [weights_shape] + [jax.ShapeDtypeStruct(extras[-1].shape, BF16)] if extras else []
         return pl.pallas_call(
-            functools.partial(chunks_kernel, heads, len(chunks), len(passed), len(before)),
-            out_shape=[jax.ShapeDtypeStruct((query_rows, size), F32) for size in (1, 1, DC)]
-            + [jax.ShapeDtypeStruct(chunk.shape, BF16) for chunk in passed],
-            in_specs=[vmem()] * (heads + 1 + len(chunks))
-            + [anywhere()] * len(before)
-            + [vmem()] * (len(passed) + len(old)),
-            out_specs=[vmem()] * (3 + len(passed)),
-            scratch_shapes=[pltpu.VMEM((len(chunks) * rows, DC + DR), BF16)],
+            functools.partial(chunks_kernel, heads, len(chunks), len(old), bool(extras)),
+            out_shape=[jax.ShapeDtypeStruct((query_rows, size), F32) for size in (1, 1, DC)] + more,
+            in_specs=[vmem()] * (heads + 1 + len(chunks) + len(old))
+            + [hbm(), hbm(), vmem()][: len(extras)],
+            out_specs=[vmem()] * 3 + [anywhere(), vmem()][: len(more)],
+            scratch_shapes=[pltpu.VMEM((len(chunks) * rows, DC + DR), BF16)]
+            + [pltpu.SemaphoreType.DMA((1 + blocks,))] * bool(extras),
             compiler_params=small,
             cost_estimate=cost(estimate),
             name=name,
-        )(*queries, bias, *chunks, *before, *passed, *old)
+        )(*queries, bias, *chunks, *old, *extras)
 
     packed = pl.pallas_call(
         pack_kernel,
@@ -297,16 +320,22 @@
         functools.partial(prepare_kernel, order),
         out_shape=[jax.ShapeDtypeStruct((rows, DC + DR), BF16)] * (heads // 2)
         + [jax.ShapeDtypeStruct(shape, F32) for shape in bias_shapes]
-        + [jax.ShapeDtypeStruct((depth, width + blocks * key_up.shape[1]), BF16)] * 2,
-        in_specs=[smem(), anywhere()] + [vmem()] * 3 + [hbm()] * 2,
-        out_specs=[vmem()] * (heads // 2 + len(bias_shapes)) + [anywhere()] * 2,
-        scratch_shapes=[pltpu.SemaphoreType.DMA((2, 1 + blocks))],
+        + [weights_shape],
+        in_specs=[smem(), anywhere()] + [hbm()] * 5,
+        out_specs=[vmem()] * (heads // 2 + len(bias_shapes)) + [anywhere()],
+        scratch_shapes=[
+            pltpu.VMEM(queries_nope.shape, BF16),
+            pltpu.VMEM(queries_rope.shape, BF16),
+            pltpu.VMEM(key_up.shape, BF16),
+            pltpu.SemaphoreType.DMA((3,)),
+            pltpu.SemaphoreType.DMA((1 + blocks,)),
+        ],
         compiler_params=small,
         cost_estimate=cost(PREPARE_COST),
         name="prepare",
     )(*in_hbm(span_order), packed, *in_hbm(queries_nope, queries_rope, key_up, value_up, out_proj))
-    queries, biases = outs[: heads // 2], outs[heads // 2 : -2]
-    weights = [outs[-2], other_core(outs[-1])]
+    queries, biases = outs[: heads // 2], outs[heads // 2 : -1]
+    weights_other = other_core(outs[-1])
     both = [*queries, *map(other_core, queries)]
 
     if direct:
@@ -314,8 +343,13 @@
         near = partners(packed, NEAR)
         beside = partners(packed, BESIDE)
         relayed = partners(far, (1, 1))
-        *running, far_after = attend(
-            "first", FIRST_COST, both, biases[0], [packed, beside, near], [far], []
+        *running, weights_own, far_after = attend(
+            "first",
+            FIRST_COST,
+            both,
+            biases[0],
+            [packed, beside, near],
+            extras=[*in_hbm(value_up, out_proj), far],
         )
         last = [other_core(relayed)]
         running = attend(
@@ -324,20 +358,28 @@
             both,
             biases[1],
             [other_core(near), far, other_core(far_after), relayed],
-            [],
             running,
         )
     else:
         last = []
-        running = pl.pallas_call(
+        *running, weights_own = pl.pallas_call(
             functools.partial(gathered_kernel, heads),
-            out_shape=[jax.ShapeDtypeStruct((query_rows, size), F32) for size in (1, 1, DC)],
-            in_specs=[vmem()] * (heads + 2),
-            out_specs=[vmem()] * 3,
-            scratch_shapes=[pltpu.VMEM((BLOCK_CHUNKS * rows, DC + DR), BF16)],
+            out_shape=[jax.ShapeDtypeStruct((query_rows, size), F32) for size in (1, 1, DC)]
+            + [weights_shape],
+            in_specs=[vmem()] * (heads + 2) + [hbm()] * 2,
+            out_specs=[vmem()] * 3 + [anywhere()],
+            scratch_shapes=[
+                pltpu.VMEM((BLOCK_CHUNKS * rows, DC + DR), BF16),
+                pltpu.SemaphoreType.DMA((1 + blocks,)),
+            ],
             compiler_params=pltpu.CompilerParams(vmem_limit_bytes=LARGE_VMEM),
             name="gathered",
-        )(*both, biases[0], lax.all_gather(packed, "ctx", axis=0))
+        )(
+            *both,
+            biases[0],
+            lax.all_gather(packed, "ctx", axis=0),
+            *in_hbm(value_up, out_proj),
+        )
 
     tiles = 7 if width % 896 == 0 else 1
     return pl.pallas_call(
@@ -352,7 +394,7 @@
         ],
         compiler_params=small,
         name="finish",
-    )(*both, *running, *biases[2:], *last, *weights)
+    )(*both, *running, *biases[2:], *last, weights_own, weights_other)
 
 
 def solution(mesh):

time: 21.3 us -> 22.4 us (1.052)
  Pallas kernels: 8.77 us -> 9.52 us
  starting transfers between devices: 8.8 us -> 9.5 us
  waiting for transfers between devices: 3.5 us -> 3.15 us
    ppermute x4, waiting for transfers between devices: 2.66 us -> 0.92 us  [partners(): return lax.ppermute(array, ('ctx', 'heads'), pairs)]
    pallas_call x2, Pallas kernels: 1.99 us -> 3.46 us  [attend(): pl.pallas_call(functools.partial(chunks_kernel, heads, len(chunks), len(o...]
    ppermute x6, waiting for transfers between devices: 0.85 us -> 2.23 us  [other_core(): return lax.ppermute(array, 'heads', [(0, 1), (1, 0)])]
    pallas_call x1, Pallas kernels: 3.25 us -> 2.54 us  [per_device(): pl.pallas_call(functools.partial(prepare_kernel, order), out_shape=[jax.S...]
    ppermute x4, starting transfers between devices: 7.66 us -> 8.29 us  [partners(): return lax.ppermute(array, ('ctx', 'heads'), pairs)]
  transfers between devices with their start and end apart: 10 -> 10, of which waited for: 4 -> 2; matrix products, arithmetic and copies ran while one was open for 0% -> 0% of each run, Pallas kernels for 25% -> 27%
where the time goes in v7:
time: 22.4 us; the launch traced here: 22.2 us
  Pallas kernels  9.52 us (42%)
  starting transfers between devices  9.5 us (42%)
  waiting for transfers between devices  3.15 us (14%)
    ppermute x4, starting transfers between devices, partners(): return lax.ppermute(array, ('ctx', 'heads'), pairs)  8.29 us
    pallas_call x2, Pallas kernels, attend(): pl.pallas_call(functools.partial(chunks_kernel, heads, len(chunks), len(o...  3.46 us
    pallas_call x1, Pallas kernels, per_device(): pl.pallas_call(functools.partial(prepare_kernel, order), out_shape=[jax.S...  2.54 us
    pallas_call x1, Pallas kernels, per_device(): pl.pallas_call(functools.partial(finish_kernel, heads, len(last)), out_sh...  2.48 us
    ppermute x6, waiting for transfers between devices, other_core(): return lax.ppermute(array, 'heads', [(0, 1), (1, 0)])  2.23 us
    ppermute x6, starting transfers between devices, other_core(): return lax.ppermute(array, 'heads', [(0, 1), (1, 0)])  1.21 us
    pallas_call x1, Pallas kernels, per_device(): pl.pallas_call(pack_kernel, out_shape=jax.ShapeDtypeStruct((rows + rows /...  1.05 us
    ppermute x4, waiting for transfers between devices, partners(): return lax.ppermute(array, ('ctx', 'heads'), pairs)  0.92 us
  transfers between devices with their start and end apart: 10, of which 2 were waited for; matrix products, arithmetic and copies ran while one was open for 0% of the time, Pallas kernels for 27%

profile of v7, /device:TPU:0, one launch (start us, length us, event | category | flops | bytes accessed | tf_op | source)
XLA Modules:
  0.0 22.2 jit_solution(13394344667051781701)
XLA Ops:
  0.0 1.0 %pack.1._.rest_5_ = bf16[112,512]{1,0:T(8,128)(2,1)S(1)} custom-call(bf16[96,512]{1,0:T(8,128)(2,1)} %latent.1, bf16[64,96]{1,0:T(8,128)(2,1)} %bitcast.1), custom_call_target="tpu_custom_call" | custom-call | tf_op jit(solution)/shard_map/pack/pallas_call | solution.py:301
  1.0 4.1 %collective-permute-start.4 = (bf16[112,512]{1,0:T(8,128)(2,1)S(1)}, bf16[112,512]{1,0:T(8,128)(2,1)S(1)}, u32[]{:S(2)}, u32[]{:S(2)}) collective-permute-start(bf16[112,512]{1,0:T(8,128)(2,1)S(1)} %pack.1._.rest_5_), channel_id=1, source_target_pairs={{0,8},{1,13},{2,10},{3,15},{4,12},{5,9},{6,14},{7,11},{8,0},{9,5},... | collective-permute-start | bytes 344072 | tf_op jit(solution)/shard_map/ppermute | solution.py:282
  5.1 1.6 %collective-permute-start.2 = (bf16[112,512]{1,0:T(8,128)(2,1)S(1)}, bf16[112,512]{1,0:T(8,128)(2,1)S(1)}, u32[]{:S(2)}, u32[]{:S(2)}) collective-permute-start(bf16[112,512]{1,0:T(8,128)(2,1)S(1)} %pack.1._.rest_5_), channel_id=1, source_target_pairs={{0,4},{1,7},{2,6},{3,5},{4,0},{5,3},{6,2},{7,1},{8,12},{9,15},{10,... | collective-permute-start | bytes 344072 | tf_op jit(solution)/shard_map/ppermute | solution.py:282
  6.7 1.5 %collective-permute-start.5 = (bf16[112,512]{1,0:T(8,128)(2,1)S(1)}, bf16[112,512]{1,0:T(8,128)(2,1)S(1)}, u32[]{:S(2)}, u32[]{:S(2)}) collective-permute-start(bf16[112,512]{1,0:T(8,128)(2,1)S(1)} %pack.1._.rest_5_), channel_id=1, source_target_pairs={{0,2},{1,3},{2,0},{3,1},{4,6},{5,7},{6,4},{7,5},{8,10},{9,11},{10,... | collective-permute-start | bytes 344072 | tf_op jit(solution)/shard_map/ppermute | solution.py:282
  8.2 2.5 %prepare.1 = (bf16[96,576]{1,0:T(8,128)(2,1)S(1)}, bf16[96,576]{1,0:T(8,128)(2,1)S(1)}, f32[1,96,288]{2,1,0:T(8,128)S(1)}, f32[1,96,384]{2,1,0:T(8,128)S(1)}, f3...) custom-call(s32[16]{0:T(128)} %span_order.1, bf16[112,512]{1,0:T(8,128)(2,1)S(1)} %pack.1._.rest_5_, ...), custom_call_target="tpu_custom_call" | custom-call | tf_op jit(solution)/shard_map/prepare/pallas_call | solution.py:319
  10.7 0.1 collective-permute-start
  10.8 0.5 %collective-permute-start.1 = (bf16[96,576]{1,0:T(8,128)(2,1)S(1)}, bf16[96,576]{1,0:T(8,128)(2,1)S(1)}, u32[]{:S(2)}, u32[]{:S(2)}) collective-permute-start(bf16[96,576]{1,0:T(8,128)(2,1)S(1)} %get-tuple-element.20.rest_1_), channel_id=1, source_target_pairs={{0,1},{1,0},{2,3},{3,2},{4,5},{5,4},{6,7},{7,6},{8,9},{9,8},{10,11... | collective-permute-start | bytes 331784 | tf_op jit(solution)/shard_map/ppermute | solution.py:274
  11.3 0.0 collective-permute-done.4.rest_10_.rest_6_
  11.3 1.2 %collective-permute-start.7 = (bf16[112,512]{1,0:T(8,128)(2,1)S(1)}, bf16[112,512]{1,0:T(8,128)(2,1)S(1)}, u32[]{:S(2)}, u32[]{:S(2)}) collective-permute-start(bf16[112,512]{1,0:T(8,128)(2,1)S(1)} %collective-permute-done.4.rest_10_.rest_6_), channel_id=1, source_target_pairs={{0,2},{1,3},{2,0},{3,1},{4,6},{5,7},{6,4},{7,5},{8,10},{9,11},{10,... | collective-permute-start | bytes 344072 | tf_op jit(solution)/shard_map/ppermute | solution.py:282
  12.5 0.0 collective-permute-done.2.rest_7_
  12.5 0.0 collective-permute-start.3
  12.5 0.0 collective-permute-done.rest_2_
  12.5 0.0 collective-permute-done.1.rest_3_
  12.5 0.0 collective-permute-done.5.rest_6_
  12.5 2.4 %first.1 = (f32[384,1]{1,0:T(8,128)S(1)}, f32[384,1]{1,0:T(8,128)S(1)}, f32[384,512]{1,0:T(8,128)S(1)}, bf16[256,4096]{1,0:T(8,128)(2,1)S(1)}, bf16[112,512]{1,0:T(8,128)(2,1)S(1)}) custom-call(bf16[96,576]{1,0:T(8,128)(2,1)S(1)} %get-tuple-element.19.rest_0_, bf16[96,576]{1,0:T(8,128)(2,1)S(1)} %get-tuple-element.20.rest_1_, ...), custom_call_target="tpu_custom_call" | custom-call | tf_op jit(solution)/shard_map/first/pallas_call | solution.py:288
  14.9 0.6 %collective-permute-start.6 = (bf16[112,512]{1,0:T(8,128)(2,1)S(1)}, bf16[112,512]{1,0:T(8,128)(2,1)S(1)}, u32[]{:S(2)}, u32[]{:S(2)}) collective-permute-start(bf16[112,512]{1,0:T(8,128)(2,1)S(1)} %get-tuple-element.23), channel_id=1, source_target_pairs={{0,1},{1,0},{2,3},{3,2},{4,5},{5,4},{6,7},{7,6},{8,9},{9,8},{10,11... | collective-permute-start | bytes 344072 | tf_op jit(solution)/shard_map/ppermute | solution.py:274
  15.4 0.1 collective-permute-start.9
  15.5 0.9 %collective-permute-done.7.rest_8_ = bf16[112,512]{1,0:T(8,128)(2,1)S(1)} collective-permute-done((bf16[112,512]{1,0:T(8,128)(2,1)S(1)}, bf16[112,512]{1,0:T(8,128)(2,1)S(1)}, u32[]{:S(2)}, u32[]{:S(2)}) %collective-permute-start.7) | collective-permute-done | bytes 114720 | tf_op jit(solution)/shard_map/ppermute | solution.py:282
  16.4 0.0 collective-permute-start.8
  16.4 0.0 collective-permute-done.3.rest_5_
  16.4 0.0 collective-permute-done.6.rest_7_
  16.4 1.1 %second.1 = (f32[384,1]{1,0:T(8,128)S(1)}, f32[384,1]{1,0:T(8,128)S(1)}, f32[384,512]{1,0:T(8,128)S(1)}) custom-call(bf16[96,576]{1,0:T(8,128)(2,1)S(1)} %get-tuple-element.19.rest_0_, bf16[96,576]{1,0:T(8,128)(2,1)S(1)} %get-tuple-element.20.rest_1_, bf16[96,576]{1,0:T(8,128)(2,1)S(1)} %collective-permute-done.rest_2_, ...), custom_call_target="tpu_custom_call" | custom-call | flops 32999999488 | tf_op jit(solution)/shard_map/second/pallas_call | solution.py:288
  17.5 2.2 %collective-permute-done.8.rest_8_ = bf16[112,512]{1,0:T(8,128)(2,1)S(1)} collective-permute-done((bf16[112,512]{1,0:T(8,128)(2,1)S(1)}, bf16[112,512]{1,0:T(8,128)(2,1)S(1)}, u32[]{:S(2)}, u32[]{:S(2)}) %collective-permute-start.8) | collective-permute-done | bytes 114720 | tf_op jit(solution)/shard_map/ppermute | solution.py:274
  19.8 0.0 collective-permute-done.9.rest_10_
  19.8 2.5 %finish.1 = bf16[96,3584]{1,0:T(8,128)(2,1)} custom-call(bf16[96,576]{1,0:T(8,128)(2,1)S(1)} %get-tuple-element.19.rest_0_, bf16[96,576]{1,0:T(8,128)(2,1)S(1)} %get-tuple-element.20.rest_1_, bf16[96,576]{1,0:T(8,128)(2,1)S(1)} %collective-permute-done.rest_2_, bf16[96,576]{1,0:T(8,128)(2,1)S(1)} %collective-permute-done.1.rest_3_, ...), custom_call_target="tpu_custom_call" | custom-call | tf_op jit(solution)/shard_map/finish/pallas_call | solution.py:385
Async XLA Ops:
  1.0 10.2 %collective-permute-start.4 = (bf16[112,512]{1,0:T(8,128)(2,1)S(1)}, bf16[112,512]{1,0:T(8,128)(2,1)S(1)}, u32[]{:S(2)}, u32[]{:S(2)}) collective-permute-start(bf16[112,512]{1,0:T(8,128)(2,1)S(1)} %pack.1._.rest_5_), channel_id=1, source_target_pairs={{0,8},{1,13},{2,10},{3,15},{4,12},{5,9},{6,14},{7,11},{8,0},{9,5},... | collective-permute-start | bytes 344072 | tf_op jit(solution)/shard_map/ppermute | solution.py:282
  5.1 7.4 %collective-permute-start.2 = (bf16[112,512]{1,0:T(8,128)(2,1)S(1)}, bf16[112,512]{1,0:T(8,128)(2,1)S(1)}, u32[]{:S(2)}, u32[]{:S(2)}) collective-permute-start(bf16[112,512]{1,0:T(8,128)(2,1)S(1)} %pack.1._.rest_5_), channel_id=1, source_target_pairs={{0,4},{1,7},{2,6},{3,5},{4,0},{5,3},{6,2},{7,1},{8,12},{9,15},{10,... | collective-permute-start | bytes 344072 | tf_op jit(solution)/shard_map/ppermute | solution.py:282
  6.7 5.8 %collective-permute-start.5 = (bf16[112,512]{1,0:T(8,128)(2,1)S(1)}, bf16[112,512]{1,0:T(8,128)(2,1)S(1)}, u32[]{:S(2)}, u32[]{:S(2)}) collective-permute-start(bf16[112,512]{1,0:T(8,128)(2,1)S(1)} %pack.1._.rest_5_), channel_id=1, source_target_pairs={{0,2},{1,3},{2,0},{3,1},{4,6},{5,7},{6,4},{7,5},{8,10},{9,11},{10,... | collective-permute-start | bytes 344072 | tf_op jit(solution)/shard_map/ppermute | solution.py:282
  10.7 1.8 %collective-permute-start = (bf16[96,576]{1,0:T(8,128)(2,1)S(1)}, bf16[96,576]{1,0:T(8,128)(2,1)S(1)}, u32[]{:S(2)}, u32[]{:S(2)}) collective-permute-start(bf16[96,576]{1,0:T(8,128)(2,1)S(1)} %get-tuple-element.19.rest_0_), channel_id=1, source_target_pairs={{0,1},{1,0},{2,3},{3,2},{4,5},{5,4},{6,7},{7,6},{8,9},{9,8},{10,11... | collective-permute-start | bytes 331784 | tf_op jit(solution)/shard_map/ppermute | solution.py:274
  10.8 1.7 %collective-permute-start.1 = (bf16[96,576]{1,0:T(8,128)(2,1)S(1)}, bf16[96,576]{1,0:T(8,128)(2,1)S(1)}, u32[]{:S(2)}, u32[]{:S(2)}) collective-permute-start(bf16[96,576]{1,0:T(8,128)(2,1)S(1)} %get-tuple-element.20.rest_1_), channel_id=1, source_target_pairs={{0,1},{1,0},{2,3},{3,2},{4,5},{5,4},{6,7},{7,6},{8,9},{9,8},{10,11... | collective-permute-start | bytes 331784 | tf_op jit(solution)/shard_map/ppermute | solution.py:274
  11.3 5.1 %collective-permute-start.7 = (bf16[112,512]{1,0:T(8,128)(2,1)S(1)}, bf16[112,512]{1,0:T(8,128)(2,1)S(1)}, u32[]{:S(2)}, u32[]{:S(2)}) collective-permute-start(bf16[112,512]{1,0:T(8,128)(2,1)S(1)} %collective-permute-done.4.rest_10_.rest_6_), channel_id=1, source_target_pairs={{0,2},{1,3},{2,0},{3,1},{4,6},{5,7},{6,4},{7,5},{8,10},{9,11},{10,... | collective-permute-start | bytes 344072 | tf_op jit(solution)/shard_map/ppermute | solution.py:282
  12.5 4.0 %collective-permute-start.3 = (bf16[112,512]{1,0:T(8,128)(2,1)S(1)}, bf16[112,512]{1,0:T(8,128)(2,1)S(1)}, u32[]{:S(2)}, u32[]{:S(2)}) collective-permute-start(bf16[112,512]{1,0:T(8,128)(2,1)S(1)} %collective-permute-done.2.rest_7_), channel_id=1, source_target_pairs={{0,1},{1,0},{2,3},{3,2},{4,5},{5,4},{6,7},{7,6},{8,9},{9,8},{10,11... | collective-permute-start | bytes 344072 | tf_op jit(solution)/shard_map/ppermute | solution.py:274
  14.9 1.6 %collective-permute-start.6 = (bf16[112,512]{1,0:T(8,128)(2,1)S(1)}, bf16[112,512]{1,0:T(8,128)(2,1)S(1)}, u32[]{:S(2)}, u32[]{:S(2)}) collective-permute-start(bf16[112,512]{1,0:T(8,128)(2,1)S(1)} %get-tuple-element.23), channel_id=1, source_target_pairs={{0,1},{1,0},{2,3},{3,2},{4,5},{5,4},{6,7},{7,6},{8,9},{9,8},{10,11... | collective-permute-start | bytes 344072 | tf_op jit(solution)/shard_map/ppermute | solution.py:274
  15.4 4.3 %collective-permute-start.9 = (bf16[256,4096]{1,0:T(8,128)(2,1)S(1)}, bf16[256,4096]{1,0:T(8,128)(2,1)S(1)}, u32[]{:S(2)}, u32[]{:S(2)}) collective-permute-start(bf16[256,4096]{1,0:T(8,128)(2,1)S(1)} %get-tuple-element.32), channel_id=1, source_target_pairs={{0,1},{1,0},{2,3},{3,2},{4,5},{5,4},{6,7},{7,6},{8,9},{9,8},{10,11... | collective-permute-start | bytes 6291464 | tf_op jit(solution)/shard_map/ppermute | solution.py:274
  16.4 3.3 %collective-permute-start.8 = (bf16[112,512]{1,0:T(8,128)(2,1)S(1)}, bf16[112,512]{1,0:T(8,128)(2,1)S(1)}, u32[]{:S(2)}, u32[]{:S(2)}) collective-permute-start(bf16[112,512]{1,0:T(8,128)(2,1)S(1)} %collective-permute-done.7.rest_8_), channel_id=1, source_target_pairs={{0,1},{1,0},{2,3},{3,2},{4,5},{5,4},{6,7},{7,6},{8,9},{9,8},{10,11... | collective-permute-start | bytes 344072 | tf_op jit(solution)/shard_map/ppermute | solution.py:274

commit v8 on v7

--- a/solution.py
+++ b/solution.py
@@ -15,7 +15,8 @@
 F32 = jnp.float32
 MASKED = -1e30
 BLOCK_CHUNKS = 8
-PREPARE_COST, FIRST_COST, SECOND_COST = 0, 0, 30
+PREPARE_COST, FIRST_COST, SECOND_COST = 0, 3, 18
+PIECES = 4
 SMALL_VMEM = 20 * 1024 * 1024
 LARGE_VMEM = 56 * 1024 * 1024
 FAR = (4, 6)
@@ -67,7 +68,10 @@
     depth, width = out_proj.shape[0], out_proj.shape[1] // 2
     part = lax.axis_index("heads") ^ other
     columns = pl.ds(pl.multiple_of(part * width, 128), width)
-    pairs = [(out_proj.at[:, columns], target.at[:, pl.ds(0, width)])]
+    pairs = []
+    for piece in range(PIECES):
+        some = pl.ds(piece * (depth // PIECES), depth // PIECES)
+        pairs.append((out_proj.at[some, columns], target.at[some, pl.ds(0, width)]))
     for block in range(DC // depth):
         place = pl.ds(width + block * value_up.shape[1], value_up.shape[1])
         pairs.append((value_up.at[pl.ds(block * depth, depth)], target.at[:, place]))
@@ -292,7 +296,7 @@
             + [hbm(), hbm(), vmem()][: len(extras)],
             out_specs=[vmem()] * 3 + [anywhere(), vmem()][: len(more)],
             scratch_shapes=[pltpu.VMEM((len(chunks) * rows, DC + DR), BF16)]
-            + [pltpu.SemaphoreType.DMA((1 + blocks,))] * bool(extras),
+            + [pltpu.SemaphoreType.DMA((PIECES + blocks,))] * bool(extras),
             compiler_params=small,
             cost_estimate=cost(estimate),
             name=name,
@@ -328,7 +332,7 @@
             pltpu.VMEM(queries_rope.shape, BF16),
             pltpu.VMEM(key_up.shape, BF16),
             pltpu.SemaphoreType.DMA((3,)),
-            pltpu.SemaphoreType.DMA((1 + blocks,)),
+            pltpu.SemaphoreType.DMA((PIECES + blocks,)),
         ],
         compiler_params=small,
         cost_estimate=cost(PREPARE_COST),
@@ -370,7 +374,7 @@
             out_specs=[vmem()] * 3 + [anywhere()],
             scratch_shapes=[
                 pltpu.VMEM((BLOCK_CHUNKS * rows, DC + DR), BF16),
-                pltpu.SemaphoreType.DMA((1 + blocks,)),
+                pltpu.SemaphoreType.DMA((PIECES + blocks,)),
             ],
             compiler_params=pltpu.CompilerParams(vmem_limit_bytes=LARGE_VMEM),
             name="gathered",

time: 22.4 us -> 21.7 us (0.969)
  starting transfers between devices: 9.5 us -> 8.97 us
    ppermute x6, waiting for transfers between devices: 2.23 us -> 1.04 us  [other_core(): return lax.ppermute(array, 'heads', [(0, 1), (1, 0)])]
    ppermute x4, waiting for transfers between devices: 0.92 us -> 1.89 us  [partners(): return lax.ppermute(array, ('ctx', 'heads'), pairs)]
    ppermute x4, starting transfers between devices: 8.29 us -> 7.67 us  [partners(): return lax.ppermute(array, ('ctx', 'heads'), pairs)]
  transfers between devices with their start and end apart: 10 -> 10, of which waited for: 2 -> 3; matrix products, arithmetic and copies ran while one was open for 0% -> 0% of each run, Pallas kernels for 27% -> 28%
where the time goes in v8:
time: 21.7 us; the launch traced here: 21.5 us
  Pallas kernels  9.57 us (44%)
  starting transfers between devices  8.97 us (41%)
  waiting for transfers between devices  2.94 us (14%)
    ppermute x4, starting transfers between devices, partners(): return lax.ppermute(array, ('ctx', 'heads'), pairs)  7.67 us
    pallas_call x2, Pallas kernels, attend(): pl.pallas_call(functools.partial(chunks_kernel, heads, len(chunks), len(o...  3.48 us
    pallas_call x1, Pallas kernels, per_device(): pl.pallas_call(functools.partial(prepare_kernel, order), out_shape=[jax.S...  2.57 us
    pallas_call x1, Pallas kernels, per_device(): pl.pallas_call(functools.partial(finish_kernel, heads, len(last)), out_sh...  2.48 us
    ppermute x4, waiting for transfers between devices, partners(): return lax.ppermute(array, ('ctx', 'heads'), pairs)  1.89 us
    ppermute x6, starting transfers between devices, other_core(): return lax.ppermute(array, 'heads', [(0, 1), (1, 0)])  1.3 us
    pallas_call x1, Pallas kernels, per_device(): pl.pallas_call(pack_kernel, out_shape=jax.ShapeDtypeStruct((rows + rows /...  1.05 us
    ppermute x6, waiting for transfers between devices, other_core(): return lax.ppermute(array, 'heads', [(0, 1), (1, 0)])  1.04 us
  transfers between devices with their start and end apart: 10, of which 3 were waited for; matrix products, arithmetic and copies ran while one was open for 0% of the time, Pallas kernels for 28%

profile of v8, /device:TPU:0, one launch (start us, length us, event | category | flops | bytes accessed | tf_op | source)
XLA Modules:
  0.0 21.5 jit_solution(17196689980199879631)
XLA Ops:
  0.0 1.0 %pack.1._.rest_5_ = bf16[112,512]{1,0:T(8,128)(2,1)S(1)} custom-call(bf16[96,512]{1,0:T(8,128)(2,1)} %latent.1, bf16[64,96]{1,0:T(8,128)(2,1)} %bitcast.1), custom_call_target="tpu_custom_call" | custom-call | tf_op jit(solution)/shard_map/pack/pallas_call | solution.py:305
  1.0 4.1 %collective-permute-start.4 = (bf16[112,512]{1,0:T(8,128)(2,1)S(1)}, bf16[112,512]{1,0:T(8,128)(2,1)S(1)}, u32[]{:S(2)}, u32[]{:S(2)}) collective-permute-start(bf16[112,512]{1,0:T(8,128)(2,1)S(1)} %pack.1._.rest_5_), channel_id=1, source_target_pairs={{0,8},{1,13},{2,10},{3,15},{4,12},{5,9},{6,14},{7,11},{8,0},{9,5},... | collective-permute-start | bytes 344072 | tf_op jit(solution)/shard_map/ppermute | solution.py:286
  5.1 1.6 %collective-permute-start.2 = (bf16[112,512]{1,0:T(8,128)(2,1)S(1)}, bf16[112,512]{1,0:T(8,128)(2,1)S(1)}, u32[]{:S(2)}, u32[]{:S(2)}) collective-permute-start(bf16[112,512]{1,0:T(8,128)(2,1)S(1)} %pack.1._.rest_5_), channel_id=1, source_target_pairs={{0,4},{1,7},{2,6},{3,5},{4,0},{5,3},{6,2},{7,1},{8,12},{9,15},{10,... | collective-permute-start | bytes 344072 | tf_op jit(solution)/shard_map/ppermute | solution.py:286
  6.7 1.5 %collective-permute-start.5 = (bf16[112,512]{1,0:T(8,128)(2,1)S(1)}, bf16[112,512]{1,0:T(8,128)(2,1)S(1)}, u32[]{:S(2)}, u32[]{:S(2)}) collective-permute-start(bf16[112,512]{1,0:T(8,128)(2,1)S(1)} %pack.1._.rest_5_), channel_id=1, source_target_pairs={{0,2},{1,3},{2,0},{3,1},{4,6},{5,7},{6,4},{7,5},{8,10},{9,11},{10,... | collective-permute-start | bytes 344072 | tf_op jit(solution)/shard_map/ppermute | solution.py:286
  8.2 2.6 %prepare.1 = (bf16[96,576]{1,0:T(8,128)(2,1)S(1)}, bf16[96,576]{1,0:T(8,128)(2,1)S(1)}, f32[1,96,288]{2,1,0:T(8,128)S(1)}, f32[1,96,384]{2,1,0:T(8,128)S(1)}, f3...) custom-call(s32[16]{0:T(128)} %span_order.1, bf16[112,512]{1,0:T(8,128)(2,1)S(1)} %pack.1._.rest_5_, ...), custom_call_target="tpu_custom_call" | custom-call | tf_op jit(solution)/shard_map/prepare/pallas_call | solution.py:323
  10.7 0.1 collective-permute-start
  10.8 0.5 %collective-permute-start.1 = (bf16[96,576]{1,0:T(8,128)(2,1)S(1)}, bf16[96,576]{1,0:T(8,128)(2,1)S(1)}, u32[]{:S(2)}, u32[]{:S(2)}) collective-permute-start(bf16[96,576]{1,0:T(8,128)(2,1)S(1)} %get-tuple-element.20.rest_1_), channel_id=1, source_target_pairs={{0,1},{1,0},{2,3},{3,2},{4,5},{5,4},{6,7},{7,6},{8,9},{9,8},{10,11... | collective-permute-start | bytes 331784 | tf_op jit(solution)/shard_map/ppermute | solution.py:278
  11.3 0.8 %collective-permute-done.rest_2_ = bf16[96,576]{1,0:T(8,128)(2,1)S(1)} collective-permute-done((bf16[96,576]{1,0:T(8,128)(2,1)S(1)}, bf16[96,576]{1,0:T(8,128)(2,1)S(1)}, u32[]{:S(2)}, u32[]{:S(2)}) %collective-permute-start) | collective-permute-done | bytes 110624 | tf_op jit(solution)/shard_map/ppermute | solution.py:278
  12.1 0.1 collective-permute-start.9
  12.3 0.0 collective-permute-done.4.rest_10_.rest_6_
  12.3 0.6 %collective-permute-start.7 = (bf16[112,512]{1,0:T(8,128)(2,1)S(1)}, bf16[112,512]{1,0:T(8,128)(2,1)S(1)}, u32[]{:S(2)}, u32[]{:S(2)}) collective-permute-start(bf16[112,512]{1,0:T(8,128)(2,1)S(1)} %collective-permute-done.4.rest_10_.rest_6_), channel_id=1, source_target_pairs={{0,2},{1,3},{2,0},{3,1},{4,6},{5,7},{6,4},{7,5},{8,10},{9,11},{10,... | collective-permute-start | bytes 344072 | tf_op jit(solution)/shard_map/ppermute | solution.py:286
  12.9 0.0 collective-permute-done.2.rest_7_
  12.9 0.1 collective-permute-start.3
  12.9 0.0 collective-permute-done.1.rest_3_
  12.9 0.0 collective-permute-done.5.rest_6_
  12.9 2.4 %first.1 = (f32[384,1]{1,0:T(8,128)S(1)}, f32[384,1]{1,0:T(8,128)S(1)}, f32[384,512]{1,0:T(8,128)S(1)}, bf16[256,4096]{1,0:T(8,128)(2,1)S(1)}, bf16[112,512]{1,0:T(8,128)(2,1)S(1)}) custom-call(bf16[96,576]{1,0:T(8,128)(2,1)S(1)} %get-tuple-element.19.rest_0_, bf16[96,576]{1,0:T(8,128)(2,1)S(1)} %get-tuple-element.20.rest_1_, ...), custom_call_target="tpu_custom_call" | custom-call | flops 3300000000 | tf_op jit(solution)/shard_map/first/pallas_call | solution.py:292
  15.3 0.5 %collective-permute-start.6 = (bf16[112,512]{1,0:T(8,128)(2,1)S(1)}, bf16[112,512]{1,0:T(8,128)(2,1)S(1)}, u32[]{:S(2)}, u32[]{:S(2)}) collective-permute-start(bf16[112,512]{1,0:T(8,128)(2,1)S(1)} %get-tuple-element.23), channel_id=1, source_target_pairs={{0,1},{1,0},{2,3},{3,2},{4,5},{5,4},{6,7},{7,6},{8,9},{9,8},{10,11... | collective-permute-start | bytes 344072 | tf_op jit(solution)/shard_map/ppermute | solution.py:278
  15.8 1.9 %collective-permute-done.7.rest_8_ = bf16[112,512]{1,0:T(8,128)(2,1)S(1)} collective-permute-done((bf16[112,512]{1,0:T(8,128)(2,1)S(1)}, bf16[112,512]{1,0:T(8,128)(2,1)S(1)}, u32[]{:S(2)}, u32[]{:S(2)}) %collective-permute-start.7) | collective-permute-done | bytes 114720 | tf_op jit(solution)/shard_map/ppermute | solution.py:286
  17.7 0.0 collective-permute-start.8
  17.7 0.0 collective-permute-done.3.rest_5_
  17.7 0.0 collective-permute-done.6.rest_7_
  17.7 1.1 %second.1 = (f32[384,1]{1,0:T(8,128)S(1)}, f32[384,1]{1,0:T(8,128)S(1)}, f32[384,512]{1,0:T(8,128)S(1)}) custom-call(bf16[96,576]{1,0:T(8,128)(2,1)S(1)} %get-tuple-element.19.rest_0_, bf16[96,576]{1,0:T(8,128)(2,1)S(1)} %get-tuple-element.20.rest_1_, bf16[96,576]{1,0:T(8,128)(2,1)S(1)} %collective-permute-done.rest_2_, ...), custom_call_target="tpu_custom_call" | custom-call | flops 19800000512 | tf_op jit(solution)/shard_map/second/pallas_call | solution.py:292
  18.8 0.2 collective-permute-done.8.rest_8_
  19.0 0.0 collective-permute-done.9.rest_10_
  19.0 2.5 %finish.1 = bf16[96,3584]{1,0:T(8,128)(2,1)} custom-call(bf16[96,576]{1,0:T(8,128)(2,1)S(1)} %get-tuple-element.19.rest_0_, bf16[96,576]{1,0:T(8,128)(2,1)S(1)} %get-tuple-element.20.rest_1_, bf16[96,576]{1,0:T(8,128)(2,1)S(1)} %collective-permute-done.rest_2_, bf16[96,576]{1,0:T(8,128)(2,1)S(1)} %collective-permute-done.1.rest_3_, ...), custom_call_target="tpu_custom_call" | custom-call | tf_op jit(solution)/shard_map/finish/pallas_call | solution.py:389
Async XLA Ops:
  1.0 11.3 %collective-permute-start.4 = (bf16[112,512]{1,0:T(8,128)(2,1)S(1)}, bf16[112,512]{1,0:T(8,128)(2,1)S(1)}, u32[]{:S(2)}, u32[]{:S(2)}) collective-permute-start(bf16[112,512]{1,0:T(8,128)(2,1)S(1)} %pack.1._.rest_5_), channel_id=1, source_target_pairs={{0,8},{1,13},{2,10},{3,15},{4,12},{5,9},{6,14},{7,11},{8,0},{9,5},... | collective-permute-start | bytes 344072 | tf_op jit(solution)/shard_map/ppermute | solution.py:286
  5.1 7.8 %collective-permute-start.2 = (bf16[112,512]{1,0:T(8,128)(2,1)S(1)}, bf16[112,512]{1,0:T(8,128)(2,1)S(1)}, u32[]{:S(2)}, u32[]{:S(2)}) collective-permute-start(bf16[112,512]{1,0:T(8,128)(2,1)S(1)} %pack.1._.rest_5_), channel_id=1, source_target_pairs={{0,4},{1,7},{2,6},{3,5},{4,0},{5,3},{6,2},{7,1},{8,12},{9,15},{10,... | collective-permute-start | bytes 344072 | tf_op jit(solution)/shard_map/ppermute | solution.py:286
  6.7 6.2 %collective-permute-start.5 = (bf16[112,512]{1,0:T(8,128)(2,1)S(1)}, bf16[112,512]{1,0:T(8,128)(2,1)S(1)}, u32[]{:S(2)}, u32[]{:S(2)}) collective-permute-start(bf16[112,512]{1,0:T(8,128)(2,1)S(1)} %pack.1._.rest_5_), channel_id=1, source_target_pairs={{0,2},{1,3},{2,0},{3,1},{4,6},{5,7},{6,4},{7,5},{8,10},{9,11},{10,... | collective-permute-start | bytes 344072 | tf_op jit(solution)/shard_map/ppermute | solution.py:286
  10.7 1.4 %collective-permute-start = (bf16[96,576]{1,0:T(8,128)(2,1)S(1)}, bf16[96,576]{1,0:T(8,128)(2,1)S(1)}, u32[]{:S(2)}, u32[]{:S(2)}) collective-permute-start(bf16[96,576]{1,0:T(8,128)(2,1)S(1)} %get-tuple-element.19.rest_0_), channel_id=1, source_target_pairs={{0,1},{1,0},{2,3},{3,2},{4,5},{5,4},{6,7},{7,6},{8,9},{9,8},{10,11... | collective-permute-start | bytes 331784 | tf_op jit(solution)/shard_map/ppermute | solution.py:278
  10.8 2.1 %collective-permute-start.1 = (bf16[96,576]{1,0:T(8,128)(2,1)S(1)}, bf16[96,576]{1,0:T(8,128)(2,1)S(1)}, u32[]{:S(2)}, u32[]{:S(2)}) collective-permute-start(bf16[96,576]{1,0:T(8,128)(2,1)S(1)} %get-tuple-element.20.rest_1_), channel_id=1, source_target_pairs={{0,1},{1,0},{2,3},{3,2},{4,5},{5,4},{6,7},{7,6},{8,9},{9,8},{10,11... | collective-permute-start | bytes 331784 | tf_op jit(solution)/shard_map/ppermute | solution.py:278
  12.1 6.9 %collective-permute-start.9 = (bf16[256,4096]{1,0:T(8,128)(2,1)S(1)}, bf16[256,4096]{1,0:T(8,128)(2,1)S(1)}, u32[]{:S(2)}, u32[]{:S(2)}) collective-permute-start(bf16[256,4096]{1,0:T(8,128)(2,1)S(1)} %get-tuple-element.32), channel_id=1, source_target_pairs={{0,1},{1,0},{2,3},{3,2},{4,5},{5,4},{6,7},{7,6},{8,9},{9,8},{10,11... | collective-permute-start | bytes 6291464 | tf_op jit(solution)/shard_map/ppermute | solution.py:278
  12.3 5.4 %collective-permute-start.7 = (bf16[112,512]{1,0:T(8,128)(2,1)S(1)}, bf16[112,512]{1,0:T(8,128)(2,1)S(1)}, u32[]{:S(2)}, u32[]{:S(2)}) collective-permute-start(bf16[112,512]{1,0:T(8,128)(2,1)S(1)} %collective-permute-done.4.rest_10_.rest_6_), channel_id=1, source_target_pairs={{0,2},{1,3},{2,0},{3,1},{4,6},{5,7},{6,4},{7,5},{8,10},{9,11},{10,... | collective-permute-start | bytes 344072 | tf_op jit(solution)/shard_map/ppermute | solution.py:286
  12.9 4.9 %collective-permute-start.3 = (bf16[112,512]{1,0:T(8,128)(2,1)S(1)}, bf16[112,512]{1,0:T(8,128)(2,1)S(1)}, u32[]{:S(2)}, u32[]{:S(2)}) collective-permute-start(bf16[112,512]{1,0:T(8,128)(2,1)S(1)} %collective-permute-done.2.rest_7_), channel_id=1, source_target_pairs={{0,1},{1,0},{2,3},{3,2},{4,5},{5,4},{6,7},{7,6},{8,9},{9,8},{10,11... | collective-permute-start | bytes 344072 | tf_op jit(solution)/shard_map/ppermute | solution.py:278
  15.3 2.4 %collective-permute-start.6 = (bf16[112,512]{1,0:T(8,128)(2,1)S(1)}, bf16[112,512]{1,0:T(8,128)(2,1)S(1)}, u32[]{:S(2)}, u32[]{:S(2)}) collective-permute-start(bf16[112,512]{1,0:T(8,128)(2,1)S(1)} %get-tuple-element.23), channel_id=1, source_target_pairs={{0,1},{1,0},{2,3},{3,2},{4,5},{5,4},{6,7},{7,6},{8,9},{9,8},{10,11... | collective-permute-start | bytes 344072 | tf_op jit(solution)/shard_map/ppermute | solution.py:278
  17.7 1.3 %collective-permute-start.8 = (bf16[112,512]{1,0:T(8,128)(2,1)S(1)}, bf16[112,512]{1,0:T(8,128)(2,1)S(1)}, u32[]{:S(2)}, u32[]{:S(2)}) collective-permute-start(bf16[112,512]{1,0:T(8,128)(2,1)S(1)} %collective-permute-done.7.rest_8_), channel_id=1, source_target_pairs={{0,1},{1,0},{2,3},{3,2},{4,5},{5,4},{6,7},{7,6},{8,9},{9,8},{10,11... | collective-permute-start | bytes 344072 | tf_op jit(solution)/shard_map/ppermute | solution.py:278

commit v9 on v8

--- a/solution.py
+++ b/solution.py
@@ -64,32 +64,42 @@
         keys[pl.ds(base + index * group, group), DC:] = part
 
 
-def fetch_weights(value_up, out_proj, target, other, sems):
+def fetch_weights(value_up, out_proj, target, other, value, sems):
     depth, width = out_proj.shape[0], out_proj.shape[1] // 2
     part = lax.axis_index("heads") ^ other
     columns = pl.ds(pl.multiple_of(part * width, 128), width)
-    pairs = []
+    fetches = [pltpu.make_async_copy(value_up, value, sems.at[PIECES])]
     for piece in range(PIECES):
         some = pl.ds(piece * (depth // PIECES), depth // PIECES)
-        pairs.append((out_proj.at[some, columns], target.at[some, pl.ds(0, width)]))
-    for block in range(DC // depth):
-        place = pl.ds(width + block * value_up.shape[1], value_up.shape[1])
-        pairs.append((value_up.at[pl.ds(block * depth, depth)], target.at[:, place]))
-    fetches = [pltpu.make_async_copy(*pair, sems.at[i]) for i, pair in enumerate(pairs)]
+        fetches.append(
+            pltpu.make_async_copy(
+                out_proj.at[some, columns], target.at[some, pl.ds(0, width)], sems.at[piece]
+            )
+        )
     for fetch in fetches:
         fetch.start()
-    return fetches
+
+    def finish():
+        fetches[0].wait()
+        columns = value.shape[1]
+        for block in range(DC // depth):
+            place = pl.ds(width + block * columns, columns)
+            target[:, place] = value[pl.ds(block * depth, depth), :]
+        for fetch in fetches[1:]:
+            fetch.wait()
+
+    return finish
 
 
 def prepare_kernel(order, span_order, _, nope_in, rope_in, up_in, value_up, out_proj, *outs):
-    weights_sent, nope, rope, up, input_sems, sems = outs[-6:]
+    weights_sent, nope, rope, up, value, input_sems, sems = outs[-7:]
     inputs = [
         pltpu.make_async_copy(source, target, input_sems.at[index])
         for index, (source, target) in enumerate(((nope_in, nope), (rope_in, rope), (up_in, up)))
     ]
     for fetch in inputs:
         fetch.start()
-    fetches = fetch_weights(value_up, out_proj, weights_sent, 1, sems)
+    finish = fetch_weights(value_up, out_proj, weights_sent, 1, value, sems)
     for fetch in inputs:
         fetch.wait()
     rows = nope.shape[0]
@@ -106,7 +116,7 @@
         )
         outs[head][:, :DC] = latent.astype(BF16)
         outs[head][:, DC:] = rope[:, head * DR : (head + 1) * DR]
-    biases = outs[heads:-6]
+    biases = outs[heads:-7]
     row = lax.broadcasted_iota(jnp.int32, (rows, 1), 0)
     query_pos = jnp.where(
         row < span_rows,
@@ -138,8 +148,7 @@
 
         lax.fori_loop(0, bias_ref.shape[0], step, 0)
 
-    for fetch in fetches:
-        fetch.wait()
+    finish()
 
 
 def attend_block(queries, keys, bias, old):
@@ -169,8 +178,8 @@
     old, rest = rest[:old_count], rest[old_count:]
     if extras:
         (value_up, out_proj, passed), rest = rest[:3], rest[3:]
-        running, (weights, handed), (keys, sems) = rest[:3], rest[3:5], rest[5:]
-        fetches = fetch_weights(value_up, out_proj, weights, 0, sems)
+        running, (weights, handed), (keys, own, sems) = rest[:3], rest[3:5], rest[5:]
+        finish = fetch_weights(value_up, out_proj, weights, 0, own, sems)
         handed[...] = passed[...]
     else:
         running, (keys,) = rest[:3], rest[3:]
@@ -182,14 +191,13 @@
     for state, value in zip(running, values):
         state[...] = value
     if extras:
-        for fetch in fetches:
-            fetch.wait()
+        finish()
 
 
 def gathered_kernel(heads, *rest):
     queries, (bias, gathered, value_up, out_proj) = rest[:heads], rest[heads : heads + 4]
-    running, (weights, keys, sems) = rest[heads + 4 : heads + 7], rest[heads + 7 :]
-    fetches = fetch_weights(value_up, out_proj, weights, 0, sems)
+    running, (weights, keys, own, sems) = rest[heads + 4 : heads + 7], rest[heads + 7 :]
+    finish = fetch_weights(value_up, out_proj, weights, 0, own, sems)
     blocks, rows, _ = bias.shape
 
     def fill(block):
@@ -211,8 +219,7 @@
         return carry
 
     lax.fori_loop(0, blocks - 1, step, 0)
-    for fetch in fetches:
-        fetch.wait()
+    finish()
 
 
 def finish_kernel(heads, chunk_count, *rest):
@@ -294,9 +301,9 @@
             out_shape=[jax.ShapeDtypeStruct((query_rows, size), F32) for size in (1, 1, DC)] + more,
             in_specs=[vmem()] * (heads + 1 + len(chunks) + len(old))
             + [hbm(), hbm(), vmem()][: len(extras)],
-            out_specs=[vmem()] * 3 + [anywhere(), vmem()][: len(more)],
+            out_specs=[vmem()] * (3 + len(more)),
             scratch_shapes=[pltpu.VMEM((len(chunks) * rows, DC + DR), BF16)]
-            + [pltpu.SemaphoreType.DMA((PIECES + blocks,))] * bool(extras),
+            + [pltpu.VMEM(value_up.shape, BF16), pltpu.SemaphoreType.DMA((PIECES + 1,))][: len(more)],
             compiler_params=small,
             cost_estimate=cost(estimate),
             name=name,
@@ -326,13 +333,14 @@
         + [jax.ShapeDtypeStruct(shape, F32) for shape in bias_shapes]
         + [weights_shape],
         in_specs=[smem(), anywhere()] + [hbm()] * 5,
-        out_specs=[vmem()] * (heads // 2 + len(bias_shapes)) + [anywhere()],
+        out_specs=[vmem()] * (heads // 2 + len(bias_shapes) + 1),
         scratch_shapes=[
             pltpu.VMEM(queries_nope.shape, BF16),
             pltpu.VMEM(queries_rope.shape, BF16),
             pltpu.VMEM(key_up.shape, BF16),
+            pltpu.VMEM(value_up.shape, BF16),
             pltpu.SemaphoreType.DMA((3,)),
-            pltpu.SemaphoreType.DMA((PIECES + blocks,)),
+            pltpu.SemaphoreType.DMA((PIECES + 1,)),
         ],
         compiler_params=small,
         cost_estimate=cost(PREPARE_COST),
@@ -371,10 +379,11 @@
             out_shape=[jax.ShapeDtypeStruct((query_rows, size), F32) for size in (1, 1, DC)]
             + [weights_shape],
             in_specs=[vmem()] * (heads + 2) + [hbm()] * 2,
-            out_specs=[vmem()] * 3 + [anywhere()],
+            out_specs=[vmem()] * 4,
             scratch_shapes=[
                 pltpu.VMEM((BLOCK_CHUNKS * rows, DC + DR), BF16),
-                pltpu.SemaphoreType.DMA((PIECES + blocks,)),
+                pltpu.VMEM(value_up.shape, BF16),
+                pltpu.SemaphoreType.DMA((PIECES + 1,)),
             ],
             compiler_params=pltpu.CompilerParams(vmem_limit_bytes=LARGE_VMEM),
             name="gathered",

time: 21.7 us -> 21.7 us (level)
  no operation moved by 1% of the time
where the time goes in v9:
time: 21.7 us; the launch traced here: 21.4 us
  Pallas kernels  9.44 us (44%)
  starting transfers between devices  8.97 us (41%)
  waiting for transfers between devices  2.99 us (14%)
    ppermute x4, starting transfers between devices, partners(): return lax.ppermute(array, ('ctx', 'heads'), pairs)  7.67 us
    pallas_call x2, Pallas kernels, attend(): pl.pallas_call(functools.partial(chunks_kernel, heads, len(chunks), len(o...  3.42 us
    pallas_call x1, Pallas kernels, per_device(): pl.pallas_call(functools.partial(prepare_kernel, order), out_shape=[jax.S...  2.49 us
    pallas_call x1, Pallas kernels, per_device(): pl.pallas_call(functools.partial(finish_kernel, heads, len(last)), out_sh...  2.48 us
    ppermute x4, waiting for transfers between devices, partners(): return lax.ppermute(array, ('ctx', 'heads'), pairs)  1.95 us
    ppermute x6, starting transfers between devices, other_core(): return lax.ppermute(array, 'heads', [(0, 1), (1, 0)])  1.3 us
    pallas_call x1, Pallas kernels, per_device(): pl.pallas_call(pack_kernel, out_shape=jax.ShapeDtypeStruct((rows + rows /...  1.05 us
    ppermute x6, waiting for transfers between devices, other_core(): return lax.ppermute(array, 'heads', [(0, 1), (1, 0)])  1.05 us
  transfers between devices with their start and end apart: 10, of which 3 were waited for; matrix products, arithmetic and copies ran while one was open for 0% of the time, Pallas kernels for 28%

profile of v9, /device:TPU:0, one launch (start us, length us, event | category | flops | bytes accessed | tf_op | source)
XLA Modules:
  0.0 21.4 jit_solution(14650251052430295827)
XLA Ops:
  0.0 1.0 %pack.1._.rest_5_ = bf16[112,512]{1,0:T(8,128)(2,1)S(1)} custom-call(bf16[96,512]{1,0:T(8,128)(2,1)} %latent.1, bf16[64,96]{1,0:T(8,128)(2,1)} %bitcast.1), custom_call_target="tpu_custom_call" | custom-call | tf_op jit(solution)/shard_map/pack/pallas_call | solution.py:312
  1.0 4.1 %collective-permute-start.4 = (bf16[112,512]{1,0:T(8,128)(2,1)S(1)}, bf16[112,512]{1,0:T(8,128)(2,1)S(1)}, u32[]{:S(2)}, u32[]{:S(2)}) collective-permute-start(bf16[112,512]{1,0:T(8,128)(2,1)S(1)} %pack.1._.rest_5_), channel_id=1, source_target_pairs={{0,8},{1,13},{2,10},{3,15},{4,12},{5,9},{6,14},{7,11},{8,0},{9,5},... | collective-permute-start | bytes 344072 | tf_op jit(solution)/shard_map/ppermute | solution.py:293
  5.1 1.6 %collective-permute-start.2 = (bf16[112,512]{1,0:T(8,128)(2,1)S(1)}, bf16[112,512]{1,0:T(8,128)(2,1)S(1)}, u32[]{:S(2)}, u32[]{:S(2)}) collective-permute-start(bf16[112,512]{1,0:T(8,128)(2,1)S(1)} %pack.1._.rest_5_), channel_id=1, source_target_pairs={{0,4},{1,7},{2,6},{3,5},{4,0},{5,3},{6,2},{7,1},{8,12},{9,15},{10,... | collective-permute-start | bytes 344072 | tf_op jit(solution)/shard_map/ppermute | solution.py:293
  6.7 1.5 %collective-permute-start.5 = (bf16[112,512]{1,0:T(8,128)(2,1)S(1)}, bf16[112,512]{1,0:T(8,128)(2,1)S(1)}, u32[]{:S(2)}, u32[]{:S(2)}) collective-permute-start(bf16[112,512]{1,0:T(8,128)(2,1)S(1)} %pack.1._.rest_5_), channel_id=1, source_target_pairs={{0,2},{1,3},{2,0},{3,1},{4,6},{5,7},{6,4},{7,5},{8,10},{9,11},{10,... | collective-permute-start | bytes 344072 | tf_op jit(solution)/shard_map/ppermute | solution.py:293
  8.2 2.5 %prepare.1 = (bf16[96,576]{1,0:T(8,128)(2,1)S(1)}, bf16[96,576]{1,0:T(8,128)(2,1)S(1)}, f32[1,96,288]{2,1,0:T(8,128)S(1)}, f32[1,96,384]{2,1,0:T(8,128)S(1)}, f3...) custom-call(s32[16]{0:T(128)} %span_order.1, bf16[112,512]{1,0:T(8,128)(2,1)S(1)} %pack.1._.rest_5_, ...), custom_call_target="tpu_custom_call" | custom-call | tf_op jit(solution)/shard_map/prepare/pallas_call | solution.py:330
  10.7 0.1 collective-permute-start
  10.7 0.5 %collective-permute-start.1 = (bf16[96,576]{1,0:T(8,128)(2,1)S(1)}, bf16[96,576]{1,0:T(8,128)(2,1)S(1)}, u32[]{:S(2)}, u32[]{:S(2)}) collective-permute-start(bf16[96,576]{1,0:T(8,128)(2,1)S(1)} %get-tuple-element.20.rest_1_), channel_id=1, source_target_pairs={{0,1},{1,0},{2,3},{3,2},{4,5},{5,4},{6,7},{7,6},{8,9},{9,8},{10,11... | collective-permute-start | bytes 331784 | tf_op jit(solution)/shard_map/ppermute | solution.py:285
  11.2 0.8 %collective-permute-done.rest_2_ = bf16[96,576]{1,0:T(8,128)(2,1)S(1)} collective-permute-done((bf16[96,576]{1,0:T(8,128)(2,1)S(1)}, bf16[96,576]{1,0:T(8,128)(2,1)S(1)}, u32[]{:S(2)}, u32[]{:S(2)}) %collective-permute-start) | collective-permute-done | bytes 110624 | tf_op jit(solution)/shard_map/ppermute | solution.py:285
  12.1 0.1 collective-permute-start.9
  12.2 0.0 collective-permute-done.4.rest_10_.rest_6_
  12.2 0.5 %collective-permute-start.7 = (bf16[112,512]{1,0:T(8,128)(2,1)S(1)}, bf16[112,512]{1,0:T(8,128)(2,1)S(1)}, u32[]{:S(2)}, u32[]{:S(2)}) collective-permute-start(bf16[112,512]{1,0:T(8,128)(2,1)S(1)} %collective-permute-done.4.rest_10_.rest_6_), channel_id=1, source_target_pairs={{0,2},{1,3},{2,0},{3,1},{4,6},{5,7},{6,4},{7,5},{8,10},{9,11},{10,... | collective-permute-start | bytes 344072 | tf_op jit(solution)/shard_map/ppermute | solution.py:293
  12.8 0.0 collective-permute-done.2.rest_7_
  12.8 0.1 collective-permute-start.3
  12.8 0.0 collective-permute-done.1.rest_3_
  12.8 0.0 collective-permute-done.5.rest_6_
  12.8 2.3 %first.1 = (f32[384,1]{1,0:T(8,128)S(1)}, f32[384,1]{1,0:T(8,128)S(1)}, f32[384,512]{1,0:T(8,128)S(1)}, bf16[256,4096]{1,0:T(8,128)(2,1)S(1)}, bf16[112,512]{1,0:T(8,128)(2,1)S(1)}) custom-call(bf16[96,576]{1,0:T(8,128)(2,1)S(1)} %get-tuple-element.19.rest_0_, bf16[96,576]{1,0:T(8,128)(2,1)S(1)} %get-tuple-element.20.rest_1_, ...), custom_call_target="tpu_custom_call" | custom-call | flops 3300000000 | tf_op jit(solution)/shard_map/first/pallas_call | solution.py:299
  15.2 0.5 %collective-permute-start.6 = (bf16[112,512]{1,0:T(8,128)(2,1)S(1)}, bf16[112,512]{1,0:T(8,128)(2,1)S(1)}, u32[]{:S(2)}, u32[]{:S(2)}) collective-permute-start(bf16[112,512]{1,0:T(8,128)(2,1)S(1)} %get-tuple-element.23), channel_id=1, source_target_pairs={{0,1},{1,0},{2,3},{3,2},{4,5},{5,4},{6,7},{7,6},{8,9},{9,8},{10,11... | collective-permute-start | bytes 344072 | tf_op jit(solution)/shard_map/ppermute | solution.py:285
  15.7 1.9 %collective-permute-done.7.rest_8_ = bf16[112,512]{1,0:T(8,128)(2,1)S(1)} collective-permute-done((bf16[112,512]{1,0:T(8,128)(2,1)S(1)}, bf16[112,512]{1,0:T(8,128)(2,1)S(1)}, u32[]{:S(2)}, u32[]{:S(2)}) %collective-permute-start.7) | collective-permute-done | bytes 114720 | tf_op jit(solution)/shard_map/ppermute | solution.py:293
  17.6 0.0 collective-permute-start.8
  17.6 0.0 collective-permute-done.3.rest_5_
  17.6 0.0 collective-permute-done.6.rest_7_
  17.6 1.1 %second.1 = (f32[384,1]{1,0:T(8,128)S(1)}, f32[384,1]{1,0:T(8,128)S(1)}, f32[384,512]{1,0:T(8,128)S(1)}) custom-call(bf16[96,576]{1,0:T(8,128)(2,1)S(1)} %get-tuple-element.19.rest_0_, bf16[96,576]{1,0:T(8,128)(2,1)S(1)} %get-tuple-element.20.rest_1_, bf16[96,576]{1,0:T(8,128)(2,1)S(1)} %collective-permute-done.rest_2_, ...), custom_call_target="tpu_custom_call" | custom-call | flops 19800000512 | tf_op jit(solution)/shard_map/second/pallas_call | solution.py:299
  18.8 0.2 collective-permute-done.8.rest_8_
  19.0 0.0 collective-permute-done.9.rest_10_
  19.0 2.5 %finish.1 = bf16[96,3584]{1,0:T(8,128)(2,1)} custom-call(bf16[96,576]{1,0:T(8,128)(2,1)S(1)} %get-tuple-element.19.rest_0_, bf16[96,576]{1,0:T(8,128)(2,1)S(1)} %get-tuple-element.20.rest_1_, bf16[96,576]{1,0:T(8,128)(2,1)S(1)} %collective-permute-done.rest_2_, bf16[96,576]{1,0:T(8,128)(2,1)S(1)} %collective-permute-done.1.rest_3_, ...), custom_call_target="tpu_custom_call" | custom-call | tf_op jit(solution)/shard_map/finish/pallas_call | solution.py:398
Async XLA Ops:
  1.0 11.2 %collective-permute-start.4 = (bf16[112,512]{1,0:T(8,128)(2,1)S(1)}, bf16[112,512]{1,0:T(8,128)(2,1)S(1)}, u32[]{:S(2)}, u32[]{:S(2)}) collective-permute-start(bf16[112,512]{1,0:T(8,128)(2,1)S(1)} %pack.1._.rest_5_), channel_id=1, source_target_pairs={{0,8},{1,13},{2,10},{3,15},{4,12},{5,9},{6,14},{7,11},{8,0},{9,5},... | collective-permute-start | bytes 344072 | tf_op jit(solution)/shard_map/ppermute | solution.py:293
  5.1 7.7 %collective-permute-start.2 = (bf16[112,512]{1,0:T(8,128)(2,1)S(1)}, bf16[112,512]{1,0:T(8,128)(2,1)S(1)}, u32[]{:S(2)}, u32[]{:S(2)}) collective-permute-start(bf16[112,512]{1,0:T(8,128)(2,1)S(1)} %pack.1._.rest_5_), channel_id=1, source_target_pairs={{0,4},{1,7},{2,6},{3,5},{4,0},{5,3},{6,2},{7,1},{8,12},{9,15},{10,... | collective-permute-start | bytes 344072 | tf_op jit(solution)/shard_map/ppermute | solution.py:293
  6.7 6.2 %collective-permute-start.5 = (bf16[112,512]{1,0:T(8,128)(2,1)S(1)}, bf16[112,512]{1,0:T(8,128)(2,1)S(1)}, u32[]{:S(2)}, u32[]{:S(2)}) collective-permute-start(bf16[112,512]{1,0:T(8,128)(2,1)S(1)} %pack.1._.rest_5_), channel_id=1, source_target_pairs={{0,2},{1,3},{2,0},{3,1},{4,6},{5,7},{6,4},{7,5},{8,10},{9,11},{10,... | collective-permute-start | bytes 344072 | tf_op jit(solution)/shard_map/ppermute | solution.py:293
  10.7 1.4 %collective-permute-start = (bf16[96,576]{1,0:T(8,128)(2,1)S(1)}, bf16[96,576]{1,0:T(8,128)(2,1)S(1)}, u32[]{:S(2)}, u32[]{:S(2)}) collective-permute-start(bf16[96,576]{1,0:T(8,128)(2,1)S(1)} %get-tuple-element.19.rest_0_), channel_id=1, source_target_pairs={{0,1},{1,0},{2,3},{3,2},{4,5},{5,4},{6,7},{7,6},{8,9},{9,8},{10,11... | collective-permute-start | bytes 331784 | tf_op jit(solution)/shard_map/ppermute | solution.py:285
  10.7 2.1 %collective-permute-start.1 = (bf16[96,576]{1,0:T(8,128)(2,1)S(1)}, bf16[96,576]{1,0:T(8,128)(2,1)S(1)}, u32[]{:S(2)}, u32[]{:S(2)}) collective-permute-start(bf16[96,576]{1,0:T(8,128)(2,1)S(1)} %get-tuple-element.20.rest_1_), channel_id=1, source_target_pairs={{0,1},{1,0},{2,3},{3,2},{4,5},{5,4},{6,7},{7,6},{8,9},{9,8},{10,11... | collective-permute-start | bytes 331784 | tf_op jit(solution)/shard_map/ppermute | solution.py:285
  12.1 6.9 %collective-permute-start.9 = (bf16[256,4096]{1,0:T(8,128)(2,1)S(1)}, bf16[256,4096]{1,0:T(8,128)(2,1)S(1)}, u32[]{:S(2)}, u32[]{:S(2)}) collective-permute-start(bf16[256,4096]{1,0:T(8,128)(2,1)S(1)} %get-tuple-element.32), channel_id=1, source_target_pairs={{0,1},{1,0},{2,3},{3,2},{4,5},{5,4},{6,7},{7,6},{8,9},{9,8},{10,11... | collective-permute-start | bytes 6291464 | tf_op jit(solution)/shard_map/ppermute | solution.py:285
  12.2 5.4 %collective-permute-start.7 = (bf16[112,512]{1,0:T(8,128)(2,1)S(1)}, bf16[112,512]{1,0:T(8,128)(2,1)S(1)}, u32[]{:S(2)}, u32[]{:S(2)}) collective-permute-start(bf16[112,512]{1,0:T(8,128)(2,1)S(1)} %collective-permute-done.4.rest_10_.rest_6_), channel_id=1, source_target_pairs={{0,2},{1,3},{2,0},{3,1},{4,6},{5,7},{6,4},{7,5},{8,10},{9,11},{10,... | collective-permute-start | bytes 344072 | tf_op jit(solution)/shard_map/ppermute | solution.py:293
  12.8 4.9 %collective-permute-start.3 = (bf16[112,512]{1,0:T(8,128)(2,1)S(1)}, bf16[112,512]{1,0:T(8,128)(2,1)S(1)}, u32[]{:S(2)}, u32[]{:S(2)}) collective-permute-start(bf16[112,512]{1,0:T(8,128)(2,1)S(1)} %collective-permute-done.2.rest_7_), channel_id=1, source_target_pairs={{0,1},{1,0},{2,3},{3,2},{4,5},{5,4},{6,7},{7,6},{8,9},{9,8},{10,11... | collective-permute-start | bytes 344072 | tf_op jit(solution)/shard_map/ppermute | solution.py:285
  15.2 2.5 %collective-permute-start.6 = (bf16[112,512]{1,0:T(8,128)(2,1)S(1)}, bf16[112,512]{1,0:T(8,128)(2,1)S(1)}, u32[]{:S(2)}, u32[]{:S(2)}) collective-permute-start(bf16[112,512]{1,0:T(8,128)(2,1)S(1)} %get-tuple-element.23), channel_id=1, source_target_pairs={{0,1},{1,0},{2,3},{3,2},{4,5},{5,4},{6,7},{7,6},{8,9},{9,8},{10,11... | collective-permute-start | bytes 344072 | tf_op jit(solution)/shard_map/ppermute | solution.py:285
  17.6 1.3 %collective-permute-start.8 = (bf16[112,512]{1,0:T(8,128)(2,1)S(1)}, bf16[112,512]{1,0:T(8,128)(2,1)S(1)}, u32[]{:S(2)}, u32[]{:S(2)}) collective-permute-start(bf16[112,512]{1,0:T(8,128)(2,1)S(1)} %collective-permute-done.7.rest_8_), channel_id=1, source_target_pairs={{0,1},{1,0},{2,3},{3,2},{4,5},{5,4},{6,7},{7,6},{8,9},{9,8},{10,11... | collective-permute-start | bytes 344072 | tf_op jit(solution)/shard_map/ppermute | solution.py:285

commit v10 on v6

--- a/solution.py
+++ b/solution.py
@@ -15,12 +15,12 @@
 F32 = jnp.float32
 MASKED = -1e30
 BLOCK_CHUNKS = 8
-PREPARE_COST, FIRST_COST, SECOND_COST = 0, 0, 30
+PREPARE_COST, FIRST_COST, SECOND_COST = 0, 20, 1
 SMALL_VMEM = 20 * 1024 * 1024
 LARGE_VMEM = 56 * 1024 * 1024
 FAR = (4, 6)
-NEAR = (2, 3)
-BESIDE = (1, 1)
+NEAR = (2, 1)
+CORNER = (3, 3)
 RELAYED = (5, 7)
 
 
@@ -38,10 +38,6 @@
 
 def cost(microseconds):
     return pl.CostEstimate(flops=int(microseconds * 1.1e9), bytes_accessed=0, transcendentals=0)
-
-
-def smem():
-    return pl.BlockSpec(memory_space=pltpu.SMEM)
 
 
 def pack_kernel(latent, key_rope_turned, out_ref):
@@ -54,7 +50,10 @@
     out_ref[rows:] = jnp.concatenate(parts, axis=1)
 
 
-def unpack(chunk, keys, base):
+def unpack(chunk, keys, base, other=None):
+    chunk = chunk[...]
+    if other is not None:
+        chunk = jnp.where(lax.axis_index("heads") == 0, other[...], chunk)
     rows = 6 * chunk.shape[0] // 7
     group = rows // 6
     keys[pl.ds(base, rows), :DC] = chunk[:rows]
@@ -63,23 +62,29 @@
         keys[pl.ds(base + index * group, group), DC:] = part
 
 
-def prepare_kernel(order, span_order, _, nope, rope, up, value_up, out_proj, *outs):
-    weights_own, weights_sent, sems = outs[-3:]
+def prepare_kernel(order, *refs):
+    sources, out_proj, rest = refs[:5], refs[5], refs[7:]
+    outs, copied, sems = rest[:-6], rest[-6:-1], rest[-1]
+    weights = outs[-1]
     depth, width = out_proj.shape[0], out_proj.shape[1] // 2
-    fetches = []
-    for index, target in enumerate((weights_sent, weights_own)):
-        part = lax.axis_index("heads") ^ (1 - index)
-        columns = pl.ds(pl.multiple_of(part * width, 128), width)
-        pairs = [(out_proj.at[:, columns], target.at[:, pl.ds(0, width)])]
-        for block in range(DC // depth):
-            place = pl.ds(width + block * value_up.shape[1], value_up.shape[1])
-            pairs.append((value_up.at[pl.ds(block * depth, depth)], target.at[:, place]))
-        for place, pair in enumerate(pairs):
-            fetches.append(pltpu.make_async_copy(*pair, sems.at[index, place]))
-            fetches[-1].start()
+    fetches = [
+        pltpu.make_async_copy(source, target, sems.at[index])
+        for index, (source, target) in enumerate(zip(sources, copied))
+    ]
+    base = pl.multiple_of((1 - lax.axis_index("heads")) * width, 128)
+    fetches.append(
+        pltpu.make_async_copy(
+            out_proj.at[:, pl.ds(base, width)], weights.at[:, pl.ds(0, width)], sems.at[5]
+        )
+    )
+    for fetch in fetches:
+        fetch.start()
+    nope, rope, up, span_order, value_up = copied
     rows = nope.shape[0]
     heads = nope.shape[1] // DH
     span_rows = rows // 2
+    for fetch in fetches[:3]:
+        fetch.wait()
     own_index = lax.axis_index("ctx")
     core = lax.axis_index("heads")
     for head in range(heads):
@@ -91,7 +96,8 @@
         )
         outs[head][:, :DC] = latent.astype(BF16)
         outs[head][:, DC:] = rope[:, head * DR : (head + 1) * DR]
-    biases = outs[heads:-3]
+    biases = outs[heads:-1]
+    fetches[3].wait()
     row = lax.broadcasted_iota(jnp.int32, (rows, 1), 0)
     query_pos = jnp.where(
         row < span_rows,
@@ -123,8 +129,12 @@
 
         lax.fori_loop(0, bias_ref.shape[0], step, 0)
 
-    for fetch in fetches:
-        fetch.wait()
+    fetches[4].wait()
+    columns = value_up.shape[1]
+    for block in range(DC // depth):
+        part = value_up[block * depth : (block + 1) * depth, :]
+        weights[:, width + block * columns : width + (block + 1) * columns] = part
+    fetches[5].wait()
 
 
 def attend_block(queries, keys, bias, old):
@@ -148,16 +158,22 @@
     return top, total, added
 
 
-def chunks_kernel(heads, chunk_count, passed, later, *rest):
+def chunks_kernel(heads, chunk_count, old_count, paired, *rest):
     queries, bias, rest = rest[:heads], rest[heads], rest[heads + 1 :]
-    chunks, rest = rest[:chunk_count], rest[chunk_count + later :]
-    if passed:
-        rest[-2][...] = rest[0][...]
-        rest = rest[1:-2] + rest[-1:]
-    old, running, keys = rest[:-4], rest[-4:-1], rest[-1]
+    chunks, rest = rest[:chunk_count], rest[chunk_count:]
+    old, rest = rest[:old_count], rest[old_count:]
+    if len(rest) == 6:
+        passed, handed = rest[0], rest[4]
+        handed[...] = passed[...]
+        rest = rest[1:4] + rest[5:]
+    running, keys = rest[:3], rest[3]
     rows = bias.shape[1]
+    if paired:
+        unpack(chunks[0], keys, 0, chunks[1])
+        chunks = chunks[1:]
     for index, chunk in enumerate(chunks):
-        unpack(chunk, keys, index * rows)
+        if index or not paired:
+            unpack(chunk, keys, index * rows)
     before = [state[...] for state in old] if old else None
     values = attend_block(queries, keys, bias[0], before)
     for state, value in zip(running, values):
@@ -194,7 +210,7 @@
     queries, (top, total, context), rest = rest[:heads], rest[heads : heads + 3], rest[heads + 3 :]
     bias, chunks = rest[:chunk_count][:1], rest[1 : 1 + chunk_count]
     rest = rest[len(bias) + len(chunks) :]
-    weights, (out_ref, out_tiles, keys, out_sems) = rest[:2], rest[2:]
+    value_own, proj_own, weights, out_ref, out_tiles, keys, out_sems = rest
     rows, width = out_ref.shape
     running = (top[...], total[...], context[...])
     if chunk_count:
@@ -203,18 +219,23 @@
         running = attend_block(queries, keys, bias[0][0], running)
     mixed = (running[2] / running[1]).astype(BF16)
     half = heads // 2
-    depth = weights[0].shape[0]
+    depth = weights.shape[0]
+    base = lax.axis_index("heads") * width
     sides = []
-    for group, weight in enumerate(weights):
+    for group in range(2):
         parts = []
         for head in range(half):
-            rows_of = slice((group * half + head) * rows, (group * half + head + 1) * rows)
+            first = (group * half + head) * rows
             per_head = 0.0
             for block in range(DC // depth):
-                first = width + block * half * DH + head * DH
+                if group == 0:
+                    value = value_own[block * depth : (block + 1) * depth, head * DH : (head + 1) * DH]
+                else:
+                    start = width + (block * half + head) * DH
+                    value = weights[:, start : start + DH]
                 per_head = per_head + jnp.dot(
-                    mixed[rows_of, block * depth : (block + 1) * depth],
-                    weight[:, first : first + DH],
+                    mixed[first : first + rows, block * depth : (block + 1) * depth],
+                    value,
                     preferred_element_type=F32,
                 )
             parts.append(per_head.astype(BF16))
@@ -224,8 +245,9 @@
     sends = []
     for index in range(tiles):
         part = pl.ds(index * tile, tile)
-        out = jnp.dot(sides[0], weights[0][:, part], preferred_element_type=F32)
-        out = out + jnp.dot(sides[1], weights[1][:, part], preferred_element_type=F32)
+        own = proj_own[:, pl.ds(pl.multiple_of(base + index * tile, 128), tile)]
+        out = jnp.dot(sides[0], own, preferred_element_type=F32)
+        out = out + jnp.dot(sides[1], weights[:, part], preferred_element_type=F32)
         out_tiles[:, part] = out.astype(BF16)
         sends.append(
             pltpu.make_async_copy(out_tiles.at[:, part], out_ref.at[:, part], out_sems.at[index])
@@ -240,7 +262,6 @@
 ):
     rows = latent.shape[0]
     depth, width = out_proj.shape[0], out_proj.shape[1] // 2
-    blocks = DC // depth
     heads = 2 * (key_up.shape[1] // DH)
     query_rows = heads * rows
     direct = count == 8
@@ -252,28 +273,26 @@
     def other_core(array):
         return lax.ppermute(array, "heads", [(0, 1), (1, 0)])
 
-    def partners(array, steps):
+    def partners(array, steps, cores=(0, 1)):
         pairs = [
             (2 * index + core, 2 * (index ^ steps[core]) + core)
             for index in range(count)
-            for core in range(2)
+            for core in cores
         ]
         return lax.ppermute(array, ("ctx", "heads"), pairs)
 
-    def attend(name, estimate, queries, bias, chunks, passed, old, *before):
+    def attend(name, estimate, queries, bias, chunks, old=(), passed=(), paired=False):
         return pl.pallas_call(
-            functools.partial(chunks_kernel, heads, len(chunks), len(passed), len(before)),
+            functools.partial(chunks_kernel, heads, len(chunks), len(old), paired),
             out_shape=[jax.ShapeDtypeStruct((query_rows, size), F32) for size in (1, 1, DC)]
             + [jax.ShapeDtypeStruct(chunk.shape, BF16) for chunk in passed],
-            in_specs=[vmem()] * (heads + 1 + len(chunks))
-            + [anywhere()] * len(before)
-            + [vmem()] * (len(passed) + len(old)),
+            in_specs=[vmem()] * (heads + 1 + len(chunks) + len(old) + len(passed)),
             out_specs=[vmem()] * (3 + len(passed)),
-            scratch_shapes=[pltpu.VMEM((len(chunks) * rows, DC + DR), BF16)],
+            scratch_shapes=[pltpu.VMEM((bias.shape[2], DC + DR), BF16)],
             compiler_params=small,
             cost_estimate=cost(estimate),
             name=name,
-        )(*queries, bias, *chunks, *before, *passed, *old)
+        )(*queries, bias, *chunks, *old, *passed)
 
     packed = pl.pallas_call(
         pack_kernel,
@@ -285,8 +304,8 @@
     )(*in_hbm(latent, key_rope.T))
     if direct:
         order = [
-            [(0, 0), BESIDE, NEAR],
-            [NEAR[::-1], FAR, FAR[::-1], RELAYED],
+            [(0, 0), NEAR],
+            [CORNER, NEAR[::-1], FAR, FAR[::-1], RELAYED],
             [RELAYED[::-1]],
         ]
         bias_shapes = [(1, rows, len(steps) * rows) for steps in order]
@@ -297,25 +316,32 @@
         functools.partial(prepare_kernel, order),
         out_shape=[jax.ShapeDtypeStruct((rows, DC + DR), BF16)] * (heads // 2)
         + [jax.ShapeDtypeStruct(shape, F32) for shape in bias_shapes]
-        + [jax.ShapeDtypeStruct((depth, width + blocks * key_up.shape[1]), BF16)] * 2,
-        in_specs=[smem(), anywhere()] + [vmem()] * 3 + [hbm()] * 2,
-        out_specs=[vmem()] * (heads // 2 + len(bias_shapes)) + [anywhere()] * 2,
-        scratch_shapes=[pltpu.SemaphoreType.DMA((2, 1 + blocks))],
+        + [jax.ShapeDtypeStruct((depth, width + DC // depth * key_up.shape[1]), BF16)],
+        in_specs=[hbm()] * 6 + [anywhere()],
+        out_specs=[vmem()] * (heads // 2 + len(bias_shapes) + 1),
+        scratch_shapes=[
+            pltpu.VMEM(queries_nope.shape, BF16),
+            pltpu.VMEM(queries_rope.shape, BF16),
+            pltpu.VMEM(key_up.shape, BF16),
+            pltpu.SMEM(span_order.shape, jnp.int32),
+            pltpu.VMEM(value_up.shape, BF16),
+            pltpu.SemaphoreType.DMA((6,)),
+        ],
         compiler_params=small,
         cost_estimate=cost(PREPARE_COST),
         name="prepare",
-    )(*in_hbm(span_order), packed, *in_hbm(queries_nope, queries_rope, key_up, value_up, out_proj))
-    queries, biases = outs[: heads // 2], outs[heads // 2 : -2]
-    weights = [outs[-2], other_core(outs[-1])]
+    )(*in_hbm(queries_nope, queries_rope, key_up, span_order, value_up, out_proj), packed)
+    queries, biases = outs[: heads // 2], outs[heads // 2 : -1]
+    weights_other = other_core(outs[-1])
     both = [*queries, *map(other_core, queries)]
 
     if direct:
         far = partners(packed, FAR)
         near = partners(packed, NEAR)
-        beside = partners(packed, BESIDE)
+        corner = partners(packed, CORNER, cores=(1,))
         relayed = partners(far, (1, 1))
         *running, far_after = attend(
-            "first", FIRST_COST, both, biases[0], [packed, beside, near], [far], []
+            "first", FIRST_COST, both, biases[0], [packed, near], passed=[far]
         )
         last = [other_core(relayed)]
         running = attend(
@@ -323,9 +349,9 @@
             SECOND_COST,
             both,
             biases[1],
-            [other_core(near), far, other_core(far_after), relayed],
-            [],
+            [corner, other_core(corner), other_core(near), far, other_core(far_after), relayed],
             running,
+            paired=True,
         )
     else:
         last = []
@@ -343,7 +369,7 @@
     return pl.pallas_call(
         functools.partial(finish_kernel, heads, len(last)),
         out_shape=jax.ShapeDtypeStruct((rows, width), BF16),
-        in_specs=[vmem()] * (heads + 3 + len(biases[2:]) + len(last) + 2),
+        in_specs=[vmem()] * (heads + 3 + len(biases[2:]) + len(last) + 3),
         out_specs=anywhere(),
         scratch_shapes=[
             pltpu.VMEM((rows, width), BF16),
@@ -352,7 +378,7 @@
         ],
         compiler_params=small,
         name="finish",
-    )(*both, *running, *biases[2:], *last, *weights)
+    )(*both, *running, *biases[2:], *last, value_up, out_proj, weights_other)
 
 
 def solution(mesh):

time: 21.3 us -> 21.2 us (level)
  Pallas kernels: 8.77 us -> 7.14 us
  starting transfers between devices: 8.8 us -> 9.63 us
  waiting for transfers between devices: 3.5 us -> 4.14 us
    pallas_call x1, Pallas kernels: 3.25 us -> 1.77 us  [per_device(): pl.pallas_call(functools.partial(prepare_kernel, order), out_shape=[jax.S...]
    ppermute x6 -> x7, starting transfers between devices: 1.15 us -> 2.62 us  [other_core(): return lax.ppermute(array, 'heads', [(0, 1), (1, 0)])]
    ppermute x4, starting transfers between devices: 7.66 us -> 7.01 us  [partners(): return lax.ppermute(array, ('ctx', 'heads'), pairs)]
    ppermute x4, waiting for transfers between devices: 2.66 us -> 3.04 us  [partners(): return lax.ppermute(array, ('ctx', 'heads'), pairs)]
    ppermute x6 -> x7, waiting for transfers between devices: 0.85 us -> 1.1 us  [other_core(): return lax.ppermute(array, 'heads', [(0, 1), (1, 0)])]
  transfers between devices with their start and end apart: 10 -> 11, of which waited for: 4 -> 3; matrix products, arithmetic and copies ran while one was open for 0% -> 0% of each run, Pallas kernels for 25% -> 17%
where the time goes in v10:
time: 21.2 us; the launch traced here: 21 us
  starting transfers between devices  9.63 us (45%)
  Pallas kernels  7.14 us (34%)
  waiting for transfers between devices  4.14 us (20%)
    ppermute x4, starting transfers between devices, partners(): return lax.ppermute(array, ('ctx', 'heads'), pairs)  7.01 us
    ppermute x4, waiting for transfers between devices, partners(): return lax.ppermute(array, ('ctx', 'heads'), pairs)  3.04 us
    ppermute x7, starting transfers between devices, other_core(): return lax.ppermute(array, 'heads', [(0, 1), (1, 0)])  2.62 us
    pallas_call x1, Pallas kernels, per_device(): pl.pallas_call(functools.partial(finish_kernel, heads, len(last)), out_sh...  2.47 us
    pallas_call x2, Pallas kernels, attend(): pl.pallas_call(functools.partial(chunks_kernel, heads, len(chunks), len(o...  1.84 us
    pallas_call x1, Pallas kernels, per_device(): pl.pallas_call(functools.partial(prepare_kernel, order), out_shape=[jax.S...  1.77 us
    ppermute x7, waiting for transfers between devices, other_core(): return lax.ppermute(array, 'heads', [(0, 1), (1, 0)])  1.1 us
    pallas_call x1, Pallas kernels, per_device(): pl.pallas_call(pack_kernel, out_shape=jax.ShapeDtypeStruct((rows + rows /...  1.05 us
  transfers between devices with their start and end apart: 11, of which 3 were waited for; matrix products, arithmetic and copies ran while one was open for 0% of the time, Pallas kernels for 17%

profile of v10, /device:TPU:0, one launch (start us, length us, event | category | flops | bytes accessed | tf_op | source)
XLA Modules:
  0.0 21.0 jit_solution(2226594981092714521)
XLA Ops:
  0.0 1.0 %pack.1.refs_6_.rest_5_ = bf16[112,512]{1,0:T(8,128)(2,1)S(1)} custom-call(bf16[96,512]{1,0:T(8,128)(2,1)} %latent.1, bf16[64,96]{1,0:T(8,128)(2,1)} %bitcast.1), custom_call_target="tpu_custom_call" | custom-call | tf_op jit(solution)/shard_map/pack/pallas_call | solution.py:297
  1.0 4.1 %collective-permute-start.6 = (bf16[112,512]{1,0:T(8,128)(2,1)S(1)}, bf16[112,512]{1,0:T(8,128)(2,1)S(1)}, u32[]{:S(2)}, u32[]{:S(2)}) collective-permute-start(bf16[112,512]{1,0:T(8,128)(2,1)S(1)} %pack.1.refs_6_.rest_5_), channel_id=1, source_target_pairs={{0,8},{1,13},{2,10},{3,15},{4,12},{5,9},{6,14},{7,11},{8,0},{9,5},... | collective-permute-start | bytes 344072 | tf_op jit(solution)/shard_map/ppermute | solution.py:282
  5.1 1.6 %collective-permute-start.4 = (bf16[112,512]{1,0:T(8,128)(2,1)S(1)}, bf16[112,512]{1,0:T(8,128)(2,1)S(1)}, u32[]{:S(2)}, u32[]{:S(2)}) collective-permute-start(bf16[112,512]{1,0:T(8,128)(2,1)S(1)} %pack.1.refs_6_.rest_5_), channel_id=1, source_target_pairs={{0,4},{1,3},{2,6},{3,1},{4,0},{5,7},{6,2},{7,5},{8,12},{9,11},{10,... | collective-permute-start | bytes 344072 | tf_op jit(solution)/shard_map/ppermute | solution.py:282
  6.7 0.7 %collective-permute-start.2 = (bf16[112,512]{1,0:T(8,128)(2,1)S(1)}, bf16[112,512]{1,0:T(8,128)(2,1)S(1)}, u32[]{:S(2)}, u32[]{:S(2)}) collective-permute-start(bf16[112,512]{1,0:T(8,128)(2,1)S(1)} %pack.1.refs_6_.rest_5_), channel_id=1, source_target_pairs={{1,7},{3,5},{5,3},{7,1},{9,15},{11,13},{13,11},{15,9},{17,23},{19,... | collective-permute-start | bytes 344072 | tf_op jit(solution)/shard_map/ppermute | solution.py:282
  7.3 1.8 %prepare.1 = (bf16[96,576]{1,0:T(8,128)(2,1)S(1)}, bf16[96,576]{1,0:T(8,128)(2,1)S(1)}, f32[1,96,192]{2,1,0:T(8,128)S(1)}, f32[1,96,480]{2,1,0:T(8,128)S(1)}, f3...) custom-call(bf16[96,256]{1,0:T(8,128)(2,1)} %refs_0_.1, bf16[96,128]{1,0:T(8,128)(2,1)} %refs_1_.1, ...), custom_call_target="tpu_custom_call" | custom-call | tf_op jit(solution)/shard_map/prepare/pallas_call | solution.py:315
  9.1 1.5 %collective-permute-start = (bf16[96,576]{1,0:T(8,128)(2,1)S(1)}, bf16[96,576]{1,0:T(8,128)(2,1)S(1)}, u32[]{:S(2)}, u32[]{:S(2)}) collective-permute-start(bf16[96,576]{1,0:T(8,128)(2,1)S(1)} %get-tuple-element.18.rest_0_), channel_id=1, source_target_pairs={{0,1},{1,0},{2,3},{3,2},{4,5},{5,4},{6,7},{7,6},{8,9},{9,8},{10,11... | collective-permute-start | bytes 331784 | tf_op jit(solution)/shard_map/ppermute | solution.py:274
  10.6 0.1 collective-permute-start.1
  10.7 0.9 %collective-permute-done.rest_2_ = bf16[96,576]{1,0:T(8,128)(2,1)S(1)} collective-permute-done((bf16[96,576]{1,0:T(8,128)(2,1)S(1)}, bf16[96,576]{1,0:T(8,128)(2,1)S(1)}, u32[]{:S(2)}, u32[]{:S(2)}) %collective-permute-start) | collective-permute-done | bytes 110624 | tf_op jit(solution)/shard_map/ppermute | solution.py:274
  11.6 0.4 %collective-permute-start.10 = (bf16[256,4096]{1,0:T(8,128)(2,1)S(1)}, bf16[256,4096]{1,0:T(8,128)(2,1)S(1)}, u32[]{:S(2)}, u32[]{:S(2)}) collective-permute-start(bf16[256,4096]{1,0:T(8,128)(2,1)S(1)} %get-tuple-element.30), channel_id=1, source_target_pairs={{0,1},{1,0},{2,3},{3,2},{4,5},{5,4},{6,7},{7,6},{8,9},{9,8},{10,11... | collective-permute-start | bytes 6291464 | tf_op jit(solution)/shard_map/ppermute | solution.py:274
  12.0 0.0 collective-permute-done.6.rest_7_.rest_8_
  12.0 0.7 %collective-permute-start.8 = (bf16[112,512]{1,0:T(8,128)(2,1)S(1)}, bf16[112,512]{1,0:T(8,128)(2,1)S(1)}, u32[]{:S(2)}, u32[]{:S(2)}) collective-permute-start(bf16[112,512]{1,0:T(8,128)(2,1)S(1)} %collective-permute-done.6.rest_7_.rest_8_), channel_id=1, source_target_pairs={{0,2},{1,3},{2,0},{3,1},{4,6},{5,7},{6,4},{7,5},{8,10},{9,11},{10,... | collective-permute-start | bytes 344072 | tf_op jit(solution)/shard_map/ppermute | solution.py:282
  12.7 0.0 collective-permute-done.4.rest_6_
  12.7 0.0 collective-permute-start.5
  12.7 0.0 collective-permute-done.2.rest_5_
  12.7 0.6 %collective-permute-start.3 = (bf16[112,512]{1,0:T(8,128)(2,1)S(1)}, bf16[112,512]{1,0:T(8,128)(2,1)S(1)}, u32[]{:S(2)}, u32[]{:S(2)}) collective-permute-start(bf16[112,512]{1,0:T(8,128)(2,1)S(1)} %collective-permute-done.2.rest_5_), channel_id=1, source_target_pairs={{0,1},{1,0},{2,3},{3,2},{4,5},{5,4},{6,7},{7,6},{8,9},{9,8},{10,11... | collective-permute-start | bytes 344072 | tf_op jit(solution)/shard_map/ppermute | solution.py:274
  13.3 0.0 collective-permute-done.1.rest_3_
  13.3 0.7 %first.1 = (f32[384,1]{1,0:T(8,128)S(1)}, f32[384,1]{1,0:T(8,128)S(1)}, f32[384,512]{1,0:T(8,128)S(1)}, bf16[112,512]{1,0:T(8,128)(2,1)S(1)}) custom-call(bf16[96,576]{1,0:T(8,128)(2,1)S(1)} %get-tuple-element.18.rest_0_, bf16[96,576]{1,0:T(8,128)(2,1)S(1)} %get-tuple-element.19.rest_1_, bf16[96,576]{1,0:T(8,128)(2,1)S(1)} %collective-permute-done.rest_2_, ...), custom_call_target="tpu_custom_call" | custom-call | flops 22000001024 | tf_op jit(solution)/shard_map/first/pallas_call | solution.py:285
  14.0 0.0 copy-start
  14.1 0.0 copy-start.1
  14.1 0.1 collective-permute-start.7
  14.2 3.0 %collective-permute-done.8.rest_10_ = bf16[112,512]{1,0:T(8,128)(2,1)S(1)} collective-permute-done((bf16[112,512]{1,0:T(8,128)(2,1)S(1)}, bf16[112,512]{1,0:T(8,128)(2,1)S(1)}, u32[]{:S(2)}, u32[]{:S(2)}) %collective-permute-start.8) | collective-permute-done | bytes 114720 | tf_op jit(solution)/shard_map/ppermute | solution.py:282
  17.2 0.0 collective-permute-start.9
  17.2 0.0 collective-permute-done.5.rest_7_
  17.2 0.0 collective-permute-done.3.rest_6_
  17.2 0.0 collective-permute-done.7.rest_9_
  17.2 1.1 %second.1 = (f32[384,1]{1,0:T(8,128)S(1)}, f32[384,1]{1,0:T(8,128)S(1)}, f32[384,512]{1,0:T(8,128)S(1)}) custom-call(bf16[96,576]{1,0:T(8,128)(2,1)S(1)} %get-tuple-element.18.rest_0_, bf16[96,576]{1,0:T(8,128)(2,1)S(1)} %get-tuple-element.19.rest_1_, bf16[96,576]{1,0:T(8,128)(2,1)S(1)} %collective-permute-done.rest_2_, ...), custom_call_target="tpu_custom_call" | custom-call | flops 1100000000 | tf_op jit(solution)/shard_map/second/pallas_call | solution.py:285
  18.3 0.2 collective-permute-done.9.rest_8_
  18.5 0.0 collective-permute-done.10.rest_11_
  18.5 0.0 copy-done
  18.5 0.0 copy-done.1
  18.5 2.5 %finish.1 = bf16[96,3584]{1,0:T(8,128)(2,1)} custom-call(bf16[96,576]{1,0:T(8,128)(2,1)S(1)} %get-tuple-element.18.rest_0_, bf16[96,576]{1,0:T(8,128)(2,1)S(1)} %get-tuple-element.19.rest_1_, bf16[96,576]{1,0:T(8,128)(2,1)S(1)} %collective-permute-done.rest_2_, bf16[96,576]{1,0:T(8,128)(2,1)S(1)} %collective-permute-done.1.rest_3_, ...), custom_call_target="tpu_custom_call" | custom-call | tf_op jit(solution)/shard_map/finish/pallas_call | solution.py:369
Async XLA Ops:
  1.0 10.9 %collective-permute-start.6 = (bf16[112,512]{1,0:T(8,128)(2,1)S(1)}, bf16[112,512]{1,0:T(8,128)(2,1)S(1)}, u32[]{:S(2)}, u32[]{:S(2)}) collective-permute-start(bf16[112,512]{1,0:T(8,128)(2,1)S(1)} %pack.1.refs_6_.rest_5_), channel_id=1, source_target_pairs={{0,8},{1,13},{2,10},{3,15},{4,12},{5,9},{6,14},{7,11},{8,0},{9,5},... | collective-permute-start | bytes 344072 | tf_op jit(solution)/shard_map/ppermute | solution.py:282
  5.1 7.6 %collective-permute-start.4 = (bf16[112,512]{1,0:T(8,128)(2,1)S(1)}, bf16[112,512]{1,0:T(8,128)(2,1)S(1)}, u32[]{:S(2)}, u32[]{:S(2)}) collective-permute-start(bf16[112,512]{1,0:T(8,128)(2,1)S(1)} %pack.1.refs_6_.rest_5_), channel_id=1, source_target_pairs={{0,4},{1,3},{2,6},{3,1},{4,0},{5,7},{6,2},{7,5},{8,12},{9,11},{10,... | collective-permute-start | bytes 344072 | tf_op jit(solution)/shard_map/ppermute | solution.py:282
  6.7 6.0 %collective-permute-start.2 = (bf16[112,512]{1,0:T(8,128)(2,1)S(1)}, bf16[112,512]{1,0:T(8,128)(2,1)S(1)}, u32[]{:S(2)}, u32[]{:S(2)}) collective-permute-start(bf16[112,512]{1,0:T(8,128)(2,1)S(1)} %pack.1.refs_6_.rest_5_), channel_id=1, source_target_pairs={{1,7},{3,5},{5,3},{7,1},{9,15},{11,13},{13,11},{15,9},{17,23},{19,... | collective-permute-start | bytes 344072 | tf_op jit(solution)/shard_map/ppermute | solution.py:282
  9.1 2.5 %collective-permute-start = (bf16[96,576]{1,0:T(8,128)(2,1)S(1)}, bf16[96,576]{1,0:T(8,128)(2,1)S(1)}, u32[]{:S(2)}, u32[]{:S(2)}) collective-permute-start(bf16[96,576]{1,0:T(8,128)(2,1)S(1)} %get-tuple-element.18.rest_0_), channel_id=1, source_target_pairs={{0,1},{1,0},{2,3},{3,2},{4,5},{5,4},{6,7},{7,6},{8,9},{9,8},{10,11... | collective-permute-start | bytes 331784 | tf_op jit(solution)/shard_map/ppermute | solution.py:274
  10.6 2.7 %collective-permute-start.1 = (bf16[96,576]{1,0:T(8,128)(2,1)S(1)}, bf16[96,576]{1,0:T(8,128)(2,1)S(1)}, u32[]{:S(2)}, u32[]{:S(2)}) collective-permute-start(bf16[96,576]{1,0:T(8,128)(2,1)S(1)} %get-tuple-element.19.rest_1_), channel_id=1, source_target_pairs={{0,1},{1,0},{2,3},{3,2},{4,5},{5,4},{6,7},{7,6},{8,9},{9,8},{10,11... | collective-permute-start | bytes 331784 | tf_op jit(solution)/shard_map/ppermute | solution.py:274
  11.6 6.9 %collective-permute-start.10 = (bf16[256,4096]{1,0:T(8,128)(2,1)S(1)}, bf16[256,4096]{1,0:T(8,128)(2,1)S(1)}, u32[]{:S(2)}, u32[]{:S(2)}) collective-permute-start(bf16[256,4096]{1,0:T(8,128)(2,1)S(1)} %get-tuple-element.30), channel_id=1, source_target_pairs={{0,1},{1,0},{2,3},{3,2},{4,5},{5,4},{6,7},{7,6},{8,9},{9,8},{10,11... | collective-permute-start | bytes 6291464 | tf_op jit(solution)/shard_map/ppermute | solution.py:274
  12.0 5.2 %collective-permute-start.8 = (bf16[112,512]{1,0:T(8,128)(2,1)S(1)}, bf16[112,512]{1,0:T(8,128)(2,1)S(1)}, u32[]{:S(2)}, u32[]{:S(2)}) collective-permute-start(bf16[112,512]{1,0:T(8,128)(2,1)S(1)} %collective-permute-done.6.rest_7_.rest_8_), channel_id=1, source_target_pairs={{0,2},{1,3},{2,0},{3,1},{4,6},{5,7},{6,4},{7,5},{8,10},{9,11},{10,... | collective-permute-start | bytes 344072 | tf_op jit(solution)/shard_map/ppermute | solution.py:282
  12.7 4.5 %collective-permute-start.5 = (bf16[112,512]{1,0:T(8,128)(2,1)S(1)}, bf16[112,512]{1,0:T(8,128)(2,1)S(1)}, u32[]{:S(2)}, u32[]{:S(2)}) collective-permute-start(bf16[112,512]{1,0:T(8,128)(2,1)S(1)} %collective-permute-done.4.rest_6_), channel_id=1, source_target_pairs={{0,1},{1,0},{2,3},{3,2},{4,5},{5,4},{6,7},{7,6},{8,9},{9,8},{10,11... | collective-permute-start | bytes 344072 | tf_op jit(solution)/shard_map/ppermute | solution.py:274
  12.7 4.5 %collective-permute-start.3 = (bf16[112,512]{1,0:T(8,128)(2,1)S(1)}, bf16[112,512]{1,0:T(8,128)(2,1)S(1)}, u32[]{:S(2)}, u32[]{:S(2)}) collective-permute-start(bf16[112,512]{1,0:T(8,128)(2,1)S(1)} %collective-permute-done.2.rest_5_), channel_id=1, source_target_pairs={{0,1},{1,0},{2,3},{3,2},{4,5},{5,4},{6,7},{7,6},{8,9},{9,8},{10,11... | collective-permute-start | bytes 344072 | tf_op jit(solution)/shard_map/ppermute | solution.py:274
  14.0 4.5 %copy-start = (bf16[256,7168]{1,0:T(8,128)(2,1)S(1)}, bf16[256,7168]{1,0:T(8,128)(2,1)}, u32[]{:S(2)}) copy-start(bf16[256,7168]{1,0:T(8,128)(2,1)} %rest_10_.1) | copy-start | bytes 11010052
  14.1 4.5 %copy-start.1 = (bf16[512,256]{1,0:T(8,128)(2,1)S(1)}, bf16[512,256]{1,0:T(8,128)(2,1)}, u32[]{:S(2)}) copy-start(bf16[512,256]{1,0:T(8,128)(2,1)} %rest_9_.1) | copy-start | bytes 786436
  14.1 3.1 %collective-permute-start.7 = (bf16[112,512]{1,0:T(8,128)(2,1)S(1)}, bf16[112,512]{1,0:T(8,128)(2,1)S(1)}, u32[]{:S(2)}, u32[]{:S(2)}) collective-permute-start(bf16[112,512]{1,0:T(8,128)(2,1)S(1)} %get-tuple-element.22), channel_id=1, source_target_pairs={{0,1},{1,0},{2,3},{3,2},{4,5},{5,4},{6,7},{7,6},{8,9},{9,8},{10,11... | collective-permute-start | bytes 344072 | tf_op jit(solution)/shard_map/ppermute | solution.py:274
  17.2 1.3 %collective-permute-start.9 = (bf16[112,512]{1,0:T(8,128)(2,1)S(1)}, bf16[112,512]{1,0:T(8,128)(2,1)S(1)}, u32[]{:S(2)}, u32[]{:S(2)}) collective-permute-start(bf16[112,512]{1,0:T(8,128)(2,1)S(1)} %collective-permute-done.8.rest_10_), channel_id=1, source_target_pairs={{0,1},{1,0},{2,3},{3,2},{4,5},{5,4},{6,7},{7,6},{8,9},{9,8},{10,11... | collective-permute-start | bytes 344072 | tf_op jit(solution)/shard_map/ppermute | solution.py:274

commit v11 on v10

--- a/solution.py
+++ b/solution.py
@@ -338,7 +338,7 @@
     if direct:
         far = partners(packed, FAR)
         near = partners(packed, NEAR)
-        corner = partners(packed, CORNER, cores=(1,))
+        corner = partners(near, (2, 2), cores=(1,))
         relayed = partners(far, (1, 1))
         *running, far_after = attend(
             "first", FIRST_COST, both, biases[0], [packed, near], passed=[far]

time: 21.2 us -> 21 us (level)
  waiting for transfers between devices: 4.14 us -> 2.71 us
  starting transfers between devices: 9.63 us -> 10.9 us
    ppermute x4, waiting for transfers between devices: 3.04 us -> 1.75 us  [partners(): return lax.ppermute(array, ('ctx', 'heads'), pairs)]
    ppermute x4, starting transfers between devices: 7.01 us -> 7.78 us  [partners(): return lax.ppermute(array, ('ctx', 'heads'), pairs)]
    ppermute x7, starting transfers between devices: 2.62 us -> 3.13 us  [other_core(): return lax.ppermute(array, 'heads', [(0, 1), (1, 0)])]
  transfers between devices with their start and end apart: 11 -> 11, of which waited for: 3 -> 2; matrix products, arithmetic and copies ran while one was open for 0% -> 0% of each run, Pallas kernels for 17% -> 17%
where the time goes in v11:
time: 21 us; the launch traced here: 20.9 us
  starting transfers between devices  10.9 us (52%)
  Pallas kernels  7.12 us (34%)
  waiting for transfers between devices  2.71 us (13%)
    ppermute x4, starting transfers between devices, partners(): return lax.ppermute(array, ('ctx', 'heads'), pairs)  7.78 us
    ppermute x7, starting transfers between devices, other_core(): return lax.ppermute(array, 'heads', [(0, 1), (1, 0)])  3.13 us
    pallas_call x1, Pallas kernels, per_device(): pl.pallas_call(functools.partial(finish_kernel, heads, len(last)), out_sh...  2.47 us
    pallas_call x2, Pallas kernels, attend(): pl.pallas_call(functools.partial(chunks_kernel, heads, len(chunks), len(o...  1.84 us
    pallas_call x1, Pallas kernels, per_device(): pl.pallas_call(functools.partial(prepare_kernel, order), out_shape=[jax.S...  1.76 us
    ppermute x4, waiting for transfers between devices, partners(): return lax.ppermute(array, ('ctx', 'heads'), pairs)  1.75 us
    pallas_call x1, Pallas kernels, per_device(): pl.pallas_call(pack_kernel, out_shape=jax.ShapeDtypeStruct((rows + rows /...  1.05 us
    ppermute x7, waiting for transfers between devices, other_core(): return lax.ppermute(array, 'heads', [(0, 1), (1, 0)])  0.96 us
  transfers between devices with their start and end apart: 11, of which 2 were waited for; matrix products, arithmetic and copies ran while one was open for 0% of the time, Pallas kernels for 17%

profile of v11, /device:TPU:0, one launch (start us, length us, event | category | flops | bytes accessed | tf_op | source)
XLA Modules:
  0.0 20.9 jit_solution(8449223569513539992)
XLA Ops:
  0.0 1.0 %pack.1.refs_6_.rest_5_ = bf16[112,512]{1,0:T(8,128)(2,1)S(1)} custom-call(bf16[96,512]{1,0:T(8,128)(2,1)} %latent.1, bf16[64,96]{1,0:T(8,128)(2,1)} %bitcast.1), custom_call_target="tpu_custom_call" | custom-call | tf_op jit(solution)/shard_map/pack/pallas_call | solution.py:297
  1.0 4.1 %collective-permute-start.6 = (bf16[112,512]{1,0:T(8,128)(2,1)S(1)}, bf16[112,512]{1,0:T(8,128)(2,1)S(1)}, u32[]{:S(2)}, u32[]{:S(2)}) collective-permute-start(bf16[112,512]{1,0:T(8,128)(2,1)S(1)} %pack.1.refs_6_.rest_5_), channel_id=1, source_target_pairs={{0,8},{1,13},{2,10},{3,15},{4,12},{5,9},{6,14},{7,11},{8,0},{9,5},... | collective-permute-start | bytes 344072 | tf_op jit(solution)/shard_map/ppermute | solution.py:282
  5.1 1.6 %collective-permute-start.2 = (bf16[112,512]{1,0:T(8,128)(2,1)S(1)}, bf16[112,512]{1,0:T(8,128)(2,1)S(1)}, u32[]{:S(2)}, u32[]{:S(2)}) collective-permute-start(bf16[112,512]{1,0:T(8,128)(2,1)S(1)} %pack.1.refs_6_.rest_5_), channel_id=1, source_target_pairs={{0,4},{1,3},{2,6},{3,1},{4,0},{5,7},{6,2},{7,5},{8,12},{9,11},{10,... | collective-permute-start | bytes 344072 | tf_op jit(solution)/shard_map/ppermute | solution.py:282
  6.7 1.8 %prepare.1 = (bf16[96,576]{1,0:T(8,128)(2,1)S(1)}, bf16[96,576]{1,0:T(8,128)(2,1)S(1)}, f32[1,96,192]{2,1,0:T(8,128)S(1)}, f32[1,96,480]{2,1,0:T(8,128)S(1)}, f3...) custom-call(bf16[96,256]{1,0:T(8,128)(2,1)} %refs_0_.1, bf16[96,128]{1,0:T(8,128)(2,1)} %refs_1_.1, ...), custom_call_target="tpu_custom_call" | custom-call | tf_op jit(solution)/shard_map/prepare/pallas_call | solution.py:315
  8.4 0.3 %collective-permute-start = (bf16[96,576]{1,0:T(8,128)(2,1)S(1)}, bf16[96,576]{1,0:T(8,128)(2,1)S(1)}, u32[]{:S(2)}, u32[]{:S(2)}) collective-permute-start(bf16[96,576]{1,0:T(8,128)(2,1)S(1)} %get-tuple-element.18.rest_0_), channel_id=1, source_target_pairs={{0,1},{1,0},{2,3},{3,2},{4,5},{5,4},{6,7},{7,6},{8,9},{9,8},{10,11... | collective-permute-start | bytes 331784 | tf_op jit(solution)/shard_map/ppermute | solution.py:274
  8.7 0.3 %collective-permute-start.1 = (bf16[96,576]{1,0:T(8,128)(2,1)S(1)}, bf16[96,576]{1,0:T(8,128)(2,1)S(1)}, u32[]{:S(2)}, u32[]{:S(2)}) collective-permute-start(bf16[96,576]{1,0:T(8,128)(2,1)S(1)} %get-tuple-element.19.rest_1_), channel_id=1, source_target_pairs={{0,1},{1,0},{2,3},{3,2},{4,5},{5,4},{6,7},{7,6},{8,9},{9,8},{10,11... | collective-permute-start | bytes 331784 | tf_op jit(solution)/shard_map/ppermute | solution.py:274
  9.0 0.2 collective-permute-start.10
  9.2 1.7 %collective-permute-done.6.rest_7_.rest_8_ = bf16[112,512]{1,0:T(8,128)(2,1)S(1)} collective-permute-done((bf16[112,512]{1,0:T(8,128)(2,1)S(1)}, bf16[112,512]{1,0:T(8,128)(2,1)S(1)}, u32[]{:S(2)}, u32[]{:S(2)}) %collective-permute-start.6) | collective-permute-done | bytes 114720 | tf_op jit(solution)/shard_map/ppermute | solution.py:282
  11.0 1.5 %collective-permute-start.8 = (bf16[112,512]{1,0:T(8,128)(2,1)S(1)}, bf16[112,512]{1,0:T(8,128)(2,1)S(1)}, u32[]{:S(2)}, u32[]{:S(2)}) collective-permute-start(bf16[112,512]{1,0:T(8,128)(2,1)S(1)} %collective-permute-done.6.rest_7_.rest_8_), channel_id=1, source_target_pairs={{0,2},{1,3},{2,0},{3,1},{4,6},{5,7},{6,4},{7,5},{8,10},{9,11},{10,... | collective-permute-start | bytes 344072 | tf_op jit(solution)/shard_map/ppermute | solution.py:282
  12.5 0.0 collective-permute-done.2.rest_6_
  12.5 0.7 %collective-permute-start.3 = (bf16[112,512]{1,0:T(8,128)(2,1)S(1)}, bf16[112,512]{1,0:T(8,128)(2,1)S(1)}, u32[]{:S(2)}, u32[]{:S(2)}) collective-permute-start(bf16[112,512]{1,0:T(8,128)(2,1)S(1)} %collective-permute-done.2.rest_6_), channel_id=1, source_target_pairs={{1,5},{3,7},{5,1},{7,3},{9,13},{11,15},{13,9},{15,11},{17,21},{19,... | collective-permute-start | bytes 344072 | tf_op jit(solution)/shard_map/ppermute | solution.py:282
  13.1 0.0 collective-permute-done.rest_2_
  13.1 0.0 collective-permute-done.1.rest_3_
  13.2 0.7 %first.1 = (f32[384,1]{1,0:T(8,128)S(1)}, f32[384,1]{1,0:T(8,128)S(1)}, f32[384,512]{1,0:T(8,128)S(1)}, bf16[112,512]{1,0:T(8,128)(2,1)S(1)}) custom-call(bf16[96,576]{1,0:T(8,128)(2,1)S(1)} %get-tuple-element.18.rest_0_, bf16[96,576]{1,0:T(8,128)(2,1)S(1)} %get-tuple-element.19.rest_1_, bf16[96,576]{1,0:T(8,128)(2,1)S(1)} %collective-permute-done.rest_2_, ...), custom_call_target="tpu_custom_call" | custom-call | flops 22000001024 | tf_op jit(solution)/shard_map/first/pallas_call | solution.py:285
  13.9 0.0 copy-start
  13.9 0.0 copy-start.1
  13.9 0.1 collective-permute-start.7
  14.0 0.5 %collective-permute-start.5 = (bf16[112,512]{1,0:T(8,128)(2,1)S(1)}, bf16[112,512]{1,0:T(8,128)(2,1)S(1)}, u32[]{:S(2)}, u32[]{:S(2)}) collective-permute-start(bf16[112,512]{1,0:T(8,128)(2,1)S(1)} %collective-permute-done.2.rest_6_), channel_id=1, source_target_pairs={{0,1},{1,0},{2,3},{3,2},{4,5},{5,4},{6,7},{7,6},{8,9},{9,8},{10,11... | collective-permute-start | bytes 344072 | tf_op jit(solution)/shard_map/ppermute | solution.py:274
  14.5 0.0 collective-permute-done.3.rest_5_
  14.5 1.8 %collective-permute-start.4 = (bf16[112,512]{1,0:T(8,128)(2,1)S(1)}, bf16[112,512]{1,0:T(8,128)(2,1)S(1)}, u32[]{:S(2)}, u32[]{:S(2)}) collective-permute-start(bf16[112,512]{1,0:T(8,128)(2,1)S(1)} %collective-permute-done.3.rest_5_), channel_id=1, source_target_pairs={{0,1},{1,0},{2,3},{3,2},{4,5},{5,4},{6,7},{7,6},{8,9},{9,8},{10,11... | collective-permute-start | bytes 344072 | tf_op jit(solution)/shard_map/ppermute | solution.py:274
  16.3 0.0 collective-permute-done.8.rest_10_
  16.3 0.0 collective-permute-start.9
  16.3 0.0 collective-permute-done.5.rest_7_
  16.3 0.0 collective-permute-done.7.rest_9_
  16.3 0.9 %collective-permute-done.4.rest_6_ = bf16[112,512]{1,0:T(8,128)(2,1)S(1)} collective-permute-done((bf16[112,512]{1,0:T(8,128)(2,1)S(1)}, bf16[112,512]{1,0:T(8,128)(2,1)S(1)}, u32[]{:S(2)}, u32[]{:S(2)}) %collective-permute-start.4) | collective-permute-done | bytes 114720 | tf_op jit(solution)/shard_map/ppermute | solution.py:274
  17.2 1.1 %second.1 = (f32[384,1]{1,0:T(8,128)S(1)}, f32[384,1]{1,0:T(8,128)S(1)}, f32[384,512]{1,0:T(8,128)S(1)}) custom-call(bf16[96,576]{1,0:T(8,128)(2,1)S(1)} %get-tuple-element.18.rest_0_, bf16[96,576]{1,0:T(8,128)(2,1)S(1)} %get-tuple-element.19.rest_1_, bf16[96,576]{1,0:T(8,128)(2,1)S(1)} %collective-permute-done.rest_2_, ...), custom_call_target="tpu_custom_call" | custom-call | flops 1100000000 | tf_op jit(solution)/shard_map/second/pallas_call | solution.py:285
  18.3 0.0 collective-permute-done.9.rest_8_
  18.4 0.0 collective-permute-done.10.rest_11_
  18.4 0.0 copy-done
  18.4 0.0 copy-done.1
  18.4 2.5 %finish.1 = bf16[96,3584]{1,0:T(8,128)(2,1)} custom-call(bf16[96,576]{1,0:T(8,128)(2,1)S(1)} %get-tuple-element.18.rest_0_, bf16[96,576]{1,0:T(8,128)(2,1)S(1)} %get-tuple-element.19.rest_1_, bf16[96,576]{1,0:T(8,128)(2,1)S(1)} %collective-permute-done.rest_2_, bf16[96,576]{1,0:T(8,128)(2,1)S(1)} %collective-permute-done.1.rest_3_, ...), custom_call_target="tpu_custom_call" | custom-call | tf_op jit(solution)/shard_map/finish/pallas_call | solution.py:369
Async XLA Ops:
  1.0 9.9 %collective-permute-start.6 = (bf16[112,512]{1,0:T(8,128)(2,1)S(1)}, bf16[112,512]{1,0:T(8,128)(2,1)S(1)}, u32[]{:S(2)}, u32[]{:S(2)}) collective-permute-start(bf16[112,512]{1,0:T(8,128)(2,1)S(1)} %pack.1.refs_6_.rest_5_), channel_id=1, source_target_pairs={{0,8},{1,13},{2,10},{3,15},{4,12},{5,9},{6,14},{7,11},{8,0},{9,5},... | collective-permute-start | bytes 344072 | tf_op jit(solution)/shard_map/ppermute | solution.py:282
  5.1 7.4 %collective-permute-start.2 = (bf16[112,512]{1,0:T(8,128)(2,1)S(1)}, bf16[112,512]{1,0:T(8,128)(2,1)S(1)}, u32[]{:S(2)}, u32[]{:S(2)}) collective-permute-start(bf16[112,512]{1,0:T(8,128)(2,1)S(1)} %pack.1.refs_6_.rest_5_), channel_id=1, source_target_pairs={{0,4},{1,3},{2,6},{3,1},{4,0},{5,7},{6,2},{7,5},{8,12},{9,11},{10,... | collective-permute-start | bytes 344072 | tf_op jit(solution)/shard_map/ppermute | solution.py:282
  8.4 4.7 %collective-permute-start = (bf16[96,576]{1,0:T(8,128)(2,1)S(1)}, bf16[96,576]{1,0:T(8,128)(2,1)S(1)}, u32[]{:S(2)}, u32[]{:S(2)}) collective-permute-start(bf16[96,576]{1,0:T(8,128)(2,1)S(1)} %get-tuple-element.18.rest_0_), channel_id=1, source_target_pairs={{0,1},{1,0},{2,3},{3,2},{4,5},{5,4},{6,7},{7,6},{8,9},{9,8},{10,11... | collective-permute-start | bytes 331784 | tf_op jit(solution)/shard_map/ppermute | solution.py:274
  8.7 4.4 %collective-permute-start.1 = (bf16[96,576]{1,0:T(8,128)(2,1)S(1)}, bf16[96,576]{1,0:T(8,128)(2,1)S(1)}, u32[]{:S(2)}, u32[]{:S(2)}) collective-permute-start(bf16[96,576]{1,0:T(8,128)(2,1)S(1)} %get-tuple-element.19.rest_1_), channel_id=1, source_target_pairs={{0,1},{1,0},{2,3},{3,2},{4,5},{5,4},{6,7},{7,6},{8,9},{9,8},{10,11... | collective-permute-start | bytes 331784 | tf_op jit(solution)/shard_map/ppermute | solution.py:274
  9.0 9.3 %collective-permute-start.10 = (bf16[256,4096]{1,0:T(8,128)(2,1)S(1)}, bf16[256,4096]{1,0:T(8,128)(2,1)S(1)}, u32[]{:S(2)}, u32[]{:S(2)}) collective-permute-start(bf16[256,4096]{1,0:T(8,128)(2,1)S(1)} %get-tuple-element.30), channel_id=1, source_target_pairs={{0,1},{1,0},{2,3},{3,2},{4,5},{5,4},{6,7},{7,6},{8,9},{9,8},{10,11... | collective-permute-start | bytes 6291464 | tf_op jit(solution)/shard_map/ppermute | solution.py:274
  11.0 5.3 %collective-permute-start.8 = (bf16[112,512]{1,0:T(8,128)(2,1)S(1)}, bf16[112,512]{1,0:T(8,128)(2,1)S(1)}, u32[]{:S(2)}, u32[]{:S(2)}) collective-permute-start(bf16[112,512]{1,0:T(8,128)(2,1)S(1)} %collective-permute-done.6.rest_7_.rest_8_), channel_id=1, source_target_pairs={{0,2},{1,3},{2,0},{3,1},{4,6},{5,7},{6,4},{7,5},{8,10},{9,11},{10,... | collective-permute-start | bytes 344072 | tf_op jit(solution)/shard_map/ppermute | solution.py:282
  12.5 2.0 %collective-permute-start.3 = (bf16[112,512]{1,0:T(8,128)(2,1)S(1)}, bf16[112,512]{1,0:T(8,128)(2,1)S(1)}, u32[]{:S(2)}, u32[]{:S(2)}) collective-permute-start(bf16[112,512]{1,0:T(8,128)(2,1)S(1)} %collective-permute-done.2.rest_6_), channel_id=1, source_target_pairs={{1,5},{3,7},{5,1},{7,3},{9,13},{11,15},{13,9},{15,11},{17,21},{19,... | collective-permute-start | bytes 344072 | tf_op jit(solution)/shard_map/ppermute | solution.py:282
  13.9 4.5 %copy-start = (bf16[256,7168]{1,0:T(8,128)(2,1)S(1)}, bf16[256,7168]{1,0:T(8,128)(2,1)}, u32[]{:S(2)}) copy-start(bf16[256,7168]{1,0:T(8,128)(2,1)} %rest_10_.1) | copy-start | bytes 11010052
  13.9 4.5 %copy-start.1 = (bf16[512,256]{1,0:T(8,128)(2,1)S(1)}, bf16[512,256]{1,0:T(8,128)(2,1)}, u32[]{:S(2)}) copy-start(bf16[512,256]{1,0:T(8,128)(2,1)} %rest_9_.1) | copy-start | bytes 786436
  13.9 2.4 %collective-permute-start.7 = (bf16[112,512]{1,0:T(8,128)(2,1)S(1)}, bf16[112,512]{1,0:T(8,128)(2,1)S(1)}, u32[]{:S(2)}, u32[]{:S(2)}) collective-permute-start(bf16[112,512]{1,0:T(8,128)(2,1)S(1)} %get-tuple-element.22), channel_id=1, source_target_pairs={{0,1},{1,0},{2,3},{3,2},{4,5},{5,4},{6,7},{7,6},{8,9},{9,8},{10,11... | collective-permute-start | bytes 344072 | tf_op jit(solution)/shard_map/ppermute | solution.py:274
  14.0 2.3 %collective-permute-start.5 = (bf16[112,512]{1,0:T(8,128)(2,1)S(1)}, bf16[112,512]{1,0:T(8,128)(2,1)S(1)}, u32[]{:S(2)}, u32[]{:S(2)}) collective-permute-start(bf16[112,512]{1,0:T(8,128)(2,1)S(1)} %collective-permute-done.2.rest_6_), channel_id=1, source_target_pairs={{0,1},{1,0},{2,3},{3,2},{4,5},{5,4},{6,7},{7,6},{8,9},{9,8},{10,11... | collective-permute-start | bytes 344072 | tf_op jit(solution)/shard_map/ppermute | solution.py:274
  14.5 2.7 %collective-permute-start.4 = (bf16[112,512]{1,0:T(8,128)(2,1)S(1)}, bf16[112,512]{1,0:T(8,128)(2,1)S(1)}, u32[]{:S(2)}, u32[]{:S(2)}) collective-permute-start(bf16[112,512]{1,0:T(8,128)(2,1)S(1)} %collective-permute-done.3.rest_5_), channel_id=1, source_target_pairs={{0,1},{1,0},{2,3},{3,2},{4,5},{5,4},{6,7},{7,6},{8,9},{9,8},{10,11... | collective-permute-start | bytes 344072 | tf_op jit(solution)/shard_map/ppermute | solution.py:274
  16.3 2.1 %collective-permute-start.9 = (bf16[112,512]{1,0:T(8,128)(2,1)S(1)}, bf16[112,512]{1,0:T(8,128)(2,1)S(1)}, u32[]{:S(2)}, u32[]{:S(2)}) collective-permute-start(bf16[112,512]{1,0:T(8,128)(2,1)S(1)} %collective-permute-done.8.rest_10_), channel_id=1, source_target_pairs={{0,1},{1,0},{2,3},{3,2},{4,5},{5,4},{6,7},{7,6},{8,9},{9,8},{10,11... | collective-permute-start | bytes 344072 | tf_op jit(solution)/shard_map/ppermute | solution.py:274

commit v12 on v11

--- a/solution.py
+++ b/solution.py
@@ -63,9 +63,9 @@
 
 
 def prepare_kernel(order, *refs):
-    sources, out_proj, rest = refs[:5], refs[5], refs[7:]
+    sources, (out_proj, packed), rest = refs[:5], refs[5:7], refs[7:]
     outs, copied, sems = rest[:-6], rest[-6:-1], rest[-1]
-    weights = outs[-1]
+    weights, packed_after = outs[-2:]
     depth, width = out_proj.shape[0], out_proj.shape[1] // 2
     fetches = [
         pltpu.make_async_copy(source, target, sems.at[index])
@@ -79,6 +79,7 @@
     )
     for fetch in fetches:
         fetch.start()
+    packed_after[...] = packed[...]
     nope, rope, up, span_order, value_up = copied
     rows = nope.shape[0]
     heads = nope.shape[1] // DH
@@ -96,7 +97,7 @@
         )
         outs[head][:, :DC] = latent.astype(BF16)
         outs[head][:, DC:] = rope[:, head * DR : (head + 1) * DR]
-    biases = outs[heads:-1]
+    biases = outs[heads:-2]
     fetches[3].wait()
     row = lax.broadcasted_iota(jnp.int32, (rows, 1), 0)
     query_pos = jnp.where(
@@ -316,9 +317,12 @@
         functools.partial(prepare_kernel, order),
         out_shape=[jax.ShapeDtypeStruct((rows, DC + DR), BF16)] * (heads // 2)
         + [jax.ShapeDtypeStruct(shape, F32) for shape in bias_shapes]
-        + [jax.ShapeDtypeStruct((depth, width + DC // depth * key_up.shape[1]), BF16)],
-        in_specs=[hbm()] * 6 + [anywhere()],
-        out_specs=[vmem()] * (heads // 2 + len(bias_shapes) + 1),
+        + [
+            jax.ShapeDtypeStruct((depth, width + DC // depth * key_up.shape[1]), BF16),
+            jax.ShapeDtypeStruct(packed.shape, BF16),
+        ],
+        in_specs=[hbm()] * 6 + [vmem()],
+        out_specs=[vmem()] * (heads // 2 + len(bias_shapes) + 2),
         scratch_shapes=[
             pltpu.VMEM(queries_nope.shape, BF16),
             pltpu.VMEM(queries_rope.shape, BF16),
@@ -331,14 +335,15 @@
         cost_estimate=cost(PREPARE_COST),
         name="prepare",
     )(*in_hbm(queries_nope, queries_rope, key_up, span_order, value_up, out_proj), packed)
-    queries, biases = outs[: heads // 2], outs[heads // 2 : -1]
-    weights_other = other_core(outs[-1])
+    queries, biases = outs[: heads // 2], outs[heads // 2 : -2]
+    weights, packed_after = outs[-2:]
+    weights_other = other_core(weights)
     both = [*queries, *map(other_core, queries)]
 
     if direct:
         far = partners(packed, FAR)
         near = partners(packed, NEAR)
-        corner = partners(near, (2, 2), cores=(1,))
+        corner = partners(packed_after, CORNER, cores=(1,))
         relayed = partners(far, (1, 1))
         *running, far_after = attend(
             "first", FIRST_COST, both, biases[0], [packed, near], passed=[far]

time: 21 us -> 21.7 us (1.033)
  starting transfers between devices: 10.9 us -> 11.5 us
    ppermute x7, starting transfers between devices: 3.13 us -> 4.46 us  [other_core(): return lax.ppermute(array, 'heads', [(0, 1), (1, 0)])]
    ppermute x4, starting transfers between devices: 7.78 us -> 7.02 us  [partners(): return lax.ppermute(array, ('ctx', 'heads'), pairs)]
  transfers between devices with their start and end apart: 11 -> 11, of which waited for: 2 -> 3; matrix products, arithmetic and copies ran while one was open for 0% -> 0% of each run, Pallas kernels for 17% -> 17%
where the time goes in v12:
time: 21.7 us; the launch traced here: 21.5 us
  starting transfers between devices  11.5 us (53%)
  Pallas kernels  7.13 us (33%)
  waiting for transfers between devices  2.84 us (13%)
    ppermute x4, starting transfers between devices, partners(): return lax.ppermute(array, ('ctx', 'heads'), pairs)  7.02 us
    ppermute x7, starting transfers between devices, other_core(): return lax.ppermute(array, 'heads', [(0, 1), (1, 0)])  4.46 us
    pallas_call x1, Pallas kernels, per_device(): pl.pallas_call(functools.partial(finish_kernel, heads, len(last)), out_sh...  2.47 us
    pallas_call x2, Pallas kernels, attend(): pl.pallas_call(functools.partial(chunks_kernel, heads, len(chunks), len(o...  1.85 us
    pallas_call x1, Pallas kernels, per_device(): pl.pallas_call(functools.partial(prepare_kernel, order), out_shape=[jax.S...  1.77 us
    ppermute x4, waiting for transfers between devices, partners(): return lax.ppermute(array, ('ctx', 'heads'), pairs)  1.74 us
    ppermute x7, waiting for transfers between devices, other_core(): return lax.ppermute(array, 'heads', [(0, 1), (1, 0)])  1.1 us
    pallas_call x1, Pallas kernels, per_device(): pl.pallas_call(pack_kernel, out_shape=jax.ShapeDtypeStruct((rows + rows /...  1.05 us
  transfers between devices with their start and end apart: 11, of which 3 were waited for; matrix products, arithmetic and copies ran while one was open for 0% of the time, Pallas kernels for 17%

profile of v12, /device:TPU:0, one launch (start us, length us, event | category | flops | bytes accessed | tf_op | source)
XLA Modules:
  0.0 21.5 jit_solution(6544767949745062740)
XLA Ops:
  0.0 1.0 %pack.1.refs_6_.rest_5_ = bf16[112,512]{1,0:T(8,128)(2,1)S(1)} custom-call(bf16[96,512]{1,0:T(8,128)(2,1)} %latent.1, bf16[64,96]{1,0:T(8,128)(2,1)} %bitcast.1), custom_call_target="tpu_custom_call" | custom-call | tf_op jit(solution)/shard_map/pack/pallas_call | solution.py:298
  1.0 4.1 %collective-permute-start.6 = (bf16[112,512]{1,0:T(8,128)(2,1)S(1)}, bf16[112,512]{1,0:T(8,128)(2,1)S(1)}, u32[]{:S(2)}, u32[]{:S(2)}) collective-permute-start(bf16[112,512]{1,0:T(8,128)(2,1)S(1)} %pack.1.refs_6_.rest_5_), channel_id=1, source_target_pairs={{0,8},{1,13},{2,10},{3,15},{4,12},{5,9},{6,14},{7,11},{8,0},{9,5},... | collective-permute-start | bytes 344072 | tf_op jit(solution)/shard_map/ppermute | solution.py:283
  5.1 1.6 %collective-permute-start.4 = (bf16[112,512]{1,0:T(8,128)(2,1)S(1)}, bf16[112,512]{1,0:T(8,128)(2,1)S(1)}, u32[]{:S(2)}, u32[]{:S(2)}) collective-permute-start(bf16[112,512]{1,0:T(8,128)(2,1)S(1)} %pack.1.refs_6_.rest_5_), channel_id=1, source_target_pairs={{0,4},{1,3},{2,6},{3,1},{4,0},{5,7},{6,2},{7,5},{8,12},{9,11},{10,... | collective-permute-start | bytes 344072 | tf_op jit(solution)/shard_map/ppermute | solution.py:283
  6.7 1.8 %prepare.1 = (bf16[96,576]{1,0:T(8,128)(2,1)S(1)}, bf16[96,576]{1,0:T(8,128)(2,1)S(1)}, f32[1,96,192]{2,1,0:T(8,128)S(1)}, f32[1,96,480]{2,1,0:T(8,128)S(1)}, f3...) custom-call(bf16[96,256]{1,0:T(8,128)(2,1)} %refs_0_.1, ...), custom_call_target="tpu_custom_call" | custom-call | tf_op jit(solution)/shard_map/prepare/pallas_call | solution.py:316
  8.5 0.7 %collective-permute-start.2 = (bf16[112,512]{1,0:T(8,128)(2,1)S(1)}, bf16[112,512]{1,0:T(8,128)(2,1)S(1)}, u32[]{:S(2)}, u32[]{:S(2)}) collective-permute-start(bf16[112,512]{1,0:T(8,128)(2,1)S(1)} %get-tuple-element.22), channel_id=1, source_target_pairs={{1,7},{3,5},{5,3},{7,1},{9,15},{11,13},{13,11},{15,9},{17,23},{19,... | collective-permute-start | bytes 344072 | tf_op jit(solution)/shard_map/ppermute | solution.py:283
  9.1 1.5 %collective-permute-start = (bf16[96,576]{1,0:T(8,128)(2,1)S(1)}, bf16[96,576]{1,0:T(8,128)(2,1)S(1)}, u32[]{:S(2)}, u32[]{:S(2)}) collective-permute-start(bf16[96,576]{1,0:T(8,128)(2,1)S(1)} %get-tuple-element.19.rest_0_), channel_id=1, source_target_pairs={{0,1},{1,0},{2,3},{3,2},{4,5},{5,4},{6,7},{7,6},{8,9},{9,8},{10,11... | collective-permute-start | bytes 331784 | tf_op jit(solution)/shard_map/ppermute | solution.py:275
  10.6 0.1 collective-permute-start.1
  10.7 0.9 %collective-permute-done.rest_2_ = bf16[96,576]{1,0:T(8,128)(2,1)S(1)} collective-permute-done((bf16[96,576]{1,0:T(8,128)(2,1)S(1)}, bf16[96,576]{1,0:T(8,128)(2,1)S(1)}, u32[]{:S(2)}, u32[]{:S(2)}) %collective-permute-start) | collective-permute-done | bytes 110624 | tf_op jit(solution)/shard_map/ppermute | solution.py:275
  11.6 0.4 %collective-permute-start.10 = (bf16[256,4096]{1,0:T(8,128)(2,1)S(1)}, bf16[256,4096]{1,0:T(8,128)(2,1)S(1)}, u32[]{:S(2)}, u32[]{:S(2)}) collective-permute-start(bf16[256,4096]{1,0:T(8,128)(2,1)S(1)} %get-tuple-element.32), channel_id=1, source_target_pairs={{0,1},{1,0},{2,3},{3,2},{4,5},{5,4},{6,7},{7,6},{8,9},{9,8},{10,11... | collective-permute-start | bytes 6291464 | tf_op jit(solution)/shard_map/ppermute | solution.py:275
  12.0 0.0 collective-permute-done.6.rest_7_.rest_8_
  12.0 0.7 %collective-permute-start.8 = (bf16[112,512]{1,0:T(8,128)(2,1)S(1)}, bf16[112,512]{1,0:T(8,128)(2,1)S(1)}, u32[]{:S(2)}, u32[]{:S(2)}) collective-permute-start(bf16[112,512]{1,0:T(8,128)(2,1)S(1)} %collective-permute-done.6.rest_7_.rest_8_), channel_id=1, source_target_pairs={{0,2},{1,3},{2,0},{3,1},{4,6},{5,7},{6,4},{7,5},{8,10},{9,11},{10,... | collective-permute-start | bytes 344072 | tf_op jit(solution)/shard_map/ppermute | solution.py:283
  12.7 0.0 collective-permute-done.4.rest_6_
  12.7 0.0 collective-permute-start.5
  12.7 0.0 collective-permute-done.2.rest_5_
  12.7 2.4 %collective-permute-start.3 = (bf16[112,512]{1,0:T(8,128)(2,1)S(1)}, bf16[112,512]{1,0:T(8,128)(2,1)S(1)}, u32[]{:S(2)}, u32[]{:S(2)}) collective-permute-start(bf16[112,512]{1,0:T(8,128)(2,1)S(1)} %collective-permute-done.2.rest_5_), channel_id=1, source_target_pairs={{0,1},{1,0},{2,3},{3,2},{4,5},{5,4},{6,7},{7,6},{8,9},{9,8},{10,11... | collective-permute-start | bytes 344072 | tf_op jit(solution)/shard_map/ppermute | solution.py:275
  15.1 0.0 collective-permute-done.1.rest_3_
  15.1 0.7 %first.1 = (f32[384,1]{1,0:T(8,128)S(1)}, f32[384,1]{1,0:T(8,128)S(1)}, f32[384,512]{1,0:T(8,128)S(1)}, bf16[112,512]{1,0:T(8,128)(2,1)S(1)}) custom-call(bf16[96,576]{1,0:T(8,128)(2,1)S(1)} %get-tuple-element.19.rest_0_, bf16[96,576]{1,0:T(8,128)(2,1)S(1)} %get-tuple-element.20.rest_1_, bf16[96,576]{1,0:T(8,128)(2,1)S(1)} %collective-permute-done.rest_2_, ...), custom_call_target="tpu_custom_call" | custom-call | flops 22000001024 | tf_op jit(solution)/shard_map/first/pallas_call | solution.py:286
  15.9 0.0 copy-start
  15.9 0.0 copy-start.1
  15.9 0.1 collective-permute-start.7
  16.0 1.7 %collective-permute-done.8.rest_10_ = bf16[112,512]{1,0:T(8,128)(2,1)S(1)} collective-permute-done((bf16[112,512]{1,0:T(8,128)(2,1)S(1)}, bf16[112,512]{1,0:T(8,128)(2,1)S(1)}, u32[]{:S(2)}, u32[]{:S(2)}) %collective-permute-start.8) | collective-permute-done | bytes 114720 | tf_op jit(solution)/shard_map/ppermute | solution.py:283
  17.7 0.0 collective-permute-start.9
  17.7 0.0 collective-permute-done.5.rest_7_
  17.7 0.0 collective-permute-done.3.rest_6_
  17.7 0.0 collective-permute-done.7.rest_9_
  17.7 1.1 %second.1 = (f32[384,1]{1,0:T(8,128)S(1)}, f32[384,1]{1,0:T(8,128)S(1)}, f32[384,512]{1,0:T(8,128)S(1)}) custom-call(bf16[96,576]{1,0:T(8,128)(2,1)S(1)} %get-tuple-element.19.rest_0_, bf16[96,576]{1,0:T(8,128)(2,1)S(1)} %get-tuple-element.20.rest_1_, bf16[96,576]{1,0:T(8,128)(2,1)S(1)} %collective-permute-done.rest_2_, ...), custom_call_target="tpu_custom_call" | custom-call | flops 1100000000 | tf_op jit(solution)/shard_map/second/pallas_call | solution.py:286
  18.9 0.2 collective-permute-done.9.rest_8_
  19.1 0.0 collective-permute-done.10.rest_11_
  19.1 0.0 copy-done
  19.1 0.0 copy-done.1
  19.1 2.5 %finish.1 = bf16[96,3584]{1,0:T(8,128)(2,1)} custom-call(bf16[96,576]{1,0:T(8,128)(2,1)S(1)} %get-tuple-element.19.rest_0_, bf16[96,576]{1,0:T(8,128)(2,1)S(1)} %get-tuple-element.20.rest_1_, bf16[96,576]{1,0:T(8,128)(2,1)S(1)} %collective-permute-done.rest_2_, bf16[96,576]{1,0:T(8,128)(2,1)S(1)} %collective-permute-done.1.rest_3_, ...), custom_call_target="tpu_custom_call" | custom-call | tf_op jit(solution)/shard_map/finish/pallas_call | solution.py:374
Async XLA Ops:
  1.0 10.9 %collective-permute-start.6 = (bf16[112,512]{1,0:T(8,128)(2,1)S(1)}, bf16[112,512]{1,0:T(8,128)(2,1)S(1)}, u32[]{:S(2)}, u32[]{:S(2)}) collective-permute-start(bf16[112,512]{1,0:T(8,128)(2,1)S(1)} %pack.1.refs_6_.rest_5_), channel_id=1, source_target_pairs={{0,8},{1,13},{2,10},{3,15},{4,12},{5,9},{6,14},{7,11},{8,0},{9,5},... | collective-permute-start | bytes 344072 | tf_op jit(solution)/shard_map/ppermute | solution.py:283
  5.1 7.6 %collective-permute-start.4 = (bf16[112,512]{1,0:T(8,128)(2,1)S(1)}, bf16[112,512]{1,0:T(8,128)(2,1)S(1)}, u32[]{:S(2)}, u32[]{:S(2)}) collective-permute-start(bf16[112,512]{1,0:T(8,128)(2,1)S(1)} %pack.1.refs_6_.rest_5_), channel_id=1, source_target_pairs={{0,4},{1,3},{2,6},{3,1},{4,0},{5,7},{6,2},{7,5},{8,12},{9,11},{10,... | collective-permute-start | bytes 344072 | tf_op jit(solution)/shard_map/ppermute | solution.py:283
  8.5 4.3 %collective-permute-start.2 = (bf16[112,512]{1,0:T(8,128)(2,1)S(1)}, bf16[112,512]{1,0:T(8,128)(2,1)S(1)}, u32[]{:S(2)}, u32[]{:S(2)}) collective-permute-start(bf16[112,512]{1,0:T(8,128)(2,1)S(1)} %get-tuple-element.22), channel_id=1, source_target_pairs={{1,7},{3,5},{5,3},{7,1},{9,15},{11,13},{13,11},{15,9},{17,23},{19,... | collective-permute-start | bytes 344072 | tf_op jit(solution)/shard_map/ppermute | solution.py:283
  9.1 2.5 %collective-permute-start = (bf16[96,576]{1,0:T(8,128)(2,1)S(1)}, bf16[96,576]{1,0:T(8,128)(2,1)S(1)}, u32[]{:S(2)}, u32[]{:S(2)}) collective-permute-start(bf16[96,576]{1,0:T(8,128)(2,1)S(1)} %get-tuple-element.19.rest_0_), channel_id=1, source_target_pairs={{0,1},{1,0},{2,3},{3,2},{4,5},{5,4},{6,7},{7,6},{8,9},{9,8},{10,11... | collective-permute-start | bytes 331784 | tf_op jit(solution)/shard_map/ppermute | solution.py:275
  10.6 4.5 %collective-permute-start.1 = (bf16[96,576]{1,0:T(8,128)(2,1)S(1)}, bf16[96,576]{1,0:T(8,128)(2,1)S(1)}, u32[]{:S(2)}, u32[]{:S(2)}) collective-permute-start(bf16[96,576]{1,0:T(8,128)(2,1)S(1)} %get-tuple-element.20.rest_1_), channel_id=1, source_target_pairs={{0,1},{1,0},{2,3},{3,2},{4,5},{5,4},{6,7},{7,6},{8,9},{9,8},{10,11... | collective-permute-start | bytes 331784 | tf_op jit(solution)/shard_map/ppermute | solution.py:275
  11.6 7.4 %collective-permute-start.10 = (bf16[256,4096]{1,0:T(8,128)(2,1)S(1)}, bf16[256,4096]{1,0:T(8,128)(2,1)S(1)}, u32[]{:S(2)}, u32[]{:S(2)}) collective-permute-start(bf16[256,4096]{1,0:T(8,128)(2,1)S(1)} %get-tuple-element.32), channel_id=1, source_target_pairs={{0,1},{1,0},{2,3},{3,2},{4,5},{5,4},{6,7},{7,6},{8,9},{9,8},{10,11... | collective-permute-start | bytes 6291464 | tf_op jit(solution)/shard_map/ppermute | solution.py:275
  12.0 5.7 %collective-permute-start.8 = (bf16[112,512]{1,0:T(8,128)(2,1)S(1)}, bf16[112,512]{1,0:T(8,128)(2,1)S(1)}, u32[]{:S(2)}, u32[]{:S(2)}) collective-permute-start(bf16[112,512]{1,0:T(8,128)(2,1)S(1)} %collective-permute-done.6.rest_7_.rest_8_), channel_id=1, source_target_pairs={{0,2},{1,3},{2,0},{3,1},{4,6},{5,7},{6,4},{7,5},{8,10},{9,11},{10,... | collective-permute-start | bytes 344072 | tf_op jit(solution)/shard_map/ppermute | solution.py:283
  12.7 5.0 %collective-permute-start.5 = (bf16[112,512]{1,0:T(8,128)(2,1)S(1)}, bf16[112,512]{1,0:T(8,128)(2,1)S(1)}, u32[]{:S(2)}, u32[]{:S(2)}) collective-permute-start(bf16[112,512]{1,0:T(8,128)(2,1)S(1)} %collective-permute-done.4.rest_6_), channel_id=1, source_target_pairs={{0,1},{1,0},{2,3},{3,2},{4,5},{5,4},{6,7},{7,6},{8,9},{9,8},{10,11... | collective-permute-start | bytes 344072 | tf_op jit(solution)/shard_map/ppermute | solution.py:275
  12.7 5.0 %collective-permute-start.3 = (bf16[112,512]{1,0:T(8,128)(2,1)S(1)}, bf16[112,512]{1,0:T(8,128)(2,1)S(1)}, u32[]{:S(2)}, u32[]{:S(2)}) collective-permute-start(bf16[112,512]{1,0:T(8,128)(2,1)S(1)} %collective-permute-done.2.rest_5_), channel_id=1, source_target_pairs={{0,1},{1,0},{2,3},{3,2},{4,5},{5,4},{6,7},{7,6},{8,9},{9,8},{10,11... | collective-permute-start | bytes 344072 | tf_op jit(solution)/shard_map/ppermute | solution.py:275
  15.9 3.2 %copy-start = (bf16[256,7168]{1,0:T(8,128)(2,1)S(1)}, bf16[256,7168]{1,0:T(8,128)(2,1)}, u32[]{:S(2)}) copy-start(bf16[256,7168]{1,0:T(8,128)(2,1)} %rest_10_.1) | copy-start | bytes 11010052
  15.9 3.2 %copy-start.1 = (bf16[512,256]{1,0:T(8,128)(2,1)S(1)}, bf16[512,256]{1,0:T(8,128)(2,1)}, u32[]{:S(2)}) copy-start(bf16[512,256]{1,0:T(8,128)(2,1)} %rest_9_.1) | copy-start | bytes 786436
  15.9 1.8 %collective-permute-start.7 = (bf16[112,512]{1,0:T(8,128)(2,1)S(1)}, bf16[112,512]{1,0:T(8,128)(2,1)S(1)}, u32[]{:S(2)}, u32[]{:S(2)}) collective-permute-start(bf16[112,512]{1,0:T(8,128)(2,1)S(1)} %get-tuple-element.24), channel_id=1, source_target_pairs={{0,1},{1,0},{2,3},{3,2},{4,5},{5,4},{6,7},{7,6},{8,9},{9,8},{10,11... | collective-permute-start | bytes 344072 | tf_op jit(solution)/shard_map/ppermute | solution.py:275
  17.7 1.3 %collective-permute-start.9 = (bf16[112,512]{1,0:T(8,128)(2,1)S(1)}, bf16[112,512]{1,0:T(8,128)(2,1)S(1)}, u32[]{:S(2)}, u32[]{:S(2)}) collective-permute-start(bf16[112,512]{1,0:T(8,128)(2,1)S(1)} %collective-permute-done.8.rest_10_), channel_id=1, source_target_pairs={{0,1},{1,0},{2,3},{3,2},{4,5},{5,4},{6,7},{7,6},{8,9},{9,8},{10,11... | collective-permute-start | bytes 344072 | tf_op jit(solution)/shard_map/ppermute | solution.py:275

commit v13 on v10

--- a/solution.py
+++ b/solution.py
@@ -15,7 +15,7 @@
 F32 = jnp.float32
 MASKED = -1e30
 BLOCK_CHUNKS = 8
-PREPARE_COST, FIRST_COST, SECOND_COST = 0, 20, 1
+PREPARE_COST, GATE_COST, FIRST_COST, SECOND_COST = 0, 3, 20, 1
 SMALL_VMEM = 20 * 1024 * 1024
 LARGE_VMEM = 56 * 1024 * 1024
 FAR = (4, 6)
@@ -48,6 +48,10 @@
     parts = [rope[index * group : (index + 1) * group] for index in range(6)]
     parts.append(jnp.zeros((group, DC - 6 * DR), BF16))
     out_ref[rows:] = jnp.concatenate(parts, axis=1)
+
+
+def gate_kernel(chunk, out_ref):
+    out_ref[...] = chunk[...]
 
 
 def unpack(chunk, keys, base, other=None):
@@ -94,9 +98,10 @@
             (((1,), (1,)), ((), ())),
             preferred_element_type=F32,
         )
-        outs[head][:, :DC] = latent.astype(BF16)
-        outs[head][:, DC:] = rope[:, head * DR : (head + 1) * DR]
-    biases = outs[heads:-1]
+        part = pl.ds(head * rows, rows)
+        outs[0][part, :DC] = latent.astype(BF16)
+        outs[0][part, DC:] = rope[:, head * DR : (head + 1) * DR]
+    biases = outs[1:-1]
     fetches[3].wait()
     row = lax.broadcasted_iota(jnp.int32, (rows, 1), 0)
     query_pos = jnp.where(
@@ -138,7 +143,7 @@
 
 
 def attend_block(queries, keys, bias, old):
-    copies = len(queries)
+    copies = len(queries) * queries[0].shape[0] // bias.shape[0]
     scale = math.log2(math.e) / math.sqrt(DH + DR)
     heads = jnp.concatenate([part[...] for part in queries], axis=0)
     scores = lax.dot_general(
@@ -158,8 +163,8 @@
     return top, total, added
 
 
-def chunks_kernel(heads, chunk_count, old_count, paired, *rest):
-    queries, bias, rest = rest[:heads], rest[heads], rest[heads + 1 :]
+def chunks_kernel(chunk_count, old_count, paired, *rest):
+    queries, bias, rest = rest[:2], rest[2], rest[3:]
     chunks, rest = rest[:chunk_count], rest[chunk_count:]
     old, rest = rest[:old_count], rest[old_count:]
     if len(rest) == 6:
@@ -180,9 +185,9 @@
         state[...] = value
 
 
-def gathered_kernel(heads, *rest):
-    queries, (bias, gathered) = rest[:heads], rest[heads : heads + 2]
-    running, keys = rest[heads + 2 : heads + 5], rest[heads + 5]
+def gathered_kernel(queries_own, queries_other, bias, gathered, *rest):
+    queries = (queries_own, queries_other)
+    running, keys = rest[:3], rest[3]
     blocks, rows, _ = bias.shape
 
     def fill(block):
@@ -207,7 +212,7 @@
 
 
 def finish_kernel(heads, chunk_count, *rest):
-    queries, (top, total, context), rest = rest[:heads], rest[heads : heads + 3], rest[heads + 3 :]
+    queries, (top, total, context), rest = rest[:2], rest[2:5], rest[5:]
     bias, chunks = rest[:chunk_count][:1], rest[1 : 1 + chunk_count]
     rest = rest[len(bias) + len(chunks) :]
     value_own, proj_own, weights, out_ref, out_tiles, keys, out_sems = rest
@@ -283,10 +288,10 @@
 
     def attend(name, estimate, queries, bias, chunks, old=(), passed=(), paired=False):
         return pl.pallas_call(
-            functools.partial(chunks_kernel, heads, len(chunks), len(old), paired),
+            functools.partial(chunks_kernel, len(chunks), len(old), paired),
             out_shape=[jax.ShapeDtypeStruct((query_rows, size), F32) for size in (1, 1, DC)]
             + [jax.ShapeDtypeStruct(chunk.shape, BF16) for chunk in passed],
-            in_specs=[vmem()] * (heads + 1 + len(chunks) + len(old) + len(passed)),
+            in_specs=[vmem()] * (3 + len(chunks) + len(old) + len(passed)),
             out_specs=[vmem()] * (3 + len(passed)),
             scratch_shapes=[pltpu.VMEM((bias.shape[2], DC + DR), BF16)],
             compiler_params=small,
@@ -314,11 +319,11 @@
         bias_shapes = [(count // BLOCK_CHUNKS, rows, BLOCK_CHUNKS * rows)]
     outs = pl.pallas_call(
         functools.partial(prepare_kernel, order),
-        out_shape=[jax.ShapeDtypeStruct((rows, DC + DR), BF16)] * (heads // 2)
+        out_shape=[jax.ShapeDtypeStruct((query_rows // 2, DC + DR), BF16)]
         + [jax.ShapeDtypeStruct(shape, F32) for shape in bias_shapes]
         + [jax.ShapeDtypeStruct((depth, width + DC // depth * key_up.shape[1]), BF16)],
         in_specs=[hbm()] * 6 + [anywhere()],
-        out_specs=[vmem()] * (heads // 2 + len(bias_shapes) + 1),
+        out_specs=[vmem()] * (len(bias_shapes) + 2),
         scratch_shapes=[
             pltpu.VMEM(queries_nope.shape, BF16),
             pltpu.VMEM(queries_rope.shape, BF16),
@@ -331,17 +336,26 @@
         cost_estimate=cost(PREPARE_COST),
         name="prepare",
     )(*in_hbm(queries_nope, queries_rope, key_up, span_order, value_up, out_proj), packed)
-    queries, biases = outs[: heads // 2], outs[heads // 2 : -1]
+    queries, biases = outs[0], outs[1:-1]
     weights_other = other_core(outs[-1])
-    both = [*queries, *map(other_core, queries)]
+    both = [queries, other_core(queries)]
 
     if direct:
         far = partners(packed, FAR)
         near = partners(packed, NEAR)
         corner = partners(packed, CORNER, cores=(1,))
         relayed = partners(far, (1, 1))
+        gated = pl.pallas_call(
+            gate_kernel,
+            out_shape=jax.ShapeDtypeStruct(far.shape, BF16),
+            in_specs=[vmem()],
+            out_specs=vmem(),
+            compiler_params=small,
+            cost_estimate=cost(GATE_COST),
+            name="gate",
+        )(far)
         *running, far_after = attend(
-            "first", FIRST_COST, both, biases[0], [packed, near], passed=[far]
+            "first", FIRST_COST, both, biases[0], [packed, near], passed=[gated]
         )
         last = [other_core(relayed)]
         running = attend(
@@ -356,9 +370,9 @@
     else:
         last = []
         running = pl.pallas_call(
-            functools.partial(gathered_kernel, heads),
+            gathered_kernel,
             out_shape=[jax.ShapeDtypeStruct((query_rows, size), F32) for size in (1, 1, DC)],
-            in_specs=[vmem()] * (heads + 2),
+            in_specs=[vmem()] * 4,
             out_specs=[vmem()] * 3,
             scratch_shapes=[pltpu.VMEM((BLOCK_CHUNKS * rows, DC + DR), BF16)],
             compiler_params=pltpu.CompilerParams(vmem_limit_bytes=LARGE_VMEM),
@@ -369,7 +383,7 @@
     return pl.pallas_call(
         functools.partial(finish_kernel, heads, len(last)),
         out_shape=jax.ShapeDtypeStruct((rows, width), BF16),
-        in_specs=[vmem()] * (heads + 3 + len(biases[2:]) + len(last) + 3),
+        in_specs=[vmem()] * (5 + len(biases[2:]) + len(last) + 3),
         out_specs=anywhere(),
         scratch_shapes=[
             pltpu.VMEM((rows, width), BF16),

time: 21.2 us -> 20.2 us (0.953)
  waiting for transfers between devices: 4.14 us -> 2.51 us
  starting transfers between devices: 9.63 us -> 10.3 us
    ppermute x7 -> x6, waiting for transfers between devices: 1.1 us -> 0.21 us  [other_core(): return lax.ppermute(array, 'heads', [(0, 1), (1, 0)])]
    ppermute x4, starting transfers between devices: 7.01 us -> 7.78 us  [partners(): return lax.ppermute(array, ('ctx', 'heads'), pairs)]
    ppermute x4, waiting for transfers between devices: 3.04 us -> 2.29 us  [partners(): return lax.ppermute(array, ('ctx', 'heads'), pairs)]
    ppermute x7 -> x6, starting transfers between devices: 2.62 us -> 2.5 us  [other_core(): return lax.ppermute(array, 'heads', [(0, 1), (1, 0)])]
    pallas_call x2 -> x3, Pallas kernels: 1.84 us -> 1.85 us  [the longest x2 1.84 us: attend(): pl.pallas_call(functools.partial(chunks_kernel, len(chunks), len(old), pa...]
  transfers between devices with their start and end apart: 11 -> 10, of which waited for: 3 -> 3; matrix products, arithmetic and copies ran while one was open for 0% -> 0% of each run, Pallas kernels for 17% -> 18%
where the time goes in v13:
time: 20.2 us; the launch traced here: 20 us
  starting transfers between devices  10.3 us (51%)
  Pallas kernels  7.13 us (35%)
  waiting for transfers between devices  2.51 us (12%)
    ppermute x4, starting transfers between devices, partners(): return lax.ppermute(array, ('ctx', 'heads'), pairs)  7.78 us
    ppermute x6, starting transfers between devices, other_core(): return lax.ppermute(array, 'heads', [(0, 1), (1, 0)])  2.5 us
    pallas_call x1, Pallas kernels, per_device(): pl.pallas_call(functools.partial(finish_kernel, heads, len(last)), out_sh...  2.47 us
    ppermute x4, waiting for transfers between devices, partners(): return lax.ppermute(array, ('ctx', 'heads'), pairs)  2.29 us
    pallas_call x2, Pallas kernels, attend(): pl.pallas_call(functools.partial(chunks_kernel, len(chunks), len(old), pa...  1.84 us
    pallas_call x1, Pallas kernels, per_device(): pl.pallas_call(functools.partial(prepare_kernel, order), out_shape=[jax.S...  1.77 us
    pallas_call x1, Pallas kernels, per_device(): pl.pallas_call(pack_kernel, out_shape=jax.ShapeDtypeStruct((rows + rows /...  1.05 us
  transfers between devices with their start and end apart: 10, of which 3 were waited for; matrix products, arithmetic and copies ran while one was open for 0% of the time, Pallas kernels for 18%

profile of v13, /device:TPU:0, one launch (start us, length us, event | category | flops | bytes accessed | tf_op | source)
XLA Modules:
  0.0 20.0 jit_solution(7741233331519257331)
XLA Ops:
  0.0 1.0 %pack.1.refs_6_.rest_3_ = bf16[112,512]{1,0:T(8,128)(2,1)S(1)} custom-call(bf16[96,512]{1,0:T(8,128)(2,1)} %latent.1, bf16[64,96]{1,0:T(8,128)(2,1)} %bitcast.1), custom_call_target="tpu_custom_call" | custom-call | tf_op jit(solution)/shard_map/pack/pallas_call | solution.py:302
  1.0 4.1 %collective-permute-start.5 = (bf16[112,512]{1,0:T(8,128)(2,1)S(1)}, bf16[112,512]{1,0:T(8,128)(2,1)S(1)}, u32[]{:S(2)}, u32[]{:S(2)}) collective-permute-start(bf16[112,512]{1,0:T(8,128)(2,1)S(1)} %pack.1.refs_6_.rest_3_), channel_id=1, source_target_pairs={{0,8},{1,13},{2,10},{3,15},{4,12},{5,9},{6,14},{7,11},{8,0},{9,5},... | collective-permute-start | bytes 344072 | tf_op jit(solution)/shard_map/ppermute | solution.py:287
  5.1 1.6 %collective-permute-start.3 = (bf16[112,512]{1,0:T(8,128)(2,1)S(1)}, bf16[112,512]{1,0:T(8,128)(2,1)S(1)}, u32[]{:S(2)}, u32[]{:S(2)}) collective-permute-start(bf16[112,512]{1,0:T(8,128)(2,1)S(1)} %pack.1.refs_6_.rest_3_), channel_id=1, source_target_pairs={{0,4},{1,3},{2,6},{3,1},{4,0},{5,7},{6,2},{7,5},{8,12},{9,11},{10,... | collective-permute-start | bytes 344072 | tf_op jit(solution)/shard_map/ppermute | solution.py:287
  6.7 0.7 %collective-permute-start.1 = (bf16[112,512]{1,0:T(8,128)(2,1)S(1)}, bf16[112,512]{1,0:T(8,128)(2,1)S(1)}, u32[]{:S(2)}, u32[]{:S(2)}) collective-permute-start(bf16[112,512]{1,0:T(8,128)(2,1)S(1)} %pack.1.refs_6_.rest_3_), channel_id=1, source_target_pairs={{1,7},{3,5},{5,3},{7,1},{9,15},{11,13},{13,11},{15,9},{17,23},{19,... | collective-permute-start | bytes 344072 | tf_op jit(solution)/shard_map/ppermute | solution.py:287
  7.3 1.8 %prepare.1 = (bf16[192,576]{1,0:T(8,128)(2,1)S(1)}, f32[1,96,192]{2,1,0:T(8,128)S(1)}, f32[1,96,480]{2,1,0:T(8,128)S(1)}, f32[1,96,96]{2,1,0:T(8,128)S(1)}, bf16[256,4096]{1,0:T(8,128)(2,1)S(1)}) custom-call(bf16[96,256]{1,0:T(8,128)(2,1)} %refs_0_.1, bf16[96,128]{1,0:T(8,128)(2,1)} %refs_1_.1, bf16[512,256]{1,0:T(8,128)(2,1)} %refs_2_.1, s32[16]{0:T(128)} %refs_3_.1, ...), custom_call_target="tpu_custom_call" | custom-call | tf_op jit(solution)/shard_map/prepare/pallas_call | solution.py:320
  9.1 1.5 %collective-permute-start = (bf16[192,576]{1,0:T(8,128)(2,1)S(1)}, bf16[192,576]{1,0:T(8,128)(2,1)S(1)}, u32[]{:S(2)}, u32[]{:S(2)}) collective-permute-start(bf16[192,576]{1,0:T(8,128)(2,1)S(1)} %get-tuple-element.17.rest_0_), channel_id=1, source_target_pairs={{0,1},{1,0},{2,3},{3,2},{4,5},{5,4},{6,7},{7,6},{8,9},{9,8},{10,11... | collective-permute-start | bytes 663560 | tf_op jit(solution)/shard_map/ppermute | solution.py:279
  10.6 0.1 collective-permute-start.9
  10.7 0.3 %collective-permute-done.5.chunk.rest_6_ = bf16[112,512]{1,0:T(8,128)(2,1)S(1)} collective-permute-done((bf16[112,512]{1,0:T(8,128)(2,1)S(1)}, bf16[112,512]{1,0:T(8,128)(2,1)S(1)}, u32[]{:S(2)}, u32[]{:S(2)}) %collective-permute-start.5) | collective-permute-done | bytes 114720 | tf_op jit(solution)/shard_map/ppermute | solution.py:287
  11.0 1.5 %collective-permute-start.7 = (bf16[112,512]{1,0:T(8,128)(2,1)S(1)}, bf16[112,512]{1,0:T(8,128)(2,1)S(1)}, u32[]{:S(2)}, u32[]{:S(2)}) collective-permute-start(bf16[112,512]{1,0:T(8,128)(2,1)S(1)} %collective-permute-done.5.chunk.rest_6_), channel_id=1, source_target_pairs={{0,2},{1,3},{2,0},{3,1},{4,6},{5,7},{6,4},{7,5},{8,10},{9,11},{10,... | collective-permute-start | bytes 344072 | tf_op jit(solution)/shard_map/ppermute | solution.py:287
  12.5 0.0 collective-permute-done.3.rest_4_
  12.5 0.0 collective-permute-start.4
  12.5 0.0 collective-permute-done.1.rest_3_
  12.5 0.8 %collective-permute-start.2 = (bf16[112,512]{1,0:T(8,128)(2,1)S(1)}, bf16[112,512]{1,0:T(8,128)(2,1)S(1)}, u32[]{:S(2)}, u32[]{:S(2)}) collective-permute-start(bf16[112,512]{1,0:T(8,128)(2,1)S(1)} %collective-permute-done.1.rest_3_), channel_id=1, source_target_pairs={{0,1},{1,0},{2,3},{3,2},{4,5},{5,4},{6,7},{7,6},{8,9},{9,8},{10,11... | collective-permute-start | bytes 344072 | tf_op jit(solution)/shard_map/ppermute | solution.py:279
  13.3 0.0 collective-permute-done.rest_1_
  13.3 0.7 %first.1 = (f32[384,1]{1,0:T(8,128)S(1)}, f32[384,1]{1,0:T(8,128)S(1)}, f32[384,512]{1,0:T(8,128)S(1)}, bf16[112,512]{1,0:T(8,128)(2,1)S(1)}) custom-call(bf16[192,576]{1,0:T(8,128)(2,1)S(1)} %get-tuple-element.17.rest_0_, bf16[192,576]{1,0:T(8,128)(2,1)S(1)} %collective-permute-done.rest_1_, f32[1,96,192]{2,1,0:T(8,128)S(1)} %get-tuple-element.19.rest_2_, ...), custom_call_target="tpu_custom_call" | custom-call | flops 22000001024 | tf_op jit(solution)/shard_map/first/pallas_call | solution.py:290
  14.1 0.0 copy-start
  14.1 0.0 copy-start.1
  14.1 0.1 collective-permute-start.6
  14.2 2.0 %collective-permute-done.7.rest_8_ = bf16[112,512]{1,0:T(8,128)(2,1)S(1)} collective-permute-done((bf16[112,512]{1,0:T(8,128)(2,1)S(1)}, bf16[112,512]{1,0:T(8,128)(2,1)S(1)}, u32[]{:S(2)}, u32[]{:S(2)}) %collective-permute-start.7) | collective-permute-done | bytes 114720 | tf_op jit(solution)/shard_map/ppermute | solution.py:287
  16.2 0.0 collective-permute-start.8
  16.2 0.0 collective-permute-done.4.rest_5_
  16.2 0.0 collective-permute-done.2.rest_4_
  16.2 0.0 collective-permute-done.6.rest_7_
  16.2 1.1 %second.1 = (f32[384,1]{1,0:T(8,128)S(1)}, f32[384,1]{1,0:T(8,128)S(1)}, f32[384,512]{1,0:T(8,128)S(1)}) custom-call(bf16[192,576]{1,0:T(8,128)(2,1)S(1)} %get-tuple-element.17.rest_0_, bf16[192,576]{1,0:T(8,128)(2,1)S(1)} %collective-permute-done.rest_1_, f32[1,96,480]{2,1,0:T(8,128)S(1)} %get-tuple-element.18.rest_2_, ...), custom_call_target="tpu_custom_call" | custom-call | flops 1100000000 | tf_op jit(solution)/shard_map/second/pallas_call | solution.py:290
  17.3 0.2 collective-permute-done.8.rest_6_
  17.5 0.0 collective-permute-done.9.rest_9_
  17.5 0.0 copy-done
  17.5 0.0 copy-done.1
  17.5 2.5 %finish.1 = bf16[96,3584]{1,0:T(8,128)(2,1)} custom-call(bf16[192,576]{1,0:T(8,128)(2,1)S(1)} %get-tuple-element.17.rest_0_, bf16[192,576]{1,0:T(8,128)(2,1)S(1)} %collective-permute-done.rest_1_, f32[384,1]{1,0:T(8,128)S(1)} %get-tuple-element.24.rest_2_, f32[384,1]{1,0:T(8,128)S(1)} %get-tuple-element.25.rest_3_, ...), custom_call_target="tpu_custom_call" | custom-call | tf_op jit(solution)/shard_map/finish/pallas_call | solution.py:383
  (1 shorter events, 0.0 us)
Async XLA Ops:
  1.0 9.9 %collective-permute-start.5 = (bf16[112,512]{1,0:T(8,128)(2,1)S(1)}, bf16[112,512]{1,0:T(8,128)(2,1)S(1)}, u32[]{:S(2)}, u32[]{:S(2)}) collective-permute-start(bf16[112,512]{1,0:T(8,128)(2,1)S(1)} %pack.1.refs_6_.rest_3_), channel_id=1, source_target_pairs={{0,8},{1,13},{2,10},{3,15},{4,12},{5,9},{6,14},{7,11},{8,0},{9,5},... | collective-permute-start | bytes 344072 | tf_op jit(solution)/shard_map/ppermute | solution.py:287
  5.1 7.4 %collective-permute-start.3 = (bf16[112,512]{1,0:T(8,128)(2,1)S(1)}, bf16[112,512]{1,0:T(8,128)(2,1)S(1)}, u32[]{:S(2)}, u32[]{:S(2)}) collective-permute-start(bf16[112,512]{1,0:T(8,128)(2,1)S(1)} %pack.1.refs_6_.rest_3_), channel_id=1, source_target_pairs={{0,4},{1,3},{2,6},{3,1},{4,0},{5,7},{6,2},{7,5},{8,12},{9,11},{10,... | collective-permute-start | bytes 344072 | tf_op jit(solution)/shard_map/ppermute | solution.py:287
  6.7 5.8 %collective-permute-start.1 = (bf16[112,512]{1,0:T(8,128)(2,1)S(1)}, bf16[112,512]{1,0:T(8,128)(2,1)S(1)}, u32[]{:S(2)}, u32[]{:S(2)}) collective-permute-start(bf16[112,512]{1,0:T(8,128)(2,1)S(1)} %pack.1.refs_6_.rest_3_), channel_id=1, source_target_pairs={{1,7},{3,5},{5,3},{7,1},{9,15},{11,13},{13,11},{15,9},{17,23},{19,... | collective-permute-start | bytes 344072 | tf_op jit(solution)/shard_map/ppermute | solution.py:287
  9.1 4.2 %collective-permute-start = (bf16[192,576]{1,0:T(8,128)(2,1)S(1)}, bf16[192,576]{1,0:T(8,128)(2,1)S(1)}, u32[]{:S(2)}, u32[]{:S(2)}) collective-permute-start(bf16[192,576]{1,0:T(8,128)(2,1)S(1)} %get-tuple-element.17.rest_0_), channel_id=1, source_target_pairs={{0,1},{1,0},{2,3},{3,2},{4,5},{5,4},{6,7},{7,6},{8,9},{9,8},{10,11... | collective-permute-start | bytes 663560 | tf_op jit(solution)/shard_map/ppermute | solution.py:279
  10.6 6.9 %collective-permute-start.9 = (bf16[256,4096]{1,0:T(8,128)(2,1)S(1)}, bf16[256,4096]{1,0:T(8,128)(2,1)S(1)}, u32[]{:S(2)}, u32[]{:S(2)}) collective-permute-start(bf16[256,4096]{1,0:T(8,128)(2,1)S(1)} %get-tuple-element.28), channel_id=1, source_target_pairs={{0,1},{1,0},{2,3},{3,2},{4,5},{5,4},{6,7},{7,6},{8,9},{9,8},{10,11... | collective-permute-start | bytes 6291464 | tf_op jit(solution)/shard_map/ppermute | solution.py:279
  11.0 5.2 %collective-permute-start.7 = (bf16[112,512]{1,0:T(8,128)(2,1)S(1)}, bf16[112,512]{1,0:T(8,128)(2,1)S(1)}, u32[]{:S(2)}, u32[]{:S(2)}) collective-permute-start(bf16[112,512]{1,0:T(8,128)(2,1)S(1)} %collective-permute-done.5.chunk.rest_6_), channel_id=1, source_target_pairs={{0,2},{1,3},{2,0},{3,1},{4,6},{5,7},{6,4},{7,5},{8,10},{9,11},{10,... | collective-permute-start | bytes 344072 | tf_op jit(solution)/shard_map/ppermute | solution.py:287
  12.5 3.7 %collective-permute-start.4 = (bf16[112,512]{1,0:T(8,128)(2,1)S(1)}, bf16[112,512]{1,0:T(8,128)(2,1)S(1)}, u32[]{:S(2)}, u32[]{:S(2)}) collective-permute-start(bf16[112,512]{1,0:T(8,128)(2,1)S(1)} %collective-permute-done.3.rest_4_), channel_id=1, source_target_pairs={{0,1},{1,0},{2,3},{3,2},{4,5},{5,4},{6,7},{7,6},{8,9},{9,8},{10,11... | collective-permute-start | bytes 344072 | tf_op jit(solution)/shard_map/ppermute | solution.py:279
  12.5 3.7 %collective-permute-start.2 = (bf16[112,512]{1,0:T(8,128)(2,1)S(1)}, bf16[112,512]{1,0:T(8,128)(2,1)S(1)}, u32[]{:S(2)}, u32[]{:S(2)}) collective-permute-start(bf16[112,512]{1,0:T(8,128)(2,1)S(1)} %collective-permute-done.1.rest_3_), channel_id=1, source_target_pairs={{0,1},{1,0},{2,3},{3,2},{4,5},{5,4},{6,7},{7,6},{8,9},{9,8},{10,11... | collective-permute-start | bytes 344072 | tf_op jit(solution)/shard_map/ppermute | solution.py:279
  14.1 3.5 %copy-start = (bf16[256,7168]{1,0:T(8,128)(2,1)S(1)}, bf16[256,7168]{1,0:T(8,128)(2,1)}, u32[]{:S(2)}) copy-start(bf16[256,7168]{1,0:T(8,128)(2,1)} %rest_8_.1) | copy-start | bytes 11010052
  14.1 3.5 %copy-start.1 = (bf16[512,256]{1,0:T(8,128)(2,1)S(1)}, bf16[512,256]{1,0:T(8,128)(2,1)}, u32[]{:S(2)}) copy-start(bf16[512,256]{1,0:T(8,128)(2,1)} %rest_7_.1) | copy-start | bytes 786436
  14.1 2.1 %collective-permute-start.6 = (bf16[112,512]{1,0:T(8,128)(2,1)S(1)}, bf16[112,512]{1,0:T(8,128)(2,1)S(1)}, u32[]{:S(2)}, u32[]{:S(2)}) collective-permute-start(bf16[112,512]{1,0:T(8,128)(2,1)S(1)} %get-tuple-element.20), channel_id=1, source_target_pairs={{0,1},{1,0},{2,3},{3,2},{4,5},{5,4},{6,7},{7,6},{8,9},{9,8},{10,11... | collective-permute-start | bytes 344072 | tf_op jit(solution)/shard_map/ppermute | solution.py:279
  16.2 1.3 %collective-permute-start.8 = (bf16[112,512]{1,0:T(8,128)(2,1)S(1)}, bf16[112,512]{1,0:T(8,128)(2,1)S(1)}, u32[]{:S(2)}, u32[]{:S(2)}) collective-permute-start(bf16[112,512]{1,0:T(8,128)(2,1)S(1)} %collective-permute-done.7.rest_8_), channel_id=1, source_target_pairs={{0,1},{1,0},{2,3},{3,2},{4,5},{5,4},{6,7},{7,6},{8,9},{9,8},{10,11... | collective-permute-start | bytes 344072 | tf_op jit(solution)/shard_map/ppermute | solution.py:279

commit v14 on v13

--- a/solution.py
+++ b/solution.py
@@ -15,12 +15,12 @@
 F32 = jnp.float32
 MASKED = -1e30
 BLOCK_CHUNKS = 8
-PREPARE_COST, GATE_COST, FIRST_COST, SECOND_COST = 0, 3, 20, 1
+PREPARE_COST, HAND_COST, PICK_COST, FIRST_COST, SECOND_COST = 0, 3, 3, 20, 1
 SMALL_VMEM = 20 * 1024 * 1024
 LARGE_VMEM = 56 * 1024 * 1024
-FAR = (4, 6)
-NEAR = (2, 1)
-CORNER = (3, 3)
+FIRST_OUT = (4, 1)
+SECOND_OUT = (2, 3)
+LAST_OUT = (6, 6)
 RELAYED = (5, 7)
 
 
@@ -50,8 +50,12 @@
     out_ref[rows:] = jnp.concatenate(parts, axis=1)
 
 
-def gate_kernel(chunk, out_ref):
-    out_ref[...] = chunk[...]
+def hand_kernel(chunk, *refs):
+    refs[-1][...] = chunk[...]
+
+
+def pick_kernel(first, last, out_ref):
+    out_ref[...] = jnp.where(lax.axis_index("heads") == 0, first[...], last[...])
 
 
 def unpack(chunk, keys, base, other=None):
@@ -286,6 +290,17 @@
         ]
         return lax.ppermute(array, ("ctx", "heads"), pairs)
 
+    def small_kernel(name, body, estimate, *chunks):
+        return pl.pallas_call(
+            body,
+            out_shape=jax.ShapeDtypeStruct(chunks[0].shape, BF16),
+            in_specs=[vmem()] * len(chunks),
+            out_specs=vmem(),
+            compiler_params=small,
+            cost_estimate=cost(estimate),
+            name=name,
+        )(*chunks)
+
     def attend(name, estimate, queries, bias, chunks, old=(), passed=(), paired=False):
         return pl.pallas_call(
             functools.partial(chunks_kernel, len(chunks), len(old), paired),
@@ -309,8 +324,8 @@
     )(*in_hbm(latent, key_rope.T))
     if direct:
         order = [
-            [(0, 0), NEAR],
-            [CORNER, NEAR[::-1], FAR, FAR[::-1], RELAYED],
+            [(0, 0), FIRST_OUT, FIRST_OUT[::-1], SECOND_OUT, SECOND_OUT[::-1]],
+            [LAST_OUT, RELAYED],
             [RELAYED[::-1]],
         ]
         bias_shapes = [(1, rows, len(steps) * rows) for steps in order]
@@ -341,29 +356,22 @@
     both = [queries, other_core(queries)]
 
     if direct:
-        far = partners(packed, FAR)
-        near = partners(packed, NEAR)
-        corner = partners(packed, CORNER, cores=(1,))
-        relayed = partners(far, (1, 1))
-        gated = pl.pallas_call(
-            gate_kernel,
-            out_shape=jax.ShapeDtypeStruct(far.shape, BF16),
-            in_specs=[vmem()],
-            out_specs=vmem(),
-            compiler_params=small,
-            cost_estimate=cost(GATE_COST),
-            name="gate",
-        )(far)
-        *running, far_after = attend(
-            "first", FIRST_COST, both, biases[0], [packed, near], passed=[gated]
-        )
+        out_first = partners(packed, FIRST_OUT)
+        out_second = partners(packed, SECOND_OUT)
+        out_last = partners(packed, LAST_OUT, cores=(1,))
+        picked = small_kernel("pick", pick_kernel, PICK_COST, out_first, out_last)
+        out_first = small_kernel("hand_first", hand_kernel, HAND_COST, out_first)
+        out_second = small_kernel("hand_second", hand_kernel, HAND_COST, out_second, out_first)
+        relayed = partners(picked, (1, 1))
+        early = [packed, out_first, other_core(out_first), out_second, other_core(out_second)]
+        *running, last_after = attend("first", FIRST_COST, both, biases[0], early, passed=[out_last])
         last = [other_core(relayed)]
         running = attend(
             "second",
             SECOND_COST,
             both,
             biases[1],
-            [corner, other_core(corner), other_core(near), far, other_core(far_after), relayed],
+            [out_last, lax.ppermute(last_after, "heads", [(1, 0)]), relayed],
             running,
             paired=True,
         )

time: 20.2 us -> 23.3 us (1.15)
  starting transfers between devices: 10.3 us -> 13 us
  waiting for transfers between devices: 2.51 us -> 2.89 us
    ppermute x4, waiting for transfers between devices: 2.29 us -> 0.01 us  [partners(): return lax.ppermute(array, ('ctx', 'heads'), pairs)]
    ppermute x6 -> x5, waiting for transfers between devices: 0.21 us -> 2.16 us  [other_core(): return lax.ppermute(array, 'heads', [(0, 1), (1, 0)])]
    ppermute x0 -> x1, starting transfers between devices: none -> 1.56 us  [per_device(): lax.ppermute(last_after, 'heads', [(1, 0)])]
    ppermute x6 -> x5, starting transfers between devices: 2.5 us -> 3.56 us  [other_core(): return lax.ppermute(array, 'heads', [(0, 1), (1, 0)])]
    ppermute x0 -> x1, waiting for transfers between devices: none -> 0.71 us  [per_device(): lax.ppermute(last_after, 'heads', [(1, 0)])]
  transfers between devices with their start and end apart: 10 -> 10, of which waited for: 3 -> 2; matrix products, arithmetic and copies ran while one was open for 0% -> 0% of each run, Pallas kernels for 18% -> 16%
where the time goes in v14:
time: 23.3 us; the launch traced here: 23.1 us
  starting transfers between devices  13 us (56%)
  Pallas kernels  7.16 us (31%)
  waiting for transfers between devices  2.89 us (12%)
    ppermute x4, starting transfers between devices, partners(): return lax.ppermute(array, ('ctx', 'heads'), pairs)  7.84 us
    ppermute x5, starting transfers between devices, other_core(): return lax.ppermute(array, 'heads', [(0, 1), (1, 0)])  3.56 us
    pallas_call x1, Pallas kernels, per_device(): pl.pallas_call(functools.partial(finish_kernel, heads, len(last)), out_sh...  2.47 us
    ppermute x5, waiting for transfers between devices, other_core(): return lax.ppermute(array, 'heads', [(0, 1), (1, 0)])  2.16 us
    pallas_call x2, Pallas kernels, attend(): pl.pallas_call(functools.partial(chunks_kernel, len(chunks), len(old), pa...  1.84 us
    pallas_call x1, Pallas kernels, per_device(): pl.pallas_call(functools.partial(prepare_kernel, order), out_shape=[jax.S...  1.77 us
    ppermute x1, starting transfers between devices, per_device(): lax.ppermute(last_after, 'heads', [(1, 0)])  1.56 us
    pallas_call x1, Pallas kernels, per_device(): pl.pallas_call(pack_kernel, out_shape=jax.ShapeDtypeStruct((rows + rows /...  1.05 us
  transfers between devices with their start and end apart: 10, of which 2 were waited for; matrix products, arithmetic and copies ran while one was open for 0% of the time, Pallas kernels for 16%

profile of v14, /device:TPU:0, one launch (start us, length us, event | category | flops | bytes accessed | tf_op | source)
XLA Modules:
  0.0 23.1 jit_solution(10920855275753392499)
XLA Ops:
  0.0 1.0 %pack.1.refs_6_.rest_3_ = bf16[112,512]{1,0:T(8,128)(2,1)S(1)} custom-call(bf16[96,512]{1,0:T(8,128)(2,1)} %latent.1, bf16[64,96]{1,0:T(8,128)(2,1)} %bitcast.1), custom_call_target="tpu_custom_call" | custom-call | tf_op jit(solution)/shard_map/pack/pallas_call | solution.py:317
  1.0 4.1 %collective-permute-start.2 = (bf16[112,512]{1,0:T(8,128)(2,1)S(1)}, bf16[112,512]{1,0:T(8,128)(2,1)S(1)}, u32[]{:S(2)}, u32[]{:S(2)}) collective-permute-start(bf16[112,512]{1,0:T(8,128)(2,1)S(1)} %pack.1.refs_6_.rest_3_), channel_id=1, source_target_pairs={{0,8},{1,3},{2,10},{3,1},{4,12},{5,7},{6,14},{7,5},{8,0},{9,11},{1... | collective-permute-start | bytes 344072 | tf_op jit(solution)/shard_map/ppermute | solution.py:291
  5.1 1.6 %collective-permute-start.4 = (bf16[112,512]{1,0:T(8,128)(2,1)S(1)}, bf16[112,512]{1,0:T(8,128)(2,1)S(1)}, u32[]{:S(2)}, u32[]{:S(2)}) collective-permute-start(bf16[112,512]{1,0:T(8,128)(2,1)S(1)} %pack.1.refs_6_.rest_3_), channel_id=1, source_target_pairs={{0,4},{1,7},{2,6},{3,5},{4,0},{5,3},{6,2},{7,1},{8,12},{9,15},{10,... | collective-permute-start | bytes 344072 | tf_op jit(solution)/shard_map/ppermute | solution.py:291
  6.7 0.7 %collective-permute-start.1 = (bf16[112,512]{1,0:T(8,128)(2,1)S(1)}, bf16[112,512]{1,0:T(8,128)(2,1)S(1)}, u32[]{:S(2)}, u32[]{:S(2)}) collective-permute-start(bf16[112,512]{1,0:T(8,128)(2,1)S(1)} %pack.1.refs_6_.rest_3_), channel_id=1, source_target_pairs={{1,13},{3,15},{5,9},{7,11},{9,5},{11,7},{13,1},{15,3},{17,29},{19,... | collective-permute-start | bytes 344072 | tf_op jit(solution)/shard_map/ppermute | solution.py:291
  7.3 1.8 %prepare.1 = (bf16[192,576]{1,0:T(8,128)(2,1)S(1)}, f32[1,96,480]{2,1,0:T(8,128)S(1)}, f32[1,96,192]{2,1,0:T(8,128)S(1)}, f32[1,96,96]{2,1,0:T(8,128)S(1)}, bf16[256,4096]{1,0:T(8,128)(2,1)S(1)}) custom-call(bf16[96,256]{1,0:T(8,128)(2,1)} %refs_0_.1, bf16[96,128]{1,0:T(8,128)(2,1)} %refs_1_.1, bf16[512,256]{1,0:T(8,128)(2,1)} %refs_2_.1, s32[16]{0:T(128)} %refs_3_.1, ...), custom_call_target="tpu_custom_call" | custom-call | tf_op jit(solution)/shard_map/prepare/pallas_call | solution.py:335
  9.1 1.6 %collective-permute-start = (bf16[192,576]{1,0:T(8,128)(2,1)S(1)}, bf16[192,576]{1,0:T(8,128)(2,1)S(1)}, u32[]{:S(2)}, u32[]{:S(2)}) collective-permute-start(bf16[192,576]{1,0:T(8,128)(2,1)S(1)} %get-tuple-element.17.rest_0_), channel_id=1, source_target_pairs={{0,1},{1,0},{2,3},{3,2},{4,5},{5,4},{6,7},{7,6},{8,9},{9,8},{10,11... | collective-permute-start | bytes 663560 | tf_op jit(solution)/shard_map/ppermute | solution.py:283
  10.8 0.1 collective-permute-start.9
  10.9 0.0 collective-permute-done.2.chunk.first
  10.9 0.5 %collective-permute-start.3 = (bf16[112,512]{1,0:T(8,128)(2,1)S(1)}, bf16[112,512]{1,0:T(8,128)(2,1)S(1)}, u32[]{:S(2)}, u32[]{:S(2)}) collective-permute-start(bf16[112,512]{1,0:T(8,128)(2,1)S(1)} %hand_first.1.refs_0_.rest_4_), channel_id=1, source_target_pairs={{0,1},{1,0},{2,3},{3,2},{4,5},{5,4},{6,7},{7,6},{8,9},{9,8},{10,11... | collective-permute-start | bytes 344072 | tf_op jit(solution)/shard_map/ppermute | solution.py:283
  11.4 0.0 collective-permute-done.4.chunk
  11.4 0.1 collective-permute-start.5
  11.5 0.0 collective-permute-done.1.rest_8_.last.rest_3_
  11.5 1.6 %collective-permute-start.7 = (bf16[112,512]{1,0:T(8,128)(2,1)S(1)}, bf16[112,512]{1,0:T(8,128)(2,1)S(1)}, u32[]{:S(2)}, u32[]{:S(2)}) collective-permute-start(bf16[112,512]{1,0:T(8,128)(2,1)S(1)} %pick.1), channel_id=1, source_target_pairs={{0,2},{1,3},{2,0},{3,1},{4,6},{5,7},{6,4},{7,5},{8,10},{9,11},{10,... | collective-permute-start | bytes 344072 | tf_op jit(solution)/shard_map/ppermute | solution.py:291
  13.1 0.0 collective-permute-done.rest_1_
  13.1 2.2 %collective-permute-done.5.rest_7_ = bf16[112,512]{1,0:T(8,128)(2,1)S(1)} collective-permute-done((bf16[112,512]{1,0:T(8,128)(2,1)S(1)}, bf16[112,512]{1,0:T(8,128)(2,1)S(1)}, u32[]{:S(2)}, u32[]{:S(2)}) %collective-permute-start.5) | collective-permute-done | bytes 114720 | tf_op jit(solution)/shard_map/ppermute | solution.py:283
  15.3 0.0 collective-permute-done.3.rest_5_
  15.3 0.9 %first.1 = (f32[384,1]{1,0:T(8,128)S(1)}, f32[384,1]{1,0:T(8,128)S(1)}, f32[384,512]{1,0:T(8,128)S(1)}, bf16[112,512]{1,0:T(8,128)(2,1)S(1)}) custom-call(bf16[192,576]{1,0:T(8,128)(2,1)S(1)} %get-tuple-element.17.rest_0_, bf16[192,576]{1,0:T(8,128)(2,1)S(1)} %collective-permute-done.rest_1_, f32[1,96,480]{2,1,0:T(8,128)S(1)} %get-tuple-element.19.rest_2_, ...), custom_call_target="tpu_custom_call" | custom-call | flops 22000001024 | tf_op jit(solution)/shard_map/first/pallas_call | solution.py:305
  16.1 0.0 copy-start
  16.2 0.0 copy-start.1
  16.2 1.6 %collective-permute-start.6 = (bf16[112,512]{1,0:T(8,128)(2,1)S(1)}, bf16[112,512]{1,0:T(8,128)(2,1)S(1)}, u32[]{:S(2)}, u32[]{:S(2)}) collective-permute-start(bf16[112,512]{1,0:T(8,128)(2,1)S(1)} %get-tuple-element.20), channel_id=1, source_target_pairs={{1,0},{3,2},{5,4},{7,6},{9,8},{11,10},{13,12},{15,14},{17,16},{19,... | collective-permute-start | bytes 344072 | tf_op jit(solution)/shard_map/ppermute | solution.py:374
  17.7 0.0 collective-permute-done.7.rest_5_
  17.7 1.2 %collective-permute-start.8 = (bf16[112,512]{1,0:T(8,128)(2,1)S(1)}, bf16[112,512]{1,0:T(8,128)(2,1)S(1)}, u32[]{:S(2)}, u32[]{:S(2)}) collective-permute-start(bf16[112,512]{1,0:T(8,128)(2,1)S(1)} %collective-permute-done.7.rest_5_), channel_id=1, source_target_pairs={{0,1},{1,0},{2,3},{3,2},{4,5},{5,4},{6,7},{7,6},{8,9},{9,8},{10,11... | collective-permute-start | bytes 344072 | tf_op jit(solution)/shard_map/ppermute | solution.py:283
  18.9 0.7 %collective-permute-done.6.rest_4_ = bf16[112,512]{1,0:T(8,128)(2,1)S(1)} collective-permute-done((bf16[112,512]{1,0:T(8,128)(2,1)S(1)}, bf16[112,512]{1,0:T(8,128)(2,1)S(1)}, u32[]{:S(2)}, u32[]{:S(2)}) %collective-permute-start.6) | collective-permute-done | bytes 114720 | tf_op jit(solution)/shard_map/ppermute | solution.py:374
  19.6 1.0 %second.1 = (f32[384,1]{1,0:T(8,128)S(1)}, f32[384,1]{1,0:T(8,128)S(1)}, f32[384,512]{1,0:T(8,128)S(1)}) custom-call(bf16[192,576]{1,0:T(8,128)(2,1)S(1)} %get-tuple-element.17.rest_0_, bf16[192,576]{1,0:T(8,128)(2,1)S(1)} %collective-permute-done.rest_1_, f32[1,96,192]{2,1,0:T(8,128)S(1)} %get-tuple-element.18.rest_2_, ...), custom_call_target="tpu_custom_call" | custom-call | flops 1100000000 | tf_op jit(solution)/shard_map/second/pallas_call | solution.py:305
  20.6 0.0 collective-permute-done.8.rest_6_
  20.6 0.0 collective-permute-done.9.rest_9_
  20.6 0.0 copy-done
  20.7 0.0 copy-done.1
  20.7 2.5 %finish.1 = bf16[96,3584]{1,0:T(8,128)(2,1)} custom-call(bf16[192,576]{1,0:T(8,128)(2,1)S(1)} %get-tuple-element.17.rest_0_, bf16[192,576]{1,0:T(8,128)(2,1)S(1)} %collective-permute-done.rest_1_, f32[384,1]{1,0:T(8,128)S(1)} %get-tuple-element.24.rest_2_, f32[384,1]{1,0:T(8,128)S(1)} %get-tuple-element.25.rest_3_, ...), custom_call_target="tpu_custom_call" | custom-call | tf_op jit(solution)/shard_map/finish/pallas_call | solution.py:391
  (3 shorter events, 0.0 us)
Async XLA Ops:
  1.0 9.8 %collective-permute-start.2 = (bf16[112,512]{1,0:T(8,128)(2,1)S(1)}, bf16[112,512]{1,0:T(8,128)(2,1)S(1)}, u32[]{:S(2)}, u32[]{:S(2)}) collective-permute-start(bf16[112,512]{1,0:T(8,128)(2,1)S(1)} %pack.1.refs_6_.rest_3_), channel_id=1, source_target_pairs={{0,8},{1,3},{2,10},{3,1},{4,12},{5,7},{6,14},{7,5},{8,0},{9,11},{1... | collective-permute-start | bytes 344072 | tf_op jit(solution)/shard_map/ppermute | solution.py:291
  5.1 6.3 %collective-permute-start.4 = (bf16[112,512]{1,0:T(8,128)(2,1)S(1)}, bf16[112,512]{1,0:T(8,128)(2,1)S(1)}, u32[]{:S(2)}, u32[]{:S(2)}) collective-permute-start(bf16[112,512]{1,0:T(8,128)(2,1)S(1)} %pack.1.refs_6_.rest_3_), channel_id=1, source_target_pairs={{0,4},{1,7},{2,6},{3,5},{4,0},{5,3},{6,2},{7,1},{8,12},{9,15},{10,... | collective-permute-start | bytes 344072 | tf_op jit(solution)/shard_map/ppermute | solution.py:291
  6.7 4.8 %collective-permute-start.1 = (bf16[112,512]{1,0:T(8,128)(2,1)S(1)}, bf16[112,512]{1,0:T(8,128)(2,1)S(1)}, u32[]{:S(2)}, u32[]{:S(2)}) collective-permute-start(bf16[112,512]{1,0:T(8,128)(2,1)S(1)} %pack.1.refs_6_.rest_3_), channel_id=1, source_target_pairs={{1,13},{3,15},{5,9},{7,11},{9,5},{11,7},{13,1},{15,3},{17,29},{19,... | collective-permute-start | bytes 344072 | tf_op jit(solution)/shard_map/ppermute | solution.py:291
  9.1 4.0 %collective-permute-start = (bf16[192,576]{1,0:T(8,128)(2,1)S(1)}, bf16[192,576]{1,0:T(8,128)(2,1)S(1)}, u32[]{:S(2)}, u32[]{:S(2)}) collective-permute-start(bf16[192,576]{1,0:T(8,128)(2,1)S(1)} %get-tuple-element.17.rest_0_), channel_id=1, source_target_pairs={{0,1},{1,0},{2,3},{3,2},{4,5},{5,4},{6,7},{7,6},{8,9},{9,8},{10,11... | collective-permute-start | bytes 663560 | tf_op jit(solution)/shard_map/ppermute | solution.py:283
  10.8 9.9 %collective-permute-start.9 = (bf16[256,4096]{1,0:T(8,128)(2,1)S(1)}, bf16[256,4096]{1,0:T(8,128)(2,1)S(1)}, u32[]{:S(2)}, u32[]{:S(2)}) collective-permute-start(bf16[256,4096]{1,0:T(8,128)(2,1)S(1)} %get-tuple-element.28), channel_id=1, source_target_pairs={{0,1},{1,0},{2,3},{3,2},{4,5},{5,4},{6,7},{7,6},{8,9},{9,8},{10,11... | collective-permute-start | bytes 6291464 | tf_op jit(solution)/shard_map/ppermute | solution.py:283
  10.9 4.4 %collective-permute-start.3 = (bf16[112,512]{1,0:T(8,128)(2,1)S(1)}, bf16[112,512]{1,0:T(8,128)(2,1)S(1)}, u32[]{:S(2)}, u32[]{:S(2)}) collective-permute-start(bf16[112,512]{1,0:T(8,128)(2,1)S(1)} %hand_first.1.refs_0_.rest_4_), channel_id=1, source_target_pairs={{0,1},{1,0},{2,3},{3,2},{4,5},{5,4},{6,7},{7,6},{8,9},{9,8},{10,11... | collective-permute-start | bytes 344072 | tf_op jit(solution)/shard_map/ppermute | solution.py:283
  11.4 3.9 %collective-permute-start.5 = (bf16[112,512]{1,0:T(8,128)(2,1)S(1)}, bf16[112,512]{1,0:T(8,128)(2,1)S(1)}, u32[]{:S(2)}, u32[]{:S(2)}) collective-permute-start(bf16[112,512]{1,0:T(8,128)(2,1)S(1)} %hand_second.1.rest_6_), channel_id=1, source_target_pairs={{0,1},{1,0},{2,3},{3,2},{4,5},{5,4},{6,7},{7,6},{8,9},{9,8},{10,11... | collective-permute-start | bytes 344072 | tf_op jit(solution)/shard_map/ppermute | solution.py:283
  11.5 6.2 %collective-permute-start.7 = (bf16[112,512]{1,0:T(8,128)(2,1)S(1)}, bf16[112,512]{1,0:T(8,128)(2,1)S(1)}, u32[]{:S(2)}, u32[]{:S(2)}) collective-permute-start(bf16[112,512]{1,0:T(8,128)(2,1)S(1)} %pick.1), channel_id=1, source_target_pairs={{0,2},{1,3},{2,0},{3,1},{4,6},{5,7},{6,4},{7,5},{8,10},{9,11},{10,... | collective-permute-start | bytes 344072 | tf_op jit(solution)/shard_map/ppermute | solution.py:291
  16.1 4.5 %copy-start = (bf16[256,7168]{1,0:T(8,128)(2,1)S(1)}, bf16[256,7168]{1,0:T(8,128)(2,1)}, u32[]{:S(2)}) copy-start(bf16[256,7168]{1,0:T(8,128)(2,1)} %rest_8_.1) | copy-start | bytes 11010052
  16.2 4.5 %copy-start.1 = (bf16[512,256]{1,0:T(8,128)(2,1)S(1)}, bf16[512,256]{1,0:T(8,128)(2,1)}, u32[]{:S(2)}) copy-start(bf16[512,256]{1,0:T(8,128)(2,1)} %rest_7_.1) | copy-start | bytes 786436
  16.2 3.5 %collective-permute-start.6 = (bf16[112,512]{1,0:T(8,128)(2,1)S(1)}, bf16[112,512]{1,0:T(8,128)(2,1)S(1)}, u32[]{:S(2)}, u32[]{:S(2)}) collective-permute-start(bf16[112,512]{1,0:T(8,128)(2,1)S(1)} %get-tuple-element.20), channel_id=1, source_target_pairs={{1,0},{3,2},{5,4},{7,6},{9,8},{11,10},{13,12},{15,14},{17,16},{19,... | collective-permute-start | bytes 344072 | tf_op jit(solution)/shard_map/ppermute | solution.py:374
  17.7 2.9 %collective-permute-start.8 = (bf16[112,512]{1,0:T(8,128)(2,1)S(1)}, bf16[112,512]{1,0:T(8,128)(2,1)S(1)}, u32[]{:S(2)}, u32[]{:S(2)}) collective-permute-start(bf16[112,512]{1,0:T(8,128)(2,1)S(1)} %collective-permute-done.7.rest_5_), channel_id=1, source_target_pairs={{0,1},{1,0},{2,3},{3,2},{4,5},{5,4},{6,7},{7,6},{8,9},{9,8},{10,11... | collective-permute-start | bytes 344072 | tf_op jit(solution)/shard_map/ppermute | solution.py:283

commit v15 on v13

--- a/solution.py
+++ b/solution.py
@@ -211,51 +211,52 @@
     lax.fori_loop(0, blocks - 1, step, 0)
 
 
-def finish_kernel(heads, chunk_count, *rest):
-    queries, (top, total, context), rest = rest[:2], rest[2:5], rest[5:]
+def last_kernel(chunk_count, queries_own, queries_other, top, total, context, *rest):
     bias, chunks = rest[:chunk_count][:1], rest[1 : 1 + chunk_count]
-    rest = rest[len(bias) + len(chunks) :]
-    value_own, proj_own, weights, out_ref, out_tiles, keys, out_sems = rest
-    rows, width = out_ref.shape
+    value_own, weights, out_ref, keys = rest[len(bias) + len(chunks) :]
+    rows = out_ref.shape[0]
     running = (top[...], total[...], context[...])
     if chunk_count:
         for index, chunk in enumerate(chunks):
             unpack(chunk, keys, index * rows)
-        running = attend_block(queries, keys, bias[0][0], running)
-    mixed = (running[2] / running[1]).astype(BF16)
-    half = heads // 2
+        running = attend_block((queries_own, queries_other), keys, bias[0][0], running)
+    mixed = (running[2] * (1.0 / running[1])).astype(BF16)
+    columns = value_own.shape[1]
+    heads = columns // DH
     depth = weights.shape[0]
-    base = lax.axis_index("heads") * width
-    sides = []
+    width = weights.shape[1] - DC // depth * columns
     for group in range(2):
-        parts = []
-        for head in range(half):
-            first = (group * half + head) * rows
+        for head in range(heads):
+            place = group * heads + head
             per_head = 0.0
             for block in range(DC // depth):
+                part = slice(block * depth, (block + 1) * depth)
                 if group == 0:
-                    value = value_own[block * depth : (block + 1) * depth, head * DH : (head + 1) * DH]
+                    value = value_own[part, head * DH : (head + 1) * DH]
                 else:
-                    start = width + (block * half + head) * DH
+                    start = width + block * columns + head * DH
                     value = weights[:, start : start + DH]
                 per_head = per_head + jnp.dot(
-                    mixed[first : first + rows, block * depth : (block + 1) * depth],
+                    mixed[place * rows : (place + 1) * rows, part],
                     value,
                     preferred_element_type=F32,
                 )
-            parts.append(per_head.astype(BF16))
-        sides.append(jnp.concatenate(parts, axis=1))
-    tiles = out_sems.shape[0]
-    tile = width // tiles
+            out_ref[:, place * DH : (place + 1) * DH] = per_head.astype(BF16)
+
+
+def project_kernel(tiles, heads_out, proj_own, weights, out_ref, out_tiles, sems):
+    width = out_ref.shape[1]
+    half = heads_out.shape[1] // 2
+    base = lax.axis_index("heads") * width
     sends = []
-    for index in range(tiles):
-        part = pl.ds(index * tile, tile)
-        own = proj_own[:, pl.ds(pl.multiple_of(base + index * tile, 128), tile)]
-        out = jnp.dot(sides[0], own, preferred_element_type=F32)
-        out = out + jnp.dot(sides[1], weights[:, part], preferred_element_type=F32)
+    for index, (start, size) in enumerate(tiles):
+        own = proj_own[:, pl.ds(pl.multiple_of(base + start, 128), size)]
+        out = jnp.dot(heads_out[:, :half], own, preferred_element_type=F32)
+        part = pl.ds(start, size)
+        out = out + jnp.dot(heads_out[:, half:], weights[:, part], preferred_element_type=F32)
         out_tiles[:, part] = out.astype(BF16)
         sends.append(
-            pltpu.make_async_copy(out_tiles.at[:, part], out_ref.at[:, part], out_sems.at[index])
+            pltpu.make_async_copy(out_tiles.at[:, part], out_ref.at[:, part], sems.at[index])
         )
         sends[-1].start()
     for send in sends:
@@ -379,20 +380,33 @@
             name="gathered",
         )(*both, biases[0], lax.all_gather(packed, "ctx", axis=0))
 
-    tiles = 7 if width % 896 == 0 else 1
+    heads_out = pl.pallas_call(
+        functools.partial(last_kernel, len(last)),
+        out_shape=jax.ShapeDtypeStruct((rows, heads * DH), BF16),
+        in_specs=[vmem()] * (5 + len(biases[2:]) + len(last) + 2),
+        out_specs=vmem(),
+        scratch_shapes=[pltpu.VMEM((rows, DC + DR), BF16)],
+        compiler_params=small,
+        cost_estimate=cost(0),
+        name="last",
+    )(*both, *running, *biases[2:], *last, value_up, weights_other)
+
+    tile = 512 if width % 512 == 0 else width
+    tiles = [(start, tile) for start in range(0, width, tile)]
+    if tile == 512:
+        tiles[-1:] = [(width - 512, 256), (width - 256, 256)]
     return pl.pallas_call(
-        functools.partial(finish_kernel, heads, len(last)),
+        functools.partial(project_kernel, tiles),
         out_shape=jax.ShapeDtypeStruct((rows, width), BF16),
-        in_specs=[vmem()] * (5 + len(biases[2:]) + len(last) + 3),
+        in_specs=[vmem()] * 3,
         out_specs=anywhere(),
         scratch_shapes=[
             pltpu.VMEM((rows, width), BF16),
-            pltpu.VMEM((rows, DC + DR), BF16),
-            pltpu.SemaphoreType.DMA((tiles,)),
+            pltpu.SemaphoreType.DMA((len(tiles),)),
         ],
         compiler_params=small,
-        name="finish",
-    )(*both, *running, *biases[2:], *last, value_up, out_proj, weights_other)
+        name="project",
+    )(heads_out, out_proj, weights_other)
 
 
 def solution(mesh):

time: 20.2 us -> 21.2 us (1.050)
  local copies, waits for them, and re-layouts: 0.01 us -> 0.96 us
    unnamed x4, local copies, waits for them, and re-layouts: 0.01 us -> 0.96 us
    pallas_call x1 -> x2, Pallas kernels: 2.47 us -> 2.51 us  [the longest x1 1.43 us: per_device(): pl.pallas_call(functools.partial(project_kernel, tiles), out_shape=jax.Sh...]
  transfers between devices with their start and end apart: 10 -> 10, of which waited for: 3 -> 3; matrix products, arithmetic and copies ran while one was open for 0% -> 0% of each run, Pallas kernels for 18% -> 17%
where the time goes in v15:
time: 21.2 us; the launch traced here: 21 us
  starting transfers between devices  10.3 us (49%)
  Pallas kernels  7.17 us (34%)
  waiting for transfers between devices  2.52 us (12%)
  local copies, waits for them, and re-layouts  0.96 us (5%)
    ppermute x4, starting transfers between devices, partners(): return lax.ppermute(array, ('ctx', 'heads'), pairs)  7.78 us
    ppermute x6, starting transfers between devices, other_core(): return lax.ppermute(array, 'heads', [(0, 1), (1, 0)])  2.5 us
    ppermute x4, waiting for transfers between devices, partners(): return lax.ppermute(array, ('ctx', 'heads'), pairs)  2.31 us
    pallas_call x2, Pallas kernels, attend(): pl.pallas_call(functools.partial(chunks_kernel, len(chunks), len(old), pa...  1.84 us
    pallas_call x1, Pallas kernels, per_device(): pl.pallas_call(functools.partial(prepare_kernel, order), out_shape=[jax.S...  1.77 us
    pallas_call x1, Pallas kernels, per_device(): pl.pallas_call(functools.partial(project_kernel, tiles), out_shape=jax.Sh...  1.43 us
    pallas_call x1, Pallas kernels, per_device(): pl.pallas_call(functools.partial(last_kernel, len(last)), out_shape=jax.S...  1.08 us
    pallas_call x1, Pallas kernels, per_device(): pl.pallas_call(pack_kernel, out_shape=jax.ShapeDtypeStruct((rows + rows /...  1.05 us
  transfers between devices with their start and end apart: 10, of which 3 were waited for; matrix products, arithmetic and copies ran while one was open for 0% of the time, Pallas kernels for 17%

profile of v15, /device:TPU:0, one launch (start us, length us, event | category | flops | bytes accessed | tf_op | source)
XLA Modules:
  0.0 21.0 jit_solution(8379004389705576767)
XLA Ops:
  0.0 1.0 %pack.1.refs_6_.rest_3_ = bf16[112,512]{1,0:T(8,128)(2,1)S(1)} custom-call(bf16[96,512]{1,0:T(8,128)(2,1)} %latent.1, bf16[64,96]{1,0:T(8,128)(2,1)} %bitcast.1), custom_call_target="tpu_custom_call" | custom-call | tf_op jit(solution)/shard_map/pack/pallas_call | solution.py:303
  1.0 4.1 %collective-permute-start.5 = (bf16[112,512]{1,0:T(8,128)(2,1)S(1)}, bf16[112,512]{1,0:T(8,128)(2,1)S(1)}, u32[]{:S(2)}, u32[]{:S(2)}) collective-permute-start(bf16[112,512]{1,0:T(8,128)(2,1)S(1)} %pack.1.refs_6_.rest_3_), channel_id=1, source_target_pairs={{0,8},{1,13},{2,10},{3,15},{4,12},{5,9},{6,14},{7,11},{8,0},{9,5},... | collective-permute-start | bytes 344072 | tf_op jit(solution)/shard_map/ppermute | solution.py:288
  5.1 1.6 %collective-permute-start.3 = (bf16[112,512]{1,0:T(8,128)(2,1)S(1)}, bf16[112,512]{1,0:T(8,128)(2,1)S(1)}, u32[]{:S(2)}, u32[]{:S(2)}) collective-permute-start(bf16[112,512]{1,0:T(8,128)(2,1)S(1)} %pack.1.refs_6_.rest_3_), channel_id=1, source_target_pairs={{0,4},{1,3},{2,6},{3,1},{4,0},{5,7},{6,2},{7,5},{8,12},{9,11},{10,... | collective-permute-start | bytes 344072 | tf_op jit(solution)/shard_map/ppermute | solution.py:288
  6.7 0.7 %collective-permute-start.1 = (bf16[112,512]{1,0:T(8,128)(2,1)S(1)}, bf16[112,512]{1,0:T(8,128)(2,1)S(1)}, u32[]{:S(2)}, u32[]{:S(2)}) collective-permute-start(bf16[112,512]{1,0:T(8,128)(2,1)S(1)} %pack.1.refs_6_.rest_3_), channel_id=1, source_target_pairs={{1,7},{3,5},{5,3},{7,1},{9,15},{11,13},{13,11},{15,9},{17,23},{19,... | collective-permute-start | bytes 344072 | tf_op jit(solution)/shard_map/ppermute | solution.py:288
  7.3 1.8 %prepare.1 = (bf16[192,576]{1,0:T(8,128)(2,1)S(1)}, f32[1,96,192]{2,1,0:T(8,128)S(1)}, f32[1,96,480]{2,1,0:T(8,128)S(1)}, f32[1,96,96]{2,1,0:T(8,128)S(1)}, bf16[256,4096]{1,0:T(8,128)(2,1)S(1)}) custom-call(bf16[96,256]{1,0:T(8,128)(2,1)} %refs_0_.1, bf16[96,128]{1,0:T(8,128)(2,1)} %refs_1_.1, bf16[512,256]{1,0:T(8,128)(2,1)} %refs_2_.1, s32[16]{0:T(128)} %refs_3_.1, ...), custom_call_target="tpu_custom_call" | custom-call | tf_op jit(solution)/shard_map/prepare/pallas_call | solution.py:321
  9.1 1.5 %collective-permute-start = (bf16[192,576]{1,0:T(8,128)(2,1)S(1)}, bf16[192,576]{1,0:T(8,128)(2,1)S(1)}, u32[]{:S(2)}, u32[]{:S(2)}) collective-permute-start(bf16[192,576]{1,0:T(8,128)(2,1)S(1)} %get-tuple-element.17.rest_0_.queries_own), channel_id=1, source_target_pairs={{0,1},{1,0},{2,3},{3,2},{4,5},{5,4},{6,7},{7,6},{8,9},{9,8},{10,11... | collective-permute-start | bytes 663560 | tf_op jit(solution)/shard_map/ppermute | solution.py:280
  10.6 0.1 collective-permute-start.9
  10.7 0.3 %collective-permute-done.5.chunk.rest_6_ = bf16[112,512]{1,0:T(8,128)(2,1)S(1)} collective-permute-done((bf16[112,512]{1,0:T(8,128)(2,1)S(1)}, bf16[112,512]{1,0:T(8,128)(2,1)S(1)}, u32[]{:S(2)}, u32[]{:S(2)}) %collective-permute-start.5) | collective-permute-done | bytes 114720 | tf_op jit(solution)/shard_map/ppermute | solution.py:288
  11.0 1.5 %collective-permute-start.7 = (bf16[112,512]{1,0:T(8,128)(2,1)S(1)}, bf16[112,512]{1,0:T(8,128)(2,1)S(1)}, u32[]{:S(2)}, u32[]{:S(2)}) collective-permute-start(bf16[112,512]{1,0:T(8,128)(2,1)S(1)} %collective-permute-done.5.chunk.rest_6_), channel_id=1, source_target_pairs={{0,2},{1,3},{2,0},{3,1},{4,6},{5,7},{6,4},{7,5},{8,10},{9,11},{10,... | collective-permute-start | bytes 344072 | tf_op jit(solution)/shard_map/ppermute | solution.py:288
  12.5 0.0 collective-permute-done.3.rest_4_
  12.5 0.0 collective-permute-start.4
  12.5 0.0 collective-permute-done.1.rest_3_
  12.5 0.8 %collective-permute-start.2 = (bf16[112,512]{1,0:T(8,128)(2,1)S(1)}, bf16[112,512]{1,0:T(8,128)(2,1)S(1)}, u32[]{:S(2)}, u32[]{:S(2)}) collective-permute-start(bf16[112,512]{1,0:T(8,128)(2,1)S(1)} %collective-permute-done.1.rest_3_), channel_id=1, source_target_pairs={{0,1},{1,0},{2,3},{3,2},{4,5},{5,4},{6,7},{7,6},{8,9},{9,8},{10,11... | collective-permute-start | bytes 344072 | tf_op jit(solution)/shard_map/ppermute | solution.py:280
  13.3 0.0 collective-permute-done.rest_1_.queries_other
  13.3 0.7 %first.1 = (f32[384,1]{1,0:T(8,128)S(1)}, f32[384,1]{1,0:T(8,128)S(1)}, f32[384,512]{1,0:T(8,128)S(1)}, bf16[112,512]{1,0:T(8,128)(2,1)S(1)}) custom-call(bf16[192,576]{1,0:T(8,128)(2,1)S(1)} %get-tuple-element.17.rest_0_.queries_own, bf16[192,576]{1,0:T(8,128)(2,1)S(1)} %collective-permute-done.rest_1_.queries_other, ...), custom_call_target="tpu_custom_call" | custom-call | flops 22000001024 | tf_op jit(solution)/shard_map/first/pallas_call | solution.py:291
  14.1 0.0 copy-start.1
  14.1 0.1 collective-permute-start.6
  14.2 2.0 %collective-permute-done.7.rest_8_ = bf16[112,512]{1,0:T(8,128)(2,1)S(1)} collective-permute-done((bf16[112,512]{1,0:T(8,128)(2,1)S(1)}, bf16[112,512]{1,0:T(8,128)(2,1)S(1)}, u32[]{:S(2)}, u32[]{:S(2)}) %collective-permute-start.7) | collective-permute-done | bytes 114720 | tf_op jit(solution)/shard_map/ppermute | solution.py:288
  16.2 0.0 collective-permute-start.8
  16.2 0.0 collective-permute-done.4.rest_5_
  16.2 0.0 collective-permute-done.2.rest_4_
  16.2 0.0 collective-permute-done.6.rest_7_
  16.2 1.1 %second.1 = (f32[384,1]{1,0:T(8,128)S(1)}, f32[384,1]{1,0:T(8,128)S(1)}, f32[384,512]{1,0:T(8,128)S(1)}) custom-call(bf16[192,576]{1,0:T(8,128)(2,1)S(1)} %get-tuple-element.17.rest_0_.queries_own, bf16[192,576]{1,0:T(8,128)(2,1)S(1)} %collective-permute-done.rest_1_.queries_other, f32[1,96,480]{2,1,0:T(8,128)S(1)} %get-tuple-element.18.rest_2_, ...), custom_call_target="tpu_custom_call" | custom-call | flops 1100000000 | tf_op jit(solution)/shard_map/second/pallas_call | solution.py:291
  17.3 0.2 collective-permute-done.8.rest_1_
  17.5 0.0 collective-permute-done.9.rest_3_.weights
  17.5 0.0 copy-done.1
  17.5 0.0 copy-start
  17.5 1.1 %last.1.heads_out = bf16[96,512]{1,0:T(8,128)(2,1)S(1)} custom-call(bf16[192,576]{1,0:T(8,128)(2,1)S(1)} %get-tuple-element.17.rest_0_.queries_own, bf16[192,576]{1,0:T(8,128)(2,1)S(1)} %collective-permute-done.rest_1_.queries_other, f32[384,1]{1,0:T(8,128)S(1)} %get-tuple-element.24.top, f32[384,1]{1,0:T(8,128)S(1)} %get-tuple-element.25.total, ...), custom_call_target="tpu_custom_call" | custom-call | tf_op jit(solution)/shard_map/last/pallas_call | solution.py:383
  18.6 1.0 %copy-done = bf16[256,7168]{1,0:T(8,128)(2,1)S(1)} copy-done((bf16[256,7168]{1,0:T(8,128)(2,1)S(1)}, bf16[256,7168]{1,0:T(8,128)(2,1)}, u32[]{:S(2)}) %copy-start) | copy-done | bytes 3670040
  19.6 1.4 %project.1 = bf16[96,3584]{1,0:T(8,128)(2,1)} custom-call(bf16[96,512]{1,0:T(8,128)(2,1)S(1)} %last.1.heads_out, bf16[256,7168]{1,0:T(8,128)(2,1)S(1)} %copy-done, bf16[256,4096]{1,0:T(8,128)(2,1)S(1)} %collective-permute-done.9.rest_3_.weights), custom_call_target="tpu_custom_call" | custom-call | tf_op jit(solution)/shard_map/project/pallas_call | solution.py:398
  (1 shorter events, 0.0 us)
Async XLA Ops:
  1.0 9.9 %collective-permute-start.5 = (bf16[112,512]{1,0:T(8,128)(2,1)S(1)}, bf16[112,512]{1,0:T(8,128)(2,1)S(1)}, u32[]{:S(2)}, u32[]{:S(2)}) collective-permute-start(bf16[112,512]{1,0:T(8,128)(2,1)S(1)} %pack.1.refs_6_.rest_3_), channel_id=1, source_target_pairs={{0,8},{1,13},{2,10},{3,15},{4,12},{5,9},{6,14},{7,11},{8,0},{9,5},... | collective-permute-start | bytes 344072 | tf_op jit(solution)/shard_map/ppermute | solution.py:288
  5.1 7.4 %collective-permute-start.3 = (bf16[112,512]{1,0:T(8,128)(2,1)S(1)}, bf16[112,512]{1,0:T(8,128)(2,1)S(1)}, u32[]{:S(2)}, u32[]{:S(2)}) collective-permute-start(bf16[112,512]{1,0:T(8,128)(2,1)S(1)} %pack.1.refs_6_.rest_3_), channel_id=1, source_target_pairs={{0,4},{1,3},{2,6},{3,1},{4,0},{5,7},{6,2},{7,5},{8,12},{9,11},{10,... | collective-permute-start | bytes 344072 | tf_op jit(solution)/shard_map/ppermute | solution.py:288
  6.7 5.8 %collective-permute-start.1 = (bf16[112,512]{1,0:T(8,128)(2,1)S(1)}, bf16[112,512]{1,0:T(8,128)(2,1)S(1)}, u32[]{:S(2)}, u32[]{:S(2)}) collective-permute-start(bf16[112,512]{1,0:T(8,128)(2,1)S(1)} %pack.1.refs_6_.rest_3_), channel_id=1, source_target_pairs={{1,7},{3,5},{5,3},{7,1},{9,15},{11,13},{13,11},{15,9},{17,23},{19,... | collective-permute-start | bytes 344072 | tf_op jit(solution)/shard_map/ppermute | solution.py:288
  9.1 4.2 %collective-permute-start = (bf16[192,576]{1,0:T(8,128)(2,1)S(1)}, bf16[192,576]{1,0:T(8,128)(2,1)S(1)}, u32[]{:S(2)}, u32[]{:S(2)}) collective-permute-start(bf16[192,576]{1,0:T(8,128)(2,1)S(1)} %get-tuple-element.17.rest_0_.queries_own), channel_id=1, source_target_pairs={{0,1},{1,0},{2,3},{3,2},{4,5},{5,4},{6,7},{7,6},{8,9},{9,8},{10,11... | collective-permute-start | bytes 663560 | tf_op jit(solution)/shard_map/ppermute | solution.py:280
  10.6 6.9 %collective-permute-start.9 = (bf16[256,4096]{1,0:T(8,128)(2,1)S(1)}, bf16[256,4096]{1,0:T(8,128)(2,1)S(1)}, u32[]{:S(2)}, u32[]{:S(2)}) collective-permute-start(bf16[256,4096]{1,0:T(8,128)(2,1)S(1)} %get-tuple-element.28), channel_id=1, source_target_pairs={{0,1},{1,0},{2,3},{3,2},{4,5},{5,4},{6,7},{7,6},{8,9},{9,8},{10,11... | collective-permute-start | bytes 6291464 | tf_op jit(solution)/shard_map/ppermute | solution.py:280
  11.0 5.2 %collective-permute-start.7 = (bf16[112,512]{1,0:T(8,128)(2,1)S(1)}, bf16[112,512]{1,0:T(8,128)(2,1)S(1)}, u32[]{:S(2)}, u32[]{:S(2)}) collective-permute-start(bf16[112,512]{1,0:T(8,128)(2,1)S(1)} %collective-permute-done.5.chunk.rest_6_), channel_id=1, source_target_pairs={{0,2},{1,3},{2,0},{3,1},{4,6},{5,7},{6,4},{7,5},{8,10},{9,11},{10,... | collective-permute-start | bytes 344072 | tf_op jit(solution)/shard_map/ppermute | solution.py:288
  12.5 3.7 %collective-permute-start.4 = (bf16[112,512]{1,0:T(8,128)(2,1)S(1)}, bf16[112,512]{1,0:T(8,128)(2,1)S(1)}, u32[]{:S(2)}, u32[]{:S(2)}) collective-permute-start(bf16[112,512]{1,0:T(8,128)(2,1)S(1)} %collective-permute-done.3.rest_4_), channel_id=1, source_target_pairs={{0,1},{1,0},{2,3},{3,2},{4,5},{5,4},{6,7},{7,6},{8,9},{9,8},{10,11... | collective-permute-start | bytes 344072 | tf_op jit(solution)/shard_map/ppermute | solution.py:280
  12.5 3.7 %collective-permute-start.2 = (bf16[112,512]{1,0:T(8,128)(2,1)S(1)}, bf16[112,512]{1,0:T(8,128)(2,1)S(1)}, u32[]{:S(2)}, u32[]{:S(2)}) collective-permute-start(bf16[112,512]{1,0:T(8,128)(2,1)S(1)} %collective-permute-done.1.rest_3_), channel_id=1, source_target_pairs={{0,1},{1,0},{2,3},{3,2},{4,5},{5,4},{6,7},{7,6},{8,9},{9,8},{10,11... | collective-permute-start | bytes 344072 | tf_op jit(solution)/shard_map/ppermute | solution.py:280
  14.1 3.5 %copy-start.1 = (bf16[512,256]{1,0:T(8,128)(2,1)S(1)}, bf16[512,256]{1,0:T(8,128)(2,1)}, u32[]{:S(2)}) copy-start(bf16[512,256]{1,0:T(8,128)(2,1)} %rest_2_.1) | copy-start | bytes 786436
  14.1 2.1 %collective-permute-start.6 = (bf16[112,512]{1,0:T(8,128)(2,1)S(1)}, bf16[112,512]{1,0:T(8,128)(2,1)S(1)}, u32[]{:S(2)}, u32[]{:S(2)}) collective-permute-start(bf16[112,512]{1,0:T(8,128)(2,1)S(1)} %get-tuple-element.20), channel_id=1, source_target_pairs={{0,1},{1,0},{2,3},{3,2},{4,5},{5,4},{6,7},{7,6},{8,9},{9,8},{10,11... | collective-permute-start | bytes 344072 | tf_op jit(solution)/shard_map/ppermute | solution.py:280
  16.2 1.3 %collective-permute-start.8 = (bf16[112,512]{1,0:T(8,128)(2,1)S(1)}, bf16[112,512]{1,0:T(8,128)(2,1)S(1)}, u32[]{:S(2)}, u32[]{:S(2)}) collective-permute-start(bf16[112,512]{1,0:T(8,128)(2,1)S(1)} %collective-permute-done.7.rest_8_), channel_id=1, source_target_pairs={{0,1},{1,0},{2,3},{3,2},{4,5},{5,4},{6,7},{7,6},{8,9},{9,8},{10,11... | collective-permute-start | bytes 344072 | tf_op jit(solution)/shard_map/ppermute | solution.py:280
  17.5 2.0 %copy-start = (bf16[256,7168]{1,0:T(8,128)(2,1)S(1)}, bf16[256,7168]{1,0:T(8,128)(2,1)}, u32[]{:S(2)}) copy-start(bf16[256,7168]{1,0:T(8,128)(2,1)} %proj_own.1) | copy-start | bytes 11010052

commit v16 on v13

--- a/solution.py
+++ b/solution.py
@@ -40,14 +40,32 @@
     return pl.CostEstimate(flops=int(microseconds * 1.1e9), bytes_accessed=0, transcendentals=0)
 
 
-def pack_kernel(latent, key_rope_turned, out_ref):
+def pack_kernel(latent, key_rope_turned, out_ref, turned, sems):
     rows = latent.shape[0]
     group = rows // 6
-    out_ref[:rows] = latent[...]
-    rope = key_rope_turned[...].astype(F32).T.astype(BF16)
-    parts = [rope[index * group : (index + 1) * group] for index in range(6)]
-    parts.append(jnp.zeros((group, DC - 6 * DR), BF16))
-    out_ref[rows:] = jnp.concatenate(parts, axis=1)
+    half = DC // 2
+    fetches = [pltpu.make_async_copy(key_rope_turned, turned, sems.at[2])]
+    for side in range(2):
+        fetches.append(
+            pltpu.make_async_copy(
+                latent.at[:, pl.ds(side * half, half)],
+                out_ref.at[pl.ds(side * rows, rows)],
+                sems.at[side],
+            )
+        )
+    for fetch in fetches:
+        fetch.start()
+    fetches[0].wait()
+    rope = turned[...].astype(F32).T.astype(BF16)
+    first = 0
+    base = 2 * rows
+    for size in (group, group // 2):
+        parts = [rope[first + index * size : first + (index + 1) * size] for index in range(4)]
+        out_ref[pl.ds(base, size), :] = jnp.concatenate(parts, axis=1)
+        first += 4 * size
+        base += size
+    for fetch in fetches[1:]:
+        fetch.wait()
 
 
 def gate_kernel(chunk, out_ref):
@@ -58,12 +76,17 @@
     chunk = chunk[...]
     if other is not None:
         chunk = jnp.where(lax.axis_index("heads") == 0, other[...], chunk)
-    rows = 6 * chunk.shape[0] // 7
+    rows = 4 * chunk.shape[0] // 9
     group = rows // 6
-    keys[pl.ds(base, rows), :DC] = chunk[:rows]
-    for index in range(6):
-        part = chunk[rows:, index * DR : (index + 1) * DR]
-        keys[pl.ds(base + index * group, group), DC:] = part
+    keys[pl.ds(base, rows), : DC // 2] = chunk[:rows]
+    keys[pl.ds(base, rows), DC // 2 : DC] = chunk[rows : 2 * rows]
+    place = 2 * rows
+    for size in (group, group // 2):
+        for index in range(4):
+            part = chunk[place : place + size, index * DR : (index + 1) * DR]
+            keys[pl.ds(base, size), DC:] = part
+            base += size
+        place += size
 
 
 def prepare_kernel(order, *refs):
@@ -301,9 +324,13 @@
 
     packed = pl.pallas_call(
         pack_kernel,
-        out_shape=jax.ShapeDtypeStruct((rows + rows // 6, DC), BF16),
-        in_specs=[vmem()] * 2,
+        out_shape=jax.ShapeDtypeStruct((2 * rows + rows // 4, DC // 2), BF16),
+        in_specs=[hbm()] * 2,
         out_specs=vmem(),
+        scratch_shapes=[
+            pltpu.VMEM((DR, rows), BF16),
+            pltpu.SemaphoreType.DMA((3,)),
+        ],
         compiler_params=small,
         name="pack",
     )(*in_hbm(latent, key_rope.T))

time: 20.2 us -> 20.1 us (level)
  waiting for transfers between devices: 2.51 us -> 2.29 us
    ppermute x4, waiting for transfers between devices: 2.29 us -> 2.07 us  [partners(): return lax.ppermute(array, ('ctx', 'heads'), pairs)]
where the time goes in v16:
time: 20.1 us; the launch traced here: 19.9 us
  starting transfers between devices  10.5 us (52%)
  Pallas kernels  7.01 us (35%)
  waiting for transfers between devices  2.29 us (11%)
    ppermute x4, starting transfers between devices, partners(): return lax.ppermute(array, ('ctx', 'heads'), pairs)  7.82 us
    ppermute x6, starting transfers between devices, other_core(): return lax.ppermute(array, 'heads', [(0, 1), (1, 0)])  2.63 us
    pallas_call x1, Pallas kernels, per_device(): pl.pallas_call(functools.partial(finish_kernel, heads, len(last)), out_sh...  2.5 us
    ppermute x4, waiting for transfers between devices, partners(): return lax.ppermute(array, ('ctx', 'heads'), pairs)  2.07 us
    pallas_call x2, Pallas kernels, attend(): pl.pallas_call(functools.partial(chunks_kernel, len(chunks), len(old), pa...  1.83 us
    pallas_call x1, Pallas kernels, per_device(): pl.pallas_call(functools.partial(prepare_kernel, order), out_shape=[jax.S...  1.77 us
    pallas_call x1, Pallas kernels, per_device(): pl.pallas_call(pack_kernel, out_shape=jax.ShapeDtypeStruct((2 * rows + ro...  0.91 us
  transfers between devices with their start and end apart: 10, of which 3 were waited for; matrix products, arithmetic and copies ran while one was open for 0% of the time, Pallas kernels for 18%

profile of v16, /device:TPU:0, one launch (start us, length us, event | category | flops | bytes accessed | tf_op | source)
XLA Modules:
  0.0 19.9 jit_solution(10568147468754085414)
XLA Ops:
  0.0 0.9 %pack.1.refs_6_.rest_3_ = bf16[216,256]{1,0:T(8,128)(2,1)S(1)} custom-call(bf16[96,512]{1,0:T(8,128)(2,1)} %latent.1, bf16[64,96]{1,0:T(8,128)(2,1)} %bitcast.1), custom_call_target="tpu_custom_call" | custom-call | tf_op jit(solution)/shard_map/pack/pallas_call | solution.py:325
  0.9 4.1 %collective-permute-start.5 = (bf16[216,256]{1,0:T(8,128)(2,1)S(1)}, bf16[216,256]{1,0:T(8,128)(2,1)S(1)}, u32[]{:S(2)}, u32[]{:S(2)}) collective-permute-start(bf16[216,256]{1,0:T(8,128)(2,1)S(1)} %pack.1.refs_6_.rest_3_), channel_id=1, source_target_pairs={{0,8},{1,13},{2,10},{3,15},{4,12},{5,9},{6,14},{7,11},{8,0},{9,5},... | collective-permute-start | bytes 331784 | tf_op jit(solution)/shard_map/ppermute | solution.py:310
  5.0 1.6 %collective-permute-start.3 = (bf16[216,256]{1,0:T(8,128)(2,1)S(1)}, bf16[216,256]{1,0:T(8,128)(2,1)S(1)}, u32[]{:S(2)}, u32[]{:S(2)}) collective-permute-start(bf16[216,256]{1,0:T(8,128)(2,1)S(1)} %pack.1.refs_6_.rest_3_), channel_id=1, source_target_pairs={{0,4},{1,3},{2,6},{3,1},{4,0},{5,7},{6,2},{7,5},{8,12},{9,11},{10,... | collective-permute-start | bytes 331784 | tf_op jit(solution)/shard_map/ppermute | solution.py:310
  6.6 0.7 %collective-permute-start.1 = (bf16[216,256]{1,0:T(8,128)(2,1)S(1)}, bf16[216,256]{1,0:T(8,128)(2,1)S(1)}, u32[]{:S(2)}, u32[]{:S(2)}) collective-permute-start(bf16[216,256]{1,0:T(8,128)(2,1)S(1)} %pack.1.refs_6_.rest_3_), channel_id=1, source_target_pairs={{1,7},{3,5},{5,3},{7,1},{9,15},{11,13},{13,11},{15,9},{17,23},{19,... | collective-permute-start | bytes 331784 | tf_op jit(solution)/shard_map/ppermute | solution.py:310
  7.3 1.8 %prepare.1 = (bf16[192,576]{1,0:T(8,128)(2,1)S(1)}, f32[1,96,192]{2,1,0:T(8,128)S(1)}, f32[1,96,480]{2,1,0:T(8,128)S(1)}, f32[1,96,96]{2,1,0:T(8,128)S(1)}, bf16[256,4096]{1,0:T(8,128)(2,1)S(1)}) custom-call(bf16[96,256]{1,0:T(8,128)(2,1)} %refs_0_.1, bf16[96,128]{1,0:T(8,128)(2,1)} %refs_1_.1, bf16[512,256]{1,0:T(8,128)(2,1)} %refs_2_.1, s32[16]{0:T(128)} %refs_3_.1, ...), custom_call_target="tpu_custom_call" | custom-call | tf_op jit(solution)/shard_map/prepare/pallas_call | solution.py:347
  9.0 1.5 %collective-permute-start = (bf16[192,576]{1,0:T(8,128)(2,1)S(1)}, bf16[192,576]{1,0:T(8,128)(2,1)S(1)}, u32[]{:S(2)}, u32[]{:S(2)}) collective-permute-start(bf16[192,576]{1,0:T(8,128)(2,1)S(1)} %get-tuple-element.17.rest_0_), channel_id=1, source_target_pairs={{0,1},{1,0},{2,3},{3,2},{4,5},{5,4},{6,7},{7,6},{8,9},{9,8},{10,11... | collective-permute-start | bytes 663560 | tf_op jit(solution)/shard_map/ppermute | solution.py:302
  10.6 0.1 collective-permute-start.9
  10.6 0.1 collective-permute-done.5.chunk.rest_6_
  10.7 1.5 %collective-permute-start.7 = (bf16[216,256]{1,0:T(8,128)(2,1)S(1)}, bf16[216,256]{1,0:T(8,128)(2,1)S(1)}, u32[]{:S(2)}, u32[]{:S(2)}) collective-permute-start(bf16[216,256]{1,0:T(8,128)(2,1)S(1)} %collective-permute-done.5.chunk.rest_6_), channel_id=1, source_target_pairs={{0,2},{1,3},{2,0},{3,1},{4,6},{5,7},{6,4},{7,5},{8,10},{9,11},{10,... | collective-permute-start | bytes 331784 | tf_op jit(solution)/shard_map/ppermute | solution.py:310
  12.2 0.0 collective-permute-done.3.rest_4_
  12.2 0.0 collective-permute-start.4
  12.2 0.0 collective-permute-done.1.rest_3_
  12.2 1.0 %collective-permute-start.2 = (bf16[216,256]{1,0:T(8,128)(2,1)S(1)}, bf16[216,256]{1,0:T(8,128)(2,1)S(1)}, u32[]{:S(2)}, u32[]{:S(2)}) collective-permute-start(bf16[216,256]{1,0:T(8,128)(2,1)S(1)} %collective-permute-done.1.rest_3_), channel_id=1, source_target_pairs={{0,1},{1,0},{2,3},{3,2},{4,5},{5,4},{6,7},{7,6},{8,9},{9,8},{10,11... | collective-permute-start | bytes 331784 | tf_op jit(solution)/shard_map/ppermute | solution.py:302
  13.2 0.0 collective-permute-done.rest_1_
  13.2 0.7 %first.1 = (f32[384,1]{1,0:T(8,128)S(1)}, f32[384,1]{1,0:T(8,128)S(1)}, f32[384,512]{1,0:T(8,128)S(1)}, bf16[216,256]{1,0:T(8,128)(2,1)S(1)}) custom-call(bf16[192,576]{1,0:T(8,128)(2,1)S(1)} %get-tuple-element.17.rest_0_, bf16[192,576]{1,0:T(8,128)(2,1)S(1)} %collective-permute-done.rest_1_, f32[1,96,192]{2,1,0:T(8,128)S(1)} %get-tuple-element.19.rest_2_, ...), custom_call_target="tpu_custom_call" | custom-call | flops 22000001024 | tf_op jit(solution)/shard_map/first/pallas_call | solution.py:313
  13.9 0.0 copy-start
  14.0 0.0 copy-start.1
  14.0 0.1 collective-permute-start.6
  14.0 2.0 %collective-permute-done.7.rest_8_ = bf16[216,256]{1,0:T(8,128)(2,1)S(1)} collective-permute-done((bf16[216,256]{1,0:T(8,128)(2,1)S(1)}, bf16[216,256]{1,0:T(8,128)(2,1)S(1)}, u32[]{:S(2)}, u32[]{:S(2)}) %collective-permute-start.7) | collective-permute-done | bytes 110624 | tf_op jit(solution)/shard_map/ppermute | solution.py:310
  16.0 0.0 collective-permute-start.8
  16.0 0.0 collective-permute-done.4.rest_5_
  16.0 0.0 collective-permute-done.2.rest_4_
  16.1 0.0 collective-permute-done.6.rest_7_
  16.1 1.1 %second.1 = (f32[384,1]{1,0:T(8,128)S(1)}, f32[384,1]{1,0:T(8,128)S(1)}, f32[384,512]{1,0:T(8,128)S(1)}) custom-call(bf16[192,576]{1,0:T(8,128)(2,1)S(1)} %get-tuple-element.17.rest_0_, bf16[192,576]{1,0:T(8,128)(2,1)S(1)} %collective-permute-done.rest_1_, f32[1,96,480]{2,1,0:T(8,128)S(1)} %get-tuple-element.18.rest_2_, ...), custom_call_target="tpu_custom_call" | custom-call | flops 1100000000 | tf_op jit(solution)/shard_map/second/pallas_call | solution.py:313
  17.2 0.2 %collective-permute-done.8.rest_6_ = bf16[216,256]{1,0:T(8,128)(2,1)S(1)} collective-permute-done((bf16[216,256]{1,0:T(8,128)(2,1)S(1)}, bf16[216,256]{1,0:T(8,128)(2,1)S(1)}, u32[]{:S(2)}, u32[]{:S(2)}) %collective-permute-start.8) | collective-permute-done | bytes 110624 | tf_op jit(solution)/shard_map/ppermute | solution.py:302
  17.4 0.0 collective-permute-done.9.rest_9_
  17.4 0.0 copy-done
  17.4 0.0 copy-done.1
  17.4 2.5 %finish.1 = bf16[96,3584]{1,0:T(8,128)(2,1)} custom-call(bf16[192,576]{1,0:T(8,128)(2,1)S(1)} %get-tuple-element.17.rest_0_, bf16[192,576]{1,0:T(8,128)(2,1)S(1)} %collective-permute-done.rest_1_, f32[384,1]{1,0:T(8,128)S(1)} %get-tuple-element.24.rest_2_, f32[384,1]{1,0:T(8,128)S(1)} %get-tuple-element.25.rest_3_, ...), custom_call_target="tpu_custom_call" | custom-call | tf_op jit(solution)/shard_map/finish/pallas_call | solution.py:410
  (1 shorter events, 0.0 us)
Async XLA Ops:
  0.9 9.8 %collective-permute-start.5 = (bf16[216,256]{1,0:T(8,128)(2,1)S(1)}, bf16[216,256]{1,0:T(8,128)(2,1)S(1)}, u32[]{:S(2)}, u32[]{:S(2)}) collective-permute-start(bf16[216,256]{1,0:T(8,128)(2,1)S(1)} %pack.1.refs_6_.rest_3_), channel_id=1, source_target_pairs={{0,8},{1,13},{2,10},{3,15},{4,12},{5,9},{6,14},{7,11},{8,0},{9,5},... | collective-permute-start | bytes 331784 | tf_op jit(solution)/shard_map/ppermute | solution.py:310
  5.0 7.2 %collective-permute-start.3 = (bf16[216,256]{1,0:T(8,128)(2,1)S(1)}, bf16[216,256]{1,0:T(8,128)(2,1)S(1)}, u32[]{:S(2)}, u32[]{:S(2)}) collective-permute-start(bf16[216,256]{1,0:T(8,128)(2,1)S(1)} %pack.1.refs_6_.rest_3_), channel_id=1, source_target_pairs={{0,4},{1,3},{2,6},{3,1},{4,0},{5,7},{6,2},{7,5},{8,12},{9,11},{10,... | collective-permute-start | bytes 331784 | tf_op jit(solution)/shard_map/ppermute | solution.py:310
  6.6 5.6 %collective-permute-start.1 = (bf16[216,256]{1,0:T(8,128)(2,1)S(1)}, bf16[216,256]{1,0:T(8,128)(2,1)S(1)}, u32[]{:S(2)}, u32[]{:S(2)}) collective-permute-start(bf16[216,256]{1,0:T(8,128)(2,1)S(1)} %pack.1.refs_6_.rest_3_), channel_id=1, source_target_pairs={{1,7},{3,5},{5,3},{7,1},{9,15},{11,13},{13,11},{15,9},{17,23},{19,... | collective-permute-start | bytes 331784 | tf_op jit(solution)/shard_map/ppermute | solution.py:310
  9.0 4.2 %collective-permute-start = (bf16[192,576]{1,0:T(8,128)(2,1)S(1)}, bf16[192,576]{1,0:T(8,128)(2,1)S(1)}, u32[]{:S(2)}, u32[]{:S(2)}) collective-permute-start(bf16[192,576]{1,0:T(8,128)(2,1)S(1)} %get-tuple-element.17.rest_0_), channel_id=1, source_target_pairs={{0,1},{1,0},{2,3},{3,2},{4,5},{5,4},{6,7},{7,6},{8,9},{9,8},{10,11... | collective-permute-start | bytes 663560 | tf_op jit(solution)/shard_map/ppermute | solution.py:302
  10.6 6.8 %collective-permute-start.9 = (bf16[256,4096]{1,0:T(8,128)(2,1)S(1)}, bf16[256,4096]{1,0:T(8,128)(2,1)S(1)}, u32[]{:S(2)}, u32[]{:S(2)}) collective-permute-start(bf16[256,4096]{1,0:T(8,128)(2,1)S(1)} %get-tuple-element.28), channel_id=1, source_target_pairs={{0,1},{1,0},{2,3},{3,2},{4,5},{5,4},{6,7},{7,6},{8,9},{9,8},{10,11... | collective-permute-start | bytes 6291464 | tf_op jit(solution)/shard_map/ppermute | solution.py:302
  10.7 5.3 %collective-permute-start.7 = (bf16[216,256]{1,0:T(8,128)(2,1)S(1)}, bf16[216,256]{1,0:T(8,128)(2,1)S(1)}, u32[]{:S(2)}, u32[]{:S(2)}) collective-permute-start(bf16[216,256]{1,0:T(8,128)(2,1)S(1)} %collective-permute-done.5.chunk.rest_6_), channel_id=1, source_target_pairs={{0,2},{1,3},{2,0},{3,1},{4,6},{5,7},{6,4},{7,5},{8,10},{9,11},{10,... | collective-permute-start | bytes 331784 | tf_op jit(solution)/shard_map/ppermute | solution.py:310
  12.2 3.8 %collective-permute-start.4 = (bf16[216,256]{1,0:T(8,128)(2,1)S(1)}, bf16[216,256]{1,0:T(8,128)(2,1)S(1)}, u32[]{:S(2)}, u32[]{:S(2)}) collective-permute-start(bf16[216,256]{1,0:T(8,128)(2,1)S(1)} %collective-permute-done.3.rest_4_), channel_id=1, source_target_pairs={{0,1},{1,0},{2,3},{3,2},{4,5},{5,4},{6,7},{7,6},{8,9},{9,8},{10,11... | collective-permute-start | bytes 331784 | tf_op jit(solution)/shard_map/ppermute | solution.py:302
  12.2 3.8 %collective-permute-start.2 = (bf16[216,256]{1,0:T(8,128)(2,1)S(1)}, bf16[216,256]{1,0:T(8,128)(2,1)S(1)}, u32[]{:S(2)}, u32[]{:S(2)}) collective-permute-start(bf16[216,256]{1,0:T(8,128)(2,1)S(1)} %collective-permute-done.1.rest_3_), channel_id=1, source_target_pairs={{0,1},{1,0},{2,3},{3,2},{4,5},{5,4},{6,7},{7,6},{8,9},{9,8},{10,11... | collective-permute-start | bytes 331784 | tf_op jit(solution)/shard_map/ppermute | solution.py:302
  13.9 3.4 %copy-start = (bf16[256,7168]{1,0:T(8,128)(2,1)S(1)}, bf16[256,7168]{1,0:T(8,128)(2,1)}, u32[]{:S(2)}) copy-start(bf16[256,7168]{1,0:T(8,128)(2,1)} %rest_8_.1) | copy-start | bytes 11010052
  14.0 3.4 %copy-start.1 = (bf16[512,256]{1,0:T(8,128)(2,1)S(1)}, bf16[512,256]{1,0:T(8,128)(2,1)}, u32[]{:S(2)}) copy-start(bf16[512,256]{1,0:T(8,128)(2,1)} %rest_7_.1) | copy-start | bytes 786436
  14.0 2.1 %collective-permute-start.6 = (bf16[216,256]{1,0:T(8,128)(2,1)S(1)}, bf16[216,256]{1,0:T(8,128)(2,1)S(1)}, u32[]{:S(2)}, u32[]{:S(2)}) collective-permute-start(bf16[216,256]{1,0:T(8,128)(2,1)S(1)} %get-tuple-element.20), channel_id=1, source_target_pairs={{0,1},{1,0},{2,3},{3,2},{4,5},{5,4},{6,7},{7,6},{8,9},{9,8},{10,11... | collective-permute-start | bytes 331784 | tf_op jit(solution)/shard_map/ppermute | solution.py:302
  16.0 1.3 %collective-permute-start.8 = (bf16[216,256]{1,0:T(8,128)(2,1)S(1)}, bf16[216,256]{1,0:T(8,128)(2,1)S(1)}, u32[]{:S(2)}, u32[]{:S(2)}) collective-permute-start(bf16[216,256]{1,0:T(8,128)(2,1)S(1)} %collective-permute-done.7.rest_8_), channel_id=1, source_target_pairs={{0,1},{1,0},{2,3},{3,2},{4,5},{5,4},{6,7},{7,6},{8,9},{9,8},{10,11... | collective-permute-start | bytes 331784 | tf_op jit(solution)/shard_map/ppermute | solution.py:302

commit v17 on v16

--- a/solution.py
+++ b/solution.py
@@ -90,9 +90,9 @@
 
 
 def prepare_kernel(order, *refs):
-    sources, out_proj, rest = refs[:5], refs[5], refs[7:]
+    sources, (out_proj, packed), rest = refs[:5], refs[5:7], refs[7:]
     outs, copied, sems = rest[:-6], rest[-6:-1], rest[-1]
-    weights = outs[-1]
+    weights, packed_after = outs[-2:]
     depth, width = out_proj.shape[0], out_proj.shape[1] // 2
     fetches = [
         pltpu.make_async_copy(source, target, sems.at[index])
@@ -106,6 +106,7 @@
     )
     for fetch in fetches:
         fetch.start()
+    packed_after[...] = packed[...]
     nope, rope, up, span_order, value_up = copied
     rows = nope.shape[0]
     heads = nope.shape[1] // DH
@@ -124,7 +125,7 @@
         part = pl.ds(head * rows, rows)
         outs[0][part, :DC] = latent.astype(BF16)
         outs[0][part, DC:] = rope[:, head * DR : (head + 1) * DR]
-    biases = outs[1:-1]
+    biases = outs[1:-2]
     fetches[3].wait()
     row = lax.broadcasted_iota(jnp.int32, (rows, 1), 0)
     query_pos = jnp.where(
@@ -348,9 +349,12 @@
         functools.partial(prepare_kernel, order),
         out_shape=[jax.ShapeDtypeStruct((query_rows // 2, DC + DR), BF16)]
         + [jax.ShapeDtypeStruct(shape, F32) for shape in bias_shapes]
-        + [jax.ShapeDtypeStruct((depth, width + DC // depth * key_up.shape[1]), BF16)],
-        in_specs=[hbm()] * 6 + [anywhere()],
-        out_specs=[vmem()] * (len(bias_shapes) + 2),
+        + [
+            jax.ShapeDtypeStruct((depth, width + DC // depth * key_up.shape[1]), BF16),
+            jax.ShapeDtypeStruct(packed.shape, BF16),
+        ],
+        in_specs=[hbm()] * 6 + [vmem()],
+        out_specs=[vmem()] * (len(bias_shapes) + 3),
         scratch_shapes=[
             pltpu.VMEM(queries_nope.shape, BF16),
             pltpu.VMEM(queries_rope.shape, BF16),
@@ -363,14 +367,15 @@
         cost_estimate=cost(PREPARE_COST),
         name="prepare",
     )(*in_hbm(queries_nope, queries_rope, key_up, span_order, value_up, out_proj), packed)
-    queries, biases = outs[0], outs[1:-1]
-    weights_other = other_core(outs[-1])
+    queries, biases = outs[0], outs[1:-2]
+    weights, packed_after = outs[-2:]
+    weights_other = other_core(weights)
     both = [queries, other_core(queries)]
 
     if direct:
         far = partners(packed, FAR)
-        near = partners(packed, NEAR)
-        corner = partners(packed, CORNER, cores=(1,))
+        near = partners(packed_after, NEAR)
+        corner = partners(packed_after, CORNER, cores=(1,))
         relayed = partners(far, (1, 1))
         gated = pl.pallas_call(
             gate_kernel,

time: 20.1 us -> 21.4 us (1.065)
  starting transfers between devices: 10.5 us -> 12.5 us
  waiting for transfers between devices: 2.29 us -> 1.52 us
    ppermute x6, starting transfers between devices: 2.63 us -> 4.67 us  [other_core(): return lax.ppermute(array, 'heads', [(0, 1), (1, 0)])]
    ppermute x4, waiting for transfers between devices: 2.07 us -> 1.31 us  [partners(): return lax.ppermute(array, ('ctx', 'heads'), pairs)]
  transfers between devices with their start and end apart: 10 -> 10, of which waited for: 3 -> 2; matrix products, arithmetic and copies ran while one was open for 0% -> 0% of each run, Pallas kernels for 18% -> 17%
where the time goes in v17:
time: 21.4 us; the launch traced here: 21.1 us
  starting transfers between devices  12.5 us (58%)
  Pallas kernels  7.01 us (33%)
  waiting for transfers between devices  1.52 us (7%)
    ppermute x4, starting transfers between devices, partners(): return lax.ppermute(array, ('ctx', 'heads'), pairs)  7.82 us
    ppermute x6, starting transfers between devices, other_core(): return lax.ppermute(array, 'heads', [(0, 1), (1, 0)])  4.67 us
    pallas_call x1, Pallas kernels, per_device(): pl.pallas_call(functools.partial(finish_kernel, heads, len(last)), out_sh...  2.5 us
    pallas_call x2, Pallas kernels, attend(): pl.pallas_call(functools.partial(chunks_kernel, len(chunks), len(old), pa...  1.83 us
    pallas_call x1, Pallas kernels, per_device(): pl.pallas_call(functools.partial(prepare_kernel, order), out_shape=[jax.S...  1.77 us
    ppermute x4, waiting for transfers between devices, partners(): return lax.ppermute(array, ('ctx', 'heads'), pairs)  1.31 us
    pallas_call x1, Pallas kernels, per_device(): pl.pallas_call(pack_kernel, out_shape=jax.ShapeDtypeStruct((2 * rows + ro...  0.91 us
  transfers between devices with their start and end apart: 10, of which 2 were waited for; matrix products, arithmetic and copies ran while one was open for 0% of the time, Pallas kernels for 17%

profile of v17, /device:TPU:0, one launch (start us, length us, event | category | flops | bytes accessed | tf_op | source)
XLA Modules:
  0.0 21.1 jit_solution(9125844832341855495)
XLA Ops:
  0.0 0.9 %pack.1.refs_6_.rest_3_ = bf16[216,256]{1,0:T(8,128)(2,1)S(1)} custom-call(bf16[96,512]{1,0:T(8,128)(2,1)} %latent.1, bf16[64,96]{1,0:T(8,128)(2,1)} %bitcast.1), custom_call_target="tpu_custom_call" | custom-call | tf_op jit(solution)/shard_map/pack/pallas_call | solution.py:326
  0.9 4.1 %collective-permute-start.5 = (bf16[216,256]{1,0:T(8,128)(2,1)S(1)}, bf16[216,256]{1,0:T(8,128)(2,1)S(1)}, u32[]{:S(2)}, u32[]{:S(2)}) collective-permute-start(bf16[216,256]{1,0:T(8,128)(2,1)S(1)} %pack.1.refs_6_.rest_3_), channel_id=1, source_target_pairs={{0,8},{1,13},{2,10},{3,15},{4,12},{5,9},{6,14},{7,11},{8,0},{9,5},... | collective-permute-start | bytes 331784 | tf_op jit(solution)/shard_map/ppermute | solution.py:311
  5.0 1.8 %prepare.1 = (bf16[192,576]{1,0:T(8,128)(2,1)S(1)}, f32[1,96,192]{2,1,0:T(8,128)S(1)}, f32[1,96,480]{2,1,0:T(8,128)S(1)}, f32[1,96,96]{2,1,0:T(8,128)S(1)}, bf16...) custom-call(bf16[96,256]{1,0:T(8,128)(2,1)} %refs_0_.1, bf16[96,128]{1,0:T(8,128)(2,1)} %refs_1_.1, ...), custom_call_target="tpu_custom_call" | custom-call | tf_op jit(solution)/shard_map/prepare/pallas_call | solution.py:348
  6.8 1.6 %collective-permute-start.3 = (bf16[216,256]{1,0:T(8,128)(2,1)S(1)}, bf16[216,256]{1,0:T(8,128)(2,1)S(1)}, u32[]{:S(2)}, u32[]{:S(2)}) collective-permute-start(bf16[216,256]{1,0:T(8,128)(2,1)S(1)} %get-tuple-element.20), channel_id=1, source_target_pairs={{0,4},{1,3},{2,6},{3,1},{4,0},{5,7},{6,2},{7,5},{8,12},{9,11},{10,... | collective-permute-start | bytes 331784 | tf_op jit(solution)/shard_map/ppermute | solution.py:311
  8.4 0.7 %collective-permute-start.1 = (bf16[216,256]{1,0:T(8,128)(2,1)S(1)}, bf16[216,256]{1,0:T(8,128)(2,1)S(1)}, u32[]{:S(2)}, u32[]{:S(2)}) collective-permute-start(bf16[216,256]{1,0:T(8,128)(2,1)S(1)} %get-tuple-element.20), channel_id=1, source_target_pairs={{1,7},{3,5},{5,3},{7,1},{9,15},{11,13},{13,11},{15,9},{17,23},{19,... | collective-permute-start | bytes 331784 | tf_op jit(solution)/shard_map/ppermute | solution.py:311
  9.1 1.5 %collective-permute-start = (bf16[192,576]{1,0:T(8,128)(2,1)S(1)}, bf16[192,576]{1,0:T(8,128)(2,1)S(1)}, u32[]{:S(2)}, u32[]{:S(2)}) collective-permute-start(bf16[192,576]{1,0:T(8,128)(2,1)S(1)} %get-tuple-element.18.rest_0_), channel_id=1, source_target_pairs={{0,1},{1,0},{2,3},{3,2},{4,5},{5,4},{6,7},{7,6},{8,9},{9,8},{10,11... | collective-permute-start | bytes 663560 | tf_op jit(solution)/shard_map/ppermute | solution.py:303
  10.6 0.1 collective-permute-start.9
  10.7 0.0 collective-permute-done.5.chunk.rest_6_
  10.7 1.4 %collective-permute-start.7 = (bf16[216,256]{1,0:T(8,128)(2,1)S(1)}, bf16[216,256]{1,0:T(8,128)(2,1)S(1)}, u32[]{:S(2)}, u32[]{:S(2)}) collective-permute-start(bf16[216,256]{1,0:T(8,128)(2,1)S(1)} %collective-permute-done.5.chunk.rest_6_), channel_id=1, source_target_pairs={{0,2},{1,3},{2,0},{3,1},{4,6},{5,7},{6,4},{7,5},{8,10},{9,11},{10,... | collective-permute-start | bytes 331784 | tf_op jit(solution)/shard_map/ppermute | solution.py:311
  12.1 0.0 collective-permute-done.3.rest_4_
  12.1 0.0 collective-permute-start.4
  12.1 0.0 collective-permute-done.1.rest_3_
  12.1 3.0 %collective-permute-start.2 = (bf16[216,256]{1,0:T(8,128)(2,1)S(1)}, bf16[216,256]{1,0:T(8,128)(2,1)S(1)}, u32[]{:S(2)}, u32[]{:S(2)}) collective-permute-start(bf16[216,256]{1,0:T(8,128)(2,1)S(1)} %collective-permute-done.1.rest_3_), channel_id=1, source_target_pairs={{0,1},{1,0},{2,3},{3,2},{4,5},{5,4},{6,7},{7,6},{8,9},{9,8},{10,11... | collective-permute-start | bytes 331784 | tf_op jit(solution)/shard_map/ppermute | solution.py:303
  15.1 0.0 collective-permute-done.rest_1_
  15.1 0.7 %first.1 = (f32[384,1]{1,0:T(8,128)S(1)}, f32[384,1]{1,0:T(8,128)S(1)}, f32[384,512]{1,0:T(8,128)S(1)}, bf16[216,256]{1,0:T(8,128)(2,1)S(1)}) custom-call(bf16[192,576]{1,0:T(8,128)(2,1)S(1)} %get-tuple-element.18.rest_0_, bf16[192,576]{1,0:T(8,128)(2,1)S(1)} %collective-permute-done.rest_1_, f32[1,96,192]{2,1,0:T(8,128)S(1)} %get-tuple-element.21.rest_2_, ...), custom_call_target="tpu_custom_call" | custom-call | flops 22000001024 | tf_op jit(solution)/shard_map/first/pallas_call | solution.py:314
  15.9 0.0 copy-start
  15.9 0.0 copy-start.1
  15.9 0.1 collective-permute-start.6
  16.0 1.3 %collective-permute-done.7.rest_8_ = bf16[216,256]{1,0:T(8,128)(2,1)S(1)} collective-permute-done((bf16[216,256]{1,0:T(8,128)(2,1)S(1)}, bf16[216,256]{1,0:T(8,128)(2,1)S(1)}, u32[]{:S(2)}, u32[]{:S(2)}) %collective-permute-start.7) | collective-permute-done | bytes 110624 | tf_op jit(solution)/shard_map/ppermute | solution.py:311
  17.3 0.0 collective-permute-start.8
  17.3 0.0 collective-permute-done.4.rest_5_
  17.3 0.0 collective-permute-done.2.rest_4_
  17.3 0.0 collective-permute-done.6.rest_7_
  17.3 1.1 %second.1 = (f32[384,1]{1,0:T(8,128)S(1)}, f32[384,1]{1,0:T(8,128)S(1)}, f32[384,512]{1,0:T(8,128)S(1)}) custom-call(bf16[192,576]{1,0:T(8,128)(2,1)S(1)} %get-tuple-element.18.rest_0_, bf16[192,576]{1,0:T(8,128)(2,1)S(1)} %collective-permute-done.rest_1_, f32[1,96,480]{2,1,0:T(8,128)S(1)} %get-tuple-element.19.rest_2_, ...), custom_call_target="tpu_custom_call" | custom-call | flops 1100000000 | tf_op jit(solution)/shard_map/second/pallas_call | solution.py:314
  18.4 0.2 collective-permute-done.8.rest_6_
  18.6 0.0 collective-permute-done.9.rest_9_
  18.6 0.0 copy-done
  18.6 0.0 copy-done.1
  18.6 2.5 %finish.1 = bf16[96,3584]{1,0:T(8,128)(2,1)} custom-call(bf16[192,576]{1,0:T(8,128)(2,1)S(1)} %get-tuple-element.18.rest_0_, bf16[192,576]{1,0:T(8,128)(2,1)S(1)} %collective-permute-done.rest_1_, f32[384,1]{1,0:T(8,128)S(1)} %get-tuple-element.26.rest_2_, f32[384,1]{1,0:T(8,128)S(1)} %get-tuple-element.27.rest_3_, ...), custom_call_target="tpu_custom_call" | custom-call | tf_op jit(solution)/shard_map/finish/pallas_call | solution.py:415
  (1 shorter events, 0.0 us)
Async XLA Ops:
  0.9 9.8 %collective-permute-start.5 = (bf16[216,256]{1,0:T(8,128)(2,1)S(1)}, bf16[216,256]{1,0:T(8,128)(2,1)S(1)}, u32[]{:S(2)}, u32[]{:S(2)}) collective-permute-start(bf16[216,256]{1,0:T(8,128)(2,1)S(1)} %pack.1.refs_6_.rest_3_), channel_id=1, source_target_pairs={{0,8},{1,13},{2,10},{3,15},{4,12},{5,9},{6,14},{7,11},{8,0},{9,5},... | collective-permute-start | bytes 331784 | tf_op jit(solution)/shard_map/ppermute | solution.py:311
  6.8 5.3 %collective-permute-start.3 = (bf16[216,256]{1,0:T(8,128)(2,1)S(1)}, bf16[216,256]{1,0:T(8,128)(2,1)S(1)}, u32[]{:S(2)}, u32[]{:S(2)}) collective-permute-start(bf16[216,256]{1,0:T(8,128)(2,1)S(1)} %get-tuple-element.20), channel_id=1, source_target_pairs={{0,4},{1,3},{2,6},{3,1},{4,0},{5,7},{6,2},{7,5},{8,12},{9,11},{10,... | collective-permute-start | bytes 331784 | tf_op jit(solution)/shard_map/ppermute | solution.py:311
  8.4 3.7 %collective-permute-start.1 = (bf16[216,256]{1,0:T(8,128)(2,1)S(1)}, bf16[216,256]{1,0:T(8,128)(2,1)S(1)}, u32[]{:S(2)}, u32[]{:S(2)}) collective-permute-start(bf16[216,256]{1,0:T(8,128)(2,1)S(1)} %get-tuple-element.20), channel_id=1, source_target_pairs={{1,7},{3,5},{5,3},{7,1},{9,15},{11,13},{13,11},{15,9},{17,23},{19,... | collective-permute-start | bytes 331784 | tf_op jit(solution)/shard_map/ppermute | solution.py:311
  9.1 6.0 %collective-permute-start = (bf16[192,576]{1,0:T(8,128)(2,1)S(1)}, bf16[192,576]{1,0:T(8,128)(2,1)S(1)}, u32[]{:S(2)}, u32[]{:S(2)}) collective-permute-start(bf16[192,576]{1,0:T(8,128)(2,1)S(1)} %get-tuple-element.18.rest_0_), channel_id=1, source_target_pairs={{0,1},{1,0},{2,3},{3,2},{4,5},{5,4},{6,7},{7,6},{8,9},{9,8},{10,11... | collective-permute-start | bytes 663560 | tf_op jit(solution)/shard_map/ppermute | solution.py:303
  10.6 8.0 %collective-permute-start.9 = (bf16[256,4096]{1,0:T(8,128)(2,1)S(1)}, bf16[256,4096]{1,0:T(8,128)(2,1)S(1)}, u32[]{:S(2)}, u32[]{:S(2)}) collective-permute-start(bf16[256,4096]{1,0:T(8,128)(2,1)S(1)} %get-tuple-element.30), channel_id=1, source_target_pairs={{0,1},{1,0},{2,3},{3,2},{4,5},{5,4},{6,7},{7,6},{8,9},{9,8},{10,11... | collective-permute-start | bytes 6291464 | tf_op jit(solution)/shard_map/ppermute | solution.py:303
  10.7 6.6 %collective-permute-start.7 = (bf16[216,256]{1,0:T(8,128)(2,1)S(1)}, bf16[216,256]{1,0:T(8,128)(2,1)S(1)}, u32[]{:S(2)}, u32[]{:S(2)}) collective-permute-start(bf16[216,256]{1,0:T(8,128)(2,1)S(1)} %collective-permute-done.5.chunk.rest_6_), channel_id=1, source_target_pairs={{0,2},{1,3},{2,0},{3,1},{4,6},{5,7},{6,4},{7,5},{8,10},{9,11},{10,... | collective-permute-start | bytes 331784 | tf_op jit(solution)/shard_map/ppermute | solution.py:311
  12.1 5.2 %collective-permute-start.4 = (bf16[216,256]{1,0:T(8,128)(2,1)S(1)}, bf16[216,256]{1,0:T(8,128)(2,1)S(1)}, u32[]{:S(2)}, u32[]{:S(2)}) collective-permute-start(bf16[216,256]{1,0:T(8,128)(2,1)S(1)} %collective-permute-done.3.rest_4_), channel_id=1, source_target_pairs={{0,1},{1,0},{2,3},{3,2},{4,5},{5,4},{6,7},{7,6},{8,9},{9,8},{10,11... | collective-permute-start | bytes 331784 | tf_op jit(solution)/shard_map/ppermute | solution.py:303
  12.1 5.2 %collective-permute-start.2 = (bf16[216,256]{1,0:T(8,128)(2,1)S(1)}, bf16[216,256]{1,0:T(8,128)(2,1)S(1)}, u32[]{:S(2)}, u32[]{:S(2)}) collective-permute-start(bf16[216,256]{1,0:T(8,128)(2,1)S(1)} %collective-permute-done.1.rest_3_), channel_id=1, source_target_pairs={{0,1},{1,0},{2,3},{3,2},{4,5},{5,4},{6,7},{7,6},{8,9},{9,8},{10,11... | collective-permute-start | bytes 331784 | tf_op jit(solution)/shard_map/ppermute | solution.py:303
  15.9 2.7 %copy-start = (bf16[256,7168]{1,0:T(8,128)(2,1)S(1)}, bf16[256,7168]{1,0:T(8,128)(2,1)}, u32[]{:S(2)}) copy-start(bf16[256,7168]{1,0:T(8,128)(2,1)} %rest_8_.1) | copy-start | bytes 11010052
  15.9 2.7 %copy-start.1 = (bf16[512,256]{1,0:T(8,128)(2,1)S(1)}, bf16[512,256]{1,0:T(8,128)(2,1)}, u32[]{:S(2)}) copy-start(bf16[512,256]{1,0:T(8,128)(2,1)} %rest_7_.1) | copy-start | bytes 786436
  15.9 1.4 %collective-permute-start.6 = (bf16[216,256]{1,0:T(8,128)(2,1)S(1)}, bf16[216,256]{1,0:T(8,128)(2,1)S(1)}, u32[]{:S(2)}, u32[]{:S(2)}) collective-permute-start(bf16[216,256]{1,0:T(8,128)(2,1)S(1)} %get-tuple-element.22), channel_id=1, source_target_pairs={{0,1},{1,0},{2,3},{3,2},{4,5},{5,4},{6,7},{7,6},{8,9},{9,8},{10,11... | collective-permute-start | bytes 331784 | tf_op jit(solution)/shard_map/ppermute | solution.py:303
  17.3 1.3 %collective-permute-start.8 = (bf16[216,256]{1,0:T(8,128)(2,1)S(1)}, bf16[216,256]{1,0:T(8,128)(2,1)S(1)}, u32[]{:S(2)}, u32[]{:S(2)}) collective-permute-start(bf16[216,256]{1,0:T(8,128)(2,1)S(1)} %collective-permute-done.7.rest_8_), channel_id=1, source_target_pairs={{0,1},{1,0},{2,3},{3,2},{4,5},{5,4},{6,7},{7,6},{8,9},{9,8},{10,11... | collective-permute-start | bytes 331784 | tf_op jit(solution)/shard_map/ppermute | solution.py:303

commit v18 on v16

--- a/solution.py
+++ b/solution.py
@@ -245,37 +245,31 @@
         for index, chunk in enumerate(chunks):
             unpack(chunk, keys, index * rows)
         running = attend_block(queries, keys, bias[0][0], running)
-    mixed = (running[2] / running[1]).astype(BF16)
+    mixed = (running[2] * (1.0 / running[1])).astype(BF16)
     half = heads // 2
     depth = weights.shape[0]
     base = lax.axis_index("heads") * width
-    sides = []
-    for group in range(2):
-        parts = []
-        for head in range(half):
-            first = (group * half + head) * rows
-            per_head = 0.0
-            for block in range(DC // depth):
-                if group == 0:
-                    value = value_own[block * depth : (block + 1) * depth, head * DH : (head + 1) * DH]
-                else:
-                    start = width + (block * half + head) * DH
-                    value = weights[:, start : start + DH]
-                per_head = per_head + jnp.dot(
-                    mixed[first : first + rows, block * depth : (block + 1) * depth],
-                    value,
-                    preferred_element_type=F32,
-                )
-            parts.append(per_head.astype(BF16))
-        sides.append(jnp.concatenate(parts, axis=1))
+    parts = []
+    for place in range(heads):
+        group, head = divmod(place, half)
+        if group == 0:
+            value = value_own[:, head * DH : (head + 1) * DH]
+        else:
+            starts = [width + (block * half + head) * DH for block in range(DC // depth)]
+            value = jnp.concatenate([weights[:, start : start + DH] for start in starts], axis=0)
+        per_head = jnp.dot(
+            mixed[place * rows : (place + 1) * rows], value, preferred_element_type=F32
+        )
+        parts.append(per_head.astype(BF16))
+    heads_out = jnp.concatenate(parts, axis=1)
     tiles = out_sems.shape[0]
     tile = width // tiles
     sends = []
     for index in range(tiles):
         part = pl.ds(index * tile, tile)
         own = proj_own[:, pl.ds(pl.multiple_of(base + index * tile, 128), tile)]
-        out = jnp.dot(sides[0], own, preferred_element_type=F32)
-        out = out + jnp.dot(sides[1], weights[:, part], preferred_element_type=F32)
+        both = jnp.concatenate([own, weights[:, part]], axis=0)
+        out = jnp.dot(heads_out, both, preferred_element_type=F32)
         out_tiles[:, part] = out.astype(BF16)
         sends.append(
             pltpu.make_async_copy(out_tiles.at[:, part], out_ref.at[:, part], out_sems.at[index])

time: 20.1 us -> 20.1 us (level)
  no operation moved by 1% of the time
where the time goes in v18:
time: 20.1 us; the launch traced here: 19.8 us
  starting transfers between devices  10.5 us (52%)
  Pallas kernels  6.98 us (35%)
  waiting for transfers between devices  2.29 us (11%)
    ppermute x4, starting transfers between devices, partners(): return lax.ppermute(array, ('ctx', 'heads'), pairs)  7.82 us
    ppermute x6, starting transfers between devices, other_core(): return lax.ppermute(array, 'heads', [(0, 1), (1, 0)])  2.63 us
    pallas_call x1, Pallas kernels, per_device(): pl.pallas_call(functools.partial(finish_kernel, heads, len(last)), out_sh...  2.47 us
    ppermute x4, waiting for transfers between devices, partners(): return lax.ppermute(array, ('ctx', 'heads'), pairs)  2.07 us
    pallas_call x2, Pallas kernels, attend(): pl.pallas_call(functools.partial(chunks_kernel, len(chunks), len(old), pa...  1.83 us
    pallas_call x1, Pallas kernels, per_device(): pl.pallas_call(functools.partial(prepare_kernel, order), out_shape=[jax.S...  1.77 us
    pallas_call x1, Pallas kernels, per_device(): pl.pallas_call(pack_kernel, out_shape=jax.ShapeDtypeStruct((2 * rows + ro...  0.91 us
  transfers between devices with their start and end apart: 10, of which 3 were waited for; matrix products, arithmetic and copies ran while one was open for 0% of the time, Pallas kernels for 18%

profile of v18, /device:TPU:0, one launch (start us, length us, event | category | flops | bytes accessed | tf_op | source)
XLA Modules:
  0.0 19.8 jit_solution(8658958555359371874)
XLA Ops:
  0.0 0.9 %pack.1.refs_6_.rest_3_ = bf16[216,256]{1,0:T(8,128)(2,1)S(1)} custom-call(bf16[96,512]{1,0:T(8,128)(2,1)} %latent.1, bf16[64,96]{1,0:T(8,128)(2,1)} %bitcast.1), custom_call_target="tpu_custom_call" | custom-call | tf_op jit(solution)/shard_map/pack/pallas_call | solution.py:319
  0.9 4.1 %collective-permute-start.5 = (bf16[216,256]{1,0:T(8,128)(2,1)S(1)}, bf16[216,256]{1,0:T(8,128)(2,1)S(1)}, u32[]{:S(2)}, u32[]{:S(2)}) collective-permute-start(bf16[216,256]{1,0:T(8,128)(2,1)S(1)} %pack.1.refs_6_.rest_3_), channel_id=1, source_target_pairs={{0,8},{1,13},{2,10},{3,15},{4,12},{5,9},{6,14},{7,11},{8,0},{9,5},... | collective-permute-start | bytes 331784 | tf_op jit(solution)/shard_map/ppermute | solution.py:304
  5.0 1.6 %collective-permute-start.3 = (bf16[216,256]{1,0:T(8,128)(2,1)S(1)}, bf16[216,256]{1,0:T(8,128)(2,1)S(1)}, u32[]{:S(2)}, u32[]{:S(2)}) collective-permute-start(bf16[216,256]{1,0:T(8,128)(2,1)S(1)} %pack.1.refs_6_.rest_3_), channel_id=1, source_target_pairs={{0,4},{1,3},{2,6},{3,1},{4,0},{5,7},{6,2},{7,5},{8,12},{9,11},{10,... | collective-permute-start | bytes 331784 | tf_op jit(solution)/shard_map/ppermute | solution.py:304
  6.6 0.7 %collective-permute-start.1 = (bf16[216,256]{1,0:T(8,128)(2,1)S(1)}, bf16[216,256]{1,0:T(8,128)(2,1)S(1)}, u32[]{:S(2)}, u32[]{:S(2)}) collective-permute-start(bf16[216,256]{1,0:T(8,128)(2,1)S(1)} %pack.1.refs_6_.rest_3_), channel_id=1, source_target_pairs={{1,7},{3,5},{5,3},{7,1},{9,15},{11,13},{13,11},{15,9},{17,23},{19,... | collective-permute-start | bytes 331784 | tf_op jit(solution)/shard_map/ppermute | solution.py:304
  7.3 1.8 %prepare.1 = (bf16[192,576]{1,0:T(8,128)(2,1)S(1)}, f32[1,96,192]{2,1,0:T(8,128)S(1)}, f32[1,96,480]{2,1,0:T(8,128)S(1)}, f32[1,96,96]{2,1,0:T(8,128)S(1)}, bf16[256,4096]{1,0:T(8,128)(2,1)S(1)}) custom-call(bf16[96,256]{1,0:T(8,128)(2,1)} %refs_0_.1, bf16[96,128]{1,0:T(8,128)(2,1)} %refs_1_.1, bf16[512,256]{1,0:T(8,128)(2,1)} %refs_2_.1, s32[16]{0:T(128)} %refs_3_.1, ...), custom_call_target="tpu_custom_call" | custom-call | tf_op jit(solution)/shard_map/prepare/pallas_call | solution.py:341
  9.0 1.5 %collective-permute-start = (bf16[192,576]{1,0:T(8,128)(2,1)S(1)}, bf16[192,576]{1,0:T(8,128)(2,1)S(1)}, u32[]{:S(2)}, u32[]{:S(2)}) collective-permute-start(bf16[192,576]{1,0:T(8,128)(2,1)S(1)} %get-tuple-element.17.rest_0_), channel_id=1, source_target_pairs={{0,1},{1,0},{2,3},{3,2},{4,5},{5,4},{6,7},{7,6},{8,9},{9,8},{10,11... | collective-permute-start | bytes 663560 | tf_op jit(solution)/shard_map/ppermute | solution.py:296
  10.6 0.1 collective-permute-start.9
  10.6 0.1 collective-permute-done.5.chunk.rest_6_
  10.7 1.5 %collective-permute-start.7 = (bf16[216,256]{1,0:T(8,128)(2,1)S(1)}, bf16[216,256]{1,0:T(8,128)(2,1)S(1)}, u32[]{:S(2)}, u32[]{:S(2)}) collective-permute-start(bf16[216,256]{1,0:T(8,128)(2,1)S(1)} %collective-permute-done.5.chunk.rest_6_), channel_id=1, source_target_pairs={{0,2},{1,3},{2,0},{3,1},{4,6},{5,7},{6,4},{7,5},{8,10},{9,11},{10,... | collective-permute-start | bytes 331784 | tf_op jit(solution)/shard_map/ppermute | solution.py:304
  12.2 0.0 collective-permute-done.3.rest_4_
  12.2 0.0 collective-permute-start.4
  12.2 0.0 collective-permute-done.1.rest_3_
  12.2 1.0 %collective-permute-start.2 = (bf16[216,256]{1,0:T(8,128)(2,1)S(1)}, bf16[216,256]{1,0:T(8,128)(2,1)S(1)}, u32[]{:S(2)}, u32[]{:S(2)}) collective-permute-start(bf16[216,256]{1,0:T(8,128)(2,1)S(1)} %collective-permute-done.1.rest_3_), channel_id=1, source_target_pairs={{0,1},{1,0},{2,3},{3,2},{4,5},{5,4},{6,7},{7,6},{8,9},{9,8},{10,11... | collective-permute-start | bytes 331784 | tf_op jit(solution)/shard_map/ppermute | solution.py:296
  13.2 0.0 collective-permute-done.rest_1_
  13.2 0.7 %first.1 = (f32[384,1]{1,0:T(8,128)S(1)}, f32[384,1]{1,0:T(8,128)S(1)}, f32[384,512]{1,0:T(8,128)S(1)}, bf16[216,256]{1,0:T(8,128)(2,1)S(1)}) custom-call(bf16[192,576]{1,0:T(8,128)(2,1)S(1)} %get-tuple-element.17.rest_0_, bf16[192,576]{1,0:T(8,128)(2,1)S(1)} %collective-permute-done.rest_1_, f32[1,96,192]{2,1,0:T(8,128)S(1)} %get-tuple-element.19.rest_2_, ...), custom_call_target="tpu_custom_call" | custom-call | flops 22000001024 | tf_op jit(solution)/shard_map/first/pallas_call | solution.py:307
  13.9 0.0 copy-start
  14.0 0.0 copy-start.1
  14.0 0.1 collective-permute-start.6
  14.0 2.0 %collective-permute-done.7.rest_8_ = bf16[216,256]{1,0:T(8,128)(2,1)S(1)} collective-permute-done((bf16[216,256]{1,0:T(8,128)(2,1)S(1)}, bf16[216,256]{1,0:T(8,128)(2,1)S(1)}, u32[]{:S(2)}, u32[]{:S(2)}) %collective-permute-start.7) | collective-permute-done | bytes 110624 | tf_op jit(solution)/shard_map/ppermute | solution.py:304
  16.0 0.0 collective-permute-start.8
  16.0 0.0 collective-permute-done.4.rest_5_
  16.0 0.0 collective-permute-done.2.rest_4_
  16.1 0.0 collective-permute-done.6.rest_7_
  16.1 1.1 %second.1 = (f32[384,1]{1,0:T(8,128)S(1)}, f32[384,1]{1,0:T(8,128)S(1)}, f32[384,512]{1,0:T(8,128)S(1)}) custom-call(bf16[192,576]{1,0:T(8,128)(2,1)S(1)} %get-tuple-element.17.rest_0_, bf16[192,576]{1,0:T(8,128)(2,1)S(1)} %collective-permute-done.rest_1_, f32[1,96,480]{2,1,0:T(8,128)S(1)} %get-tuple-element.18.rest_2_, ...), custom_call_target="tpu_custom_call" | custom-call | flops 1100000000 | tf_op jit(solution)/shard_map/second/pallas_call | solution.py:307
  17.2 0.2 %collective-permute-done.8.rest_6_ = bf16[216,256]{1,0:T(8,128)(2,1)S(1)} collective-permute-done((bf16[216,256]{1,0:T(8,128)(2,1)S(1)}, bf16[216,256]{1,0:T(8,128)(2,1)S(1)}, u32[]{:S(2)}, u32[]{:S(2)}) %collective-permute-start.8) | collective-permute-done | bytes 110624 | tf_op jit(solution)/shard_map/ppermute | solution.py:296
  17.4 0.0 collective-permute-done.9.rest_9_
  17.4 0.0 copy-done
  17.4 0.0 copy-done.1
  17.4 2.5 %finish.1 = bf16[96,3584]{1,0:T(8,128)(2,1)} custom-call(bf16[192,576]{1,0:T(8,128)(2,1)S(1)} %get-tuple-element.17.rest_0_, bf16[192,576]{1,0:T(8,128)(2,1)S(1)} %collective-permute-done.rest_1_, f32[384,1]{1,0:T(8,128)S(1)} %get-tuple-element.24.rest_2_, f32[384,1]{1,0:T(8,128)S(1)} %get-tuple-element.25.rest_3_, ...), custom_call_target="tpu_custom_call" | custom-call | tf_op jit(solution)/shard_map/finish/pallas_call | solution.py:404
  (1 shorter events, 0.0 us)
Async XLA Ops:
  0.9 9.8 %collective-permute-start.5 = (bf16[216,256]{1,0:T(8,128)(2,1)S(1)}, bf16[216,256]{1,0:T(8,128)(2,1)S(1)}, u32[]{:S(2)}, u32[]{:S(2)}) collective-permute-start(bf16[216,256]{1,0:T(8,128)(2,1)S(1)} %pack.1.refs_6_.rest_3_), channel_id=1, source_target_pairs={{0,8},{1,13},{2,10},{3,15},{4,12},{5,9},{6,14},{7,11},{8,0},{9,5},... | collective-permute-start | bytes 331784 | tf_op jit(solution)/shard_map/ppermute | solution.py:304
  5.0 7.2 %collective-permute-start.3 = (bf16[216,256]{1,0:T(8,128)(2,1)S(1)}, bf16[216,256]{1,0:T(8,128)(2,1)S(1)}, u32[]{:S(2)}, u32[]{:S(2)}) collective-permute-start(bf16[216,256]{1,0:T(8,128)(2,1)S(1)} %pack.1.refs_6_.rest_3_), channel_id=1, source_target_pairs={{0,4},{1,3},{2,6},{3,1},{4,0},{5,7},{6,2},{7,5},{8,12},{9,11},{10,... | collective-permute-start | bytes 331784 | tf_op jit(solution)/shard_map/ppermute | solution.py:304
  6.6 5.6 %collective-permute-start.1 = (bf16[216,256]{1,0:T(8,128)(2,1)S(1)}, bf16[216,256]{1,0:T(8,128)(2,1)S(1)}, u32[]{:S(2)}, u32[]{:S(2)}) collective-permute-start(bf16[216,256]{1,0:T(8,128)(2,1)S(1)} %pack.1.refs_6_.rest_3_), channel_id=1, source_target_pairs={{1,7},{3,5},{5,3},{7,1},{9,15},{11,13},{13,11},{15,9},{17,23},{19,... | collective-permute-start | bytes 331784 | tf_op jit(solution)/shard_map/ppermute | solution.py:304
  9.0 4.2 %collective-permute-start = (bf16[192,576]{1,0:T(8,128)(2,1)S(1)}, bf16[192,576]{1,0:T(8,128)(2,1)S(1)}, u32[]{:S(2)}, u32[]{:S(2)}) collective-permute-start(bf16[192,576]{1,0:T(8,128)(2,1)S(1)} %get-tuple-element.17.rest_0_), channel_id=1, source_target_pairs={{0,1},{1,0},{2,3},{3,2},{4,5},{5,4},{6,7},{7,6},{8,9},{9,8},{10,11... | collective-permute-start | bytes 663560 | tf_op jit(solution)/shard_map/ppermute | solution.py:296
  10.6 6.8 %collective-permute-start.9 = (bf16[256,4096]{1,0:T(8,128)(2,1)S(1)}, bf16[256,4096]{1,0:T(8,128)(2,1)S(1)}, u32[]{:S(2)}, u32[]{:S(2)}) collective-permute-start(bf16[256,4096]{1,0:T(8,128)(2,1)S(1)} %get-tuple-element.28), channel_id=1, source_target_pairs={{0,1},{1,0},{2,3},{3,2},{4,5},{5,4},{6,7},{7,6},{8,9},{9,8},{10,11... | collective-permute-start | bytes 6291464 | tf_op jit(solution)/shard_map/ppermute | solution.py:296
  10.7 5.3 %collective-permute-start.7 = (bf16[216,256]{1,0:T(8,128)(2,1)S(1)}, bf16[216,256]{1,0:T(8,128)(2,1)S(1)}, u32[]{:S(2)}, u32[]{:S(2)}) collective-permute-start(bf16[216,256]{1,0:T(8,128)(2,1)S(1)} %collective-permute-done.5.chunk.rest_6_), channel_id=1, source_target_pairs={{0,2},{1,3},{2,0},{3,1},{4,6},{5,7},{6,4},{7,5},{8,10},{9,11},{10,... | collective-permute-start | bytes 331784 | tf_op jit(solution)/shard_map/ppermute | solution.py:304
  12.2 3.8 %collective-permute-start.4 = (bf16[216,256]{1,0:T(8,128)(2,1)S(1)}, bf16[216,256]{1,0:T(8,128)(2,1)S(1)}, u32[]{:S(2)}, u32[]{:S(2)}) collective-permute-start(bf16[216,256]{1,0:T(8,128)(2,1)S(1)} %collective-permute-done.3.rest_4_), channel_id=1, source_target_pairs={{0,1},{1,0},{2,3},{3,2},{4,5},{5,4},{6,7},{7,6},{8,9},{9,8},{10,11... | collective-permute-start | bytes 331784 | tf_op jit(solution)/shard_map/ppermute | solution.py:296
  12.2 3.8 %collective-permute-start.2 = (bf16[216,256]{1,0:T(8,128)(2,1)S(1)}, bf16[216,256]{1,0:T(8,128)(2,1)S(1)}, u32[]{:S(2)}, u32[]{:S(2)}) collective-permute-start(bf16[216,256]{1,0:T(8,128)(2,1)S(1)} %collective-permute-done.1.rest_3_), channel_id=1, source_target_pairs={{0,1},{1,0},{2,3},{3,2},{4,5},{5,4},{6,7},{7,6},{8,9},{9,8},{10,11... | collective-permute-start | bytes 331784 | tf_op jit(solution)/shard_map/ppermute | solution.py:296
  13.9 3.4 %copy-start = (bf16[256,7168]{1,0:T(8,128)(2,1)S(1)}, bf16[256,7168]{1,0:T(8,128)(2,1)}, u32[]{:S(2)}) copy-start(bf16[256,7168]{1,0:T(8,128)(2,1)} %rest_8_.1) | copy-start | bytes 11010052
  14.0 3.4 %copy-start.1 = (bf16[512,256]{1,0:T(8,128)(2,1)S(1)}, bf16[512,256]{1,0:T(8,128)(2,1)}, u32[]{:S(2)}) copy-start(bf16[512,256]{1,0:T(8,128)(2,1)} %rest_7_.1) | copy-start | bytes 786436
  14.0 2.1 %collective-permute-start.6 = (bf16[216,256]{1,0:T(8,128)(2,1)S(1)}, bf16[216,256]{1,0:T(8,128)(2,1)S(1)}, u32[]{:S(2)}, u32[]{:S(2)}) collective-permute-start(bf16[216,256]{1,0:T(8,128)(2,1)S(1)} %get-tuple-element.20), channel_id=1, source_target_pairs={{0,1},{1,0},{2,3},{3,2},{4,5},{5,4},{6,7},{7,6},{8,9},{9,8},{10,11... | collective-permute-start | bytes 331784 | tf_op jit(solution)/shard_map/ppermute | solution.py:296
  16.0 1.3 %collective-permute-start.8 = (bf16[216,256]{1,0:T(8,128)(2,1)S(1)}, bf16[216,256]{1,0:T(8,128)(2,1)S(1)}, u32[]{:S(2)}, u32[]{:S(2)}) collective-permute-start(bf16[216,256]{1,0:T(8,128)(2,1)S(1)} %collective-permute-done.7.rest_8_), channel_id=1, source_target_pairs={{0,1},{1,0},{2,3},{3,2},{4,5},{5,4},{6,7},{7,6},{8,9},{9,8},{10,11... | collective-permute-start | bytes 331784 | tf_op jit(solution)/shard_map/ppermute | solution.py:296

commit v19 on v18

--- a/solution.py
+++ b/solution.py
@@ -15,7 +15,7 @@
 F32 = jnp.float32
 MASKED = -1e30
 BLOCK_CHUNKS = 8
-PREPARE_COST, GATE_COST, FIRST_COST, SECOND_COST = 0, 3, 20, 1
+PREPARE_COST, GATE_COST, RELAY_COST, FIRST_COST, SECOND_COST = 0, 6, 0, 20, 1
 SMALL_VMEM = 20 * 1024 * 1024
 LARGE_VMEM = 56 * 1024 * 1024
 FAR = (4, 6)
@@ -68,8 +68,8 @@
         fetch.wait()
 
 
-def gate_kernel(chunk, out_ref):
-    out_ref[...] = chunk[...]
+def gate_kernel(chunk, *refs):
+    refs[-1][...] = chunk[...]
 
 
 def unpack(chunk, keys, base, other=None):
@@ -186,7 +186,7 @@
     return top, total, added
 
 
-def chunks_kernel(chunk_count, old_count, paired, *rest):
+def chunks_kernel(chunk_count, old_count, *rest):
     queries, bias, rest = rest[:2], rest[2], rest[3:]
     chunks, rest = rest[:chunk_count], rest[chunk_count:]
     old, rest = rest[:old_count], rest[old_count:]
@@ -196,12 +196,8 @@
         rest = rest[1:4] + rest[5:]
     running, keys = rest[:3], rest[3]
     rows = bias.shape[1]
-    if paired:
-        unpack(chunks[0], keys, 0, chunks[1])
-        chunks = chunks[1:]
     for index, chunk in enumerate(chunks):
-        if index or not paired:
-            unpack(chunk, keys, index * rows)
+        unpack(chunk, keys, index * rows)
     before = [state[...] for state in old] if old else None
     values = attend_block(queries, keys, bias[0], before)
     for state, value in zip(running, values):
@@ -242,8 +238,9 @@
     rows, width = out_ref.shape
     running = (top[...], total[...], context[...])
     if chunk_count:
-        for index, chunk in enumerate(chunks):
-            unpack(chunk, keys, index * rows)
+        unpack(chunks[0], keys, 0, chunks[1])
+        for index, chunk in enumerate(chunks[2:]):
+            unpack(chunk, keys, (1 + index) * rows)
         running = attend_block(queries, keys, bias[0][0], running)
     mixed = (running[2] * (1.0 / running[1])).astype(BF16)
     half = heads // 2
@@ -303,9 +300,20 @@
         ]
         return lax.ppermute(array, ("ctx", "heads"), pairs)
 
-    def attend(name, estimate, queries, bias, chunks, old=(), passed=(), paired=False):
+    def gate(name, estimate, *chunks):
         return pl.pallas_call(
-            functools.partial(chunks_kernel, len(chunks), len(old), paired),
+            gate_kernel,
+            out_shape=jax.ShapeDtypeStruct(chunks[0].shape, BF16),
+            in_specs=[vmem()] * len(chunks),
+            out_specs=vmem(),
+            compiler_params=small,
+            cost_estimate=cost(estimate),
+            name=name,
+        )(*chunks)
+
+    def attend(name, estimate, queries, bias, chunks, old=(), passed=()):
+        return pl.pallas_call(
+            functools.partial(chunks_kernel, len(chunks), len(old)),
             out_shape=[jax.ShapeDtypeStruct((query_rows, size), F32) for size in (1, 1, DC)]
             + [jax.ShapeDtypeStruct(chunk.shape, BF16) for chunk in passed],
             in_specs=[vmem()] * (3 + len(chunks) + len(old) + len(passed)),
@@ -331,8 +339,8 @@
     if direct:
         order = [
             [(0, 0), NEAR],
-            [CORNER, NEAR[::-1], FAR, FAR[::-1], RELAYED],
-            [RELAYED[::-1]],
+            [NEAR[::-1], FAR, FAR[::-1], RELAYED],
+            [CORNER, RELAYED[::-1]],
         ]
         bias_shapes = [(1, rows, len(steps) * rows) for steps in order]
     else:
@@ -364,29 +372,20 @@
     if direct:
         far = partners(packed, FAR)
         near = partners(packed, NEAR)
-        corner = partners(packed, CORNER, cores=(1,))
-        relayed = partners(far, (1, 1))
-        gated = pl.pallas_call(
-            gate_kernel,
-            out_shape=jax.ShapeDtypeStruct(far.shape, BF16),
-            in_specs=[vmem()],
-            out_specs=vmem(),
-            compiler_params=small,
-            cost_estimate=cost(GATE_COST),
-            name="gate",
-        )(far)
+        relayed = gate("relay", RELAY_COST, partners(far, (1, 1)))
+        corner = partners(near, (2, 2), cores=(1,))
+        gated = gate("gate", GATE_COST, far)
         *running, far_after = attend(
             "first", FIRST_COST, both, biases[0], [packed, near], passed=[gated]
         )
-        last = [other_core(relayed)]
+        last = [corner, other_core(corner), other_core(relayed)]
         running = attend(
             "second",
             SECOND_COST,
             both,
             biases[1],
-            [corner, other_core(corner), other_core(near), far, other_core(far_after), relayed],
+            [other_core(near), far, other_core(far_after), relayed],
             running,
-            paired=True,
         )
     else:
         last = []
@@ -408,7 +407,7 @@
         out_specs=anywhere(),
         scratch_shapes=[
             pltpu.VMEM((rows, width), BF16),
-            pltpu.VMEM((rows, DC + DR), BF16),
+            pltpu.VMEM((max(1, len(last) - 1) * rows, DC + DR), BF16),
             pltpu.SemaphoreType.DMA((tiles,)),
         ],
         compiler_params=small,

time: 20.1 us -> 22.3 us (1.11)
  starting transfers between devices: 10.5 us -> 13 us
  waiting for transfers between devices: 2.29 us -> 1.8 us
    ppermute x6, starting transfers between devices: 2.63 us -> 5.1 us  [other_core(): return lax.ppermute(array, 'heads', [(0, 1), (1, 0)])]
    ppermute x4, waiting for transfers between devices: 2.07 us -> 1.78 us  [partners(): return lax.ppermute(array, ('ctx', 'heads'), pairs)]
    pallas_call x3 -> x4, Pallas kernels: 1.83 us -> 1.86 us  [the longest x2 1.85 us: attend(): pl.pallas_call(functools.partial(chunks_kernel, len(chunks), len(old)), o...]
  transfers between devices with their start and end apart: 10 -> 10, of which waited for: 3 -> 1; matrix products, arithmetic and copies ran while one was open for 0% -> 0% of each run, Pallas kernels for 18% -> 16%
where the time goes in v19:
time: 22.3 us; the launch traced here: 22.1 us
  starting transfers between devices  13 us (58%)
  Pallas kernels  7.18 us (32%)
  waiting for transfers between devices  1.8 us (8%)
    ppermute x4, starting transfers between devices, partners(): return lax.ppermute(array, ('ctx', 'heads'), pairs)  7.89 us
    ppermute x6, starting transfers between devices, other_core(): return lax.ppermute(array, 'heads', [(0, 1), (1, 0)])  5.1 us
    pallas_call x1, Pallas kernels, per_device(): pl.pallas_call(functools.partial(finish_kernel, heads, len(last)), out_sh...  2.64 us
    pallas_call x2, Pallas kernels, attend(): pl.pallas_call(functools.partial(chunks_kernel, len(chunks), len(old)), o...  1.85 us
    ppermute x4, waiting for transfers between devices, partners(): return lax.ppermute(array, ('ctx', 'heads'), pairs)  1.78 us
    pallas_call x1, Pallas kernels, per_device(): pl.pallas_call(functools.partial(prepare_kernel, order), out_shape=[jax.S...  1.76 us
    pallas_call x1, Pallas kernels, per_device(): pl.pallas_call(pack_kernel, out_shape=jax.ShapeDtypeStruct((2 * rows + ro...  0.91 us
  transfers between devices with their start and end apart: 10, of which 1 were waited for; matrix products, arithmetic and copies ran while one was open for 0% of the time, Pallas kernels for 16%

profile of v19, /device:TPU:0, one launch (start us, length us, event | category | flops | bytes accessed | tf_op | source)
XLA Modules:
  0.0 22.1 jit_solution(11261158669307045297)
XLA Ops:
  0.0 0.9 %pack.1.refs_6_.rest_3_ = bf16[216,256]{1,0:T(8,128)(2,1)S(1)} custom-call(bf16[96,512]{1,0:T(8,128)(2,1)} %latent.1, bf16[64,96]{1,0:T(8,128)(2,1)} %bitcast.1), custom_call_target="tpu_custom_call" | custom-call | tf_op jit(solution)/shard_map/pack/pallas_call | solution.py:327
  0.9 4.1 %collective-permute-start.3 = (bf16[216,256]{1,0:T(8,128)(2,1)S(1)}, bf16[216,256]{1,0:T(8,128)(2,1)S(1)}, u32[]{:S(2)}, u32[]{:S(2)}) collective-permute-start(bf16[216,256]{1,0:T(8,128)(2,1)S(1)} %pack.1.refs_6_.rest_3_), channel_id=1, source_target_pairs={{0,8},{1,13},{2,10},{3,15},{4,12},{5,9},{6,14},{7,11},{8,0},{9,5},... | collective-permute-start | bytes 331784 | tf_op jit(solution)/shard_map/ppermute | solution.py:301
  5.0 1.6 %collective-permute-start.1 = (bf16[216,256]{1,0:T(8,128)(2,1)S(1)}, bf16[216,256]{1,0:T(8,128)(2,1)S(1)}, u32[]{:S(2)}, u32[]{:S(2)}) collective-permute-start(bf16[216,256]{1,0:T(8,128)(2,1)S(1)} %pack.1.refs_6_.rest_3_), channel_id=1, source_target_pairs={{0,4},{1,3},{2,6},{3,1},{4,0},{5,7},{6,2},{7,5},{8,12},{9,11},{10,... | collective-permute-start | bytes 331784 | tf_op jit(solution)/shard_map/ppermute | solution.py:301
  6.6 1.8 %prepare.1 = (bf16[192,576]{1,0:T(8,128)(2,1)S(1)}, f32[1,96,192]{2,1,0:T(8,128)S(1)}, f32[1,96,384]{2,1,0:T(8,128)S(1)}, f32[1,96,192]{2,1,0:T(8,128)S(1)}, bf16[256,4096]{1,0:T(8,128)(2,1)S(1)}) custom-call(bf16[96,256]{1,0:T(8,128)(2,1)} %refs_0_.1, bf16[96,128]{1,0:T(8,128)(2,1)} %refs_1_.1, bf16[512,256]{1,0:T(8,128)(2,1)} %refs_2_.1, s32[16]{0:T(128)} %refs_3_.1, ...), custom_call_target="tpu_custom_call" | custom-call | tf_op jit(solution)/shard_map/prepare/pallas_call | solution.py:349
  8.4 0.3 %collective-permute-start = (bf16[192,576]{1,0:T(8,128)(2,1)S(1)}, bf16[192,576]{1,0:T(8,128)(2,1)S(1)}, u32[]{:S(2)}, u32[]{:S(2)}) collective-permute-start(bf16[192,576]{1,0:T(8,128)(2,1)S(1)} %get-tuple-element.17.rest_0_), channel_id=1, source_target_pairs={{0,1},{1,0},{2,3},{3,2},{4,5},{5,4},{6,7},{7,6},{8,9},{9,8},{10,11... | collective-permute-start | bytes 663560 | tf_op jit(solution)/shard_map/ppermute | solution.py:293
  8.6 0.3 %collective-permute-start.9 = (bf16[256,4096]{1,0:T(8,128)(2,1)S(1)}, bf16[256,4096]{1,0:T(8,128)(2,1)S(1)}, u32[]{:S(2)}, u32[]{:S(2)}) collective-permute-start(bf16[256,4096]{1,0:T(8,128)(2,1)S(1)} %get-tuple-element.28), channel_id=1, source_target_pairs={{0,1},{1,0},{2,3},{3,2},{4,5},{5,4},{6,7},{7,6},{8,9},{9,8},{10,11... | collective-permute-start | bytes 6291464 | tf_op jit(solution)/shard_map/ppermute | solution.py:293
  8.9 1.8 %collective-permute-done.3.chunk.rest_4_ = bf16[216,256]{1,0:T(8,128)(2,1)S(1)} collective-permute-done((bf16[216,256]{1,0:T(8,128)(2,1)S(1)}, bf16[216,256]{1,0:T(8,128)(2,1)S(1)}, u32[]{:S(2)}, u32[]{:S(2)}) %collective-permute-start.3) | collective-permute-done | bytes 110624 | tf_op jit(solution)/shard_map/ppermute | solution.py:301
  10.7 1.6 %collective-permute-start.5 = (bf16[216,256]{1,0:T(8,128)(2,1)S(1)}, bf16[216,256]{1,0:T(8,128)(2,1)S(1)}, u32[]{:S(2)}, u32[]{:S(2)}) collective-permute-start(bf16[216,256]{1,0:T(8,128)(2,1)S(1)} %collective-permute-done.3.chunk.rest_4_), channel_id=1, source_target_pairs={{0,2},{1,3},{2,0},{3,1},{4,6},{5,7},{6,4},{7,5},{8,10},{9,11},{10,... | collective-permute-start | bytes 331784 | tf_op jit(solution)/shard_map/ppermute | solution.py:301
  12.3 0.0 collective-permute-done.1.rest_4_
  12.3 0.0 collective-permute-start.2
  12.3 0.7 %collective-permute-start.6 = (bf16[216,256]{1,0:T(8,128)(2,1)S(1)}, bf16[216,256]{1,0:T(8,128)(2,1)S(1)}, u32[]{:S(2)}, u32[]{:S(2)}) collective-permute-start(bf16[216,256]{1,0:T(8,128)(2,1)S(1)} %collective-permute-done.1.rest_4_), channel_id=1, source_target_pairs={{1,5},{3,7},{5,1},{7,3},{9,13},{11,15},{13,9},{15,11},{17,21},{19,... | collective-permute-start | bytes 331784 | tf_op jit(solution)/shard_map/ppermute | solution.py:301
  13.0 0.0 collective-permute-done.rest_1_
  13.0 0.7 %first.1 = (f32[384,1]{1,0:T(8,128)S(1)}, f32[384,1]{1,0:T(8,128)S(1)}, f32[384,512]{1,0:T(8,128)S(1)}, bf16[216,256]{1,0:T(8,128)(2,1)S(1)}) custom-call(bf16[192,576]{1,0:T(8,128)(2,1)S(1)} %get-tuple-element.17.rest_0_, bf16[192,576]{1,0:T(8,128)(2,1)S(1)} %collective-permute-done.rest_1_, f32[1,96,192]{2,1,0:T(8,128)S(1)} %get-tuple-element.19.rest_2_, ...), custom_call_target="tpu_custom_call" | custom-call | flops 22000001024 | tf_op jit(solution)/shard_map/first/pallas_call | solution.py:315
  13.7 1.8 %collective-permute-start.4 = (bf16[216,256]{1,0:T(8,128)(2,1)S(1)}, bf16[216,256]{1,0:T(8,128)(2,1)S(1)}, u32[]{:S(2)}, u32[]{:S(2)}) collective-permute-start(bf16[216,256]{1,0:T(8,128)(2,1)S(1)} %get-tuple-element.20), channel_id=1, source_target_pairs={{0,1},{1,0},{2,3},{3,2},{4,5},{5,4},{6,7},{7,6},{8,9},{9,8},{10,11... | collective-permute-start | bytes 331784 | tf_op jit(solution)/shard_map/ppermute | solution.py:293
  15.5 0.0 collective-permute-done.5.chunk
  15.6 0.0 copy-start
  15.6 0.0 copy-start.1
  15.6 0.1 collective-permute-start.8
  15.7 0.0 collective-permute-done.6.rest_6_
  15.7 2.6 %collective-permute-start.7 = (bf16[216,256]{1,0:T(8,128)(2,1)S(1)}, bf16[216,256]{1,0:T(8,128)(2,1)S(1)}, u32[]{:S(2)}, u32[]{:S(2)}) collective-permute-start(bf16[216,256]{1,0:T(8,128)(2,1)S(1)} %collective-permute-done.6.rest_6_), channel_id=1, source_target_pairs={{0,1},{1,0},{2,3},{3,2},{4,5},{5,4},{6,7},{7,6},{8,9},{9,8},{10,11... | collective-permute-start | bytes 331784 | tf_op jit(solution)/shard_map/ppermute | solution.py:293
  18.3 0.0 collective-permute-done.2.rest_3_
  18.3 0.0 collective-permute-done.4.rest_5_
  18.3 1.1 %second.1 = (f32[384,1]{1,0:T(8,128)S(1)}, f32[384,1]{1,0:T(8,128)S(1)}, f32[384,512]{1,0:T(8,128)S(1)}) custom-call(bf16[192,576]{1,0:T(8,128)(2,1)S(1)} %get-tuple-element.17.rest_0_, bf16[192,576]{1,0:T(8,128)(2,1)S(1)} %collective-permute-done.rest_1_, f32[1,96,384]{2,1,0:T(8,128)S(1)} %get-tuple-element.18.rest_2_, ...), custom_call_target="tpu_custom_call" | custom-call | flops 1100000000 | tf_op jit(solution)/shard_map/second/pallas_call | solution.py:315
  19.4 0.0 collective-permute-done.8.rest_8_
  19.4 0.0 collective-permute-done.7.rest_7_
  19.4 0.0 collective-permute-done.9.rest_11_
  19.4 0.0 copy-done
  19.4 0.0 copy-done.1
  19.5 2.6 %finish.1 = bf16[96,3584]{1,0:T(8,128)(2,1)} custom-call(bf16[192,576]{1,0:T(8,128)(2,1)S(1)} %get-tuple-element.17.rest_0_, bf16[192,576]{1,0:T(8,128)(2,1)S(1)} %collective-permute-done.rest_1_, f32[384,1]{1,0:T(8,128)S(1)} %get-tuple-element.24.rest_2_, f32[384,1]{1,0:T(8,128)S(1)} %get-tuple-element.25.rest_3_, ...), custom_call_target="tpu_custom_call" | custom-call | tf_op jit(solution)/shard_map/finish/pallas_call | solution.py:403
  (2 shorter events, 0.0 us)
Async XLA Ops:
  0.9 9.8 %collective-permute-start.3 = (bf16[216,256]{1,0:T(8,128)(2,1)S(1)}, bf16[216,256]{1,0:T(8,128)(2,1)S(1)}, u32[]{:S(2)}, u32[]{:S(2)}) collective-permute-start(bf16[216,256]{1,0:T(8,128)(2,1)S(1)} %pack.1.refs_6_.rest_3_), channel_id=1, source_target_pairs={{0,8},{1,13},{2,10},{3,15},{4,12},{5,9},{6,14},{7,11},{8,0},{9,5},... | collective-permute-start | bytes 331784 | tf_op jit(solution)/shard_map/ppermute | solution.py:301
  5.0 7.3 %collective-permute-start.1 = (bf16[216,256]{1,0:T(8,128)(2,1)S(1)}, bf16[216,256]{1,0:T(8,128)(2,1)S(1)}, u32[]{:S(2)}, u32[]{:S(2)}) collective-permute-start(bf16[216,256]{1,0:T(8,128)(2,1)S(1)} %pack.1.refs_6_.rest_3_), channel_id=1, source_target_pairs={{0,4},{1,3},{2,6},{3,1},{4,0},{5,7},{6,2},{7,5},{8,12},{9,11},{10,... | collective-permute-start | bytes 331784 | tf_op jit(solution)/shard_map/ppermute | solution.py:301
  8.4 4.6 %collective-permute-start = (bf16[192,576]{1,0:T(8,128)(2,1)S(1)}, bf16[192,576]{1,0:T(8,128)(2,1)S(1)}, u32[]{:S(2)}, u32[]{:S(2)}) collective-permute-start(bf16[192,576]{1,0:T(8,128)(2,1)S(1)} %get-tuple-element.17.rest_0_), channel_id=1, source_target_pairs={{0,1},{1,0},{2,3},{3,2},{4,5},{5,4},{6,7},{7,6},{8,9},{9,8},{10,11... | collective-permute-start | bytes 663560 | tf_op jit(solution)/shard_map/ppermute | solution.py:293
  8.6 10.8 %collective-permute-start.9 = (bf16[256,4096]{1,0:T(8,128)(2,1)S(1)}, bf16[256,4096]{1,0:T(8,128)(2,1)S(1)}, u32[]{:S(2)}, u32[]{:S(2)}) collective-permute-start(bf16[256,4096]{1,0:T(8,128)(2,1)S(1)} %get-tuple-element.28), channel_id=1, source_target_pairs={{0,1},{1,0},{2,3},{3,2},{4,5},{5,4},{6,7},{7,6},{8,9},{9,8},{10,11... | collective-permute-start | bytes 6291464 | tf_op jit(solution)/shard_map/ppermute | solution.py:293
  10.7 4.8 %collective-permute-start.5 = (bf16[216,256]{1,0:T(8,128)(2,1)S(1)}, bf16[216,256]{1,0:T(8,128)(2,1)S(1)}, u32[]{:S(2)}, u32[]{:S(2)}) collective-permute-start(bf16[216,256]{1,0:T(8,128)(2,1)S(1)} %collective-permute-done.3.chunk.rest_4_), channel_id=1, source_target_pairs={{0,2},{1,3},{2,0},{3,1},{4,6},{5,7},{6,4},{7,5},{8,10},{9,11},{10,... | collective-permute-start | bytes 331784 | tf_op jit(solution)/shard_map/ppermute | solution.py:301
  12.3 6.0 %collective-permute-start.2 = (bf16[216,256]{1,0:T(8,128)(2,1)S(1)}, bf16[216,256]{1,0:T(8,128)(2,1)S(1)}, u32[]{:S(2)}, u32[]{:S(2)}) collective-permute-start(bf16[216,256]{1,0:T(8,128)(2,1)S(1)} %collective-permute-done.1.rest_4_), channel_id=1, source_target_pairs={{0,1},{1,0},{2,3},{3,2},{4,5},{5,4},{6,7},{7,6},{8,9},{9,8},{10,11... | collective-permute-start | bytes 331784 | tf_op jit(solution)/shard_map/ppermute | solution.py:293
  12.3 3.4 %collective-permute-start.6 = (bf16[216,256]{1,0:T(8,128)(2,1)S(1)}, bf16[216,256]{1,0:T(8,128)(2,1)S(1)}, u32[]{:S(2)}, u32[]{:S(2)}) collective-permute-start(bf16[216,256]{1,0:T(8,128)(2,1)S(1)} %collective-permute-done.1.rest_4_), channel_id=1, source_target_pairs={{1,5},{3,7},{5,1},{7,3},{9,13},{11,15},{13,9},{15,11},{17,21},{19,... | collective-permute-start | bytes 331784 | tf_op jit(solution)/shard_map/ppermute | solution.py:301
  13.7 4.6 %collective-permute-start.4 = (bf16[216,256]{1,0:T(8,128)(2,1)S(1)}, bf16[216,256]{1,0:T(8,128)(2,1)S(1)}, u32[]{:S(2)}, u32[]{:S(2)}) collective-permute-start(bf16[216,256]{1,0:T(8,128)(2,1)S(1)} %get-tuple-element.20), channel_id=1, source_target_pairs={{0,1},{1,0},{2,3},{3,2},{4,5},{5,4},{6,7},{7,6},{8,9},{9,8},{10,11... | collective-permute-start | bytes 331784 | tf_op jit(solution)/shard_map/ppermute | solution.py:293
  15.6 3.9 %copy-start = (bf16[256,7168]{1,0:T(8,128)(2,1)S(1)}, bf16[256,7168]{1,0:T(8,128)(2,1)}, u32[]{:S(2)}) copy-start(bf16[256,7168]{1,0:T(8,128)(2,1)} %rest_10_.1) | copy-start | bytes 11010052
  15.6 3.9 %copy-start.1 = (bf16[512,256]{1,0:T(8,128)(2,1)S(1)}, bf16[512,256]{1,0:T(8,128)(2,1)}, u32[]{:S(2)}) copy-start(bf16[512,256]{1,0:T(8,128)(2,1)} %rest_9_.1) | copy-start | bytes 786436
  15.6 3.8 %collective-permute-start.8 = (bf16[216,256]{1,0:T(8,128)(2,1)S(1)}, bf16[216,256]{1,0:T(8,128)(2,1)S(1)}, u32[]{:S(2)}, u32[]{:S(2)}) collective-permute-start(bf16[216,256]{1,0:T(8,128)(2,1)S(1)} %relay.1.rest_6_), channel_id=1, source_target_pairs={{0,1},{1,0},{2,3},{3,2},{4,5},{5,4},{6,7},{7,6},{8,9},{9,8},{10,11... | collective-permute-start | bytes 331784 | tf_op jit(solution)/shard_map/ppermute | solution.py:293
  15.7 3.7 %collective-permute-start.7 = (bf16[216,256]{1,0:T(8,128)(2,1)S(1)}, bf16[216,256]{1,0:T(8,128)(2,1)S(1)}, u32[]{:S(2)}, u32[]{:S(2)}) collective-permute-start(bf16[216,256]{1,0:T(8,128)(2,1)S(1)} %collective-permute-done.6.rest_6_), channel_id=1, source_target_pairs={{0,1},{1,0},{2,3},{3,2},{4,5},{5,4},{6,7},{7,6},{8,9},{9,8},{10,11... | collective-permute-start | bytes 331784 | tf_op jit(solution)/shard_map/ppermute | solution.py:293

commit v20 on v18

--- a/solution.py
+++ b/solution.py
@@ -19,7 +19,7 @@
 SMALL_VMEM = 20 * 1024 * 1024
 LARGE_VMEM = 56 * 1024 * 1024
 FAR = (4, 6)
-NEAR = (2, 1)
+NEAR = (1, 2)
 CORNER = (3, 3)
 RELAYED = (5, 7)
 

time: 20.1 us -> 21.3 us (1.060)
  waiting for transfers between devices: 2.29 us -> 3.37 us
    ppermute x6, starting transfers between devices: 2.63 us -> 3.78 us  [other_core(): return lax.ppermute(array, 'heads', [(0, 1), (1, 0)])]
    ppermute x4, waiting for transfers between devices: 2.07 us -> 3.15 us  [partners(): return lax.ppermute(array, ('ctx', 'heads'), pairs)]
    ppermute x4, starting transfers between devices: 7.82 us -> 6.78 us  [partners(): return lax.ppermute(array, ('ctx', 'heads'), pairs)]
  transfers between devices with their start and end apart: 10 -> 10, of which waited for: 3 -> 2; matrix products, arithmetic and copies ran while one was open for 0% -> 0% of each run, Pallas kernels for 18% -> 17%
where the time goes in v20:
time: 21.3 us; the launch traced here: 21 us
  starting transfers between devices  10.6 us (50%)
  Pallas kernels  6.99 us (33%)
  waiting for transfers between devices  3.37 us (16%)
    ppermute x4, starting transfers between devices, partners(): return lax.ppermute(array, ('ctx', 'heads'), pairs)  6.78 us
    ppermute x6, starting transfers between devices, other_core(): return lax.ppermute(array, 'heads', [(0, 1), (1, 0)])  3.78 us
    ppermute x4, waiting for transfers between devices, partners(): return lax.ppermute(array, ('ctx', 'heads'), pairs)  3.15 us
    pallas_call x1, Pallas kernels, per_device(): pl.pallas_call(functools.partial(finish_kernel, heads, len(last)), out_sh...  2.47 us
    pallas_call x2, Pallas kernels, attend(): pl.pallas_call(functools.partial(chunks_kernel, len(chunks), len(old), pa...  1.83 us
    pallas_call x1, Pallas kernels, per_device(): pl.pallas_call(functools.partial(prepare_kernel, order), out_shape=[jax.S...  1.77 us
    pallas_call x1, Pallas kernels, per_device(): pl.pallas_call(pack_kernel, out_shape=jax.ShapeDtypeStruct((2 * rows + ro...  0.91 us
  transfers between devices with their start and end apart: 10, of which 2 were waited for; matrix products, arithmetic and copies ran while one was open for 0% of the time, Pallas kernels for 17%

profile of v20, /device:TPU:0, one launch (start us, length us, event | category | flops | bytes accessed | tf_op | source)
XLA Modules:
  0.0 21.0 jit_solution(3265500522886357064)
XLA Ops:
  0.0 0.9 %pack.1.refs_6_.rest_3_ = bf16[216,256]{1,0:T(8,128)(2,1)S(1)} custom-call(bf16[96,512]{1,0:T(8,128)(2,1)} %latent.1, bf16[64,96]{1,0:T(8,128)(2,1)} %bitcast.1), custom_call_target="tpu_custom_call" | custom-call | tf_op jit(solution)/shard_map/pack/pallas_call | solution.py:319
  0.9 4.1 %collective-permute-start.5 = (bf16[216,256]{1,0:T(8,128)(2,1)S(1)}, bf16[216,256]{1,0:T(8,128)(2,1)S(1)}, u32[]{:S(2)}, u32[]{:S(2)}) collective-permute-start(bf16[216,256]{1,0:T(8,128)(2,1)S(1)} %pack.1.refs_6_.rest_3_), channel_id=1, source_target_pairs={{0,8},{1,13},{2,10},{3,15},{4,12},{5,9},{6,14},{7,11},{8,0},{9,5},... | collective-permute-start | bytes 331784 | tf_op jit(solution)/shard_map/ppermute | solution.py:304
  5.0 1.5 %collective-permute-start.3 = (bf16[216,256]{1,0:T(8,128)(2,1)S(1)}, bf16[216,256]{1,0:T(8,128)(2,1)S(1)}, u32[]{:S(2)}, u32[]{:S(2)}) collective-permute-start(bf16[216,256]{1,0:T(8,128)(2,1)S(1)} %pack.1.refs_6_.rest_3_), channel_id=1, source_target_pairs={{0,2},{1,5},{2,0},{3,7},{4,6},{5,1},{6,4},{7,3},{8,10},{9,13},{10,... | collective-permute-start | bytes 331784 | tf_op jit(solution)/shard_map/ppermute | solution.py:304
  6.5 0.7 %collective-permute-start.1 = (bf16[216,256]{1,0:T(8,128)(2,1)S(1)}, bf16[216,256]{1,0:T(8,128)(2,1)S(1)}, u32[]{:S(2)}, u32[]{:S(2)}) collective-permute-start(bf16[216,256]{1,0:T(8,128)(2,1)S(1)} %pack.1.refs_6_.rest_3_), channel_id=1, source_target_pairs={{1,7},{3,5},{5,3},{7,1},{9,15},{11,13},{13,11},{15,9},{17,23},{19,... | collective-permute-start | bytes 331784 | tf_op jit(solution)/shard_map/ppermute | solution.py:304
  7.2 1.8 %prepare.1 = (bf16[192,576]{1,0:T(8,128)(2,1)S(1)}, f32[1,96,192]{2,1,0:T(8,128)S(1)}, f32[1,96,480]{2,1,0:T(8,128)S(1)}, f32[1,96,96]{2,1,0:T(8,128)S(1)}, bf16[256,4096]{1,0:T(8,128)(2,1)S(1)}) custom-call(bf16[96,256]{1,0:T(8,128)(2,1)} %refs_0_.1, bf16[96,128]{1,0:T(8,128)(2,1)} %refs_1_.1, bf16[512,256]{1,0:T(8,128)(2,1)} %refs_2_.1, s32[16]{0:T(128)} %refs_3_.1, ...), custom_call_target="tpu_custom_call" | custom-call | tf_op jit(solution)/shard_map/prepare/pallas_call | solution.py:341
  9.0 2.8 %collective-permute-start = (bf16[192,576]{1,0:T(8,128)(2,1)S(1)}, bf16[192,576]{1,0:T(8,128)(2,1)S(1)}, u32[]{:S(2)}, u32[]{:S(2)}) collective-permute-start(bf16[192,576]{1,0:T(8,128)(2,1)S(1)} %get-tuple-element.17.rest_0_), channel_id=1, source_target_pairs={{0,1},{1,0},{2,3},{3,2},{4,5},{5,4},{6,7},{7,6},{8,9},{9,8},{10,11... | collective-permute-start | bytes 663560 | tf_op jit(solution)/shard_map/ppermute | solution.py:296
  11.7 0.1 collective-permute-start.9
  11.8 0.0 collective-permute-done.5.chunk.rest_6_
  11.8 0.5 %collective-permute-start.7 = (bf16[216,256]{1,0:T(8,128)(2,1)S(1)}, bf16[216,256]{1,0:T(8,128)(2,1)S(1)}, u32[]{:S(2)}, u32[]{:S(2)}) collective-permute-start(bf16[216,256]{1,0:T(8,128)(2,1)S(1)} %collective-permute-done.5.chunk.rest_6_), channel_id=1, source_target_pairs={{0,2},{1,3},{2,0},{3,1},{4,6},{5,7},{6,4},{7,5},{8,10},{9,11},{10,... | collective-permute-start | bytes 331784 | tf_op jit(solution)/shard_map/ppermute | solution.py:304
  12.4 0.0 collective-permute-done.3.rest_4_
  12.4 0.2 collective-permute-start.4
  12.5 0.0 collective-permute-done.1.rest_3_
  12.5 0.3 %collective-permute-start.2 = (bf16[216,256]{1,0:T(8,128)(2,1)S(1)}, bf16[216,256]{1,0:T(8,128)(2,1)S(1)}, u32[]{:S(2)}, u32[]{:S(2)}) collective-permute-start(bf16[216,256]{1,0:T(8,128)(2,1)S(1)} %collective-permute-done.1.rest_3_), channel_id=1, source_target_pairs={{0,1},{1,0},{2,3},{3,2},{4,5},{5,4},{6,7},{7,6},{8,9},{9,8},{10,11... | collective-permute-start | bytes 331784 | tf_op jit(solution)/shard_map/ppermute | solution.py:296
  12.9 0.0 collective-permute-done.rest_1_
  12.9 0.7 %first.1 = (f32[384,1]{1,0:T(8,128)S(1)}, f32[384,1]{1,0:T(8,128)S(1)}, f32[384,512]{1,0:T(8,128)S(1)}, bf16[216,256]{1,0:T(8,128)(2,1)S(1)}) custom-call(bf16[192,576]{1,0:T(8,128)(2,1)S(1)} %get-tuple-element.17.rest_0_, bf16[192,576]{1,0:T(8,128)(2,1)S(1)} %collective-permute-done.rest_1_, f32[1,96,192]{2,1,0:T(8,128)S(1)} %get-tuple-element.19.rest_2_, ...), custom_call_target="tpu_custom_call" | custom-call | flops 22000001024 | tf_op jit(solution)/shard_map/first/pallas_call | solution.py:307
  13.6 0.0 copy-start
  13.6 0.0 copy-start.1
  13.7 0.4 %collective-permute-start.6 = (bf16[216,256]{1,0:T(8,128)(2,1)S(1)}, bf16[216,256]{1,0:T(8,128)(2,1)S(1)}, u32[]{:S(2)}, u32[]{:S(2)}) collective-permute-start(bf16[216,256]{1,0:T(8,128)(2,1)S(1)} %get-tuple-element.20), channel_id=1, source_target_pairs={{0,1},{1,0},{2,3},{3,2},{4,5},{5,4},{6,7},{7,6},{8,9},{9,8},{10,11... | collective-permute-start | bytes 331784 | tf_op jit(solution)/shard_map/ppermute | solution.py:296
  14.1 3.1 %collective-permute-done.7.rest_8_ = bf16[216,256]{1,0:T(8,128)(2,1)S(1)} collective-permute-done((bf16[216,256]{1,0:T(8,128)(2,1)S(1)}, bf16[216,256]{1,0:T(8,128)(2,1)S(1)}, u32[]{:S(2)}, u32[]{:S(2)}) %collective-permute-start.7) | collective-permute-done | bytes 110624 | tf_op jit(solution)/shard_map/ppermute | solution.py:304
  17.2 0.0 collective-permute-start.8
  17.2 0.0 collective-permute-done.4.rest_5_
  17.2 0.0 collective-permute-done.2.rest_4_
  17.2 0.0 collective-permute-done.6.rest_7_
  17.2 1.1 %second.1 = (f32[384,1]{1,0:T(8,128)S(1)}, f32[384,1]{1,0:T(8,128)S(1)}, f32[384,512]{1,0:T(8,128)S(1)}) custom-call(bf16[192,576]{1,0:T(8,128)(2,1)S(1)} %get-tuple-element.17.rest_0_, bf16[192,576]{1,0:T(8,128)(2,1)S(1)} %collective-permute-done.rest_1_, f32[1,96,480]{2,1,0:T(8,128)S(1)} %get-tuple-element.18.rest_2_, ...), custom_call_target="tpu_custom_call" | custom-call | flops 1100000000 | tf_op jit(solution)/shard_map/second/pallas_call | solution.py:307
  18.3 0.2 collective-permute-done.8.rest_6_
  18.5 0.0 collective-permute-done.9.rest_9_
  18.5 0.0 copy-done
  18.5 0.0 copy-done.1
  18.6 2.5 %finish.1 = bf16[96,3584]{1,0:T(8,128)(2,1)} custom-call(bf16[192,576]{1,0:T(8,128)(2,1)S(1)} %get-tuple-element.17.rest_0_, bf16[192,576]{1,0:T(8,128)(2,1)S(1)} %collective-permute-done.rest_1_, f32[384,1]{1,0:T(8,128)S(1)} %get-tuple-element.24.rest_2_, f32[384,1]{1,0:T(8,128)S(1)} %get-tuple-element.25.rest_3_, ...), custom_call_target="tpu_custom_call" | custom-call | tf_op jit(solution)/shard_map/finish/pallas_call | solution.py:404
  (1 shorter events, 0.0 us)
Async XLA Ops:
  0.9 10.9 %collective-permute-start.5 = (bf16[216,256]{1,0:T(8,128)(2,1)S(1)}, bf16[216,256]{1,0:T(8,128)(2,1)S(1)}, u32[]{:S(2)}, u32[]{:S(2)}) collective-permute-start(bf16[216,256]{1,0:T(8,128)(2,1)S(1)} %pack.1.refs_6_.rest_3_), channel_id=1, source_target_pairs={{0,8},{1,13},{2,10},{3,15},{4,12},{5,9},{6,14},{7,11},{8,0},{9,5},... | collective-permute-start | bytes 331784 | tf_op jit(solution)/shard_map/ppermute | solution.py:304
  5.0 7.3 %collective-permute-start.3 = (bf16[216,256]{1,0:T(8,128)(2,1)S(1)}, bf16[216,256]{1,0:T(8,128)(2,1)S(1)}, u32[]{:S(2)}, u32[]{:S(2)}) collective-permute-start(bf16[216,256]{1,0:T(8,128)(2,1)S(1)} %pack.1.refs_6_.rest_3_), channel_id=1, source_target_pairs={{0,2},{1,5},{2,0},{3,7},{4,6},{5,1},{6,4},{7,3},{8,10},{9,13},{10,... | collective-permute-start | bytes 331784 | tf_op jit(solution)/shard_map/ppermute | solution.py:304
  6.5 6.0 %collective-permute-start.1 = (bf16[216,256]{1,0:T(8,128)(2,1)S(1)}, bf16[216,256]{1,0:T(8,128)(2,1)S(1)}, u32[]{:S(2)}, u32[]{:S(2)}) collective-permute-start(bf16[216,256]{1,0:T(8,128)(2,1)S(1)} %pack.1.refs_6_.rest_3_), channel_id=1, source_target_pairs={{1,7},{3,5},{5,3},{7,1},{9,15},{11,13},{13,11},{15,9},{17,23},{19,... | collective-permute-start | bytes 331784 | tf_op jit(solution)/shard_map/ppermute | solution.py:304
  9.0 3.9 %collective-permute-start = (bf16[192,576]{1,0:T(8,128)(2,1)S(1)}, bf16[192,576]{1,0:T(8,128)(2,1)S(1)}, u32[]{:S(2)}, u32[]{:S(2)}) collective-permute-start(bf16[192,576]{1,0:T(8,128)(2,1)S(1)} %get-tuple-element.17.rest_0_), channel_id=1, source_target_pairs={{0,1},{1,0},{2,3},{3,2},{4,5},{5,4},{6,7},{7,6},{8,9},{9,8},{10,11... | collective-permute-start | bytes 663560 | tf_op jit(solution)/shard_map/ppermute | solution.py:296
  11.7 6.8 %collective-permute-start.9 = (bf16[256,4096]{1,0:T(8,128)(2,1)S(1)}, bf16[256,4096]{1,0:T(8,128)(2,1)S(1)}, u32[]{:S(2)}, u32[]{:S(2)}) collective-permute-start(bf16[256,4096]{1,0:T(8,128)(2,1)S(1)} %get-tuple-element.28), channel_id=1, source_target_pairs={{0,1},{1,0},{2,3},{3,2},{4,5},{5,4},{6,7},{7,6},{8,9},{9,8},{10,11... | collective-permute-start | bytes 6291464 | tf_op jit(solution)/shard_map/ppermute | solution.py:296
  11.8 5.4 %collective-permute-start.7 = (bf16[216,256]{1,0:T(8,128)(2,1)S(1)}, bf16[216,256]{1,0:T(8,128)(2,1)S(1)}, u32[]{:S(2)}, u32[]{:S(2)}) collective-permute-start(bf16[216,256]{1,0:T(8,128)(2,1)S(1)} %collective-permute-done.5.chunk.rest_6_), channel_id=1, source_target_pairs={{0,2},{1,3},{2,0},{3,1},{4,6},{5,7},{6,4},{7,5},{8,10},{9,11},{10,... | collective-permute-start | bytes 331784 | tf_op jit(solution)/shard_map/ppermute | solution.py:304
  12.4 4.9 %collective-permute-start.4 = (bf16[216,256]{1,0:T(8,128)(2,1)S(1)}, bf16[216,256]{1,0:T(8,128)(2,1)S(1)}, u32[]{:S(2)}, u32[]{:S(2)}) collective-permute-start(bf16[216,256]{1,0:T(8,128)(2,1)S(1)} %collective-permute-done.3.rest_4_), channel_id=1, source_target_pairs={{0,1},{1,0},{2,3},{3,2},{4,5},{5,4},{6,7},{7,6},{8,9},{9,8},{10,11... | collective-permute-start | bytes 331784 | tf_op jit(solution)/shard_map/ppermute | solution.py:296
  12.5 4.7 %collective-permute-start.2 = (bf16[216,256]{1,0:T(8,128)(2,1)S(1)}, bf16[216,256]{1,0:T(8,128)(2,1)S(1)}, u32[]{:S(2)}, u32[]{:S(2)}) collective-permute-start(bf16[216,256]{1,0:T(8,128)(2,1)S(1)} %collective-permute-done.1.rest_3_), channel_id=1, source_target_pairs={{0,1},{1,0},{2,3},{3,2},{4,5},{5,4},{6,7},{7,6},{8,9},{9,8},{10,11... | collective-permute-start | bytes 331784 | tf_op jit(solution)/shard_map/ppermute | solution.py:296
  13.6 4.9 %copy-start = (bf16[256,7168]{1,0:T(8,128)(2,1)S(1)}, bf16[256,7168]{1,0:T(8,128)(2,1)}, u32[]{:S(2)}) copy-start(bf16[256,7168]{1,0:T(8,128)(2,1)} %rest_8_.1) | copy-start | bytes 11010052
  13.6 4.9 %copy-start.1 = (bf16[512,256]{1,0:T(8,128)(2,1)S(1)}, bf16[512,256]{1,0:T(8,128)(2,1)}, u32[]{:S(2)}) copy-start(bf16[512,256]{1,0:T(8,128)(2,1)} %rest_7_.1) | copy-start | bytes 786436
  13.7 3.6 %collective-permute-start.6 = (bf16[216,256]{1,0:T(8,128)(2,1)S(1)}, bf16[216,256]{1,0:T(8,128)(2,1)S(1)}, u32[]{:S(2)}, u32[]{:S(2)}) collective-permute-start(bf16[216,256]{1,0:T(8,128)(2,1)S(1)} %get-tuple-element.20), channel_id=1, source_target_pairs={{0,1},{1,0},{2,3},{3,2},{4,5},{5,4},{6,7},{7,6},{8,9},{9,8},{10,11... | collective-permute-start | bytes 331784 | tf_op jit(solution)/shard_map/ppermute | solution.py:296
  17.2 1.3 %collective-permute-start.8 = (bf16[216,256]{1,0:T(8,128)(2,1)S(1)}, bf16[216,256]{1,0:T(8,128)(2,1)S(1)}, u32[]{:S(2)}, u32[]{:S(2)}) collective-permute-start(bf16[216,256]{1,0:T(8,128)(2,1)S(1)} %collective-permute-done.7.rest_8_), channel_id=1, source_target_pairs={{0,1},{1,0},{2,3},{3,2},{4,5},{5,4},{6,7},{7,6},{8,9},{9,8},{10,11... | collective-permute-start | bytes 331784 | tf_op jit(solution)/shard_map/ppermute | solution.py:296

commit v21 on v18

--- a/solution.py
+++ b/solution.py
@@ -15,7 +15,7 @@
 F32 = jnp.float32
 MASKED = -1e30
 BLOCK_CHUNKS = 8
-PREPARE_COST, GATE_COST, FIRST_COST, SECOND_COST = 0, 3, 20, 1
+PREPARE_COST, SORT_COST, GATE_COST, FIRST_COST, SECOND_COST = 0, 3, 0, 20, 1
 SMALL_VMEM = 20 * 1024 * 1024
 LARGE_VMEM = 56 * 1024 * 1024
 FAR = (4, 6)
@@ -66,6 +66,12 @@
         base += size
     for fetch in fetches[1:]:
         fetch.wait()
+
+
+def sort_kernel(second, first, far_ref, near_ref):
+    far_first = lax.axis_index("heads") == 0
+    far_ref[...] = jnp.where(far_first, first[...], second[...])
+    near_ref[...] = jnp.where(far_first, second[...], first[...])
 
 
 def gate_kernel(chunk, out_ref):
@@ -362,8 +368,17 @@
     both = [queries, other_core(queries)]
 
     if direct:
-        far = partners(packed, FAR)
-        near = partners(packed, NEAR)
+        out_second = partners(packed, (NEAR[0], FAR[1]))
+        out_first = partners(packed, (FAR[0], NEAR[1]))
+        far, near = pl.pallas_call(
+            sort_kernel,
+            out_shape=[jax.ShapeDtypeStruct(packed.shape, BF16)] * 2,
+            in_specs=[vmem()] * 2,
+            out_specs=[vmem()] * 2,
+            compiler_params=small,
+            cost_estimate=cost(SORT_COST),
+            name="sort",
+        )(out_second, out_first)
         corner = partners(packed, CORNER, cores=(1,))
         relayed = partners(far, (1, 1))
         gated = pl.pallas_call(

time: 20.1 us -> 20.2 us (level)
  waiting for transfers between devices: 2.29 us -> 2.62 us
  starting transfers between devices: 10.5 us -> 10.2 us
    ppermute x4, waiting for transfers between devices: 2.07 us -> 2.4 us  [partners(): return lax.ppermute(array, ('ctx', 'heads'), pairs)]
    ppermute x6, starting transfers between devices: 2.63 us -> 2.37 us  [other_core(): return lax.ppermute(array, 'heads', [(0, 1), (1, 0)])]
  transfers between devices with their start and end apart: 10 -> 10, of which waited for: 3 -> 4; matrix products, arithmetic and copies ran while one was open for 0% -> 0% of each run, Pallas kernels for 18% -> 18%
where the time goes in v21:
time: 20.2 us; the launch traced here: 20 us
  starting transfers between devices  10.2 us (50%)
  Pallas kernels  7.02 us (35%)
  waiting for transfers between devices  2.62 us (13%)
    ppermute x4, starting transfers between devices, partners(): return lax.ppermute(array, ('ctx', 'heads'), pairs)  7.84 us
    pallas_call x1, Pallas kernels, per_device(): pl.pallas_call(functools.partial(finish_kernel, heads, len(last)), out_sh...  2.47 us
    ppermute x4, waiting for transfers between devices, partners(): return lax.ppermute(array, ('ctx', 'heads'), pairs)  2.4 us
    ppermute x6, starting transfers between devices, other_core(): return lax.ppermute(array, 'heads', [(0, 1), (1, 0)])  2.37 us
    pallas_call x2, Pallas kernels, attend(): pl.pallas_call(functools.partial(chunks_kernel, len(chunks), len(old), pa...  1.83 us
    pallas_call x1, Pallas kernels, per_device(): pl.pallas_call(functools.partial(prepare_kernel, order), out_shape=[jax.S...  1.77 us
    pallas_call x1, Pallas kernels, per_device(): pl.pallas_call(pack_kernel, out_shape=jax.ShapeDtypeStruct((2 * rows + ro...  0.91 us
  transfers between devices with their start and end apart: 10, of which 4 were waited for; matrix products, arithmetic and copies ran while one was open for 0% of the time, Pallas kernels for 18%

profile of v21, /device:TPU:0, one launch (start us, length us, event | category | flops | bytes accessed | tf_op | source)
XLA Modules:
  0.0 20.0 jit_solution(7836990523364133425)
XLA Ops:
  0.0 0.9 %pack.1.refs_6_.rest_3_ = bf16[216,256]{1,0:T(8,128)(2,1)S(1)} custom-call(bf16[96,512]{1,0:T(8,128)(2,1)} %latent.1, bf16[64,96]{1,0:T(8,128)(2,1)} %bitcast.1), custom_call_target="tpu_custom_call" | custom-call | tf_op jit(solution)/shard_map/pack/pallas_call | solution.py:325
  0.9 4.1 %collective-permute-start.4 = (bf16[216,256]{1,0:T(8,128)(2,1)S(1)}, bf16[216,256]{1,0:T(8,128)(2,1)S(1)}, u32[]{:S(2)}, u32[]{:S(2)}) collective-permute-start(bf16[216,256]{1,0:T(8,128)(2,1)S(1)} %pack.1.refs_6_.rest_3_), channel_id=1, source_target_pairs={{0,8},{1,3},{2,10},{3,1},{4,12},{5,7},{6,14},{7,5},{8,0},{9,11},{1... | collective-permute-start | bytes 331784 | tf_op jit(solution)/shard_map/ppermute | solution.py:310
  5.0 1.6 %collective-permute-start.3 = (bf16[216,256]{1,0:T(8,128)(2,1)S(1)}, bf16[216,256]{1,0:T(8,128)(2,1)S(1)}, u32[]{:S(2)}, u32[]{:S(2)}) collective-permute-start(bf16[216,256]{1,0:T(8,128)(2,1)S(1)} %pack.1.refs_6_.rest_3_), channel_id=1, source_target_pairs={{0,4},{1,13},{2,6},{3,15},{4,0},{5,9},{6,2},{7,11},{8,12},{9,5},{1... | collective-permute-start | bytes 331784 | tf_op jit(solution)/shard_map/ppermute | solution.py:310
  6.6 0.7 %collective-permute-start.1 = (bf16[216,256]{1,0:T(8,128)(2,1)S(1)}, bf16[216,256]{1,0:T(8,128)(2,1)S(1)}, u32[]{:S(2)}, u32[]{:S(2)}) collective-permute-start(bf16[216,256]{1,0:T(8,128)(2,1)S(1)} %pack.1.refs_6_.rest_3_), channel_id=1, source_target_pairs={{1,7},{3,5},{5,3},{7,1},{9,15},{11,13},{13,11},{15,9},{17,23},{19,... | collective-permute-start | bytes 331784 | tf_op jit(solution)/shard_map/ppermute | solution.py:310
  7.3 1.8 %prepare.1 = (bf16[192,576]{1,0:T(8,128)(2,1)S(1)}, f32[1,96,192]{2,1,0:T(8,128)S(1)}, f32[1,96,480]{2,1,0:T(8,128)S(1)}, f32[1,96,96]{2,1,0:T(8,128)S(1)}, bf16[256,4096]{1,0:T(8,128)(2,1)S(1)}) custom-call(bf16[96,256]{1,0:T(8,128)(2,1)} %refs_0_.1, bf16[96,128]{1,0:T(8,128)(2,1)} %refs_1_.1, bf16[512,256]{1,0:T(8,128)(2,1)} %refs_2_.1, s32[16]{0:T(128)} %refs_3_.1, ...), custom_call_target="tpu_custom_call" | custom-call | tf_op jit(solution)/shard_map/prepare/pallas_call | solution.py:347
  9.0 1.5 %collective-permute-start = (bf16[192,576]{1,0:T(8,128)(2,1)S(1)}, bf16[192,576]{1,0:T(8,128)(2,1)S(1)}, u32[]{:S(2)}, u32[]{:S(2)}) collective-permute-start(bf16[192,576]{1,0:T(8,128)(2,1)S(1)} %get-tuple-element.19.rest_0_), channel_id=1, source_target_pairs={{0,1},{1,0},{2,3},{3,2},{4,5},{5,4},{6,7},{7,6},{8,9},{9,8},{10,11... | collective-permute-start | bytes 663560 | tf_op jit(solution)/shard_map/ppermute | solution.py:302
  10.6 0.1 collective-permute-start.9
  10.6 0.2 %collective-permute-done.4.first = bf16[216,256]{1,0:T(8,128)(2,1)S(1)} collective-permute-done((bf16[216,256]{1,0:T(8,128)(2,1)S(1)}, bf16[216,256]{1,0:T(8,128)(2,1)S(1)}, u32[]{:S(2)}, u32[]{:S(2)}) %collective-permute-start.4) | collective-permute-done | bytes 110624 | tf_op jit(solution)/shard_map/ppermute | solution.py:310
  10.9 0.1 collective-permute-done.3.second
  11.0 1.5 %collective-permute-start.7 = (bf16[216,256]{1,0:T(8,128)(2,1)S(1)}, bf16[216,256]{1,0:T(8,128)(2,1)S(1)}, u32[]{:S(2)}, u32[]{:S(2)}) collective-permute-start(bf16[216,256]{1,0:T(8,128)(2,1)S(1)} %get-tuple-element.22.chunk.rest_6_), channel_id=1, source_target_pairs={{0,2},{1,3},{2,0},{3,1},{4,6},{5,7},{6,4},{7,5},{8,10},{9,11},{10,... | collective-permute-start | bytes 331784 | tf_op jit(solution)/shard_map/ppermute | solution.py:310
  12.5 0.0 collective-permute-start.5
  12.5 0.0 collective-permute-done.1.rest_3_
  12.5 0.7 %collective-permute-start.2 = (bf16[216,256]{1,0:T(8,128)(2,1)S(1)}, bf16[216,256]{1,0:T(8,128)(2,1)S(1)}, u32[]{:S(2)}, u32[]{:S(2)}) collective-permute-start(bf16[216,256]{1,0:T(8,128)(2,1)S(1)} %collective-permute-done.1.rest_3_), channel_id=1, source_target_pairs={{0,1},{1,0},{2,3},{3,2},{4,5},{5,4},{6,7},{7,6},{8,9},{9,8},{10,11... | collective-permute-start | bytes 331784 | tf_op jit(solution)/shard_map/ppermute | solution.py:302
  13.2 0.0 collective-permute-done.rest_1_
  13.2 0.7 %first.1 = (f32[384,1]{1,0:T(8,128)S(1)}, f32[384,1]{1,0:T(8,128)S(1)}, f32[384,512]{1,0:T(8,128)S(1)}, bf16[216,256]{1,0:T(8,128)(2,1)S(1)}) custom-call(bf16[192,576]{1,0:T(8,128)(2,1)S(1)} %get-tuple-element.19.rest_0_, bf16[192,576]{1,0:T(8,128)(2,1)S(1)} %collective-permute-done.rest_1_, f32[1,96,192]{2,1,0:T(8,128)S(1)} %get-tuple-element.23.rest_2_, ...), custom_call_target="tpu_custom_call" | custom-call | flops 22000001024 | tf_op jit(solution)/shard_map/first/pallas_call | solution.py:313
  13.9 0.0 copy-start
  13.9 0.0 copy-start.1
  14.0 0.1 collective-permute-start.6
  14.0 2.1 %collective-permute-done.7.rest_8_ = bf16[216,256]{1,0:T(8,128)(2,1)S(1)} collective-permute-done((bf16[216,256]{1,0:T(8,128)(2,1)S(1)}, bf16[216,256]{1,0:T(8,128)(2,1)S(1)}, u32[]{:S(2)}, u32[]{:S(2)}) %collective-permute-start.7) | collective-permute-done | bytes 110624 | tf_op jit(solution)/shard_map/ppermute | solution.py:310
  16.2 0.0 collective-permute-start.8
  16.2 0.0 collective-permute-done.5.rest_5_
  16.2 0.0 collective-permute-done.2.rest_4_
  16.2 0.0 collective-permute-done.6.rest_7_
  16.2 1.1 %second.1 = (f32[384,1]{1,0:T(8,128)S(1)}, f32[384,1]{1,0:T(8,128)S(1)}, f32[384,512]{1,0:T(8,128)S(1)}) custom-call(bf16[192,576]{1,0:T(8,128)(2,1)S(1)} %get-tuple-element.19.rest_0_, bf16[192,576]{1,0:T(8,128)(2,1)S(1)} %collective-permute-done.rest_1_, f32[1,96,480]{2,1,0:T(8,128)S(1)} %get-tuple-element.20.rest_2_, ...), custom_call_target="tpu_custom_call" | custom-call | flops 1100000000 | tf_op jit(solution)/shard_map/second/pallas_call | solution.py:313
  17.3 0.2 collective-permute-done.8.rest_6_
  17.5 0.0 collective-permute-done.9.rest_9_
  17.5 0.0 copy-done
  17.5 0.0 copy-done.1
  17.5 2.5 %finish.1 = bf16[96,3584]{1,0:T(8,128)(2,1)} custom-call(bf16[192,576]{1,0:T(8,128)(2,1)S(1)} %get-tuple-element.19.rest_0_, bf16[192,576]{1,0:T(8,128)(2,1)S(1)} %collective-permute-done.rest_1_, f32[384,1]{1,0:T(8,128)S(1)} %get-tuple-element.28.rest_2_, f32[384,1]{1,0:T(8,128)S(1)} %get-tuple-element.29.rest_3_, ...), custom_call_target="tpu_custom_call" | custom-call | tf_op jit(solution)/shard_map/finish/pallas_call | solution.py:419
  (2 shorter events, 0.0 us)
Async XLA Ops:
  0.9 9.9 %collective-permute-start.4 = (bf16[216,256]{1,0:T(8,128)(2,1)S(1)}, bf16[216,256]{1,0:T(8,128)(2,1)S(1)}, u32[]{:S(2)}, u32[]{:S(2)}) collective-permute-start(bf16[216,256]{1,0:T(8,128)(2,1)S(1)} %pack.1.refs_6_.rest_3_), channel_id=1, source_target_pairs={{0,8},{1,3},{2,10},{3,1},{4,12},{5,7},{6,14},{7,5},{8,0},{9,11},{1... | collective-permute-start | bytes 331784 | tf_op jit(solution)/shard_map/ppermute | solution.py:310
  5.0 5.9 %collective-permute-start.3 = (bf16[216,256]{1,0:T(8,128)(2,1)S(1)}, bf16[216,256]{1,0:T(8,128)(2,1)S(1)}, u32[]{:S(2)}, u32[]{:S(2)}) collective-permute-start(bf16[216,256]{1,0:T(8,128)(2,1)S(1)} %pack.1.refs_6_.rest_3_), channel_id=1, source_target_pairs={{0,4},{1,13},{2,6},{3,15},{4,0},{5,9},{6,2},{7,11},{8,12},{9,5},{1... | collective-permute-start | bytes 331784 | tf_op jit(solution)/shard_map/ppermute | solution.py:310
  6.6 5.9 %collective-permute-start.1 = (bf16[216,256]{1,0:T(8,128)(2,1)S(1)}, bf16[216,256]{1,0:T(8,128)(2,1)S(1)}, u32[]{:S(2)}, u32[]{:S(2)}) collective-permute-start(bf16[216,256]{1,0:T(8,128)(2,1)S(1)} %pack.1.refs_6_.rest_3_), channel_id=1, source_target_pairs={{1,7},{3,5},{5,3},{7,1},{9,15},{11,13},{13,11},{15,9},{17,23},{19,... | collective-permute-start | bytes 331784 | tf_op jit(solution)/shard_map/ppermute | solution.py:310
  9.0 4.1 %collective-permute-start = (bf16[192,576]{1,0:T(8,128)(2,1)S(1)}, bf16[192,576]{1,0:T(8,128)(2,1)S(1)}, u32[]{:S(2)}, u32[]{:S(2)}) collective-permute-start(bf16[192,576]{1,0:T(8,128)(2,1)S(1)} %get-tuple-element.19.rest_0_), channel_id=1, source_target_pairs={{0,1},{1,0},{2,3},{3,2},{4,5},{5,4},{6,7},{7,6},{8,9},{9,8},{10,11... | collective-permute-start | bytes 663560 | tf_op jit(solution)/shard_map/ppermute | solution.py:302
  10.6 6.9 %collective-permute-start.9 = (bf16[256,4096]{1,0:T(8,128)(2,1)S(1)}, bf16[256,4096]{1,0:T(8,128)(2,1)S(1)}, u32[]{:S(2)}, u32[]{:S(2)}) collective-permute-start(bf16[256,4096]{1,0:T(8,128)(2,1)S(1)} %get-tuple-element.32), channel_id=1, source_target_pairs={{0,1},{1,0},{2,3},{3,2},{4,5},{5,4},{6,7},{7,6},{8,9},{9,8},{10,11... | collective-permute-start | bytes 6291464 | tf_op jit(solution)/shard_map/ppermute | solution.py:302
  11.0 5.2 %collective-permute-start.7 = (bf16[216,256]{1,0:T(8,128)(2,1)S(1)}, bf16[216,256]{1,0:T(8,128)(2,1)S(1)}, u32[]{:S(2)}, u32[]{:S(2)}) collective-permute-start(bf16[216,256]{1,0:T(8,128)(2,1)S(1)} %get-tuple-element.22.chunk.rest_6_), channel_id=1, source_target_pairs={{0,2},{1,3},{2,0},{3,1},{4,6},{5,7},{6,4},{7,5},{8,10},{9,11},{10,... | collective-permute-start | bytes 331784 | tf_op jit(solution)/shard_map/ppermute | solution.py:310
  12.5 3.7 %collective-permute-start.5 = (bf16[216,256]{1,0:T(8,128)(2,1)S(1)}, bf16[216,256]{1,0:T(8,128)(2,1)S(1)}, u32[]{:S(2)}, u32[]{:S(2)}) collective-permute-start(bf16[216,256]{1,0:T(8,128)(2,1)S(1)} %get-tuple-element.21.rest_4_), channel_id=1, source_target_pairs={{0,1},{1,0},{2,3},{3,2},{4,5},{5,4},{6,7},{7,6},{8,9},{9,8},{10,11... | collective-permute-start | bytes 331784 | tf_op jit(solution)/shard_map/ppermute | solution.py:302
  12.5 3.7 %collective-permute-start.2 = (bf16[216,256]{1,0:T(8,128)(2,1)S(1)}, bf16[216,256]{1,0:T(8,128)(2,1)S(1)}, u32[]{:S(2)}, u32[]{:S(2)}) collective-permute-start(bf16[216,256]{1,0:T(8,128)(2,1)S(1)} %collective-permute-done.1.rest_3_), channel_id=1, source_target_pairs={{0,1},{1,0},{2,3},{3,2},{4,5},{5,4},{6,7},{7,6},{8,9},{9,8},{10,11... | collective-permute-start | bytes 331784 | tf_op jit(solution)/shard_map/ppermute | solution.py:302
  13.9 3.6 %copy-start = (bf16[256,7168]{1,0:T(8,128)(2,1)S(1)}, bf16[256,7168]{1,0:T(8,128)(2,1)}, u32[]{:S(2)}) copy-start(bf16[256,7168]{1,0:T(8,128)(2,1)} %rest_8_.1) | copy-start | bytes 11010052
  13.9 3.5 %copy-start.1 = (bf16[512,256]{1,0:T(8,128)(2,1)S(1)}, bf16[512,256]{1,0:T(8,128)(2,1)}, u32[]{:S(2)}) copy-start(bf16[512,256]{1,0:T(8,128)(2,1)} %rest_7_.1) | copy-start | bytes 786436
  14.0 2.2 %collective-permute-start.6 = (bf16[216,256]{1,0:T(8,128)(2,1)S(1)}, bf16[216,256]{1,0:T(8,128)(2,1)S(1)}, u32[]{:S(2)}, u32[]{:S(2)}) collective-permute-start(bf16[216,256]{1,0:T(8,128)(2,1)S(1)} %get-tuple-element.24), channel_id=1, source_target_pairs={{0,1},{1,0},{2,3},{3,2},{4,5},{5,4},{6,7},{7,6},{8,9},{9,8},{10,11... | collective-permute-start | bytes 331784 | tf_op jit(solution)/shard_map/ppermute | solution.py:302
  16.2 1.3 %collective-permute-start.8 = (bf16[216,256]{1,0:T(8,128)(2,1)S(1)}, bf16[216,256]{1,0:T(8,128)(2,1)S(1)}, u32[]{:S(2)}, u32[]{:S(2)}) collective-permute-start(bf16[216,256]{1,0:T(8,128)(2,1)S(1)} %collective-permute-done.7.rest_8_), channel_id=1, source_target_pairs={{0,1},{1,0},{2,3},{3,2},{4,5},{5,4},{6,7},{7,6},{8,9},{9,8},{10,11... | collective-permute-start | bytes 331784 | tf_op jit(solution)/shard_map/ppermute | solution.py:302

commit v22 on v18

--- a/solution.py
+++ b/solution.py
@@ -18,10 +18,10 @@
 PREPARE_COST, GATE_COST, FIRST_COST, SECOND_COST = 0, 3, 20, 1
 SMALL_VMEM = 20 * 1024 * 1024
 LARGE_VMEM = 56 * 1024 * 1024
-FAR = (4, 6)
+FAR = (6, 4)
 NEAR = (2, 1)
 CORNER = (3, 3)
-RELAYED = (5, 7)
+RELAYED = (7, 5)
 
 
 def vmem():

time: 20.1 us -> 20.3 us (level)
  waiting for transfers between devices: 2.29 us -> 2.6 us
    ppermute x4, starting transfers between devices: 7.82 us -> 7.27 us  [partners(): return lax.ppermute(array, ('ctx', 'heads'), pairs)]
    ppermute x6, starting transfers between devices: 2.63 us -> 3.15 us  [other_core(): return lax.ppermute(array, 'heads', [(0, 1), (1, 0)])]
    ppermute x4, waiting for transfers between devices: 2.07 us -> 2.38 us  [partners(): return lax.ppermute(array, ('ctx', 'heads'), pairs)]
  transfers between devices with their start and end apart: 10 -> 10, of which waited for: 3 -> 2; matrix products, arithmetic and copies ran while one was open for 0% -> 0% of each run, Pallas kernels for 18% -> 18%
where the time goes in v22:
time: 20.3 us; the launch traced here: 20.1 us
  starting transfers between devices  10.4 us (51%)
  Pallas kernels  6.98 us (34%)
  waiting for transfers between devices  2.6 us (13%)
    ppermute x4, starting transfers between devices, partners(): return lax.ppermute(array, ('ctx', 'heads'), pairs)  7.27 us
    ppermute x6, starting transfers between devices, other_core(): return lax.ppermute(array, 'heads', [(0, 1), (1, 0)])  3.15 us
    pallas_call x1, Pallas kernels, per_device(): pl.pallas_call(functools.partial(finish_kernel, heads, len(last)), out_sh...  2.47 us
    ppermute x4, waiting for transfers between devices, partners(): return lax.ppermute(array, ('ctx', 'heads'), pairs)  2.38 us
    pallas_call x2, Pallas kernels, attend(): pl.pallas_call(functools.partial(chunks_kernel, len(chunks), len(old), pa...  1.82 us
    pallas_call x1, Pallas kernels, per_device(): pl.pallas_call(functools.partial(prepare_kernel, order), out_shape=[jax.S...  1.77 us
    pallas_call x1, Pallas kernels, per_device(): pl.pallas_call(pack_kernel, out_shape=jax.ShapeDtypeStruct((2 * rows + ro...  0.91 us
  transfers between devices with their start and end apart: 10, of which 2 were waited for; matrix products, arithmetic and copies ran while one was open for 0% of the time, Pallas kernels for 18%

profile of v22, /device:TPU:0, one launch (start us, length us, event | category | flops | bytes accessed | tf_op | source)
XLA Modules:
  0.0 20.1 jit_solution(11551489688380167260)
XLA Ops:
  0.0 0.9 %pack.1.refs_6_.rest_3_ = bf16[216,256]{1,0:T(8,128)(2,1)S(1)} custom-call(bf16[96,512]{1,0:T(8,128)(2,1)} %latent.1, bf16[64,96]{1,0:T(8,128)(2,1)} %bitcast.1), custom_call_target="tpu_custom_call" | custom-call | tf_op jit(solution)/shard_map/pack/pallas_call | solution.py:319
  0.9 5.1 %collective-permute-start.5 = (bf16[216,256]{1,0:T(8,128)(2,1)S(1)}, bf16[216,256]{1,0:T(8,128)(2,1)S(1)}, u32[]{:S(2)}, u32[]{:S(2)}) collective-permute-start(bf16[216,256]{1,0:T(8,128)(2,1)S(1)} %pack.1.refs_6_.rest_3_), channel_id=1, source_target_pairs={{0,12},{1,9},{2,14},{3,11},{4,8},{5,13},{6,10},{7,15},{8,4},{9,1},... | collective-permute-start | bytes 331784 | tf_op jit(solution)/shard_map/ppermute | solution.py:304
  6.0 0.0 collective-permute-start.3
  6.0 0.7 %collective-permute-start.1 = (bf16[216,256]{1,0:T(8,128)(2,1)S(1)}, bf16[216,256]{1,0:T(8,128)(2,1)S(1)}, u32[]{:S(2)}, u32[]{:S(2)}) collective-permute-start(bf16[216,256]{1,0:T(8,128)(2,1)S(1)} %pack.1.refs_6_.rest_3_), channel_id=1, source_target_pairs={{1,7},{3,5},{5,3},{7,1},{9,15},{11,13},{13,11},{15,9},{17,23},{19,... | collective-permute-start | bytes 331784 | tf_op jit(solution)/shard_map/ppermute | solution.py:304
  6.7 1.8 %prepare.1 = (bf16[192,576]{1,0:T(8,128)(2,1)S(1)}, f32[1,96,192]{2,1,0:T(8,128)S(1)}, f32[1,96,480]{2,1,0:T(8,128)S(1)}, f32[1,96,96]{2,1,0:T(8,128)S(1)}, bf16[256,4096]{1,0:T(8,128)(2,1)S(1)}) custom-call(bf16[96,256]{1,0:T(8,128)(2,1)} %refs_0_.1, bf16[96,128]{1,0:T(8,128)(2,1)} %refs_1_.1, bf16[512,256]{1,0:T(8,128)(2,1)} %refs_2_.1, s32[16]{0:T(128)} %refs_3_.1, ...), custom_call_target="tpu_custom_call" | custom-call | tf_op jit(solution)/shard_map/prepare/pallas_call | solution.py:341
  8.5 2.3 %collective-permute-start = (bf16[192,576]{1,0:T(8,128)(2,1)S(1)}, bf16[192,576]{1,0:T(8,128)(2,1)S(1)}, u32[]{:S(2)}, u32[]{:S(2)}) collective-permute-start(bf16[192,576]{1,0:T(8,128)(2,1)S(1)} %get-tuple-element.17.rest_0_), channel_id=1, source_target_pairs={{0,1},{1,0},{2,3},{3,2},{4,5},{5,4},{6,7},{7,6},{8,9},{9,8},{10,11... | collective-permute-start | bytes 663560 | tf_op jit(solution)/shard_map/ppermute | solution.py:296
  10.8 0.1 collective-permute-start.9
  10.9 0.0 collective-permute-done.5.chunk.rest_6_
  10.9 1.5 %collective-permute-start.7 = (bf16[216,256]{1,0:T(8,128)(2,1)S(1)}, bf16[216,256]{1,0:T(8,128)(2,1)S(1)}, u32[]{:S(2)}, u32[]{:S(2)}) collective-permute-start(bf16[216,256]{1,0:T(8,128)(2,1)S(1)} %collective-permute-done.5.chunk.rest_6_), channel_id=1, source_target_pairs={{0,2},{1,3},{2,0},{3,1},{4,6},{5,7},{6,4},{7,5},{8,10},{9,11},{10,... | collective-permute-start | bytes 331784 | tf_op jit(solution)/shard_map/ppermute | solution.py:304
  12.4 0.0 collective-permute-done.3.rest_4_
  12.4 0.2 collective-permute-start.4
  12.5 0.0 collective-permute-done.1.rest_3_
  12.6 0.3 %collective-permute-start.2 = (bf16[216,256]{1,0:T(8,128)(2,1)S(1)}, bf16[216,256]{1,0:T(8,128)(2,1)S(1)}, u32[]{:S(2)}, u32[]{:S(2)}) collective-permute-start(bf16[216,256]{1,0:T(8,128)(2,1)S(1)} %collective-permute-done.1.rest_3_), channel_id=1, source_target_pairs={{0,1},{1,0},{2,3},{3,2},{4,5},{5,4},{6,7},{7,6},{8,9},{9,8},{10,11... | collective-permute-start | bytes 331784 | tf_op jit(solution)/shard_map/ppermute | solution.py:296
  12.9 0.0 collective-permute-done.rest_1_
  12.9 0.7 %first.1 = (f32[384,1]{1,0:T(8,128)S(1)}, f32[384,1]{1,0:T(8,128)S(1)}, f32[384,512]{1,0:T(8,128)S(1)}, bf16[216,256]{1,0:T(8,128)(2,1)S(1)}) custom-call(bf16[192,576]{1,0:T(8,128)(2,1)S(1)} %get-tuple-element.17.rest_0_, bf16[192,576]{1,0:T(8,128)(2,1)S(1)} %collective-permute-done.rest_1_, f32[1,96,192]{2,1,0:T(8,128)S(1)} %get-tuple-element.19.rest_2_, ...), custom_call_target="tpu_custom_call" | custom-call | flops 22000001024 | tf_op jit(solution)/shard_map/first/pallas_call | solution.py:307
  13.7 0.0 copy-start
  13.7 0.0 copy-start.1
  13.7 0.2 %collective-permute-start.6 = (bf16[216,256]{1,0:T(8,128)(2,1)S(1)}, bf16[216,256]{1,0:T(8,128)(2,1)S(1)}, u32[]{:S(2)}, u32[]{:S(2)}) collective-permute-start(bf16[216,256]{1,0:T(8,128)(2,1)S(1)} %get-tuple-element.20), channel_id=1, source_target_pairs={{0,1},{1,0},{2,3},{3,2},{4,5},{5,4},{6,7},{7,6},{8,9},{9,8},{10,11... | collective-permute-start | bytes 331784 | tf_op jit(solution)/shard_map/ppermute | solution.py:296
  13.9 2.4 %collective-permute-done.7.rest_8_ = bf16[216,256]{1,0:T(8,128)(2,1)S(1)} collective-permute-done((bf16[216,256]{1,0:T(8,128)(2,1)S(1)}, bf16[216,256]{1,0:T(8,128)(2,1)S(1)}, u32[]{:S(2)}, u32[]{:S(2)}) %collective-permute-start.7) | collective-permute-done | bytes 110624 | tf_op jit(solution)/shard_map/ppermute | solution.py:304
  16.3 0.0 collective-permute-start.8
  16.3 0.0 collective-permute-done.4.rest_5_
  16.3 0.0 collective-permute-done.2.rest_4_
  16.3 0.0 collective-permute-done.6.rest_7_
  16.3 1.1 %second.1 = (f32[384,1]{1,0:T(8,128)S(1)}, f32[384,1]{1,0:T(8,128)S(1)}, f32[384,512]{1,0:T(8,128)S(1)}) custom-call(bf16[192,576]{1,0:T(8,128)(2,1)S(1)} %get-tuple-element.17.rest_0_, bf16[192,576]{1,0:T(8,128)(2,1)S(1)} %collective-permute-done.rest_1_, f32[1,96,480]{2,1,0:T(8,128)S(1)} %get-tuple-element.18.rest_2_, ...), custom_call_target="tpu_custom_call" | custom-call | flops 1100000000 | tf_op jit(solution)/shard_map/second/pallas_call | solution.py:307
  17.4 0.2 %collective-permute-done.8.rest_6_ = bf16[216,256]{1,0:T(8,128)(2,1)S(1)} collective-permute-done((bf16[216,256]{1,0:T(8,128)(2,1)S(1)}, bf16[216,256]{1,0:T(8,128)(2,1)S(1)}, u32[]{:S(2)}, u32[]{:S(2)}) %collective-permute-start.8) | collective-permute-done | bytes 110624 | tf_op jit(solution)/shard_map/ppermute | solution.py:296
  17.6 0.0 collective-permute-done.9.rest_9_
  17.6 0.0 copy-done
  17.6 0.0 copy-done.1
  17.6 2.5 %finish.1 = bf16[96,3584]{1,0:T(8,128)(2,1)} custom-call(bf16[192,576]{1,0:T(8,128)(2,1)S(1)} %get-tuple-element.17.rest_0_, bf16[192,576]{1,0:T(8,128)(2,1)S(1)} %collective-permute-done.rest_1_, f32[384,1]{1,0:T(8,128)S(1)} %get-tuple-element.24.rest_2_, f32[384,1]{1,0:T(8,128)S(1)} %get-tuple-element.25.rest_3_, ...), custom_call_target="tpu_custom_call" | custom-call | tf_op jit(solution)/shard_map/finish/pallas_call | solution.py:404
  (1 shorter events, 0.0 us)
Async XLA Ops:
  0.9 10.0 %collective-permute-start.5 = (bf16[216,256]{1,0:T(8,128)(2,1)S(1)}, bf16[216,256]{1,0:T(8,128)(2,1)S(1)}, u32[]{:S(2)}, u32[]{:S(2)}) collective-permute-start(bf16[216,256]{1,0:T(8,128)(2,1)S(1)} %pack.1.refs_6_.rest_3_), channel_id=1, source_target_pairs={{0,12},{1,9},{2,14},{3,11},{4,8},{5,13},{6,10},{7,15},{8,4},{9,1},... | collective-permute-start | bytes 331784 | tf_op jit(solution)/shard_map/ppermute | solution.py:304
  6.0 6.3 %collective-permute-start.3 = (bf16[216,256]{1,0:T(8,128)(2,1)S(1)}, bf16[216,256]{1,0:T(8,128)(2,1)S(1)}, u32[]{:S(2)}, u32[]{:S(2)}) collective-permute-start(bf16[216,256]{1,0:T(8,128)(2,1)S(1)} %pack.1.refs_6_.rest_3_), channel_id=1, source_target_pairs={{0,4},{1,3},{2,6},{3,1},{4,0},{5,7},{6,2},{7,5},{8,12},{9,11},{10,... | collective-permute-start | bytes 331784 | tf_op jit(solution)/shard_map/ppermute | solution.py:304
  6.0 6.5 %collective-permute-start.1 = (bf16[216,256]{1,0:T(8,128)(2,1)S(1)}, bf16[216,256]{1,0:T(8,128)(2,1)S(1)}, u32[]{:S(2)}, u32[]{:S(2)}) collective-permute-start(bf16[216,256]{1,0:T(8,128)(2,1)S(1)} %pack.1.refs_6_.rest_3_), channel_id=1, source_target_pairs={{1,7},{3,5},{5,3},{7,1},{9,15},{11,13},{13,11},{15,9},{17,23},{19,... | collective-permute-start | bytes 331784 | tf_op jit(solution)/shard_map/ppermute | solution.py:304
  8.5 4.4 %collective-permute-start = (bf16[192,576]{1,0:T(8,128)(2,1)S(1)}, bf16[192,576]{1,0:T(8,128)(2,1)S(1)}, u32[]{:S(2)}, u32[]{:S(2)}) collective-permute-start(bf16[192,576]{1,0:T(8,128)(2,1)S(1)} %get-tuple-element.17.rest_0_), channel_id=1, source_target_pairs={{0,1},{1,0},{2,3},{3,2},{4,5},{5,4},{6,7},{7,6},{8,9},{9,8},{10,11... | collective-permute-start | bytes 663560 | tf_op jit(solution)/shard_map/ppermute | solution.py:296
  10.8 6.8 %collective-permute-start.9 = (bf16[256,4096]{1,0:T(8,128)(2,1)S(1)}, bf16[256,4096]{1,0:T(8,128)(2,1)S(1)}, u32[]{:S(2)}, u32[]{:S(2)}) collective-permute-start(bf16[256,4096]{1,0:T(8,128)(2,1)S(1)} %get-tuple-element.28), channel_id=1, source_target_pairs={{0,1},{1,0},{2,3},{3,2},{4,5},{5,4},{6,7},{7,6},{8,9},{9,8},{10,11... | collective-permute-start | bytes 6291464 | tf_op jit(solution)/shard_map/ppermute | solution.py:296
  10.9 5.4 %collective-permute-start.7 = (bf16[216,256]{1,0:T(8,128)(2,1)S(1)}, bf16[216,256]{1,0:T(8,128)(2,1)S(1)}, u32[]{:S(2)}, u32[]{:S(2)}) collective-permute-start(bf16[216,256]{1,0:T(8,128)(2,1)S(1)} %collective-permute-done.5.chunk.rest_6_), channel_id=1, source_target_pairs={{0,2},{1,3},{2,0},{3,1},{4,6},{5,7},{6,4},{7,5},{8,10},{9,11},{10,... | collective-permute-start | bytes 331784 | tf_op jit(solution)/shard_map/ppermute | solution.py:304
  12.4 3.9 %collective-permute-start.4 = (bf16[216,256]{1,0:T(8,128)(2,1)S(1)}, bf16[216,256]{1,0:T(8,128)(2,1)S(1)}, u32[]{:S(2)}, u32[]{:S(2)}) collective-permute-start(bf16[216,256]{1,0:T(8,128)(2,1)S(1)} %collective-permute-done.3.rest_4_), channel_id=1, source_target_pairs={{0,1},{1,0},{2,3},{3,2},{4,5},{5,4},{6,7},{7,6},{8,9},{9,8},{10,11... | collective-permute-start | bytes 331784 | tf_op jit(solution)/shard_map/ppermute | solution.py:296
  12.6 3.8 %collective-permute-start.2 = (bf16[216,256]{1,0:T(8,128)(2,1)S(1)}, bf16[216,256]{1,0:T(8,128)(2,1)S(1)}, u32[]{:S(2)}, u32[]{:S(2)}) collective-permute-start(bf16[216,256]{1,0:T(8,128)(2,1)S(1)} %collective-permute-done.1.rest_3_), channel_id=1, source_target_pairs={{0,1},{1,0},{2,3},{3,2},{4,5},{5,4},{6,7},{7,6},{8,9},{9,8},{10,11... | collective-permute-start | bytes 331784 | tf_op jit(solution)/shard_map/ppermute | solution.py:296
  13.7 4.0 %copy-start = (bf16[256,7168]{1,0:T(8,128)(2,1)S(1)}, bf16[256,7168]{1,0:T(8,128)(2,1)}, u32[]{:S(2)}) copy-start(bf16[256,7168]{1,0:T(8,128)(2,1)} %rest_8_.1) | copy-start | bytes 11010052
  13.7 3.9 %copy-start.1 = (bf16[512,256]{1,0:T(8,128)(2,1)S(1)}, bf16[512,256]{1,0:T(8,128)(2,1)}, u32[]{:S(2)}) copy-start(bf16[512,256]{1,0:T(8,128)(2,1)} %rest_7_.1) | copy-start | bytes 786436
  13.7 2.6 %collective-permute-start.6 = (bf16[216,256]{1,0:T(8,128)(2,1)S(1)}, bf16[216,256]{1,0:T(8,128)(2,1)S(1)}, u32[]{:S(2)}, u32[]{:S(2)}) collective-permute-start(bf16[216,256]{1,0:T(8,128)(2,1)S(1)} %get-tuple-element.20), channel_id=1, source_target_pairs={{0,1},{1,0},{2,3},{3,2},{4,5},{5,4},{6,7},{7,6},{8,9},{9,8},{10,11... | collective-permute-start | bytes 331784 | tf_op jit(solution)/shard_map/ppermute | solution.py:296
  16.3 1.3 %collective-permute-start.8 = (bf16[216,256]{1,0:T(8,128)(2,1)S(1)}, bf16[216,256]{1,0:T(8,128)(2,1)S(1)}, u32[]{:S(2)}, u32[]{:S(2)}) collective-permute-start(bf16[216,256]{1,0:T(8,128)(2,1)S(1)} %collective-permute-done.7.rest_8_), channel_id=1, source_target_pairs={{0,1},{1,0},{2,3},{3,2},{4,5},{5,4},{6,7},{7,6},{8,9},{9,8},{10,11... | collective-permute-start | bytes 331784 | tf_op jit(solution)/shard_map/ppermute | solution.py:296

commit v23 on v22

--- a/solution.py
+++ b/solution.py
@@ -19,7 +19,7 @@
 SMALL_VMEM = 20 * 1024 * 1024
 LARGE_VMEM = 56 * 1024 * 1024
 FAR = (6, 4)
-NEAR = (2, 1)
+NEAR = (1, 2)
 CORNER = (3, 3)
 RELAYED = (7, 5)
 

time: 20.3 us -> 20.2 us (level)
  starting transfers between devices: 10.4 us -> 9.6 us
  waiting for transfers between devices: 2.6 us -> 3.31 us
    ppermute x6, starting transfers between devices: 3.15 us -> 1.49 us  [other_core(): return lax.ppermute(array, 'heads', [(0, 1), (1, 0)])]
    ppermute x4, starting transfers between devices: 7.27 us -> 8.11 us  [partners(): return lax.ppermute(array, ('ctx', 'heads'), pairs)]
    ppermute x4, waiting for transfers between devices: 2.38 us -> 3.1 us  [partners(): return lax.ppermute(array, ('ctx', 'heads'), pairs)]
where the time goes in v23:
time: 20.2 us; the launch traced here: 20 us
  starting transfers between devices  9.6 us (48%)
  Pallas kernels  6.99 us (35%)
  waiting for transfers between devices  3.31 us (16%)
    ppermute x4, starting transfers between devices, partners(): return lax.ppermute(array, ('ctx', 'heads'), pairs)  8.11 us
    ppermute x4, waiting for transfers between devices, partners(): return lax.ppermute(array, ('ctx', 'heads'), pairs)  3.1 us
    pallas_call x1, Pallas kernels, per_device(): pl.pallas_call(functools.partial(finish_kernel, heads, len(last)), out_sh...  2.47 us
    pallas_call x2, Pallas kernels, attend(): pl.pallas_call(functools.partial(chunks_kernel, len(chunks), len(old), pa...  1.83 us
    pallas_call x1, Pallas kernels, per_device(): pl.pallas_call(functools.partial(prepare_kernel, order), out_shape=[jax.S...  1.77 us
    ppermute x6, starting transfers between devices, other_core(): return lax.ppermute(array, 'heads', [(0, 1), (1, 0)])  1.49 us
    pallas_call x1, Pallas kernels, per_device(): pl.pallas_call(pack_kernel, out_shape=jax.ShapeDtypeStruct((2 * rows + ro...  0.91 us
  transfers between devices with their start and end apart: 10, of which 2 were waited for; matrix products, arithmetic and copies ran while one was open for 0% of the time, Pallas kernels for 18%

profile of v23, /device:TPU:0, one launch (start us, length us, event | category | flops | bytes accessed | tf_op | source)
XLA Modules:
  0.0 20.0 jit_solution(14176152757675901820)
XLA Ops:
  0.0 0.9 %pack.1.refs_6_.rest_3_ = bf16[216,256]{1,0:T(8,128)(2,1)S(1)} custom-call(bf16[96,512]{1,0:T(8,128)(2,1)} %latent.1, bf16[64,96]{1,0:T(8,128)(2,1)} %bitcast.1), custom_call_target="tpu_custom_call" | custom-call | tf_op jit(solution)/shard_map/pack/pallas_call | solution.py:319
  0.9 5.1 %collective-permute-start.5 = (bf16[216,256]{1,0:T(8,128)(2,1)S(1)}, bf16[216,256]{1,0:T(8,128)(2,1)S(1)}, u32[]{:S(2)}, u32[]{:S(2)}) collective-permute-start(bf16[216,256]{1,0:T(8,128)(2,1)S(1)} %pack.1.refs_6_.rest_3_), channel_id=1, source_target_pairs={{0,12},{1,9},{2,14},{3,11},{4,8},{5,13},{6,10},{7,15},{8,4},{9,1},... | collective-permute-start | bytes 331784 | tf_op jit(solution)/shard_map/ppermute | solution.py:304
  6.0 1.5 %collective-permute-start.3 = (bf16[216,256]{1,0:T(8,128)(2,1)S(1)}, bf16[216,256]{1,0:T(8,128)(2,1)S(1)}, u32[]{:S(2)}, u32[]{:S(2)}) collective-permute-start(bf16[216,256]{1,0:T(8,128)(2,1)S(1)} %pack.1.refs_6_.rest_3_), channel_id=1, source_target_pairs={{0,2},{1,5},{2,0},{3,7},{4,6},{5,1},{6,4},{7,3},{8,10},{9,13},{10,... | collective-permute-start | bytes 331784 | tf_op jit(solution)/shard_map/ppermute | solution.py:304
  7.5 0.7 %collective-permute-start.1 = (bf16[216,256]{1,0:T(8,128)(2,1)S(1)}, bf16[216,256]{1,0:T(8,128)(2,1)S(1)}, u32[]{:S(2)}, u32[]{:S(2)}) collective-permute-start(bf16[216,256]{1,0:T(8,128)(2,1)S(1)} %pack.1.refs_6_.rest_3_), channel_id=1, source_target_pairs={{1,7},{3,5},{5,3},{7,1},{9,15},{11,13},{13,11},{15,9},{17,23},{19,... | collective-permute-start | bytes 331784 | tf_op jit(solution)/shard_map/ppermute | solution.py:304
  8.2 1.8 %prepare.1 = (bf16[192,576]{1,0:T(8,128)(2,1)S(1)}, f32[1,96,192]{2,1,0:T(8,128)S(1)}, f32[1,96,480]{2,1,0:T(8,128)S(1)}, f32[1,96,96]{2,1,0:T(8,128)S(1)}, bf16[256,4096]{1,0:T(8,128)(2,1)S(1)}) custom-call(bf16[96,256]{1,0:T(8,128)(2,1)} %refs_0_.1, bf16[96,128]{1,0:T(8,128)(2,1)} %refs_1_.1, bf16[512,256]{1,0:T(8,128)(2,1)} %refs_2_.1, s32[16]{0:T(128)} %refs_3_.1, ...), custom_call_target="tpu_custom_call" | custom-call | tf_op jit(solution)/shard_map/prepare/pallas_call | solution.py:341
  10.0 0.8 %collective-permute-start = (bf16[192,576]{1,0:T(8,128)(2,1)S(1)}, bf16[192,576]{1,0:T(8,128)(2,1)S(1)}, u32[]{:S(2)}, u32[]{:S(2)}) collective-permute-start(bf16[192,576]{1,0:T(8,128)(2,1)S(1)} %get-tuple-element.17.rest_0_), channel_id=1, source_target_pairs={{0,1},{1,0},{2,3},{3,2},{4,5},{5,4},{6,7},{7,6},{8,9},{9,8},{10,11... | collective-permute-start | bytes 663560 | tf_op jit(solution)/shard_map/ppermute | solution.py:296
  10.7 0.1 collective-permute-start.9
  10.8 0.0 collective-permute-done.5.chunk.rest_6_
  10.8 0.8 %collective-permute-start.7 = (bf16[216,256]{1,0:T(8,128)(2,1)S(1)}, bf16[216,256]{1,0:T(8,128)(2,1)S(1)}, u32[]{:S(2)}, u32[]{:S(2)}) collective-permute-start(bf16[216,256]{1,0:T(8,128)(2,1)S(1)} %collective-permute-done.5.chunk.rest_6_), channel_id=1, source_target_pairs={{0,2},{1,3},{2,0},{3,1},{4,6},{5,7},{6,4},{7,5},{8,10},{9,11},{10,... | collective-permute-start | bytes 331784 | tf_op jit(solution)/shard_map/ppermute | solution.py:304
  11.6 0.0 collective-permute-done.3.rest_4_
  11.7 0.0 collective-permute-start.4
  11.7 0.0 collective-permute-done.1.rest_3_
  11.7 0.6 %collective-permute-start.2 = (bf16[216,256]{1,0:T(8,128)(2,1)S(1)}, bf16[216,256]{1,0:T(8,128)(2,1)S(1)}, u32[]{:S(2)}, u32[]{:S(2)}) collective-permute-start(bf16[216,256]{1,0:T(8,128)(2,1)S(1)} %collective-permute-done.1.rest_3_), channel_id=1, source_target_pairs={{0,1},{1,0},{2,3},{3,2},{4,5},{5,4},{6,7},{7,6},{8,9},{9,8},{10,11... | collective-permute-start | bytes 331784 | tf_op jit(solution)/shard_map/ppermute | solution.py:296
  12.3 0.0 collective-permute-done.rest_1_
  12.3 0.7 %first.1 = (f32[384,1]{1,0:T(8,128)S(1)}, f32[384,1]{1,0:T(8,128)S(1)}, f32[384,512]{1,0:T(8,128)S(1)}, bf16[216,256]{1,0:T(8,128)(2,1)S(1)}) custom-call(bf16[192,576]{1,0:T(8,128)(2,1)S(1)} %get-tuple-element.17.rest_0_, bf16[192,576]{1,0:T(8,128)(2,1)S(1)} %collective-permute-done.rest_1_, f32[1,96,192]{2,1,0:T(8,128)S(1)} %get-tuple-element.19.rest_2_, ...), custom_call_target="tpu_custom_call" | custom-call | flops 22000001024 | tf_op jit(solution)/shard_map/first/pallas_call | solution.py:307
  13.0 0.0 copy-start
  13.0 0.0 copy-start.1
  13.0 0.1 collective-permute-start.6
  13.1 3.1 %collective-permute-done.7.rest_8_ = bf16[216,256]{1,0:T(8,128)(2,1)S(1)} collective-permute-done((bf16[216,256]{1,0:T(8,128)(2,1)S(1)}, bf16[216,256]{1,0:T(8,128)(2,1)S(1)}, u32[]{:S(2)}, u32[]{:S(2)}) %collective-permute-start.7) | collective-permute-done | bytes 110624 | tf_op jit(solution)/shard_map/ppermute | solution.py:304
  16.2 0.0 collective-permute-start.8
  16.2 0.0 collective-permute-done.4.rest_5_
  16.2 0.0 collective-permute-done.2.rest_4_
  16.2 0.0 collective-permute-done.6.rest_7_
  16.2 1.1 %second.1 = (f32[384,1]{1,0:T(8,128)S(1)}, f32[384,1]{1,0:T(8,128)S(1)}, f32[384,512]{1,0:T(8,128)S(1)}) custom-call(bf16[192,576]{1,0:T(8,128)(2,1)S(1)} %get-tuple-element.17.rest_0_, bf16[192,576]{1,0:T(8,128)(2,1)S(1)} %collective-permute-done.rest_1_, f32[1,96,480]{2,1,0:T(8,128)S(1)} %get-tuple-element.18.rest_2_, ...), custom_call_target="tpu_custom_call" | custom-call | flops 1100000000 | tf_op jit(solution)/shard_map/second/pallas_call | solution.py:307
  17.3 0.2 %collective-permute-done.8.rest_6_ = bf16[216,256]{1,0:T(8,128)(2,1)S(1)} collective-permute-done((bf16[216,256]{1,0:T(8,128)(2,1)S(1)}, bf16[216,256]{1,0:T(8,128)(2,1)S(1)}, u32[]{:S(2)}, u32[]{:S(2)}) %collective-permute-start.8) | collective-permute-done | bytes 110624 | tf_op jit(solution)/shard_map/ppermute | solution.py:296
  17.5 0.0 collective-permute-done.9.rest_9_
  17.5 0.0 copy-done
  17.5 0.0 copy-done.1
  17.5 2.5 %finish.1 = bf16[96,3584]{1,0:T(8,128)(2,1)} custom-call(bf16[192,576]{1,0:T(8,128)(2,1)S(1)} %get-tuple-element.17.rest_0_, bf16[192,576]{1,0:T(8,128)(2,1)S(1)} %collective-permute-done.rest_1_, f32[384,1]{1,0:T(8,128)S(1)} %get-tuple-element.24.rest_2_, f32[384,1]{1,0:T(8,128)S(1)} %get-tuple-element.25.rest_3_, ...), custom_call_target="tpu_custom_call" | custom-call | tf_op jit(solution)/shard_map/finish/pallas_call | solution.py:404
  (1 shorter events, 0.0 us)
Async XLA Ops:
  0.9 9.9 %collective-permute-start.5 = (bf16[216,256]{1,0:T(8,128)(2,1)S(1)}, bf16[216,256]{1,0:T(8,128)(2,1)S(1)}, u32[]{:S(2)}, u32[]{:S(2)}) collective-permute-start(bf16[216,256]{1,0:T(8,128)(2,1)S(1)} %pack.1.refs_6_.rest_3_), channel_id=1, source_target_pairs={{0,12},{1,9},{2,14},{3,11},{4,8},{5,13},{6,10},{7,15},{8,4},{9,1},... | collective-permute-start | bytes 331784 | tf_op jit(solution)/shard_map/ppermute | solution.py:304
  6.0 5.6 %collective-permute-start.3 = (bf16[216,256]{1,0:T(8,128)(2,1)S(1)}, bf16[216,256]{1,0:T(8,128)(2,1)S(1)}, u32[]{:S(2)}, u32[]{:S(2)}) collective-permute-start(bf16[216,256]{1,0:T(8,128)(2,1)S(1)} %pack.1.refs_6_.rest_3_), channel_id=1, source_target_pairs={{0,2},{1,5},{2,0},{3,7},{4,6},{5,1},{6,4},{7,3},{8,10},{9,13},{10,... | collective-permute-start | bytes 331784 | tf_op jit(solution)/shard_map/ppermute | solution.py:304
  7.5 4.1 %collective-permute-start.1 = (bf16[216,256]{1,0:T(8,128)(2,1)S(1)}, bf16[216,256]{1,0:T(8,128)(2,1)S(1)}, u32[]{:S(2)}, u32[]{:S(2)}) collective-permute-start(bf16[216,256]{1,0:T(8,128)(2,1)S(1)} %pack.1.refs_6_.rest_3_), channel_id=1, source_target_pairs={{1,7},{3,5},{5,3},{7,1},{9,15},{11,13},{13,11},{15,9},{17,23},{19,... | collective-permute-start | bytes 331784 | tf_op jit(solution)/shard_map/ppermute | solution.py:304
  10.0 2.3 %collective-permute-start = (bf16[192,576]{1,0:T(8,128)(2,1)S(1)}, bf16[192,576]{1,0:T(8,128)(2,1)S(1)}, u32[]{:S(2)}, u32[]{:S(2)}) collective-permute-start(bf16[192,576]{1,0:T(8,128)(2,1)S(1)} %get-tuple-element.17.rest_0_), channel_id=1, source_target_pairs={{0,1},{1,0},{2,3},{3,2},{4,5},{5,4},{6,7},{7,6},{8,9},{9,8},{10,11... | collective-permute-start | bytes 663560 | tf_op jit(solution)/shard_map/ppermute | solution.py:296
  10.7 6.8 %collective-permute-start.9 = (bf16[256,4096]{1,0:T(8,128)(2,1)S(1)}, bf16[256,4096]{1,0:T(8,128)(2,1)S(1)}, u32[]{:S(2)}, u32[]{:S(2)}) collective-permute-start(bf16[256,4096]{1,0:T(8,128)(2,1)S(1)} %get-tuple-element.28), channel_id=1, source_target_pairs={{0,1},{1,0},{2,3},{3,2},{4,5},{5,4},{6,7},{7,6},{8,9},{9,8},{10,11... | collective-permute-start | bytes 6291464 | tf_op jit(solution)/shard_map/ppermute | solution.py:296
  10.8 5.4 %collective-permute-start.7 = (bf16[216,256]{1,0:T(8,128)(2,1)S(1)}, bf16[216,256]{1,0:T(8,128)(2,1)S(1)}, u32[]{:S(2)}, u32[]{:S(2)}) collective-permute-start(bf16[216,256]{1,0:T(8,128)(2,1)S(1)} %collective-permute-done.5.chunk.rest_6_), channel_id=1, source_target_pairs={{0,2},{1,3},{2,0},{3,1},{4,6},{5,7},{6,4},{7,5},{8,10},{9,11},{10,... | collective-permute-start | bytes 331784 | tf_op jit(solution)/shard_map/ppermute | solution.py:304
  11.7 4.6 %collective-permute-start.4 = (bf16[216,256]{1,0:T(8,128)(2,1)S(1)}, bf16[216,256]{1,0:T(8,128)(2,1)S(1)}, u32[]{:S(2)}, u32[]{:S(2)}) collective-permute-start(bf16[216,256]{1,0:T(8,128)(2,1)S(1)} %collective-permute-done.3.rest_4_), channel_id=1, source_target_pairs={{0,1},{1,0},{2,3},{3,2},{4,5},{5,4},{6,7},{7,6},{8,9},{9,8},{10,11... | collective-permute-start | bytes 331784 | tf_op jit(solution)/shard_map/ppermute | solution.py:296
  11.7 4.6 %collective-permute-start.2 = (bf16[216,256]{1,0:T(8,128)(2,1)S(1)}, bf16[216,256]{1,0:T(8,128)(2,1)S(1)}, u32[]{:S(2)}, u32[]{:S(2)}) collective-permute-start(bf16[216,256]{1,0:T(8,128)(2,1)S(1)} %collective-permute-done.1.rest_3_), channel_id=1, source_target_pairs={{0,1},{1,0},{2,3},{3,2},{4,5},{5,4},{6,7},{7,6},{8,9},{9,8},{10,11... | collective-permute-start | bytes 331784 | tf_op jit(solution)/shard_map/ppermute | solution.py:296
  13.0 4.5 %copy-start = (bf16[256,7168]{1,0:T(8,128)(2,1)S(1)}, bf16[256,7168]{1,0:T(8,128)(2,1)}, u32[]{:S(2)}) copy-start(bf16[256,7168]{1,0:T(8,128)(2,1)} %rest_8_.1) | copy-start | bytes 11010052
  13.0 4.5 %copy-start.1 = (bf16[512,256]{1,0:T(8,128)(2,1)S(1)}, bf16[512,256]{1,0:T(8,128)(2,1)}, u32[]{:S(2)}) copy-start(bf16[512,256]{1,0:T(8,128)(2,1)} %rest_7_.1) | copy-start | bytes 786436
  13.0 3.2 %collective-permute-start.6 = (bf16[216,256]{1,0:T(8,128)(2,1)S(1)}, bf16[216,256]{1,0:T(8,128)(2,1)S(1)}, u32[]{:S(2)}, u32[]{:S(2)}) collective-permute-start(bf16[216,256]{1,0:T(8,128)(2,1)S(1)} %get-tuple-element.20), channel_id=1, source_target_pairs={{0,1},{1,0},{2,3},{3,2},{4,5},{5,4},{6,7},{7,6},{8,9},{9,8},{10,11... | collective-permute-start | bytes 331784 | tf_op jit(solution)/shard_map/ppermute | solution.py:296
  16.2 1.3 %collective-permute-start.8 = (bf16[216,256]{1,0:T(8,128)(2,1)S(1)}, bf16[216,256]{1,0:T(8,128)(2,1)S(1)}, u32[]{:S(2)}, u32[]{:S(2)}) collective-permute-start(bf16[216,256]{1,0:T(8,128)(2,1)S(1)} %collective-permute-done.7.rest_8_), channel_id=1, source_target_pairs={{0,1},{1,0},{2,3},{3,2},{4,5},{5,4},{6,7},{7,6},{8,9},{9,8},{10,11... | collective-permute-start | bytes 331784 | tf_op jit(solution)/shard_map/ppermute | solution.py:296

commit v24 on v18

--- a/solution.py
+++ b/solution.py
@@ -400,7 +400,7 @@
             name="gathered",
         )(*both, biases[0], lax.all_gather(packed, "ctx", axis=0))
 
-    tiles = 7 if width % 896 == 0 else 1
+    tiles = 4 if width % 512 == 0 else 1
     return pl.pallas_call(
         functools.partial(finish_kernel, heads, len(last)),
         out_shape=jax.ShapeDtypeStruct((rows, width), BF16),

time: 20.1 us -> 20 us (level)
  no operation moved by 1% of the time
where the time goes in v24:
time: 20 us; the launch traced here: 19.8 us
  starting transfers between devices  10.5 us (52%)
  Pallas kernels  6.95 us (35%)
  waiting for transfers between devices  2.29 us (11%)
    ppermute x4, starting transfers between devices, partners(): return lax.ppermute(array, ('ctx', 'heads'), pairs)  7.82 us
    ppermute x6, starting transfers between devices, other_core(): return lax.ppermute(array, 'heads', [(0, 1), (1, 0)])  2.63 us
    pallas_call x1, Pallas kernels, per_device(): pl.pallas_call(functools.partial(finish_kernel, heads, len(last)), out_sh...  2.43 us
    ppermute x4, waiting for transfers between devices, partners(): return lax.ppermute(array, ('ctx', 'heads'), pairs)  2.07 us
    pallas_call x2, Pallas kernels, attend(): pl.pallas_call(functools.partial(chunks_kernel, len(chunks), len(old), pa...  1.83 us
    pallas_call x1, Pallas kernels, per_device(): pl.pallas_call(functools.partial(prepare_kernel, order), out_shape=[jax.S...  1.77 us
    pallas_call x1, Pallas kernels, per_device(): pl.pallas_call(pack_kernel, out_shape=jax.ShapeDtypeStruct((2 * rows + ro...  0.91 us
  transfers between devices with their start and end apart: 10, of which 3 were waited for; matrix products, arithmetic and copies ran while one was open for 0% of the time, Pallas kernels for 18%

profile of v24, /device:TPU:0, one launch (start us, length us, event | category | flops | bytes accessed | tf_op | source)
XLA Modules:
  0.0 19.8 jit_solution(123031540513918471)
XLA Ops:
  0.0 0.9 %pack.1.refs_6_.rest_3_ = bf16[216,256]{1,0:T(8,128)(2,1)S(1)} custom-call(bf16[96,512]{1,0:T(8,128)(2,1)} %latent.1, bf16[64,96]{1,0:T(8,128)(2,1)} %bitcast.1), custom_call_target="tpu_custom_call" | custom-call | tf_op jit(solution)/shard_map/pack/pallas_call | solution.py:319
  0.9 4.1 %collective-permute-start.5 = (bf16[216,256]{1,0:T(8,128)(2,1)S(1)}, bf16[216,256]{1,0:T(8,128)(2,1)S(1)}, u32[]{:S(2)}, u32[]{:S(2)}) collective-permute-start(bf16[216,256]{1,0:T(8,128)(2,1)S(1)} %pack.1.refs_6_.rest_3_), channel_id=1, source_target_pairs={{0,8},{1,13},{2,10},{3,15},{4,12},{5,9},{6,14},{7,11},{8,0},{9,5},... | collective-permute-start | bytes 331784 | tf_op jit(solution)/shard_map/ppermute | solution.py:304
  5.0 1.6 %collective-permute-start.3 = (bf16[216,256]{1,0:T(8,128)(2,1)S(1)}, bf16[216,256]{1,0:T(8,128)(2,1)S(1)}, u32[]{:S(2)}, u32[]{:S(2)}) collective-permute-start(bf16[216,256]{1,0:T(8,128)(2,1)S(1)} %pack.1.refs_6_.rest_3_), channel_id=1, source_target_pairs={{0,4},{1,3},{2,6},{3,1},{4,0},{5,7},{6,2},{7,5},{8,12},{9,11},{10,... | collective-permute-start | bytes 331784 | tf_op jit(solution)/shard_map/ppermute | solution.py:304
  6.6 0.7 %collective-permute-start.1 = (bf16[216,256]{1,0:T(8,128)(2,1)S(1)}, bf16[216,256]{1,0:T(8,128)(2,1)S(1)}, u32[]{:S(2)}, u32[]{:S(2)}) collective-permute-start(bf16[216,256]{1,0:T(8,128)(2,1)S(1)} %pack.1.refs_6_.rest_3_), channel_id=1, source_target_pairs={{1,7},{3,5},{5,3},{7,1},{9,15},{11,13},{13,11},{15,9},{17,23},{19,... | collective-permute-start | bytes 331784 | tf_op jit(solution)/shard_map/ppermute | solution.py:304
  7.3 1.8 %prepare.1 = (bf16[192,576]{1,0:T(8,128)(2,1)S(1)}, f32[1,96,192]{2,1,0:T(8,128)S(1)}, f32[1,96,480]{2,1,0:T(8,128)S(1)}, f32[1,96,96]{2,1,0:T(8,128)S(1)}, bf16[256,4096]{1,0:T(8,128)(2,1)S(1)}) custom-call(bf16[96,256]{1,0:T(8,128)(2,1)} %refs_0_.1, bf16[96,128]{1,0:T(8,128)(2,1)} %refs_1_.1, bf16[512,256]{1,0:T(8,128)(2,1)} %refs_2_.1, s32[16]{0:T(128)} %refs_3_.1, ...), custom_call_target="tpu_custom_call" | custom-call | tf_op jit(solution)/shard_map/prepare/pallas_call | solution.py:341
  9.0 1.5 %collective-permute-start = (bf16[192,576]{1,0:T(8,128)(2,1)S(1)}, bf16[192,576]{1,0:T(8,128)(2,1)S(1)}, u32[]{:S(2)}, u32[]{:S(2)}) collective-permute-start(bf16[192,576]{1,0:T(8,128)(2,1)S(1)} %get-tuple-element.17.rest_0_), channel_id=1, source_target_pairs={{0,1},{1,0},{2,3},{3,2},{4,5},{5,4},{6,7},{7,6},{8,9},{9,8},{10,11... | collective-permute-start | bytes 663560 | tf_op jit(solution)/shard_map/ppermute | solution.py:296
  10.6 0.1 collective-permute-start.9
  10.6 0.1 collective-permute-done.5.chunk.rest_6_
  10.7 1.5 %collective-permute-start.7 = (bf16[216,256]{1,0:T(8,128)(2,1)S(1)}, bf16[216,256]{1,0:T(8,128)(2,1)S(1)}, u32[]{:S(2)}, u32[]{:S(2)}) collective-permute-start(bf16[216,256]{1,0:T(8,128)(2,1)S(1)} %collective-permute-done.5.chunk.rest_6_), channel_id=1, source_target_pairs={{0,2},{1,3},{2,0},{3,1},{4,6},{5,7},{6,4},{7,5},{8,10},{9,11},{10,... | collective-permute-start | bytes 331784 | tf_op jit(solution)/shard_map/ppermute | solution.py:304
  12.2 0.0 collective-permute-done.3.rest_4_
  12.2 0.0 collective-permute-start.4
  12.2 0.0 collective-permute-done.1.rest_3_
  12.2 1.0 %collective-permute-start.2 = (bf16[216,256]{1,0:T(8,128)(2,1)S(1)}, bf16[216,256]{1,0:T(8,128)(2,1)S(1)}, u32[]{:S(2)}, u32[]{:S(2)}) collective-permute-start(bf16[216,256]{1,0:T(8,128)(2,1)S(1)} %collective-permute-done.1.rest_3_), channel_id=1, source_target_pairs={{0,1},{1,0},{2,3},{3,2},{4,5},{5,4},{6,7},{7,6},{8,9},{9,8},{10,11... | collective-permute-start | bytes 331784 | tf_op jit(solution)/shard_map/ppermute | solution.py:296
  13.2 0.0 collective-permute-done.rest_1_
  13.2 0.7 %first.1 = (f32[384,1]{1,0:T(8,128)S(1)}, f32[384,1]{1,0:T(8,128)S(1)}, f32[384,512]{1,0:T(8,128)S(1)}, bf16[216,256]{1,0:T(8,128)(2,1)S(1)}) custom-call(bf16[192,576]{1,0:T(8,128)(2,1)S(1)} %get-tuple-element.17.rest_0_, bf16[192,576]{1,0:T(8,128)(2,1)S(1)} %collective-permute-done.rest_1_, f32[1,96,192]{2,1,0:T(8,128)S(1)} %get-tuple-element.19.rest_2_, ...), custom_call_target="tpu_custom_call" | custom-call | flops 22000001024 | tf_op jit(solution)/shard_map/first/pallas_call | solution.py:307
  13.9 0.0 copy-start
  14.0 0.0 copy-start.1
  14.0 0.1 collective-permute-start.6
  14.0 2.0 %collective-permute-done.7.rest_8_ = bf16[216,256]{1,0:T(8,128)(2,1)S(1)} collective-permute-done((bf16[216,256]{1,0:T(8,128)(2,1)S(1)}, bf16[216,256]{1,0:T(8,128)(2,1)S(1)}, u32[]{:S(2)}, u32[]{:S(2)}) %collective-permute-start.7) | collective-permute-done | bytes 110624 | tf_op jit(solution)/shard_map/ppermute | solution.py:304
  16.0 0.0 collective-permute-start.8
  16.0 0.0 collective-permute-done.4.rest_5_
  16.0 0.0 collective-permute-done.2.rest_4_
  16.1 0.0 collective-permute-done.6.rest_7_
  16.1 1.1 %second.1 = (f32[384,1]{1,0:T(8,128)S(1)}, f32[384,1]{1,0:T(8,128)S(1)}, f32[384,512]{1,0:T(8,128)S(1)}) custom-call(bf16[192,576]{1,0:T(8,128)(2,1)S(1)} %get-tuple-element.17.rest_0_, bf16[192,576]{1,0:T(8,128)(2,1)S(1)} %collective-permute-done.rest_1_, f32[1,96,480]{2,1,0:T(8,128)S(1)} %get-tuple-element.18.rest_2_, ...), custom_call_target="tpu_custom_call" | custom-call | flops 1100000000 | tf_op jit(solution)/shard_map/second/pallas_call | solution.py:307
  17.2 0.2 %collective-permute-done.8.rest_6_ = bf16[216,256]{1,0:T(8,128)(2,1)S(1)} collective-permute-done((bf16[216,256]{1,0:T(8,128)(2,1)S(1)}, bf16[216,256]{1,0:T(8,128)(2,1)S(1)}, u32[]{:S(2)}, u32[]{:S(2)}) %collective-permute-start.8) | collective-permute-done | bytes 110624 | tf_op jit(solution)/shard_map/ppermute | solution.py:296
  17.4 0.0 collective-permute-done.9.rest_9_
  17.4 0.0 copy-done
  17.4 0.0 copy-done.1
  17.4 2.4 %finish.1 = bf16[96,3584]{1,0:T(8,128)(2,1)} custom-call(bf16[192,576]{1,0:T(8,128)(2,1)S(1)} %get-tuple-element.17.rest_0_, bf16[192,576]{1,0:T(8,128)(2,1)S(1)} %collective-permute-done.rest_1_, f32[384,1]{1,0:T(8,128)S(1)} %get-tuple-element.24.rest_2_, f32[384,1]{1,0:T(8,128)S(1)} %get-tuple-element.25.rest_3_, ...), custom_call_target="tpu_custom_call" | custom-call | tf_op jit(solution)/shard_map/finish/pallas_call | solution.py:404
  (1 shorter events, 0.0 us)
Async XLA Ops:
  0.9 9.8 %collective-permute-start.5 = (bf16[216,256]{1,0:T(8,128)(2,1)S(1)}, bf16[216,256]{1,0:T(8,128)(2,1)S(1)}, u32[]{:S(2)}, u32[]{:S(2)}) collective-permute-start(bf16[216,256]{1,0:T(8,128)(2,1)S(1)} %pack.1.refs_6_.rest_3_), channel_id=1, source_target_pairs={{0,8},{1,13},{2,10},{3,15},{4,12},{5,9},{6,14},{7,11},{8,0},{9,5},... | collective-permute-start | bytes 331784 | tf_op jit(solution)/shard_map/ppermute | solution.py:304
  5.0 7.2 %collective-permute-start.3 = (bf16[216,256]{1,0:T(8,128)(2,1)S(1)}, bf16[216,256]{1,0:T(8,128)(2,1)S(1)}, u32[]{:S(2)}, u32[]{:S(2)}) collective-permute-start(bf16[216,256]{1,0:T(8,128)(2,1)S(1)} %pack.1.refs_6_.rest_3_), channel_id=1, source_target_pairs={{0,4},{1,3},{2,6},{3,1},{4,0},{5,7},{6,2},{7,5},{8,12},{9,11},{10,... | collective-permute-start | bytes 331784 | tf_op jit(solution)/shard_map/ppermute | solution.py:304
  6.6 5.6 %collective-permute-start.1 = (bf16[216,256]{1,0:T(8,128)(2,1)S(1)}, bf16[216,256]{1,0:T(8,128)(2,1)S(1)}, u32[]{:S(2)}, u32[]{:S(2)}) collective-permute-start(bf16[216,256]{1,0:T(8,128)(2,1)S(1)} %pack.1.refs_6_.rest_3_), channel_id=1, source_target_pairs={{1,7},{3,5},{5,3},{7,1},{9,15},{11,13},{13,11},{15,9},{17,23},{19,... | collective-permute-start | bytes 331784 | tf_op jit(solution)/shard_map/ppermute | solution.py:304
  9.0 4.2 %collective-permute-start = (bf16[192,576]{1,0:T(8,128)(2,1)S(1)}, bf16[192,576]{1,0:T(8,128)(2,1)S(1)}, u32[]{:S(2)}, u32[]{:S(2)}) collective-permute-start(bf16[192,576]{1,0:T(8,128)(2,1)S(1)} %get-tuple-element.17.rest_0_), channel_id=1, source_target_pairs={{0,1},{1,0},{2,3},{3,2},{4,5},{5,4},{6,7},{7,6},{8,9},{9,8},{10,11... | collective-permute-start | bytes 663560 | tf_op jit(solution)/shard_map/ppermute | solution.py:296
  10.6 6.8 %collective-permute-start.9 = (bf16[256,4096]{1,0:T(8,128)(2,1)S(1)}, bf16[256,4096]{1,0:T(8,128)(2,1)S(1)}, u32[]{:S(2)}, u32[]{:S(2)}) collective-permute-start(bf16[256,4096]{1,0:T(8,128)(2,1)S(1)} %get-tuple-element.28), channel_id=1, source_target_pairs={{0,1},{1,0},{2,3},{3,2},{4,5},{5,4},{6,7},{7,6},{8,9},{9,8},{10,11... | collective-permute-start | bytes 6291464 | tf_op jit(solution)/shard_map/ppermute | solution.py:296
  10.7 5.3 %collective-permute-start.7 = (bf16[216,256]{1,0:T(8,128)(2,1)S(1)}, bf16[216,256]{1,0:T(8,128)(2,1)S(1)}, u32[]{:S(2)}, u32[]{:S(2)}) collective-permute-start(bf16[216,256]{1,0:T(8,128)(2,1)S(1)} %collective-permute-done.5.chunk.rest_6_), channel_id=1, source_target_pairs={{0,2},{1,3},{2,0},{3,1},{4,6},{5,7},{6,4},{7,5},{8,10},{9,11},{10,... | collective-permute-start | bytes 331784 | tf_op jit(solution)/shard_map/ppermute | solution.py:304
  12.2 3.8 %collective-permute-start.4 = (bf16[216,256]{1,0:T(8,128)(2,1)S(1)}, bf16[216,256]{1,0:T(8,128)(2,1)S(1)}, u32[]{:S(2)}, u32[]{:S(2)}) collective-permute-start(bf16[216,256]{1,0:T(8,128)(2,1)S(1)} %collective-permute-done.3.rest_4_), channel_id=1, source_target_pairs={{0,1},{1,0},{2,3},{3,2},{4,5},{5,4},{6,7},{7,6},{8,9},{9,8},{10,11... | collective-permute-start | bytes 331784 | tf_op jit(solution)/shard_map/ppermute | solution.py:296
  12.2 3.8 %collective-permute-start.2 = (bf16[216,256]{1,0:T(8,128)(2,1)S(1)}, bf16[216,256]{1,0:T(8,128)(2,1)S(1)}, u32[]{:S(2)}, u32[]{:S(2)}) collective-permute-start(bf16[216,256]{1,0:T(8,128)(2,1)S(1)} %collective-permute-done.1.rest_3_), channel_id=1, source_target_pairs={{0,1},{1,0},{2,3},{3,2},{4,5},{5,4},{6,7},{7,6},{8,9},{9,8},{10,11... | collective-permute-start | bytes 331784 | tf_op jit(solution)/shard_map/ppermute | solution.py:296
  13.9 3.4 %copy-start = (bf16[256,7168]{1,0:T(8,128)(2,1)S(1)}, bf16[256,7168]{1,0:T(8,128)(2,1)}, u32[]{:S(2)}) copy-start(bf16[256,7168]{1,0:T(8,128)(2,1)} %rest_8_.1) | copy-start | bytes 11010052
  14.0 3.4 %copy-start.1 = (bf16[512,256]{1,0:T(8,128)(2,1)S(1)}, bf16[512,256]{1,0:T(8,128)(2,1)}, u32[]{:S(2)}) copy-start(bf16[512,256]{1,0:T(8,128)(2,1)} %rest_7_.1) | copy-start | bytes 786436
  14.0 2.1 %collective-permute-start.6 = (bf16[216,256]{1,0:T(8,128)(2,1)S(1)}, bf16[216,256]{1,0:T(8,128)(2,1)S(1)}, u32[]{:S(2)}, u32[]{:S(2)}) collective-permute-start(bf16[216,256]{1,0:T(8,128)(2,1)S(1)} %get-tuple-element.20), channel_id=1, source_target_pairs={{0,1},{1,0},{2,3},{3,2},{4,5},{5,4},{6,7},{7,6},{8,9},{9,8},{10,11... | collective-permute-start | bytes 331784 | tf_op jit(solution)/shard_map/ppermute | solution.py:296
  16.0 1.3 %collective-permute-start.8 = (bf16[216,256]{1,0:T(8,128)(2,1)S(1)}, bf16[216,256]{1,0:T(8,128)(2,1)S(1)}, u32[]{:S(2)}, u32[]{:S(2)}) collective-permute-start(bf16[216,256]{1,0:T(8,128)(2,1)S(1)} %collective-permute-done.7.rest_8_), channel_id=1, source_target_pairs={{0,1},{1,0},{2,3},{3,2},{4,5},{5,4},{6,7},{7,6},{8,9},{9,8},{10,11... | collective-permute-start | bytes 331784 | tf_op jit(solution)/shard_map/ppermute | solution.py:296

commit v25 on v23

--- a/solution.py
+++ b/solution.py
@@ -15,7 +15,7 @@
 F32 = jnp.float32
 MASKED = -1e30
 BLOCK_CHUNKS = 8
-PREPARE_COST, GATE_COST, FIRST_COST, SECOND_COST = 0, 3, 20, 1
+PREPARE_COST, ROOM_COST, GATE_COST, FIRST_COST, SECOND_COST = 0, 4, 8, 20, 1
 SMALL_VMEM = 20 * 1024 * 1024
 LARGE_VMEM = 56 * 1024 * 1024
 FAR = (6, 4)
@@ -99,14 +99,10 @@
         for index, (source, target) in enumerate(zip(sources, copied))
     ]
     base = pl.multiple_of((1 - lax.axis_index("heads")) * width, 128)
-    fetches.append(
-        pltpu.make_async_copy(
-            out_proj.at[:, pl.ds(base, width)], weights.at[:, pl.ds(0, width)], sems.at[5]
-        )
-    )
     for fetch in fetches:
         fetch.start()
     nope, rope, up, span_order, value_up = copied
+    weights[:, :width] = out_proj[:, pl.ds(base, width)]
     rows = nope.shape[0]
     heads = nope.shape[1] // DH
     span_rows = rows // 2
@@ -162,7 +158,6 @@
     for block in range(DC // depth):
         part = value_up[block * depth : (block + 1) * depth, :]
         weights[:, width + block * columns : width + (block + 1) * columns] = part
-    fetches[5].wait()
 
 
 def attend_block(queries, keys, bias, old):
@@ -343,7 +338,7 @@
         out_shape=[jax.ShapeDtypeStruct((query_rows // 2, DC + DR), BF16)]
         + [jax.ShapeDtypeStruct(shape, F32) for shape in bias_shapes]
         + [jax.ShapeDtypeStruct((depth, width + DC // depth * key_up.shape[1]), BF16)],
-        in_specs=[hbm()] * 6 + [anywhere()],
+        in_specs=[hbm()] * 5 + [vmem(), anywhere()],
         out_specs=[vmem()] * (len(bias_shapes) + 2),
         scratch_shapes=[
             pltpu.VMEM(queries_nope.shape, BF16),
@@ -351,20 +346,29 @@
             pltpu.VMEM(key_up.shape, BF16),
             pltpu.SMEM(span_order.shape, jnp.int32),
             pltpu.VMEM(value_up.shape, BF16),
-            pltpu.SemaphoreType.DMA((6,)),
+            pltpu.SemaphoreType.DMA((5,)),
         ],
         compiler_params=small,
         cost_estimate=cost(PREPARE_COST),
         name="prepare",
-    )(*in_hbm(queries_nope, queries_rope, key_up, span_order, value_up, out_proj), packed)
+    )(*in_hbm(queries_nope, queries_rope, key_up, span_order, value_up), out_proj, packed)
     queries, biases = outs[0], outs[1:-1]
     weights_other = other_core(outs[-1])
     both = [queries, other_core(queries)]
 
     if direct:
         far = partners(packed, FAR)
-        near = partners(packed, NEAR)
-        corner = partners(packed, CORNER, cores=(1,))
+        room = pl.pallas_call(
+            gate_kernel,
+            out_shape=jax.ShapeDtypeStruct(packed.shape, BF16),
+            in_specs=[vmem()],
+            out_specs=vmem(),
+            compiler_params=small,
+            cost_estimate=cost(ROOM_COST),
+            name="room",
+        )(packed)
+        near = partners(room, NEAR)
+        corner = partners(room, CORNER, cores=(1,))
         relayed = partners(far, (1, 1))
         gated = pl.pallas_call(
             gate_kernel,

time: 20.2 us -> 20.3 us (level)
  starting transfers between devices: 9.6 us -> 10.1 us
  Pallas kernels: 6.99 us -> 6.58 us
    pallas_call x1, Pallas kernels: 1.77 us -> 1.36 us  [per_device(): pl.pallas_call(functools.partial(prepare_kernel, order), out_shape=[jax.S...]
    ppermute x6, starting transfers between devices: 1.49 us -> 1.76 us  [other_core(): return lax.ppermute(array, 'heads', [(0, 1), (1, 0)])]
  transfers between devices with their start and end apart: 10 -> 10, of which waited for: 2 -> 2; matrix products, arithmetic and copies ran while one was open for 0% -> 0% of each run, Pallas kernels for 18% -> 16%
where the time goes in v25:
time: 20.3 us; the launch traced here: 20 us
  starting transfers between devices  10.1 us (50%)
  Pallas kernels  6.58 us (32%)
  waiting for transfers between devices  3.28 us (16%)
    ppermute x4, starting transfers between devices, partners(): return lax.ppermute(array, ('ctx', 'heads'), pairs)  8.3 us
    ppermute x4, waiting for transfers between devices, partners(): return lax.ppermute(array, ('ctx', 'heads'), pairs)  3.06 us
    pallas_call x1, Pallas kernels, per_device(): pl.pallas_call(functools.partial(finish_kernel, heads, len(last)), out_sh...  2.46 us
    pallas_call x2, Pallas kernels, attend(): pl.pallas_call(functools.partial(chunks_kernel, len(chunks), len(old), pa...  1.83 us
    ppermute x6, starting transfers between devices, other_core(): return lax.ppermute(array, 'heads', [(0, 1), (1, 0)])  1.76 us
    pallas_call x1, Pallas kernels, per_device(): pl.pallas_call(functools.partial(prepare_kernel, order), out_shape=[jax.S...  1.36 us
    pallas_call x1, Pallas kernels, per_device(): pl.pallas_call(pack_kernel, out_shape=jax.ShapeDtypeStruct((2 * rows + ro...  0.91 us
  transfers between devices with their start and end apart: 10, of which 2 were waited for; matrix products, arithmetic and copies ran while one was open for 0% of the time, Pallas kernels for 16%

profile of v25, /device:TPU:0, one launch (start us, length us, event | category | flops | bytes accessed | tf_op | source)
XLA Modules:
  0.0 20.0 jit_solution(5190153873589005972)
XLA Ops:
  0.0 0.9 %pack.1.refs_6_.chunk.rest_3_ = bf16[216,256]{1,0:T(8,128)(2,1)S(1)} custom-call(bf16[96,512]{1,0:T(8,128)(2,1)} %latent.1, bf16[64,96]{1,0:T(8,128)(2,1)} %bitcast.1), custom_call_target="tpu_custom_call" | custom-call | tf_op jit(solution)/shard_map/pack/pallas_call | solution.py:314
  0.9 5.1 %collective-permute-start.5 = (bf16[216,256]{1,0:T(8,128)(2,1)S(1)}, bf16[216,256]{1,0:T(8,128)(2,1)S(1)}, u32[]{:S(2)}, u32[]{:S(2)}) collective-permute-start(bf16[216,256]{1,0:T(8,128)(2,1)S(1)} %pack.1.refs_6_.chunk.rest_3_), channel_id=1, source_target_pairs={{0,12},{1,9},{2,14},{3,11},{4,8},{5,13},{6,10},{7,15},{8,4},{9,1},... | collective-permute-start | bytes 331784 | tf_op jit(solution)/shard_map/ppermute | solution.py:299
  6.0 0.0 copy-start
  6.0 1.6 %collective-permute-start.3 = (bf16[216,256]{1,0:T(8,128)(2,1)S(1)}, bf16[216,256]{1,0:T(8,128)(2,1)S(1)}, u32[]{:S(2)}, u32[]{:S(2)}) collective-permute-start(bf16[216,256]{1,0:T(8,128)(2,1)S(1)} %room.1), channel_id=1, source_target_pairs={{0,2},{1,5},{2,0},{3,7},{4,6},{5,1},{6,4},{7,3},{8,10},{9,13},{10,... | collective-permute-start | bytes 331784 | tf_op jit(solution)/shard_map/ppermute | solution.py:299
  7.6 0.7 %collective-permute-start.1 = (bf16[216,256]{1,0:T(8,128)(2,1)S(1)}, bf16[216,256]{1,0:T(8,128)(2,1)S(1)}, u32[]{:S(2)}, u32[]{:S(2)}) collective-permute-start(bf16[216,256]{1,0:T(8,128)(2,1)S(1)} %room.1), channel_id=1, source_target_pairs={{1,7},{3,5},{5,3},{7,1},{9,15},{11,13},{13,11},{15,9},{17,23},{19,... | collective-permute-start | bytes 331784 | tf_op jit(solution)/shard_map/ppermute | solution.py:299
  8.3 0.0 copy-done
  8.3 1.4 %prepare.1 = (bf16[192,576]{1,0:T(8,128)(2,1)S(1)}, f32[1,96,192]{2,1,0:T(8,128)S(1)}, f32[1,96,480]{2,1,0:T(8,128)S(1)}, f32[1,96,96]{2,1,0:T(8,128)S(1)}, bf16[256,4096]{1,0:T(8,128)(2,1)S(1)}) custom-call(bf16[96,256]{1,0:T(8,128)(2,1)} %refs_0_.1, bf16[96,128]{1,0:T(8,128)(2,1)} %refs_1_.1, bf16[512,256]{1,0:T(8,128)(2,1)} %refs_2_.1, s32[16]{0:T(128)} %refs_3_.1, ...), custom_call_target="tpu_custom_call" | custom-call | tf_op jit(solution)/shard_map/prepare/pallas_call | solution.py:336
  9.6 1.0 %collective-permute-start = (bf16[192,576]{1,0:T(8,128)(2,1)S(1)}, bf16[192,576]{1,0:T(8,128)(2,1)S(1)}, u32[]{:S(2)}, u32[]{:S(2)}) collective-permute-start(bf16[192,576]{1,0:T(8,128)(2,1)S(1)} %get-tuple-element.17.rest_0_), channel_id=1, source_target_pairs={{0,1},{1,0},{2,3},{3,2},{4,5},{5,4},{6,7},{7,6},{8,9},{9,8},{10,11... | collective-permute-start | bytes 663560 | tf_op jit(solution)/shard_map/ppermute | solution.py:291
  10.7 0.1 collective-permute-start.9
  10.7 0.0 collective-permute-done.5.chunk.rest_6_
  10.7 1.0 %collective-permute-start.7 = (bf16[216,256]{1,0:T(8,128)(2,1)S(1)}, bf16[216,256]{1,0:T(8,128)(2,1)S(1)}, u32[]{:S(2)}, u32[]{:S(2)}) collective-permute-start(bf16[216,256]{1,0:T(8,128)(2,1)S(1)} %collective-permute-done.5.chunk.rest_6_), channel_id=1, source_target_pairs={{0,2},{1,3},{2,0},{3,1},{4,6},{5,7},{6,4},{7,5},{8,10},{9,11},{10,... | collective-permute-start | bytes 331784 | tf_op jit(solution)/shard_map/ppermute | solution.py:299
  11.7 0.0 collective-permute-done.3.rest_4_
  11.7 0.0 collective-permute-start.4
  11.7 0.0 collective-permute-done.1.rest_3_
  11.7 0.6 %collective-permute-start.2 = (bf16[216,256]{1,0:T(8,128)(2,1)S(1)}, bf16[216,256]{1,0:T(8,128)(2,1)S(1)}, u32[]{:S(2)}, u32[]{:S(2)}) collective-permute-start(bf16[216,256]{1,0:T(8,128)(2,1)S(1)} %collective-permute-done.1.rest_3_), channel_id=1, source_target_pairs={{0,1},{1,0},{2,3},{3,2},{4,5},{5,4},{6,7},{7,6},{8,9},{9,8},{10,11... | collective-permute-start | bytes 331784 | tf_op jit(solution)/shard_map/ppermute | solution.py:291
  12.3 0.0 collective-permute-done.rest_1_
  12.3 0.7 %first.1 = (f32[384,1]{1,0:T(8,128)S(1)}, f32[384,1]{1,0:T(8,128)S(1)}, f32[384,512]{1,0:T(8,128)S(1)}, bf16[216,256]{1,0:T(8,128)(2,1)S(1)}) custom-call(bf16[192,576]{1,0:T(8,128)(2,1)S(1)} %get-tuple-element.17.rest_0_, bf16[192,576]{1,0:T(8,128)(2,1)S(1)} %collective-permute-done.rest_1_, f32[1,96,192]{2,1,0:T(8,128)S(1)} %get-tuple-element.19.rest_2_, ...), custom_call_target="tpu_custom_call" | custom-call | flops 22000001024 | tf_op jit(solution)/shard_map/first/pallas_call | solution.py:302
  13.1 0.0 copy-start.1
  13.1 0.1 collective-permute-start.6
  13.2 3.1 %collective-permute-done.7.rest_8_ = bf16[216,256]{1,0:T(8,128)(2,1)S(1)} collective-permute-done((bf16[216,256]{1,0:T(8,128)(2,1)S(1)}, bf16[216,256]{1,0:T(8,128)(2,1)S(1)}, u32[]{:S(2)}, u32[]{:S(2)}) %collective-permute-start.7) | collective-permute-done | bytes 110624 | tf_op jit(solution)/shard_map/ppermute | solution.py:299
  16.2 0.0 collective-permute-start.8
  16.2 0.0 collective-permute-done.4.rest_5_
  16.2 0.0 collective-permute-done.2.rest_4_
  16.2 0.0 collective-permute-done.6.rest_7_
  16.2 1.1 %second.1 = (f32[384,1]{1,0:T(8,128)S(1)}, f32[384,1]{1,0:T(8,128)S(1)}, f32[384,512]{1,0:T(8,128)S(1)}) custom-call(bf16[192,576]{1,0:T(8,128)(2,1)S(1)} %get-tuple-element.17.rest_0_, bf16[192,576]{1,0:T(8,128)(2,1)S(1)} %collective-permute-done.rest_1_, f32[1,96,480]{2,1,0:T(8,128)S(1)} %get-tuple-element.18.rest_2_, ...), custom_call_target="tpu_custom_call" | custom-call | flops 1100000000 | tf_op jit(solution)/shard_map/second/pallas_call | solution.py:302
  17.3 0.2 %collective-permute-done.8.rest_6_ = bf16[216,256]{1,0:T(8,128)(2,1)S(1)} collective-permute-done((bf16[216,256]{1,0:T(8,128)(2,1)S(1)}, bf16[216,256]{1,0:T(8,128)(2,1)S(1)}, u32[]{:S(2)}, u32[]{:S(2)}) %collective-permute-start.8) | collective-permute-done | bytes 110624 | tf_op jit(solution)/shard_map/ppermute | solution.py:291
  17.5 0.0 collective-permute-done.9.rest_9_
  17.5 0.0 copy-done.1
  17.5 2.5 %finish.1 = bf16[96,3584]{1,0:T(8,128)(2,1)} custom-call(bf16[192,576]{1,0:T(8,128)(2,1)S(1)} %get-tuple-element.17.rest_0_, bf16[192,576]{1,0:T(8,128)(2,1)S(1)} %collective-permute-done.rest_1_, f32[384,1]{1,0:T(8,128)S(1)} %get-tuple-element.24.rest_2_, f32[384,1]{1,0:T(8,128)S(1)} %get-tuple-element.25.rest_3_, ...), custom_call_target="tpu_custom_call" | custom-call | tf_op jit(solution)/shard_map/finish/pallas_call | solution.py:408
  (2 shorter events, 0.0 us)
Async XLA Ops:
  0.9 9.8 %collective-permute-start.5 = (bf16[216,256]{1,0:T(8,128)(2,1)S(1)}, bf16[216,256]{1,0:T(8,128)(2,1)S(1)}, u32[]{:S(2)}, u32[]{:S(2)}) collective-permute-start(bf16[216,256]{1,0:T(8,128)(2,1)S(1)} %pack.1.refs_6_.chunk.rest_3_), channel_id=1, source_target_pairs={{0,12},{1,9},{2,14},{3,11},{4,8},{5,13},{6,10},{7,15},{8,4},{9,1},... | collective-permute-start | bytes 331784 | tf_op jit(solution)/shard_map/ppermute | solution.py:299
  6.0 2.2 %copy-start = (bf16[256,7168]{1,0:T(8,128)(2,1)S(1)}, bf16[256,7168]{1,0:T(8,128)(2,1)}, u32[]{:S(2)}) copy-start(bf16[256,7168]{1,0:T(8,128)(2,1)} %rest_8_.1) | copy-start | bytes 11010052
  6.0 5.7 %collective-permute-start.3 = (bf16[216,256]{1,0:T(8,128)(2,1)S(1)}, bf16[216,256]{1,0:T(8,128)(2,1)S(1)}, u32[]{:S(2)}, u32[]{:S(2)}) collective-permute-start(bf16[216,256]{1,0:T(8,128)(2,1)S(1)} %room.1), channel_id=1, source_target_pairs={{0,2},{1,5},{2,0},{3,7},{4,6},{5,1},{6,4},{7,3},{8,10},{9,13},{10,... | collective-permute-start | bytes 331784 | tf_op jit(solution)/shard_map/ppermute | solution.py:299
  7.6 4.1 %collective-permute-start.1 = (bf16[216,256]{1,0:T(8,128)(2,1)S(1)}, bf16[216,256]{1,0:T(8,128)(2,1)S(1)}, u32[]{:S(2)}, u32[]{:S(2)}) collective-permute-start(bf16[216,256]{1,0:T(8,128)(2,1)S(1)} %room.1), channel_id=1, source_target_pairs={{1,7},{3,5},{5,3},{7,1},{9,15},{11,13},{13,11},{15,9},{17,23},{19,... | collective-permute-start | bytes 331784 | tf_op jit(solution)/shard_map/ppermute | solution.py:299
  9.6 2.7 %collective-permute-start = (bf16[192,576]{1,0:T(8,128)(2,1)S(1)}, bf16[192,576]{1,0:T(8,128)(2,1)S(1)}, u32[]{:S(2)}, u32[]{:S(2)}) collective-permute-start(bf16[192,576]{1,0:T(8,128)(2,1)S(1)} %get-tuple-element.17.rest_0_), channel_id=1, source_target_pairs={{0,1},{1,0},{2,3},{3,2},{4,5},{5,4},{6,7},{7,6},{8,9},{9,8},{10,11... | collective-permute-start | bytes 663560 | tf_op jit(solution)/shard_map/ppermute | solution.py:291
  10.7 6.9 %collective-permute-start.9 = (bf16[256,4096]{1,0:T(8,128)(2,1)S(1)}, bf16[256,4096]{1,0:T(8,128)(2,1)S(1)}, u32[]{:S(2)}, u32[]{:S(2)}) collective-permute-start(bf16[256,4096]{1,0:T(8,128)(2,1)S(1)} %get-tuple-element.28), channel_id=1, source_target_pairs={{0,1},{1,0},{2,3},{3,2},{4,5},{5,4},{6,7},{7,6},{8,9},{9,8},{10,11... | collective-permute-start | bytes 6291464 | tf_op jit(solution)/shard_map/ppermute | solution.py:291
  10.7 5.5 %collective-permute-start.7 = (bf16[216,256]{1,0:T(8,128)(2,1)S(1)}, bf16[216,256]{1,0:T(8,128)(2,1)S(1)}, u32[]{:S(2)}, u32[]{:S(2)}) collective-permute-start(bf16[216,256]{1,0:T(8,128)(2,1)S(1)} %collective-permute-done.5.chunk.rest_6_), channel_id=1, source_target_pairs={{0,2},{1,3},{2,0},{3,1},{4,6},{5,7},{6,4},{7,5},{8,10},{9,11},{10,... | collective-permute-start | bytes 331784 | tf_op jit(solution)/shard_map/ppermute | solution.py:299
  11.7 4.5 %collective-permute-start.4 = (bf16[216,256]{1,0:T(8,128)(2,1)S(1)}, bf16[216,256]{1,0:T(8,128)(2,1)S(1)}, u32[]{:S(2)}, u32[]{:S(2)}) collective-permute-start(bf16[216,256]{1,0:T(8,128)(2,1)S(1)} %collective-permute-done.3.rest_4_), channel_id=1, source_target_pairs={{0,1},{1,0},{2,3},{3,2},{4,5},{5,4},{6,7},{7,6},{8,9},{9,8},{10,11... | collective-permute-start | bytes 331784 | tf_op jit(solution)/shard_map/ppermute | solution.py:291
  11.7 4.5 %collective-permute-start.2 = (bf16[216,256]{1,0:T(8,128)(2,1)S(1)}, bf16[216,256]{1,0:T(8,128)(2,1)S(1)}, u32[]{:S(2)}, u32[]{:S(2)}) collective-permute-start(bf16[216,256]{1,0:T(8,128)(2,1)S(1)} %collective-permute-done.1.rest_3_), channel_id=1, source_target_pairs={{0,1},{1,0},{2,3},{3,2},{4,5},{5,4},{6,7},{7,6},{8,9},{9,8},{10,11... | collective-permute-start | bytes 331784 | tf_op jit(solution)/shard_map/ppermute | solution.py:291
  13.1 4.5 %copy-start.1 = (bf16[512,256]{1,0:T(8,128)(2,1)S(1)}, bf16[512,256]{1,0:T(8,128)(2,1)}, u32[]{:S(2)}) copy-start(bf16[512,256]{1,0:T(8,128)(2,1)} %rest_7_.1) | copy-start | bytes 786436
  13.1 3.1 %collective-permute-start.6 = (bf16[216,256]{1,0:T(8,128)(2,1)S(1)}, bf16[216,256]{1,0:T(8,128)(2,1)S(1)}, u32[]{:S(2)}, u32[]{:S(2)}) collective-permute-start(bf16[216,256]{1,0:T(8,128)(2,1)S(1)} %get-tuple-element.20), channel_id=1, source_target_pairs={{0,1},{1,0},{2,3},{3,2},{4,5},{5,4},{6,7},{7,6},{8,9},{9,8},{10,11... | collective-permute-start | bytes 331784 | tf_op jit(solution)/shard_map/ppermute | solution.py:291
  16.2 1.3 %collective-permute-start.8 = (bf16[216,256]{1,0:T(8,128)(2,1)S(1)}, bf16[216,256]{1,0:T(8,128)(2,1)S(1)}, u32[]{:S(2)}, u32[]{:S(2)}) collective-permute-start(bf16[216,256]{1,0:T(8,128)(2,1)S(1)} %collective-permute-done.7.rest_8_), channel_id=1, source_target_pairs={{0,1},{1,0},{2,3},{3,2},{4,5},{5,4},{6,7},{7,6},{8,9},{9,8},{10,11... | collective-permute-start | bytes 331784 | tf_op jit(solution)/shard_map/ppermute | solution.py:291

commit v26 on v25

--- a/solution.py
+++ b/solution.py
@@ -19,7 +19,7 @@
 SMALL_VMEM = 20 * 1024 * 1024
 LARGE_VMEM = 56 * 1024 * 1024
 FAR = (6, 4)
-NEAR = (1, 2)
+NEAR = (2, 1)
 CORNER = (3, 3)
 RELAYED = (7, 5)
 

time: 20.3 us -> 20.3 us (level)
  local copies, waits for them, and re-layouts: 0.01 us -> 1.15 us
  starting transfers between devices: 10.1 us -> 9.41 us
  waiting for transfers between devices: 3.28 us -> 2.89 us
    unnamed x4, local copies, waits for them, and re-layouts: 0.01 us -> 1.15 us
    ppermute x4, starting transfers between devices: 8.3 us -> 7.28 us  [partners(): return lax.ppermute(array, ('ctx', 'heads'), pairs)]
    ppermute x4, waiting for transfers between devices: 3.06 us -> 2.68 us  [partners(): return lax.ppermute(array, ('ctx', 'heads'), pairs)]
    ppermute x6, starting transfers between devices: 1.76 us -> 2.14 us  [other_core(): return lax.ppermute(array, 'heads', [(0, 1), (1, 0)])]
where the time goes in v26:
time: 20.3 us; the launch traced here: 20.1 us
  starting transfers between devices  9.41 us (46%)
  Pallas kernels  6.57 us (32%)
  waiting for transfers between devices  2.89 us (14%)
  local copies, waits for them, and re-layouts  1.15 us (6%)
    ppermute x4, starting transfers between devices, partners(): return lax.ppermute(array, ('ctx', 'heads'), pairs)  7.28 us
    ppermute x4, waiting for transfers between devices, partners(): return lax.ppermute(array, ('ctx', 'heads'), pairs)  2.68 us
    pallas_call x1, Pallas kernels, per_device(): pl.pallas_call(functools.partial(finish_kernel, heads, len(last)), out_sh...  2.47 us
    ppermute x6, starting transfers between devices, other_core(): return lax.ppermute(array, 'heads', [(0, 1), (1, 0)])  2.14 us
    pallas_call x2, Pallas kernels, attend(): pl.pallas_call(functools.partial(chunks_kernel, len(chunks), len(old), pa...  1.83 us
    pallas_call x1, Pallas kernels, per_device(): pl.pallas_call(functools.partial(prepare_kernel, order), out_shape=[jax.S...  1.35 us
    unnamed x4, local copies, waits for them, and re-layouts  1.15 us
    pallas_call x1, Pallas kernels, per_device(): pl.pallas_call(pack_kernel, out_shape=jax.ShapeDtypeStruct((2 * rows + ro...  0.91 us
  transfers between devices with their start and end apart: 10, of which 2 were waited for; matrix products, arithmetic and copies ran while one was open for 0% of the time, Pallas kernels for 16%

profile of v26, /device:TPU:0, one launch (start us, length us, event | category | flops | bytes accessed | tf_op | source)
XLA Modules:
  0.0 20.1 jit_solution(1629663486658249985)
XLA Ops:
  0.0 0.9 %pack.1.refs_6_.chunk.rest_3_ = bf16[216,256]{1,0:T(8,128)(2,1)S(1)} custom-call(bf16[96,512]{1,0:T(8,128)(2,1)} %latent.1, bf16[64,96]{1,0:T(8,128)(2,1)} %bitcast.1), custom_call_target="tpu_custom_call" | custom-call | tf_op jit(solution)/shard_map/pack/pallas_call | solution.py:314
  0.9 5.1 %collective-permute-start.5 = (bf16[216,256]{1,0:T(8,128)(2,1)S(1)}, bf16[216,256]{1,0:T(8,128)(2,1)S(1)}, u32[]{:S(2)}, u32[]{:S(2)}) collective-permute-start(bf16[216,256]{1,0:T(8,128)(2,1)S(1)} %pack.1.refs_6_.chunk.rest_3_), channel_id=1, source_target_pairs={{0,12},{1,9},{2,14},{3,11},{4,8},{5,13},{6,10},{7,15},{8,4},{9,1},... | collective-permute-start | bytes 331784 | tf_op jit(solution)/shard_map/ppermute | solution.py:299
  6.0 0.0 copy-start
  6.0 0.1 collective-permute-start.3
  6.1 0.8 %collective-permute-start.1 = (bf16[216,256]{1,0:T(8,128)(2,1)S(1)}, bf16[216,256]{1,0:T(8,128)(2,1)S(1)}, u32[]{:S(2)}, u32[]{:S(2)}) collective-permute-start(bf16[216,256]{1,0:T(8,128)(2,1)S(1)} %room.1), channel_id=1, source_target_pairs={{1,7},{3,5},{5,3},{7,1},{9,15},{11,13},{13,11},{15,9},{17,23},{19,... | collective-permute-start | bytes 331784 | tf_op jit(solution)/shard_map/ppermute | solution.py:299
  6.9 1.1 %copy-done = bf16[256,7168]{1,0:T(8,128)(2,1)S(1)} copy-done((bf16[256,7168]{1,0:T(8,128)(2,1)S(1)}, bf16[256,7168]{1,0:T(8,128)(2,1)}, u32[]{:S(2)}) %copy-start) | copy-done | bytes 3670040
  8.1 1.3 %prepare.1 = (bf16[192,576]{1,0:T(8,128)(2,1)S(1)}, f32[1,96,192]{2,1,0:T(8,128)S(1)}, f32[1,96,480]{2,1,0:T(8,128)S(1)}, f32[1,96,96]{2,1,0:T(8,128)S(1)}, bf16[256,4096]{1,0:T(8,128)(2,1)S(1)}) custom-call(bf16[96,256]{1,0:T(8,128)(2,1)} %refs_0_.1, bf16[96,128]{1,0:T(8,128)(2,1)} %refs_1_.1, bf16[512,256]{1,0:T(8,128)(2,1)} %refs_2_.1, s32[16]{0:T(128)} %refs_3_.1, ...), custom_call_target="tpu_custom_call" | custom-call | tf_op jit(solution)/shard_map/prepare/pallas_call | solution.py:336
  9.4 1.3 %collective-permute-start = (bf16[192,576]{1,0:T(8,128)(2,1)S(1)}, bf16[192,576]{1,0:T(8,128)(2,1)S(1)}, u32[]{:S(2)}, u32[]{:S(2)}) collective-permute-start(bf16[192,576]{1,0:T(8,128)(2,1)S(1)} %get-tuple-element.17.rest_0_), channel_id=1, source_target_pairs={{0,1},{1,0},{2,3},{3,2},{4,5},{5,4},{6,7},{7,6},{8,9},{9,8},{10,11... | collective-permute-start | bytes 663560 | tf_op jit(solution)/shard_map/ppermute | solution.py:291
  10.7 0.1 collective-permute-start.9
  10.8 0.0 collective-permute-done.5.chunk.rest_6_
  10.8 1.3 %collective-permute-start.7 = (bf16[216,256]{1,0:T(8,128)(2,1)S(1)}, bf16[216,256]{1,0:T(8,128)(2,1)S(1)}, u32[]{:S(2)}, u32[]{:S(2)}) collective-permute-start(bf16[216,256]{1,0:T(8,128)(2,1)S(1)} %collective-permute-done.5.chunk.rest_6_), channel_id=1, source_target_pairs={{0,2},{1,3},{2,0},{3,1},{4,6},{5,7},{6,4},{7,5},{8,10},{9,11},{10,... | collective-permute-start | bytes 331784 | tf_op jit(solution)/shard_map/ppermute | solution.py:299
  12.1 0.0 collective-permute-done.3.rest_4_
  12.1 0.2 collective-permute-start.4
  12.3 0.0 collective-permute-done.1.rest_3_
  12.3 0.5 %collective-permute-start.2 = (bf16[216,256]{1,0:T(8,128)(2,1)S(1)}, bf16[216,256]{1,0:T(8,128)(2,1)S(1)}, u32[]{:S(2)}, u32[]{:S(2)}) collective-permute-start(bf16[216,256]{1,0:T(8,128)(2,1)S(1)} %collective-permute-done.1.rest_3_), channel_id=1, source_target_pairs={{0,1},{1,0},{2,3},{3,2},{4,5},{5,4},{6,7},{7,6},{8,9},{9,8},{10,11... | collective-permute-start | bytes 331784 | tf_op jit(solution)/shard_map/ppermute | solution.py:291
  12.8 0.0 collective-permute-done.rest_1_
  12.8 0.7 %first.1 = (f32[384,1]{1,0:T(8,128)S(1)}, f32[384,1]{1,0:T(8,128)S(1)}, f32[384,512]{1,0:T(8,128)S(1)}, bf16[216,256]{1,0:T(8,128)(2,1)S(1)}) custom-call(bf16[192,576]{1,0:T(8,128)(2,1)S(1)} %get-tuple-element.17.rest_0_, bf16[192,576]{1,0:T(8,128)(2,1)S(1)} %collective-permute-done.rest_1_, f32[1,96,192]{2,1,0:T(8,128)S(1)} %get-tuple-element.19.rest_2_, ...), custom_call_target="tpu_custom_call" | custom-call | flops 22000001024 | tf_op jit(solution)/shard_map/first/pallas_call | solution.py:302
  13.5 0.0 copy-start.1
  13.6 0.1 collective-permute-start.6
  13.6 2.7 %collective-permute-done.7.rest_8_ = bf16[216,256]{1,0:T(8,128)(2,1)S(1)} collective-permute-done((bf16[216,256]{1,0:T(8,128)(2,1)S(1)}, bf16[216,256]{1,0:T(8,128)(2,1)S(1)}, u32[]{:S(2)}, u32[]{:S(2)}) %collective-permute-start.7) | collective-permute-done | bytes 110624 | tf_op jit(solution)/shard_map/ppermute | solution.py:299
  16.3 0.0 collective-permute-start.8
  16.3 0.0 collective-permute-done.4.rest_5_
  16.3 0.0 collective-permute-done.2.rest_4_
  16.3 0.0 collective-permute-done.6.rest_7_
  16.3 1.1 %second.1 = (f32[384,1]{1,0:T(8,128)S(1)}, f32[384,1]{1,0:T(8,128)S(1)}, f32[384,512]{1,0:T(8,128)S(1)}) custom-call(bf16[192,576]{1,0:T(8,128)(2,1)S(1)} %get-tuple-element.17.rest_0_, bf16[192,576]{1,0:T(8,128)(2,1)S(1)} %collective-permute-done.rest_1_, f32[1,96,480]{2,1,0:T(8,128)S(1)} %get-tuple-element.18.rest_2_, ...), custom_call_target="tpu_custom_call" | custom-call | flops 1100000000 | tf_op jit(solution)/shard_map/second/pallas_call | solution.py:302
  17.4 0.2 collective-permute-done.8.rest_6_
  17.6 0.0 collective-permute-done.9.rest_9_
  17.6 0.0 copy-done.1
  17.6 2.5 %finish.1 = bf16[96,3584]{1,0:T(8,128)(2,1)} custom-call(bf16[192,576]{1,0:T(8,128)(2,1)S(1)} %get-tuple-element.17.rest_0_, bf16[192,576]{1,0:T(8,128)(2,1)S(1)} %collective-permute-done.rest_1_, f32[384,1]{1,0:T(8,128)S(1)} %get-tuple-element.24.rest_2_, f32[384,1]{1,0:T(8,128)S(1)} %get-tuple-element.25.rest_3_, ...), custom_call_target="tpu_custom_call" | custom-call | tf_op jit(solution)/shard_map/finish/pallas_call | solution.py:408
  (2 shorter events, 0.0 us)
Async XLA Ops:
  0.9 9.9 %collective-permute-start.5 = (bf16[216,256]{1,0:T(8,128)(2,1)S(1)}, bf16[216,256]{1,0:T(8,128)(2,1)S(1)}, u32[]{:S(2)}, u32[]{:S(2)}) collective-permute-start(bf16[216,256]{1,0:T(8,128)(2,1)S(1)} %pack.1.refs_6_.chunk.rest_3_), channel_id=1, source_target_pairs={{0,12},{1,9},{2,14},{3,11},{4,8},{5,13},{6,10},{7,15},{8,4},{9,1},... | collective-permute-start | bytes 331784 | tf_op jit(solution)/shard_map/ppermute | solution.py:299
  6.0 2.0 %copy-start = (bf16[256,7168]{1,0:T(8,128)(2,1)S(1)}, bf16[256,7168]{1,0:T(8,128)(2,1)}, u32[]{:S(2)}) copy-start(bf16[256,7168]{1,0:T(8,128)(2,1)} %rest_8_.1) | copy-start | bytes 11010052
  6.0 6.1 %collective-permute-start.3 = (bf16[216,256]{1,0:T(8,128)(2,1)S(1)}, bf16[216,256]{1,0:T(8,128)(2,1)S(1)}, u32[]{:S(2)}, u32[]{:S(2)}) collective-permute-start(bf16[216,256]{1,0:T(8,128)(2,1)S(1)} %room.1), channel_id=1, source_target_pairs={{0,4},{1,3},{2,6},{3,1},{4,0},{5,7},{6,2},{7,5},{8,12},{9,11},{10,... | collective-permute-start | bytes 331784 | tf_op jit(solution)/shard_map/ppermute | solution.py:299
  6.1 6.2 %collective-permute-start.1 = (bf16[216,256]{1,0:T(8,128)(2,1)S(1)}, bf16[216,256]{1,0:T(8,128)(2,1)S(1)}, u32[]{:S(2)}, u32[]{:S(2)}) collective-permute-start(bf16[216,256]{1,0:T(8,128)(2,1)S(1)} %room.1), channel_id=1, source_target_pairs={{1,7},{3,5},{5,3},{7,1},{9,15},{11,13},{13,11},{15,9},{17,23},{19,... | collective-permute-start | bytes 331784 | tf_op jit(solution)/shard_map/ppermute | solution.py:299
  9.4 3.4 %collective-permute-start = (bf16[192,576]{1,0:T(8,128)(2,1)S(1)}, bf16[192,576]{1,0:T(8,128)(2,1)S(1)}, u32[]{:S(2)}, u32[]{:S(2)}) collective-permute-start(bf16[192,576]{1,0:T(8,128)(2,1)S(1)} %get-tuple-element.17.rest_0_), channel_id=1, source_target_pairs={{0,1},{1,0},{2,3},{3,2},{4,5},{5,4},{6,7},{7,6},{8,9},{9,8},{10,11... | collective-permute-start | bytes 663560 | tf_op jit(solution)/shard_map/ppermute | solution.py:291
  10.7 6.9 %collective-permute-start.9 = (bf16[256,4096]{1,0:T(8,128)(2,1)S(1)}, bf16[256,4096]{1,0:T(8,128)(2,1)S(1)}, u32[]{:S(2)}, u32[]{:S(2)}) collective-permute-start(bf16[256,4096]{1,0:T(8,128)(2,1)S(1)} %get-tuple-element.28), channel_id=1, source_target_pairs={{0,1},{1,0},{2,3},{3,2},{4,5},{5,4},{6,7},{7,6},{8,9},{9,8},{10,11... | collective-permute-start | bytes 6291464 | tf_op jit(solution)/shard_map/ppermute | solution.py:291
  10.8 5.5 %collective-permute-start.7 = (bf16[216,256]{1,0:T(8,128)(2,1)S(1)}, bf16[216,256]{1,0:T(8,128)(2,1)S(1)}, u32[]{:S(2)}, u32[]{:S(2)}) collective-permute-start(bf16[216,256]{1,0:T(8,128)(2,1)S(1)} %collective-permute-done.5.chunk.rest_6_), channel_id=1, source_target_pairs={{0,2},{1,3},{2,0},{3,1},{4,6},{5,7},{6,4},{7,5},{8,10},{9,11},{10,... | collective-permute-start | bytes 331784 | tf_op jit(solution)/shard_map/ppermute | solution.py:299
  12.1 4.2 %collective-permute-start.4 = (bf16[216,256]{1,0:T(8,128)(2,1)S(1)}, bf16[216,256]{1,0:T(8,128)(2,1)S(1)}, u32[]{:S(2)}, u32[]{:S(2)}) collective-permute-start(bf16[216,256]{1,0:T(8,128)(2,1)S(1)} %collective-permute-done.3.rest_4_), channel_id=1, source_target_pairs={{0,1},{1,0},{2,3},{3,2},{4,5},{5,4},{6,7},{7,6},{8,9},{9,8},{10,11... | collective-permute-start | bytes 331784 | tf_op jit(solution)/shard_map/ppermute | solution.py:291
  12.3 4.0 %collective-permute-start.2 = (bf16[216,256]{1,0:T(8,128)(2,1)S(1)}, bf16[216,256]{1,0:T(8,128)(2,1)S(1)}, u32[]{:S(2)}, u32[]{:S(2)}) collective-permute-start(bf16[216,256]{1,0:T(8,128)(2,1)S(1)} %collective-permute-done.1.rest_3_), channel_id=1, source_target_pairs={{0,1},{1,0},{2,3},{3,2},{4,5},{5,4},{6,7},{7,6},{8,9},{9,8},{10,11... | collective-permute-start | bytes 331784 | tf_op jit(solution)/shard_map/ppermute | solution.py:291
  13.5 4.1 %copy-start.1 = (bf16[512,256]{1,0:T(8,128)(2,1)S(1)}, bf16[512,256]{1,0:T(8,128)(2,1)}, u32[]{:S(2)}) copy-start(bf16[512,256]{1,0:T(8,128)(2,1)} %rest_7_.1) | copy-start | bytes 786436
  13.6 2.8 %collective-permute-start.6 = (bf16[216,256]{1,0:T(8,128)(2,1)S(1)}, bf16[216,256]{1,0:T(8,128)(2,1)S(1)}, u32[]{:S(2)}, u32[]{:S(2)}) collective-permute-start(bf16[216,256]{1,0:T(8,128)(2,1)S(1)} %get-tuple-element.20), channel_id=1, source_target_pairs={{0,1},{1,0},{2,3},{3,2},{4,5},{5,4},{6,7},{7,6},{8,9},{9,8},{10,11... | collective-permute-start | bytes 331784 | tf_op jit(solution)/shard_map/ppermute | solution.py:291
  16.3 1.3 %collective-permute-start.8 = (bf16[216,256]{1,0:T(8,128)(2,1)S(1)}, bf16[216,256]{1,0:T(8,128)(2,1)S(1)}, u32[]{:S(2)}, u32[]{:S(2)}) collective-permute-start(bf16[216,256]{1,0:T(8,128)(2,1)S(1)} %collective-permute-done.7.rest_8_), channel_id=1, source_target_pairs={{0,1},{1,0},{2,3},{3,2},{4,5},{5,4},{6,7},{7,6},{8,9},{9,8},{10,11... | collective-permute-start | bytes 331784 | tf_op jit(solution)/shard_map/ppermute | solution.py:291

commit v27 on v26

--- a/solution.py
+++ b/solution.py
@@ -18,10 +18,10 @@
 PREPARE_COST, ROOM_COST, GATE_COST, FIRST_COST, SECOND_COST = 0, 4, 8, 20, 1
 SMALL_VMEM = 20 * 1024 * 1024
 LARGE_VMEM = 56 * 1024 * 1024
-FAR = (6, 4)
+FAR = (4, 6)
 NEAR = (2, 1)
 CORNER = (3, 3)
-RELAYED = (7, 5)
+RELAYED = (5, 7)
 
 
 def vmem():

time: 20.3 us -> 19.8 us (0.975)
  starting transfers between devices: 9.41 us -> 10.6 us
  local copies, waits for them, and re-layouts: 1.15 us -> 0.01 us
  waiting for transfers between devices: 2.89 us -> 2.33 us
    unnamed x4, local copies, waits for them, and re-layouts: 1.15 us -> 0.01 us
    ppermute x4, starting transfers between devices: 7.28 us -> 7.96 us  [partners(): return lax.ppermute(array, ('ctx', 'heads'), pairs)]
    ppermute x4, waiting for transfers between devices: 2.68 us -> 2.12 us  [partners(): return lax.ppermute(array, ('ctx', 'heads'), pairs)]
    ppermute x6, starting transfers between devices: 2.14 us -> 2.63 us  [other_core(): return lax.ppermute(array, 'heads', [(0, 1), (1, 0)])]
  transfers between devices with their start and end apart: 10 -> 10, of which waited for: 2 -> 3; matrix products, arithmetic and copies ran while one was open for 0% -> 0% of each run, Pallas kernels for 16% -> 16%
where the time goes in v27:
time: 19.8 us; the launch traced here: 19.6 us
  starting transfers between devices  10.6 us (54%)
  Pallas kernels  6.58 us (33%)
  waiting for transfers between devices  2.33 us (12%)
    ppermute x4, starting transfers between devices, partners(): return lax.ppermute(array, ('ctx', 'heads'), pairs)  7.96 us
    ppermute x6, starting transfers between devices, other_core(): return lax.ppermute(array, 'heads', [(0, 1), (1, 0)])  2.63 us
    pallas_call x1, Pallas kernels, per_device(): pl.pallas_call(functools.partial(finish_kernel, heads, len(last)), out_sh...  2.47 us
    ppermute x4, waiting for transfers between devices, partners(): return lax.ppermute(array, ('ctx', 'heads'), pairs)  2.12 us
    pallas_call x2, Pallas kernels, attend(): pl.pallas_call(functools.partial(chunks_kernel, len(chunks), len(old), pa...  1.83 us
    pallas_call x1, Pallas kernels, per_device(): pl.pallas_call(functools.partial(prepare_kernel, order), out_shape=[jax.S...  1.35 us
    pallas_call x1, Pallas kernels, per_device(): pl.pallas_call(pack_kernel, out_shape=jax.ShapeDtypeStruct((2 * rows + ro...  0.91 us
  transfers between devices with their start and end apart: 10, of which 3 were waited for; matrix products, arithmetic and copies ran while one was open for 0% of the time, Pallas kernels for 16%

profile of v27, /device:TPU:0, one launch (start us, length us, event | category | flops | bytes accessed | tf_op | source)
XLA Modules:
  0.0 19.6 jit_solution(2818111435805273937)
XLA Ops:
  0.0 0.9 %pack.1.refs_6_.chunk.rest_3_ = bf16[216,256]{1,0:T(8,128)(2,1)S(1)} custom-call(bf16[96,512]{1,0:T(8,128)(2,1)} %latent.1, bf16[64,96]{1,0:T(8,128)(2,1)} %bitcast.1), custom_call_target="tpu_custom_call" | custom-call | tf_op jit(solution)/shard_map/pack/pallas_call | solution.py:314
  0.9 4.1 %collective-permute-start.5 = (bf16[216,256]{1,0:T(8,128)(2,1)S(1)}, bf16[216,256]{1,0:T(8,128)(2,1)S(1)}, u32[]{:S(2)}, u32[]{:S(2)}) collective-permute-start(bf16[216,256]{1,0:T(8,128)(2,1)S(1)} %pack.1.refs_6_.chunk.rest_3_), channel_id=1, source_target_pairs={{0,8},{1,13},{2,10},{3,15},{4,12},{5,9},{6,14},{7,11},{8,0},{9,5},... | collective-permute-start | bytes 331784 | tf_op jit(solution)/shard_map/ppermute | solution.py:299
  5.0 0.0 copy-start
  5.0 1.6 %collective-permute-start.3 = (bf16[216,256]{1,0:T(8,128)(2,1)S(1)}, bf16[216,256]{1,0:T(8,128)(2,1)S(1)}, u32[]{:S(2)}, u32[]{:S(2)}) collective-permute-start(bf16[216,256]{1,0:T(8,128)(2,1)S(1)} %room.1), channel_id=1, source_target_pairs={{0,4},{1,3},{2,6},{3,1},{4,0},{5,7},{6,2},{7,5},{8,12},{9,11},{10,... | collective-permute-start | bytes 331784 | tf_op jit(solution)/shard_map/ppermute | solution.py:299
  6.7 0.7 %collective-permute-start.1 = (bf16[216,256]{1,0:T(8,128)(2,1)S(1)}, bf16[216,256]{1,0:T(8,128)(2,1)S(1)}, u32[]{:S(2)}, u32[]{:S(2)}) collective-permute-start(bf16[216,256]{1,0:T(8,128)(2,1)S(1)} %room.1), channel_id=1, source_target_pairs={{1,7},{3,5},{5,3},{7,1},{9,15},{11,13},{13,11},{15,9},{17,23},{19,... | collective-permute-start | bytes 331784 | tf_op jit(solution)/shard_map/ppermute | solution.py:299
  7.3 0.0 copy-done
  7.3 1.4 %prepare.1 = (bf16[192,576]{1,0:T(8,128)(2,1)S(1)}, f32[1,96,192]{2,1,0:T(8,128)S(1)}, f32[1,96,480]{2,1,0:T(8,128)S(1)}, f32[1,96,96]{2,1,0:T(8,128)S(1)}, bf16[256,4096]{1,0:T(8,128)(2,1)S(1)}) custom-call(bf16[96,256]{1,0:T(8,128)(2,1)} %refs_0_.1, bf16[96,128]{1,0:T(8,128)(2,1)} %refs_1_.1, bf16[512,256]{1,0:T(8,128)(2,1)} %refs_2_.1, s32[16]{0:T(128)} %refs_3_.1, ...), custom_call_target="tpu_custom_call" | custom-call | tf_op jit(solution)/shard_map/prepare/pallas_call | solution.py:336
  8.7 1.5 %collective-permute-start = (bf16[192,576]{1,0:T(8,128)(2,1)S(1)}, bf16[192,576]{1,0:T(8,128)(2,1)S(1)}, u32[]{:S(2)}, u32[]{:S(2)}) collective-permute-start(bf16[192,576]{1,0:T(8,128)(2,1)S(1)} %get-tuple-element.17.rest_0_), channel_id=1, source_target_pairs={{0,1},{1,0},{2,3},{3,2},{4,5},{5,4},{6,7},{7,6},{8,9},{9,8},{10,11... | collective-permute-start | bytes 663560 | tf_op jit(solution)/shard_map/ppermute | solution.py:291
  10.2 0.1 collective-permute-start.9
  10.3 0.4 %collective-permute-done.5.chunk.rest_6_ = bf16[216,256]{1,0:T(8,128)(2,1)S(1)} collective-permute-done((bf16[216,256]{1,0:T(8,128)(2,1)S(1)}, bf16[216,256]{1,0:T(8,128)(2,1)S(1)}, u32[]{:S(2)}, u32[]{:S(2)}) %collective-permute-start.5) | collective-permute-done | bytes 110624 | tf_op jit(solution)/shard_map/ppermute | solution.py:299
  10.7 1.6 %collective-permute-start.7 = (bf16[216,256]{1,0:T(8,128)(2,1)S(1)}, bf16[216,256]{1,0:T(8,128)(2,1)S(1)}, u32[]{:S(2)}, u32[]{:S(2)}) collective-permute-start(bf16[216,256]{1,0:T(8,128)(2,1)S(1)} %collective-permute-done.5.chunk.rest_6_), channel_id=1, source_target_pairs={{0,2},{1,3},{2,0},{3,1},{4,6},{5,7},{6,4},{7,5},{8,10},{9,11},{10,... | collective-permute-start | bytes 331784 | tf_op jit(solution)/shard_map/ppermute | solution.py:299
  12.3 0.0 collective-permute-done.3.rest_4_
  12.3 0.0 collective-permute-start.4
  12.3 0.0 collective-permute-done.1.rest_3_
  12.3 1.0 %collective-permute-start.2 = (bf16[216,256]{1,0:T(8,128)(2,1)S(1)}, bf16[216,256]{1,0:T(8,128)(2,1)S(1)}, u32[]{:S(2)}, u32[]{:S(2)}) collective-permute-start(bf16[216,256]{1,0:T(8,128)(2,1)S(1)} %collective-permute-done.1.rest_3_), channel_id=1, source_target_pairs={{0,1},{1,0},{2,3},{3,2},{4,5},{5,4},{6,7},{7,6},{8,9},{9,8},{10,11... | collective-permute-start | bytes 331784 | tf_op jit(solution)/shard_map/ppermute | solution.py:291
  13.3 0.0 collective-permute-done.rest_1_
  13.3 0.7 %first.1 = (f32[384,1]{1,0:T(8,128)S(1)}, f32[384,1]{1,0:T(8,128)S(1)}, f32[384,512]{1,0:T(8,128)S(1)}, bf16[216,256]{1,0:T(8,128)(2,1)S(1)}) custom-call(bf16[192,576]{1,0:T(8,128)(2,1)S(1)} %get-tuple-element.17.rest_0_, bf16[192,576]{1,0:T(8,128)(2,1)S(1)} %collective-permute-done.rest_1_, f32[1,96,192]{2,1,0:T(8,128)S(1)} %get-tuple-element.19.rest_2_, ...), custom_call_target="tpu_custom_call" | custom-call | flops 22000001024 | tf_op jit(solution)/shard_map/first/pallas_call | solution.py:302
  14.0 0.0 copy-start.1
  14.0 0.1 collective-permute-start.6
  14.1 1.7 %collective-permute-done.7.rest_8_ = bf16[216,256]{1,0:T(8,128)(2,1)S(1)} collective-permute-done((bf16[216,256]{1,0:T(8,128)(2,1)S(1)}, bf16[216,256]{1,0:T(8,128)(2,1)S(1)}, u32[]{:S(2)}, u32[]{:S(2)}) %collective-permute-start.7) | collective-permute-done | bytes 110624 | tf_op jit(solution)/shard_map/ppermute | solution.py:299
  15.8 0.0 collective-permute-start.8
  15.8 0.0 collective-permute-done.4.rest_5_
  15.8 0.0 collective-permute-done.2.rest_4_
  15.8 0.0 collective-permute-done.6.rest_7_
  15.8 1.1 %second.1 = (f32[384,1]{1,0:T(8,128)S(1)}, f32[384,1]{1,0:T(8,128)S(1)}, f32[384,512]{1,0:T(8,128)S(1)}) custom-call(bf16[192,576]{1,0:T(8,128)(2,1)S(1)} %get-tuple-element.17.rest_0_, bf16[192,576]{1,0:T(8,128)(2,1)S(1)} %collective-permute-done.rest_1_, f32[1,96,480]{2,1,0:T(8,128)S(1)} %get-tuple-element.18.rest_2_, ...), custom_call_target="tpu_custom_call" | custom-call | flops 1100000000 | tf_op jit(solution)/shard_map/second/pallas_call | solution.py:302
  16.9 0.2 %collective-permute-done.8.rest_6_ = bf16[216,256]{1,0:T(8,128)(2,1)S(1)} collective-permute-done((bf16[216,256]{1,0:T(8,128)(2,1)S(1)}, bf16[216,256]{1,0:T(8,128)(2,1)S(1)}, u32[]{:S(2)}, u32[]{:S(2)}) %collective-permute-start.8) | collective-permute-done | bytes 110624 | tf_op jit(solution)/shard_map/ppermute | solution.py:291
  17.1 0.0 collective-permute-done.9.rest_9_
  17.1 0.0 copy-done.1
  17.1 2.5 %finish.1 = bf16[96,3584]{1,0:T(8,128)(2,1)} custom-call(bf16[192,576]{1,0:T(8,128)(2,1)S(1)} %get-tuple-element.17.rest_0_, bf16[192,576]{1,0:T(8,128)(2,1)S(1)} %collective-permute-done.rest_1_, f32[384,1]{1,0:T(8,128)S(1)} %get-tuple-element.24.rest_2_, f32[384,1]{1,0:T(8,128)S(1)} %get-tuple-element.25.rest_3_, ...), custom_call_target="tpu_custom_call" | custom-call | tf_op jit(solution)/shard_map/finish/pallas_call | solution.py:408
  (2 shorter events, 0.0 us)
Async XLA Ops:
  0.9 9.8 %collective-permute-start.5 = (bf16[216,256]{1,0:T(8,128)(2,1)S(1)}, bf16[216,256]{1,0:T(8,128)(2,1)S(1)}, u32[]{:S(2)}, u32[]{:S(2)}) collective-permute-start(bf16[216,256]{1,0:T(8,128)(2,1)S(1)} %pack.1.refs_6_.chunk.rest_3_), channel_id=1, source_target_pairs={{0,8},{1,13},{2,10},{3,15},{4,12},{5,9},{6,14},{7,11},{8,0},{9,5},... | collective-permute-start | bytes 331784 | tf_op jit(solution)/shard_map/ppermute | solution.py:299
  5.0 2.3 %copy-start = (bf16[256,7168]{1,0:T(8,128)(2,1)S(1)}, bf16[256,7168]{1,0:T(8,128)(2,1)}, u32[]{:S(2)}) copy-start(bf16[256,7168]{1,0:T(8,128)(2,1)} %rest_8_.1) | copy-start | bytes 11010052
  5.0 7.3 %collective-permute-start.3 = (bf16[216,256]{1,0:T(8,128)(2,1)S(1)}, bf16[216,256]{1,0:T(8,128)(2,1)S(1)}, u32[]{:S(2)}, u32[]{:S(2)}) collective-permute-start(bf16[216,256]{1,0:T(8,128)(2,1)S(1)} %room.1), channel_id=1, source_target_pairs={{0,4},{1,3},{2,6},{3,1},{4,0},{5,7},{6,2},{7,5},{8,12},{9,11},{10,... | collective-permute-start | bytes 331784 | tf_op jit(solution)/shard_map/ppermute | solution.py:299
  6.7 5.6 %collective-permute-start.1 = (bf16[216,256]{1,0:T(8,128)(2,1)S(1)}, bf16[216,256]{1,0:T(8,128)(2,1)S(1)}, u32[]{:S(2)}, u32[]{:S(2)}) collective-permute-start(bf16[216,256]{1,0:T(8,128)(2,1)S(1)} %room.1), channel_id=1, source_target_pairs={{1,7},{3,5},{5,3},{7,1},{9,15},{11,13},{13,11},{15,9},{17,23},{19,... | collective-permute-start | bytes 331784 | tf_op jit(solution)/shard_map/ppermute | solution.py:299
  8.7 4.5 %collective-permute-start = (bf16[192,576]{1,0:T(8,128)(2,1)S(1)}, bf16[192,576]{1,0:T(8,128)(2,1)S(1)}, u32[]{:S(2)}, u32[]{:S(2)}) collective-permute-start(bf16[192,576]{1,0:T(8,128)(2,1)S(1)} %get-tuple-element.17.rest_0_), channel_id=1, source_target_pairs={{0,1},{1,0},{2,3},{3,2},{4,5},{5,4},{6,7},{7,6},{8,9},{9,8},{10,11... | collective-permute-start | bytes 663560 | tf_op jit(solution)/shard_map/ppermute | solution.py:291
  10.2 6.9 %collective-permute-start.9 = (bf16[256,4096]{1,0:T(8,128)(2,1)S(1)}, bf16[256,4096]{1,0:T(8,128)(2,1)S(1)}, u32[]{:S(2)}, u32[]{:S(2)}) collective-permute-start(bf16[256,4096]{1,0:T(8,128)(2,1)S(1)} %get-tuple-element.28), channel_id=1, source_target_pairs={{0,1},{1,0},{2,3},{3,2},{4,5},{5,4},{6,7},{7,6},{8,9},{9,8},{10,11... | collective-permute-start | bytes 6291464 | tf_op jit(solution)/shard_map/ppermute | solution.py:291
  10.7 5.1 %collective-permute-start.7 = (bf16[216,256]{1,0:T(8,128)(2,1)S(1)}, bf16[216,256]{1,0:T(8,128)(2,1)S(1)}, u32[]{:S(2)}, u32[]{:S(2)}) collective-permute-start(bf16[216,256]{1,0:T(8,128)(2,1)S(1)} %collective-permute-done.5.chunk.rest_6_), channel_id=1, source_target_pairs={{0,2},{1,3},{2,0},{3,1},{4,6},{5,7},{6,4},{7,5},{8,10},{9,11},{10,... | collective-permute-start | bytes 331784 | tf_op jit(solution)/shard_map/ppermute | solution.py:299
  12.3 3.5 %collective-permute-start.4 = (bf16[216,256]{1,0:T(8,128)(2,1)S(1)}, bf16[216,256]{1,0:T(8,128)(2,1)S(1)}, u32[]{:S(2)}, u32[]{:S(2)}) collective-permute-start(bf16[216,256]{1,0:T(8,128)(2,1)S(1)} %collective-permute-done.3.rest_4_), channel_id=1, source_target_pairs={{0,1},{1,0},{2,3},{3,2},{4,5},{5,4},{6,7},{7,6},{8,9},{9,8},{10,11... | collective-permute-start | bytes 331784 | tf_op jit(solution)/shard_map/ppermute | solution.py:291
  12.3 3.5 %collective-permute-start.2 = (bf16[216,256]{1,0:T(8,128)(2,1)S(1)}, bf16[216,256]{1,0:T(8,128)(2,1)S(1)}, u32[]{:S(2)}, u32[]{:S(2)}) collective-permute-start(bf16[216,256]{1,0:T(8,128)(2,1)S(1)} %collective-permute-done.1.rest_3_), channel_id=1, source_target_pairs={{0,1},{1,0},{2,3},{3,2},{4,5},{5,4},{6,7},{7,6},{8,9},{9,8},{10,11... | collective-permute-start | bytes 331784 | tf_op jit(solution)/shard_map/ppermute | solution.py:291
  14.0 3.1 %copy-start.1 = (bf16[512,256]{1,0:T(8,128)(2,1)S(1)}, bf16[512,256]{1,0:T(8,128)(2,1)}, u32[]{:S(2)}) copy-start(bf16[512,256]{1,0:T(8,128)(2,1)} %rest_7_.1) | copy-start | bytes 786436
  14.0 1.8 %collective-permute-start.6 = (bf16[216,256]{1,0:T(8,128)(2,1)S(1)}, bf16[216,256]{1,0:T(8,128)(2,1)S(1)}, u32[]{:S(2)}, u32[]{:S(2)}) collective-permute-start(bf16[216,256]{1,0:T(8,128)(2,1)S(1)} %get-tuple-element.20), channel_id=1, source_target_pairs={{0,1},{1,0},{2,3},{3,2},{4,5},{5,4},{6,7},{7,6},{8,9},{9,8},{10,11... | collective-permute-start | bytes 331784 | tf_op jit(solution)/shard_map/ppermute | solution.py:291
  15.8 1.3 %collective-permute-start.8 = (bf16[216,256]{1,0:T(8,128)(2,1)S(1)}, bf16[216,256]{1,0:T(8,128)(2,1)S(1)}, u32[]{:S(2)}, u32[]{:S(2)}) collective-permute-start(bf16[216,256]{1,0:T(8,128)(2,1)S(1)} %collective-permute-done.7.rest_8_), channel_id=1, source_target_pairs={{0,1},{1,0},{2,3},{3,2},{4,5},{5,4},{6,7},{7,6},{8,9},{9,8},{10,11... | collective-permute-start | bytes 331784 | tf_op jit(solution)/shard_map/ppermute | solution.py:291
